TPU v7x, 32 devices: a whole 2x2x4 slice. The times are simulated.
32 devices in a mesh: wide: 8 (over y, x, core), narrow: 4 (over z).
Axes of the slice: x: 2, y: 2, z: 4, core: 2. Of those that a mesh axis runs over, the one named last changes fastest.
Arguments:
- inputs: bfloat16 [32768, 768], P(('wide', 'narrow')), may hold values from -6 to 6
- segment_ids: int32 [32, 1024], P(('wide', 'narrow')), may hold values from 0 to 3, never falling along the last dimension, each value on 1 to 512 neighbouring positions
- routes: int32 [32768, 2], P(('wide', 'narrow')), may hold values from 0 to 3, all different within a row; in each aligned block of 1024 rows (0 to 1023, 1024 to 2047, ...) at most 768 rows name the same one
- attention_gain: bfloat16 [768], P(('wide', 'narrow')), may hold values from 0.25 to 1.75
- qkv_weight: bfloat16 [768, 2304], P(('wide', 'narrow')), may hold values from -0.3125 to 0.3125
- output_weight: bfloat16 [768, 768], P(('wide', 'narrow')), may hold values from -1.75 to 1.75
- mixture_gain: bfloat16 [768], P(('wide', 'narrow')), may hold values from 0.25 to 1.75
- router_train: bfloat16 [768, 2], P(('wide', 'narrow')), may hold values from -0.15625 to 0.15625
- router_frozen: bfloat16 [768, 2], P(('wide', 'narrow')), may hold values from -0.15625 to 0.15625
- expert_in: bfloat16 [768, 2, 3072], P(('wide', 'narrow')), may hold values from -0.21875 to 0.21875
- expert_out: bfloat16 [3072, 2, 768], P(('wide', 'narrow')), may hold values from -0.21875 to 0.21875
- frozen_in: bfloat16 [768, 2, 3072], P(('wide', 'narrow')), may hold values from -0.21875 to 0.21875
- frozen_out: bfloat16 [3072, 2, 768], P(('wide', 'narrow')), may hold values from -0.21875 to 0.21875
- cotangent: bfloat16 [32768, 768], P(('wide', 'narrow')), may hold values from -6 to 6
Outputs:
- block_output: bfloat16 [32768, 768], P(('wide', 'narrow'))
- input_grad: float32 [32768, 768], P(('wide', 'narrow'))
- attention_gain_grad: float32 [768], P(('wide', 'narrow'))
- qkv_grad: float32 [768, 2304], P(('wide', 'narrow'))
- output_weight_grad: float32 [768, 768], P(('wide', 'narrow'))
- mixture_gain_grad: float32 [768], P(('wide', 'narrow'))
- router_grad: float32 [768, 2], P(('wide', 'narrow'))
- expert_in_grad: float32 [768, 2, 3072], P(('wide', 'narrow'))
- expert_out_grad: float32 [3072, 2, 768], P(('wide', 'narrow'))
Inputs may be any that keep to these rules, and one draw needn't show every extreme that they name: `routes`: each token names two different experts; among the 1024 tokens of one sequence no expert is named more than 768 times, a bound that some block reaches. `segment_ids`: within a sequence the document numbers never fall; each of the 4 documents has 1 to 512 tokens.
All inputs are finite; a program needn't handle non-finite values.
Results may differ from a plain program's by a relative error of at most 0.013.
The roundings to bfloat16 on the way count: a program that leaves them out, or rounds other values in their place, can miss the bound.
Values may be sent and summed in bfloat16 or wider, within the bound.
No kernel may reach another device: no remote copies, remote signals or barrier semaphores. Data moves between devices by JAX's collectives and lax.ppermute only.
A program may use at most 320 MiB of HBM per device.

v0:
```python
import jax
import jax.numpy as jnp
from jax import lax
from jax.sharding import PartitionSpec as P

HEAD_DIM = 64
CAP = 768


highest = lax.Precision.HIGHEST
norm_eps = 1e-05


def layer_norm(values, norm_gain):
    center = values - jnp.mean(values, axis=-1, keepdims=True)
    spread = jnp.mean(center * center, axis=-1, keepdims=True)
    return norm_gain * center * lax.rsqrt(spread + norm_eps)


def allowed_block(offset, block_rows, doc_ids):
    length = doc_ids.shape[0]
    row_pos = offset + jnp.arange(block_rows, dtype=jnp.int32)
    col_pos = jnp.arange(length, dtype=jnp.int32)
    row_doc = lax.dynamic_slice_in_dim(doc_ids, offset, block_rows, 0)
    return (row_pos[:, None] >= col_pos[None, :]) & (row_doc[:, None] == doc_ids[None, :])


def block_scores(queries, key_rows, doc_ids, offset, block_rows):
    query_block = lax.dynamic_slice_in_dim(queries, offset, block_rows, 0)
    scores = (
        jnp.einsum("qhd,khd->hqk", query_block, key_rows, preferred_element_type=jnp.float32)
        * 0.125
    )
    allowed = allowed_block(offset, block_rows, doc_ids)
    return (query_block, jnp.where(allowed[None], scores, -1e30))


def attend_forward(queries, key_rows, value_rows, doc_ids):
    length = queries.shape[0]
    block_rows = min(512, length)

    def one_block(block_index):
        offset = block_index * block_rows
        _, scores = block_scores(queries, key_rows, doc_ids, offset, block_rows)
        peak = jnp.max(scores, axis=-1, keepdims=True)
        raised = jnp.exp(scores - peak)
        denominator = jnp.sum(raised, axis=-1, keepdims=True)
        probs_low = (raised / denominator).astype(jnp.bfloat16)
        result = jnp.einsum(
            "hqk,khd->qhd", probs_low, value_rows, preferred_element_type=jnp.float32
        )
        return (result.astype(jnp.bfloat16), (peak + jnp.log(denominator))[..., 0])

    results, log_sums = lax.map(one_block, jnp.arange(length // block_rows, dtype=jnp.int32))
    return (results.reshape(length, queries.shape[1] * queries.shape[2]), log_sums)


def attend_backward(queries, key_rows, value_rows, doc_ids, log_sums, grad_heads):
    length = queries.shape[0]
    block_rows = min(512, length)

    def one_block(carry, block_index):
        grad_keys, grad_values = carry
        offset = block_index * block_rows
        query_block, scores = block_scores(queries, key_rows, doc_ids, offset, block_rows)
        grad_block = lax.dynamic_slice_in_dim(grad_heads, offset, block_rows, 0)
        probs = jnp.exp(scores - log_sums[block_index][..., None])
        probs_low = probs.astype(jnp.bfloat16)
        grad_values = grad_values + jnp.einsum(
            "hqk,qhd->khd", probs_low, grad_block, preferred_element_type=jnp.float32
        )
        grad_probs = jnp.einsum(
            "qhd,khd->hqk", grad_block, value_rows, preferred_element_type=jnp.float32
        )
        grad_scores = probs * (grad_probs - jnp.sum(probs * grad_probs, axis=-1, keepdims=True))
        grad_scores = grad_scores.astype(jnp.bfloat16)
        grad_query = (
            jnp.einsum("hqk,khd->qhd", grad_scores, key_rows, preferred_element_type=jnp.float32)
            * 0.125
        )
        grad_keys = (
            grad_keys
            + jnp.einsum(
                "hqk,qhd->khd", grad_scores, query_block, preferred_element_type=jnp.float32
            )
            * 0.125
        )
        return ((grad_keys, grad_values), grad_query)

    empty = jnp.zeros(key_rows.shape, jnp.float32)
    (grad_keys, grad_values), grad_queries = lax.scan(
        one_block, (empty, empty), jnp.arange(length // block_rows, dtype=jnp.int32)
    )
    return (grad_queries.reshape(queries.shape), grad_keys, grad_values)


def on_device(
    inputs,
    segment_ids,
    routes,
    attention_gain,
    qkv_weight,
    output_weight,
    mixture_gain,
    router_train,
    router_frozen,
    expert_in,
    expert_out,
    frozen_in,
    frozen_out,
    cotangent,
):
    gain_one, qkv_full, out_full, gain_two, train_route, frozen_route = (
        lax.all_gather(attention_gain, ("wide", "narrow"), axis=0, tiled=True),
        lax.all_gather(qkv_weight, ("wide", "narrow"), axis=0, tiled=True),
        lax.all_gather(output_weight, ("wide", "narrow"), axis=0, tiled=True),
        lax.all_gather(mixture_gain, ("wide", "narrow"), axis=0, tiled=True),
        lax.all_gather(router_train, ("wide", "narrow"), axis=0, tiled=True),
        lax.all_gather(router_frozen, ("wide", "narrow"), axis=0, tiled=True),
    )
    frozen_full_in, frozen_full_out = (
        lax.all_gather(frozen_in, ("wide", "narrow"), axis=0, tiled=True),
        lax.all_gather(frozen_out, ("wide", "narrow"), axis=0, tiled=True),
    )
    train_full_in, train_full_out = (
        lax.all_gather(expert_in, ("wide", "narrow"), axis=0, tiled=True),
        lax.all_gather(expert_out, ("wide", "narrow"), axis=0, tiled=True),
    )
    length, model_width = inputs.shape
    head_count = model_width // HEAD_DIM
    doc_ids = segment_ids[0]
    train_count = train_full_in.shape[1]
    inputs_f = inputs.astype(jnp.float32)
    normed_one, norm_one_back = jax.vjp(layer_norm, inputs_f, gain_one.astype(jnp.float32))
    normed_low = normed_one.astype(jnp.bfloat16)
    mixed_qkv = jnp.dot(normed_low, qkv_full, preferred_element_type=jnp.float32).astype(
        jnp.bfloat16
    )
    shaped = mixed_qkv.reshape(length, 3, head_count, HEAD_DIM)
    queries, key_rows, value_rows = (shaped[:, 0], shaped[:, 1], shaped[:, 2])
    attended, log_sums = attend_forward(queries, key_rows, value_rows, doc_ids)
    hidden_one = inputs_f + jnp.dot(attended, out_full, preferred_element_type=jnp.float32)
    normed_two, norm_two_back = jax.vjp(layer_norm, hidden_one, gain_two.astype(jnp.float32))
    normed_two_low = normed_two.astype(jnp.bfloat16)
    normed_two_wide = normed_two_low.astype(jnp.float32)
    router_all = jnp.concatenate([train_route, frozen_route], axis=1).astype(jnp.float32)
    logits = jnp.dot(normed_two_wide, router_all, precision=highest)
    expert_count = router_all.shape[1]
    picked = routes[:, :, None] == jnp.arange(expert_count, dtype=jnp.int32)[None, None, :]
    picked_f = picked.astype(jnp.float32)
    chosen = jnp.sum(logits[:, None, :] * picked_f, axis=-1)
    gate_weights = jax.nn.softmax(chosen, axis=-1)
    flags = picked.reshape(length * 2, expert_count).astype(jnp.int32)
    running = jnp.cumsum(flags, axis=0) - 1
    slot_index = jnp.sum(running * flags, axis=-1).reshape(length, 2)
    flat_slot = routes * CAP + slot_index
    token_ids = jnp.broadcast_to(jnp.arange(length, dtype=jnp.int32)[:, None], (length, 2))
    source = (
        jnp.zeros((expert_count * CAP,), jnp.int32)
        .at[flat_slot.reshape(-1)]
        .set(token_ids.reshape(-1))
    )
    slot_gate = (
        jnp.zeros((expert_count * CAP,), jnp.float32)
        .at[flat_slot.reshape(-1)]
        .set(gate_weights.reshape(-1))
    )
    dispatched = normed_two_low[source].reshape(expert_count, CAP, model_width)
    up_train = jnp.einsum(
        "ecd,def->ecf", dispatched[:train_count], train_full_in, preferred_element_type=jnp.float32
    )
    up_frozen = jnp.einsum(
        "ecd,def->ecf", dispatched[train_count:], frozen_full_in, preferred_element_type=jnp.float32
    )
    pre_act = jnp.concatenate([up_train, up_frozen], axis=0)
    activated = jax.nn.gelu(pre_act).astype(jnp.bfloat16)
    down_train = jnp.einsum(
        "ecf,fed->ecd", activated[:train_count], train_full_out, preferred_element_type=jnp.float32
    )
    down_frozen = jnp.einsum(
        "ecf,fed->ecd", activated[train_count:], frozen_full_out, preferred_element_type=jnp.float32
    )
    expert_rows = jnp.concatenate([down_train, down_frozen], axis=0).reshape(
        expert_count * CAP, model_width
    )
    picked_rows = expert_rows[flat_slot]
    output = hidden_one + jnp.sum(gate_weights[..., None] * picked_rows, axis=1)
    block_output = output.astype(jnp.bfloat16)
    grad_out = cotangent.astype(jnp.float32)
    grad_gate = jnp.sum(grad_out[:, None, :] * picked_rows, axis=-1)
    grad_chosen = gate_weights * (
        grad_gate - jnp.sum(gate_weights * grad_gate, axis=-1, keepdims=True)
    )
    grad_logits = jnp.sum(grad_chosen[..., None] * picked_f, axis=1)
    grad_result = (slot_gate[:, None] * grad_out[source]).astype(jnp.bfloat16)
    grad_result = grad_result.reshape(expert_count, CAP, model_width)
    qkv_back, out_back = (
        lax.all_gather(qkv_weight, ("wide", "narrow"), axis=0, tiled=True),
        lax.all_gather(output_weight, ("wide", "narrow"), axis=0, tiled=True),
    )
    back_in, back_out = (
        lax.all_gather(expert_in, ("wide", "narrow"), axis=0, tiled=True),
        lax.all_gather(expert_out, ("wide", "narrow"), axis=0, tiled=True),
    )
    grad_act_train = jnp.einsum(
        "ecd,fed->ecf", grad_result[:train_count], back_out, preferred_element_type=jnp.float32
    )
    grad_act_frozen = jnp.einsum(
        "ecd,fed->ecf",
        grad_result[train_count:],
        frozen_full_out,
        preferred_element_type=jnp.float32,
    )
    grad_act = jnp.concatenate([grad_act_train, grad_act_frozen], axis=0)
    _, gelu_back = jax.vjp(jax.nn.gelu, pre_act)
    grad_pre = gelu_back(grad_act)[0].astype(jnp.bfloat16)
    grad_disp_train = jnp.einsum(
        "ecf,def->ecd", grad_pre[:train_count], back_in, preferred_element_type=jnp.float32
    )
    grad_disp_frozen = jnp.einsum(
        "ecf,def->ecd", grad_pre[train_count:], frozen_full_in, preferred_element_type=jnp.float32
    )
    grad_disp = jnp.concatenate([grad_disp_train, grad_disp_frozen], axis=0).reshape(
        expert_count * CAP, model_width
    )
    grad_normed_two = jnp.sum(grad_disp[flat_slot], axis=1) + jnp.einsum(
        "le,de->ld", grad_logits, router_all, precision=highest
    )
    grad_hidden_norm, grad_gain_two = norm_two_back(grad_normed_two)
    grad_hidden = grad_out + grad_hidden_norm
    grad_branch = grad_hidden.astype(jnp.bfloat16)
    grad_attended = jnp.einsum(
        "le,de->ld", grad_branch, out_back, preferred_element_type=jnp.float32
    )
    grad_heads = grad_attended.astype(jnp.bfloat16).reshape(length, head_count, HEAD_DIM)
    grad_queries, grad_keys, grad_values = attend_backward(
        queries, key_rows, value_rows, doc_ids, log_sums, grad_heads
    )
    grad_qkv = (
        jnp.stack([grad_queries, grad_keys, grad_values], axis=1)
        .reshape(length, 3 * model_width)
        .astype(jnp.bfloat16)
    )
    grad_normed_one = jnp.einsum(
        "le,de->ld", grad_qkv, qkv_back, preferred_element_type=jnp.float32
    )
    grad_inputs_norm, grad_gain_one = norm_one_back(grad_normed_one)
    input_grad = grad_hidden + grad_inputs_norm
    qkv_term = jnp.einsum("ld,le->de", normed_low, grad_qkv, preferred_element_type=jnp.float32)
    out_term = jnp.einsum("ld,le->de", attended, grad_branch, preferred_element_type=jnp.float32)
    router_term = jnp.einsum(
        "ld,le->de", normed_two_wide, grad_logits[:, :train_count], precision=highest
    )
    gain_one_grad, qkv_grad, out_grad, gain_two_grad, router_grad = (
        lax.psum_scatter(grad_gain_one, ("wide", "narrow"), scatter_dimension=0, tiled=True),
        lax.psum_scatter(qkv_term, ("wide", "narrow"), scatter_dimension=0, tiled=True),
        lax.psum_scatter(out_term, ("wide", "narrow"), scatter_dimension=0, tiled=True),
        lax.psum_scatter(grad_gain_two, ("wide", "narrow"), scatter_dimension=0, tiled=True),
        lax.psum_scatter(router_term, ("wide", "narrow"), scatter_dimension=0, tiled=True),
    )
    columns = dispatched[:train_count]
    in_grad = lax.psum_scatter(
        jnp.einsum(
            "ecd,ecf->def", columns, grad_pre[:train_count], preferred_element_type=jnp.float32
        ),
        ("wide", "narrow"),
        scatter_dimension=0,
        tiled=True,
    )
    columns = activated[:train_count]
    down_grad = lax.psum_scatter(
        jnp.einsum(
            "ecf,ecd->fed", columns, grad_result[:train_count], preferred_element_type=jnp.float32
        ),
        ("wide", "narrow"),
        scatter_dimension=0,
        tiled=True,
    )
    return (
        block_output,
        input_grad,
        gain_one_grad,
        qkv_grad,
        out_grad,
        gain_two_grad,
        router_grad,
        in_grad,
        down_grad,
    )


def solution(mesh):
    return jax.shard_map(
        on_device,
        mesh=mesh,
        in_specs=(
            P(("wide", "narrow"), None),
            P(("wide", "narrow"), None),
            P(("wide", "narrow"), None),
            P(("wide", "narrow")),
            P(("wide", "narrow"), None),
            P(("wide", "narrow"), None),
            P(("wide", "narrow")),
            P(("wide", "narrow"), None),
            P(("wide", "narrow"), None),
            P(("wide", "narrow"), None, None),
            P(("wide", "narrow"), None, None),
            P(("wide", "narrow"), None, None),
            P(("wide", "narrow"), None, None),
            P(("wide", "narrow"), None),
        ),
        out_specs=(
            P(("wide", "narrow"), None),
            P(("wide", "narrow"), None),
            P(("wide", "narrow")),
            P(("wide", "narrow"), None),
            P(("wide", "narrow"), None),
            P(("wide", "narrow")),
            P(("wide", "narrow"), None),
            P(("wide", "narrow"), None, None),
            P(("wide", "narrow"), None, None),
        ),
        check_vma=False,
    )
```

profile of v0, /device:TPU:0, one launch (start us, length us, event | category | flops | bytes accessed | tf_op | source)
XLA Modules:
  0.0 1418.8 jit_solution(10280626151231615467)
XLA Ops:
  18.9 42.2 %all-reduce.8 = (bf16[768]{0:T(1024)(128)(2,1)S(1)}, bf16[768]{0:T(1024)(128)(2,1)S(1)}) all-reduce(bf16[768]{0:T(1024)(128)(2,1)S(1)} %dynamic-update-slice, bf16[768]{0:T(1024)(128)(2,1)S(1)} %dynamic-update-slice.1), channel_id=1, replica_groups=mesh['wide'=8,'narrow'=4] {'wide','narrow'}, use_global_device_ids=true, to_apply=%add | all-reduce | flops 1536 | bytes 6144
  65.0 8.1 scatter_custom_fusion
  73.1 65.6 %all-gather = bf16[32,24,2]{1,2,0:T(2,128)(2,1)S(1)} all-gather(bf16[1,24,2]{1,2,0:T(2,128)(2,1)S(1)} %bitcast.176), channel_id=1, replica_groups=mesh['wide'=8,'narrow'=4] {'wide','narrow'}, dimensions={0}, use_global_device_ids=true | all-gather | bytes 3168 | tf_op jit(solution)/shard_map/all_gather | solution.py:118
  139.4 63.4 %all-gather.1 = bf16[32,24,2]{1,2,0:T(2,128)(2,1)S(1)} all-gather(bf16[1,24,2]{1,2,0:T(2,128)(2,1)S(1)} %bitcast.177), channel_id=1, replica_groups=mesh['wide'=8,'narrow'=4] {'wide','narrow'}, dimensions={0}, use_global_device_ids=true | all-gather | bytes 3168 | tf_op jit(solution)/shard_map/all_gather | solution.py:119
  211.5 13.8 gather_fusion.2
  225.3 8.7 convolution_convert_fusion
  234.0 6.6 copy.156
  240.6 4.5 slice_bitcast_fusion
  245.2 75.2 %while.27 = (s32[]{:T(128)}, bf16[2,512,12,64]{1,3,2,0:T(8,128)(2,1)}, f32[2,12,512]{2,1,0:T(8,128)S(1)}, s32[2]{0:T(128)S(1)}, s32[1024]{0:T(1024)S(1)}, /*inde...) while((s32[]{:T(128)}, ...), condition=%wide.region_5.6_spmd, body=%wide.region_2.5_spmd.sunk | while | flops 1688070656 | bytes 189504240 | solution.py:54
  247.0 10.7 fusion.147
  257.7 13.4 fusion.148
  274.5 8.5 fusion.149
  284.9 11.0 fusion.147
  295.9 12.5 fusion.148
  311.7 8.5 fusion.149
  320.4 4.2 copy.157
  333.4 13.6 gather_fusion
  349.2 8.2 scatter_custom_fusion.1
  357.4 4.1 fusion.77
  361.5 5.2 multiply_convert_fusion.2
  369.2 14.4 %fusion.79 = f32[2,768,3072]{2,1,0:T(8,128)} fusion(bf16[2,768,768]{2,1,0:T(8,128)(2,1)S(1)} %bitcast.157, bf16[768,2,3072]{2,0,1:T(8,128)(2,1)} %all-gather.13.cloned.1.call-done), kind=kOutput, calls=%fused_computation.153 | convolution fusion | flops 7247757312 | bytes 30670848 | tf_op jit(solution)/shard_map/ecd,def->ecf/dot_general | solution.py:169
  383.6 15.4 %fusion.80 = f32[2,768,3072]{2,1,0:T(8,128)} fusion(bf16[2,768,768]{2,1,0:T(8,128)(2,1)} %bitcast.162, bf16[768,2,3072]{2,0,1:T(8,128)(2,1)} %all-gather.15.cloned.1.call-done), kind=kOutput, calls=%fused_computation.154 | convolution fusion | flops 7247757312 | bytes 30670848 | tf_op jit(solution)/shard_map/ecd,def->ecf/dot_general | solution.py:172
  399.0 14.2 %fusion.81 = f32[2,768,3072]{2,1,0:T(8,128)} fusion(bf16[2,768,768]{2,1,0:T(8,128)(2,1)S(1)} %bitcast.159, bf16[3072,2,768]{2,0,1:T(8,128)(2,1)} %all-gather.17.cloned.1.call-done), kind=kOutput, calls=%fused_computation.155 | convolution fusion | flops 7247757312 | bytes 30670848 | tf_op jit(solution)/shard_map/ecd,fed->ecf/dot_general | solution.py:205
  413.2 52.3 %all-gather.19.cloned.1.call-done = bf16[3072,2,768]{2,0,1:T(8,128)(2,1)} async-done(((bf16[96,2,768]{2,0,1:T(8,128)(2,1)}), bf16[3072,2,768]{2,0,1:T(8,128)(2,1)}) %all-gather.19.cloned.1.call-update) | async-done | bytes 9437200 | tf_op jit(solution)/shard_map/all_gather | solution.py:123
  465.5 14.5 %fusion.82 = f32[2,768,3072]{2,1,0:T(8,128)} fusion(bf16[2,768,768]{2,1,0:T(8,128)(2,1)} %bitcast.161, bf16[3072,2,768]{2,0,1:T(8,128)(2,1)} %all-gather.19.cloned.1.call-done), kind=kOutput, calls=%fused_computation.156 | convolution fusion | flops 7247757312 | bytes 30670848 | tf_op jit(solution)/shard_map/ecd,fed->ecf/dot_general | solution.py:208
  480.0 46.9 %fusion.37 = (bf16[4,768,3072]{2,1,0:T(8,128)(2,1)}, bf16[4,768,3072]{2,1,0:T(8,128)(2,1)}) fusion(f32[2,768,3072]{2,1,0:T(8,128)} %fusion.82, f32[2,768,3072]{2,1,0:T(8,128)} %fusion.81, f32[2,768,3072]{2,1,0:T(8,128)} %fusion.80, f32[2,768,3072]{2,1,0:T(8,128)} %fusion.79), kind=kLoop, calls=%fused_computation.57 | loop fusion | flops 226492416 | bytes 113246208 | tf_op jit(solution)/shard_map/convert_element_type | solution.py:216
  526.8 14.4 %fusion.40 = f32[3072,2,768]{0,2,1:T(8,128)} fusion(bf16[2,768,768]{2,1,0:T(8,128)(2,1)S(1)} %bitcast.160, bf16[4,768,3072]{2,1,0:T(8,128)(2,1)} %get-tuple-element.281), kind=kOutput, calls=%fused_computation.66 | convolution fusion | flops 7247757312 | bytes 30670848 | tf_op jit(solution)/shard_map/ecf,ecd->fed/dot_general | solution.py:272
  541.3 28.2 %copy.183 = f32[3072,2,768]{2,1,0:T(2,128)} copy(f32[3072,2,768]{0,2,1:T(8,128)} %fusion.40) | data formatting | bytes 37748736 | tf_op jit(solution)/shard_map/ecf,ecd->fed/transpose | solution.py:272
  569.5 17.2 %fusion.84 = f32[2,768,768]{2,1,0:T(8,128)S(1)} fusion(bf16[4,768,3072]{2,1,0:T(8,128)(2,1)} %get-tuple-element.281, bf16[3072,2,768]{2,0,1:T(8,128)(2,1)} %all-gather.17.cloned.1.call-done), kind=kOutput, calls=%fused_computation.158 | convolution fusion | flops 7247757312 | bytes 33030144 | tf_op jit(solution)/shard_map/ecf,fed->ecd/dot_general | solution.py:177
  586.8 17.0 %fusion.85 = f32[2,768,768]{2,1,0:T(8,128)} fusion(bf16[4,768,3072]{2,1,0:T(8,128)(2,1)} %get-tuple-element.281, bf16[3072,2,768]{2,0,1:T(8,128)(2,1)} %all-gather.19.cloned.1.call-done), kind=kOutput, calls=%fused_computation.159 | convolution fusion | flops 7247757312 | bytes 33030144 | tf_op jit(solution)/shard_map/ecf,fed->ecd/dot_general | solution.py:180
  603.8 6.7 pad_maximum_fusion.2
  610.5 14.6 %gather_fusion.1 = f32[2048,768]{1,0:T(8,128)} fusion(f32[3072,768]{1,0:T(8,128)} %bitcast.151, s32[2048]{0:T(1024)S(1)} %copy-done.6), kind=kCustom, calls=%fused_computation.1 | custom fusion | bytes 12591104 | tf_op jit(solution)/shard_map/gather | solution.py:186
  625.2 8.6 reshape.395
  633.8 17.3 %multiply_reduce_fusion.1 = (f32[1024,2]{1,0:T(8,128)}, f32[1024,768]{1,0:T(8,128)}) fusion(f32[1024,2,768]{2,1,0:T(2,128)} %reshape.395, f32[1024,768]{1,0:T(8,128)S(1)} %copy-done.2, f32[1024,2]{1,0:T(8,128)} %copy-done.23), kind=kLoop, calls=%fused_computation.68 | loop fusion | flops 5502976 | bytes 12599296 | tf_op jit(solution)/shard_map/reduce_sum | solution.py:190
  652.4 16.2 %convolution_bitcast_fusion = f32[768,2,3072]{0,2,1:T(8,128)} fusion(bf16[4,768,3072]{2,1,0:T(8,128)(2,1)} %get-tuple-element.280, bf16[2,768,768]{2,1,0:T(8,128)(2,1)} %bitcast.158), kind=kOutput, calls=%fused_computation.67 | convolution fusion | flops 7247757312 | bytes 40108032 | tf_op jit(solution)/shard_map/ecd,ecf->def/dot_general | solution.py:263
  668.6 28.6 %copy.181 = f32[768,2,3072]{2,1,0:T(2,128)} copy(f32[768,2,3072]{0,2,1:T(8,128)} %convolution_bitcast_fusion) | data formatting | bytes 37748736 | tf_op jit(solution)/shard_map/ecd,ecf->def/transpose | solution.py:263
  697.3 13.2 fusion.86
  710.4 14.4 %fusion.87 = f32[2,768,768]{2,1,0:T(8,128)} fusion(bf16[4,768,3072]{2,1,0:T(8,128)(2,1)} %get-tuple-element.280, bf16[768,2,3072]{2,0,1:T(8,128)(2,1)} %all-gather.15.cloned.1.call-done), kind=kOutput, calls=%fused_computation.161 | convolution fusion | flops 7247757312 | bytes 33030144 | tf_op jit(solution)/shard_map/ecf,def->ecd/dot_general | solution.py:220
  724.9 6.9 pad_maximum_fusion.3
  731.8 14.4 %gather_fusion.3 = f32[2048,768]{1,0:T(8,128)} fusion(f32[3072,768]{1,0:T(8,128)} %bitcast.150, s32[2048]{0:T(1024)S(1)} %copy-done.6), kind=kCustom, calls=%fused_computation.3 | custom fusion | bytes 12591104 | tf_op jit(solution)/shard_map/gather | solution.py:226
  746.2 9.2 reshape.415
  755.4 10.3 reduce_sum.212
  772.0 4.9 multiply_reduce_fusion.3
  788.8 182.8 %while.28 = (s32[]{:T(128)}, f32[1024,12,64]{0,2,1:T(8,128)}, f32[1024,12,64]{0,2,1:T(8,128)}, bf16[2,512,12,64]{1,3,2,0:T(8,128)(2,1)}, s32[2]{0:T(128)S(1)}, /...) while((s32[]{:T(128)}, f32[1024,12,64]{0,2,1:T(8,128)}, ...), condition=%wide.region_25.26_spmd.clone, body=%wide.region_23.25_spmd.clone.sunk | while | flops 4126796288 | bytes 213048112 | solution.py:91
  790.8 11.7 fusion.159
  804.5 18.3 %multiply_reduce_fusion.8 = (f32[12,512]{1,0:T(8,128)S(1)}, f32[12,512,1024]{2,1,0:T(8,128)}) fusion(f32[12,512,1024]{2,1,0:T(8,128)} %fusion.159, f32[12,512]{1,0:T(8,128)S(1)} %dynamic-slice_bitcast_fusion.2, pred[512,1024]{1,0:T(8,128)(4,1)S(1)} %fusion.160, bf16[1024,12,64]{0,2,1:T(8,128)(2,1)} %get-tuple-element.517, ...), kind=kOutput, calls=%fused_computation.25.clone.1 | convolution fusion | flops 836757504 | bytes 53264388 | tf_op jit(solution)/shard_map/while/body/eval_jaxpr/qhd,khd->hqk/dot_general | solution.py:72
  822.8 24.2 %multiply_convert_fusion.5 = bf16[12,512,1024]{2,1,0:T(8,128)(2,1)} fusion(f32[12,512,1024]{2,1,0:T(8,128)} %get-tuple-element.431, f32[12,512,1024]{2,1,0:T(8,128)} %fusion.159, f32[12,512]{1,0:T(8,128)S(1)} %get-tuple-element.432, f32[12,512]{1,0:T(8,128)S(1)} %dynamic-slice_bitcast_fusion.2, pred[512,1024]{1,0:T(8,128)(4,1)S(1)} %fusion.160), kind=kLoop, calls=%fused_computation.24.clone.1 | loop fusion | flops 37748736 | bytes 63488000 | tf_op jit(solution)/shard_map/while/body/eval_jaxpr/convert_element_type | solution.py:76
  847.0 9.0 bitcast_add_fusion.4
  856.0 9.5 bitcast_dynamic-update-slice_fusion.5
  865.5 13.7 bitcast_add_fusion.5
  881.0 11.6 fusion.159
  894.6 18.3 %multiply_reduce_fusion.8 = (f32[12,512]{1,0:T(8,128)S(1)}, f32[12,512,1024]{2,1,0:T(8,128)}) fusion(f32[12,512,1024]{2,1,0:T(8,128)} %fusion.159, f32[12,512]{1,0:T(8,128)S(1)} %dynamic-slice_bitcast_fusion.2, pred[512,1024]{1,0:T(8,128)(4,1)S(1)} %fusion.160, bf16[1024,12,64]{0,2,1:T(8,128)(2,1)} %get-tuple-element.517, ...), kind=kOutput, calls=%fused_computation.25.clone.1 | convolution fusion | flops 836757504 | bytes 53264388 | tf_op jit(solution)/shard_map/while/body/eval_jaxpr/qhd,khd->hqk/dot_general | solution.py:72
  912.9 23.7 %multiply_convert_fusion.5 = bf16[12,512,1024]{2,1,0:T(8,128)(2,1)} fusion(f32[12,512,1024]{2,1,0:T(8,128)} %get-tuple-element.431, f32[12,512,1024]{2,1,0:T(8,128)} %fusion.159, f32[12,512]{1,0:T(8,128)S(1)} %get-tuple-element.432, f32[12,512]{1,0:T(8,128)S(1)} %dynamic-slice_bitcast_fusion.2, pred[512,1024]{1,0:T(8,128)(4,1)S(1)} %fusion.160), kind=kLoop, calls=%fused_computation.24.clone.1 | loop fusion | flops 37748736 | bytes 63488000 | tf_op jit(solution)/shard_map/while/body/eval_jaxpr/convert_element_type | solution.py:76
  936.7 9.9 bitcast_add_fusion.4
  946.6 9.8 bitcast_dynamic-update-slice_fusion.5
  956.4 15.0 %bitcast_add_fusion.5 = f32[1024,12,64]{0,2,1:T(8,128)} fusion(f32[1024,12,64]{0,2,1:T(8,128)} %get-tuple-element.491, f32[12,512,1024]{2,1,0:T(8,128)} %fusion.159, f32[12,512]{1,0:T(8,128)S(1)} %dynamic-slice_bitcast_fusion.2, pred[512,1024]{1,0:T(8,128)(4,1)S(1)} %fusion.160, pred[]{:T(512)S(6)} %compare.3, ...), kind=kOutput, calls=%fused_computation.30.clone.1 | convolution fusion | flops 832045056 | bytes 32792580 | tf_op jit(solution)/shard_map/while/body/eval_jaxpr/hqk,qhd->khd/dot_general | solution.py:69
  971.6 4.4 copy.179
  985.9 6.2 fusion.55
  992.2 6.9 fusion.50
  1001.8 39.3 %all-reduce.7 = (f32[768]{0:T(1024)S(1)}, f32[768]{0:T(1024)S(1)}, f32[768,2]{0,1:T(2,128)S(1)}) all-reduce(f32[768]{0:T(1024)S(1)} %get-tuple-element.223, f32[768]{0:T(1024)S(1)} %copy-done.67, f32[768,2]{0,1:T(2,128)S(1)} %fusion.62), channel_id=2, replica_groups=mesh['wide'=8,'narrow'=4] {'wide','narrow'}, use_global_device_ids=true, to_apply=%region_29.30.clone | all-reduce | flops 3072 | bytes 24576
  1042.3 6.0 add_add_fusion.2
  1056.1 125.5 %all-reduce.12.cloned.1.call-done = f32[768,2,3072]{2,1,0:T(2,128)} async-done(((f32[768,2,3072]{2,1,0:T(2,128)}), f32[768,2,3072]{2,1,0:T(2,128)}) %all-reduce.12.cloned.1.call-update) | async-done | bytes 18874384
  1183.6 103.0 %reduce-scatter.6.cloned.1.call-done = f32[24,768]{1,0:T(8,128)} async-done(((f32[768,768]{1,0:T(8,128)}), f32[24,768]{1,0:T(8,128)}) %reduce-scatter.6.cloned.1.call-update) | async-done | bytes 73744 | tf_op jit(solution)/shard_map/reduce_scatter | solution.py:257
  1286.6 125.1 %reduce-scatter.4.cloned.1.call-done = f32[24,2304]{1,0:T(8,128)} async-done(((f32[768,2304]{1,0:T(8,128)}), f32[24,2304]{1,0:T(8,128)}) %reduce-scatter.4.cloned.1.call-update) | async-done | bytes 221200 | tf_op jit(solution)/shard_map/reduce_scatter | solution.py:256
  (286 shorter events, 92.3 us)
Async XLA Ops:
  7.2 8.8 copy-start.36
  7.2 9.6 copy-start.26
  7.2 218.1 %all-gather.9.cloned.1.call-start = ((), (), s32[]{:S(2)}) async-start(), calls=%async_computation.2 | async-start | bytes 3649536 | tf_op jit(solution)/shard_map/all_gather | solution.py:115
  7.9 318.2 %all-gather.11.cloned.1.call-start = ((), (), s32[]{:S(2)}) async-start(), calls=%async_computation.3 | async-start | bytes 1216512 | tf_op jit(solution)/shard_map/all_gather | solution.py:116
  8.7 360.5 %all-gather.13.cloned.1.call-start = ((), (), s32[]{:S(2)}) async-start(), calls=%async_computation.4 | async-start | bytes 9732096 | tf_op jit(solution)/shard_map/all_gather | solution.py:126
  10.5 373.1 %all-gather.15.cloned.1.call-start = ((), (), s32[]{:S(2)}) async-start(), calls=%async_computation.5 | async-start | bytes 9732096 | tf_op jit(solution)/shard_map/all_gather | solution.py:122
  12.3 386.7 %all-gather.17.cloned.1.call-start = ((), (), s32[]{:S(2)}) async-start(), calls=%async_computation.6 | async-start | bytes 9732096 | tf_op jit(solution)/shard_map/all_gather | solution.py:127
  14.1 451.4 %all-gather.19.cloned.1.call-start = ((), (), s32[]{:S(2)}) async-start(), calls=%async_computation.7 | async-start | bytes 9732096 | tf_op jit(solution)/shard_map/all_gather | solution.py:123
  15.9 1038.3 %all-reduce.14.cloned.1.call-start = ((), (), s32[]{:S(2)}) async-start(), calls=%async_computation.11 | async-start | bytes 37748736
  17.6 47.4 %copy-start.11 = (bf16[1024,768]{0,1:T(8,128)(2,1)}, bf16[1024,768]{0,1:T(8,128)(2,1)S(1)}, u32[]{:S(2)}) copy-start(bf16[1024,768]{0,1:T(8,128)(2,1)S(1)} %copy.155) | copy-start | bytes 4718596
  17.6 55.5 %copy-start.69 = (bf16[24,2]{0,1:T(2,128)(2,1)S(1)}, bf16[24,2]{0,1:T(2,128)(2,1)}, u32[]{:S(2)}) copy-start(bf16[24,2]{0,1:T(2,128)(2,1)} %param.25) | copy-start | bytes 292
  17.6 121.8 %copy-start.70 = (bf16[24,2]{0,1:T(2,128)(2,1)S(1)}, bf16[24,2]{0,1:T(2,128)(2,1)}, u32[]{:S(2)}) copy-start(bf16[24,2]{0,1:T(2,128)(2,1)} %param.26) | copy-start | bytes 292
  17.9 207.4 %copy-start.45 = (f32[1024]{0:T(1024)}, f32[1024]{0:T(1024)S(1)}, u32[]{:S(2)}) copy-start(f32[1024]{0:T(1024)S(1)} %broadcast_multiply_fusion.1) | copy-start | bytes 12292
  18.4 46.6 %copy-start.57 = (f32[1024]{0:T(1024)}, f32[1024]{0:T(1024)S(1)}, u32[]{:S(2)}) copy-start(f32[1024]{0:T(1024)S(1)} %fusion.51) | copy-start | bytes 12292
  18.4 206.9 %copy-start.53 = (f32[1024]{0:T(1024)}, f32[1024]{0:T(1024)S(1)}, u32[]{:S(2)}) copy-start(f32[1024]{0:T(1024)S(1)} %fusion.70) | copy-start | bytes 12292
  61.1 164.2 %copy-start.55 = (f32[768]{0:T(1024)}, f32[768]{0:T(1024)S(1)}, u32[]{:S(2)}) copy-start(f32[768]{0:T(1024)S(1)} %convert_element_type.67) | copy-start | bytes 9220
  64.6 138.8 %copy-start.68 = (s32[2048,1]{0,1:T(1,128)}, s32[2048,1]{0,1:T(1,128)S(1)}, u32[]{:S(2)}) copy-start(s32[2048,1]{0,1:T(1,128)S(1)} %compare_select_fusion) | copy-start | bytes 24580
  73.1 138.5 %copy-start.39 = (s32[3072]{0:T(1024)}, s32[3072]{0:T(1024)S(1)}, u32[]{:S(2)}) copy-start(s32[3072]{0:T(1024)S(1)} %fusion.61) | copy-start | bytes 36868
  208.3 17.0 %copy-start.1 = (f32[1024,768]{1,0:T(8,128)}, f32[1024,768]{1,0:T(8,128)S(1)}, u32[]{:S(2)}) copy-start(f32[1024,768]{1,0:T(8,128)S(1)} %copy.174) | copy-start | bytes 9437188
  240.6 4.5 copy-start.28
  247.0 24.1 %copy-start.8 = (bf16[1024,12,64]{0,2,1:T(8,128)(2,1)S(1)}, bf16[1024,12,64]{0,2,1:T(8,128)(2,1)}, u32[]{:S(2)}) copy-start(bf16[1024,12,64]{0,2,1:T(8,128)(2,1)} %get-tuple-element.467) | copy-start | bytes 4718596 | tf_op jit(solution)/shard_map/while
  257.7 16.8 %copy-start = (f32[12,512,1024]{2,1,0:T(8,128)S(1)}, f32[12,512,1024]{2,1,0:T(8,128)}, u32[]{:S(2)}) copy-start(f32[12,512,1024]{2,1,0:T(8,128)} %get-tuple-element.417) | copy-start | bytes 75497472 | tf_op jit(solution)/shard_map/while
  284.9 23.5 %copy-start.8 = (bf16[1024,12,64]{0,2,1:T(8,128)(2,1)S(1)}, bf16[1024,12,64]{0,2,1:T(8,128)(2,1)}, u32[]{:S(2)}) copy-start(bf16[1024,12,64]{0,2,1:T(8,128)(2,1)} %get-tuple-element.467) | copy-start | bytes 4718596 | tf_op jit(solution)/shard_map/while
  295.9 15.8 %copy-start = (f32[12,512,1024]{2,1,0:T(8,128)S(1)}, f32[12,512,1024]{2,1,0:T(8,128)}, u32[]{:S(2)}) copy-start(f32[12,512,1024]{2,1,0:T(8,128)} %get-tuple-element.417) | copy-start | bytes 75497472 | tf_op jit(solution)/shard_map/while
  320.4 5.8 copy-start.3
  320.4 5.8 copy-start.7
  320.4 5.8 copy-start.30
  332.7 14.4 %copy-start.14 = (bf16[1024,768]{0,1:T(8,128)(2,1)}, bf16[1024,768]{0,1:T(8,128)(2,1)S(1)}, u32[]{:S(2)}) copy-start(bf16[1024,768]{0,1:T(8,128)(2,1)S(1)} %multiply_convert_fusion.3) | copy-start | bytes 4718596
  333.4 13.7 copy-start.63
  333.4 13.7 copy-start.65
  333.4 14.0 copy-start.37
  348.9 12.6 copy-start.23
  361.5 7.7 copy-start.24
  383.6 15.4 %copy-start.25 = (bf16[1536,768]{1,0:T(8,128)(2,1)S(1)}, bf16[1536,768]{1,0:T(8,128)(2,1)}, u32[]{:S(2)}) copy-start(bf16[1536,768]{1,0:T(8,128)(2,1)} %get-tuple-element.282) | copy-start | bytes 7077892
  569.5 612.2 %all-reduce.12.cloned.1.call-start = ((), (), s32[]{:S(2)}) async-start(), calls=%async_computation.10 | async-start | bytes 37748736
  603.8 6.7 copy-start.6
  625.2 8.6 copy-start.2
  697.2 589.4 %reduce-scatter.6.cloned.1.call-start = ((), (), s32[]{:S(2)}) async-start(), calls=%async_computation.9 | async-start | bytes 2433024 | tf_op jit(solution)/shard_map/reduce_scatter | solution.py:257
  768.0 3.8 copy-start.33
  768.0 3.8 copy-start.42
  768.0 3.8 copy-start.48
  768.0 3.8 copy-start.38
  768.0 3.9 copy-start.10
  768.1 3.9 copy-start.44
  768.1 3.9 copy-start.50
  768.1 3.9 copy-start.52
  768.1 3.9 copy-start.64
  768.1 3.9 copy-start.66
  772.0 5.0 copy-start.34
  772.0 5.0 copy-start.60
  772.0 5.0 copy-start.19
  779.1 2.8 copy-start.27
  784.8 4.0 copy-start.4
  784.8 4.0 copy-start.29
  784.8 4.0 copy-start.31
  784.8 626.9 %reduce-scatter.4.cloned.1.call-start = ((), (), s32[]{:S(2)}) async-start(), calls=%async_computation.8 | async-start | bytes 7299072 | tf_op jit(solution)/shard_map/reduce_scatter | solution.py:256
  971.6 8.2 copy-start.5
  979.8 3.4 copy-start.21
  992.1 7.0 copy-start.58
  992.1 7.0 copy-start.15
  992.1 7.0 copy-start.35
  999.2 43.1 %copy-start.17 = (bf16[1024,768]{0,1:T(8,128)(2,1)S(1)}, bf16[1024,768]{0,1:T(8,128)(2,1)}, u32[]{:S(2)}) copy-start(bf16[1024,768]{0,1:T(8,128)(2,1)} %copy.172) | copy-start | bytes 4718596
  999.2 43.1 %copy-start.62 = (f32[1024]{0:T(1024)S(1)}, f32[1024]{0:T(1024)}, u32[]{:S(2)}) copy-start(f32[1024]{0:T(1024)} %copy-done.61) | copy-start | bytes 12292
  1048.3 3.7 copy-start.20
  (21 other events, 39.0 us)
Sparse Core Ops, SparseCore 0:
  10.8 63.1 all-gather.8
  76.8 52.8 all-gather.10
  132.8 81.0 all-gather.12
  216.9 80.7 all-gather.14
  300.5 80.7 all-gather.16
  384.8 80.6 all-gather.18
  569.6 301.9 all-reduce.13
  877.8 303.8 all-reduce.11
  1187.5 99.0 reduce-scatter.5
  1293.6 118.0 reduce-scatter.3
where the time goes:
time: 1430 us; the launch traced here: 1420 us
  waiting for transfers between devices  408 us (29%)
  matrix products  356 us (25%)
  local copies, waits for them, and re-layouts  235 us (16%)
  blocking collectives  210 us (15%)
  other arithmetic  188 us (13%)
  between operations  15.4 us (1%)
    unnamed x12, waiting for transfers between devices  127 us
    reduce_scatter x1, waiting for transfers between devices, on_device(): lax.psum_scatter(qkv_term, ('wide', 'narrow'), scatter_dimension=0, tiled...  125 us
    reduce_scatter x1, waiting for transfers between devices, on_device(): lax.psum_scatter(out_term, ('wide', 'narrow'), scatter_dimension=0, tiled...  103 us
    unnamed x2, blocking collectives  81.5 us
    all_gather x1, blocking collectives, on_device(): lax.all_gather(router_train, ('wide', 'narrow'), axis=0, tiled=True)  65.6 us
    all_gather x1, blocking collectives, on_device(): lax.all_gather(router_frozen, ('wide', 'narrow'), axis=0, tiled=True)  63.4 us
    all_gather x1, waiting for transfers between devices, on_device(): lax.all_gather(frozen_out, ('wide', 'narrow'), axis=0, tiled=True)  52.3 us
    convert_element_type x2, other arithmetic, one_block(): grad_scores = grad_scores.astype(jnp.bfloat16)  48 us
  transfers between devices with their start and end apart: 10, of which 4 were waited for; matrix products, arithmetic and copies ran while one was open for 46% of the time, Pallas kernels for 0%

commit v1 on v0

v1 whole, which is shorter than its diff:
```python
import functools

import jax
import jax.numpy as jnp
from jax import lax
from jax.experimental import pallas as pl
from jax.experimental.pallas import tpu as pltpu
from jax.sharding import Mesh, PartitionSpec as P

HEAD_DIM = 64
PAIR = 2 * HEAD_DIM
CAP = 768
MAX_DOC = 512
BLOCK = 256
WINDOW = BLOCK + 128
ROW_TILE = 256
LANES = 128
EPS = 1e-05
bf16, f32, i32 = jnp.bfloat16, jnp.float32, jnp.int32


def dot_nn(a, b):
    return lax.dot_general(a, b, (((1,), (0,)), ((), ())), preferred_element_type=f32)


def dot_nt(a, b):
    return lax.dot_general(a, b, (((1,), (1,)), ((), ())), preferred_element_type=f32)


def dot_tn(a, b):
    return lax.dot_general(a, b, (((0,), (0,)), ((), ())), preferred_element_type=f32)


def iota(shape, dim):
    return lax.broadcasted_iota(i32, shape, dim)


def flag(mask, dtype=bf16):
    return jnp.where(mask, 1.0, 0.0).astype(dtype)


def normalized(values):
    center = values - jnp.mean(values, axis=-1, keepdims=True)
    spread = jnp.mean(center * center, axis=-1, keepdims=True)
    inverse = lax.rsqrt(spread + EPS)
    return center * inverse, inverse


def norm_back(xhat, inverse, gain, grad):
    scaled = grad * gain
    return inverse * (
        scaled
        - jnp.mean(scaled, axis=-1, keepdims=True)
        - xhat * jnp.mean(scaled * xhat, axis=-1, keepdims=True)
    )


def params(limit_mib, **kw):
    return pltpu.CompilerParams(vmem_limit_bytes=limit_mib << 20, **kw)


def whole(shape):
    return pl.BlockSpec(shape, lambda *_: (0,) * len(shape))


def call(kernel, name, grid, ins, in_specs, outs, out_specs, scratch=(), limit=48, flops=0):
    size = sum(a.size * a.dtype.itemsize for a in ins) + sum(
        o.size * o.dtype.itemsize for o in outs
    )
    return pl.pallas_call(
        kernel,
        name=name,
        grid=grid,
        in_specs=in_specs,
        out_specs=out_specs,
        out_shape=outs,
        scratch_shapes=list(scratch),
        compiler_params=params(limit),
        cost_estimate=pl.CostEstimate(flops=flops, bytes_accessed=size, transcendentals=0),
    )(*ins)


def shape_of(shape, dtype):
    return jax.ShapeDtypeStruct(shape, dtype)


def gathered_specs(pieces, columns, index):
    return [pl.BlockSpec((p.shape[0], columns), lambda *i: (0, index(*i))) for p in pieces]


def put_together(rows_ref, piece_refs, whole_ref):
    for number, piece in enumerate(piece_refs):
        height = piece.shape[0]
        start = pl.multiple_of(rows_ref[number], 16 if height % 16 == 0 else 8)
        whole_ref[pl.ds(start, height), :] = piece[...]


def lay_out(order_ref, staged_ref, own_ref, other_ref):
    parts = order_ref.shape[0] // 2
    height = own_ref.shape[0] // parts
    for half, ref in enumerate((own_ref, other_ref)):
        for part in range(parts):
            start = order_ref[half * parts + part]
            start = pl.multiple_of(start, 16 if height % 16 == 0 else 8)
            ref[part * height : (part + 1) * height, :] = staged_ref[pl.ds(start, height), :]


SMEM = pl.BlockSpec(memory_space=pltpu.SMEM)


def route_kernel(routes_ref, routes_t_ref, place_ref, place_t_ref):
    length = routes_ref.shape[0]
    lane = iota((length, LANES), 1)
    mask = (lane == routes_ref[:, 0:1]) | (lane == routes_ref[:, 1:2])
    before = flag(iota((length, length), 1) < iota((length, length), 0))
    place_ref[...] = jnp.where(mask, dot_nn(before, flag(mask)), -1.0).astype(i32)
    sub = iota((8, length), 0)
    mask_t = (sub == routes_t_ref[0:1, :]) | (sub == routes_t_ref[1:2, :])
    before_t = flag(iota((length, length), 0) < iota((length, length), 1))
    place_t_ref[...] = jnp.where(mask_t, dot_nn(flag(mask_t), before_t), -1.0).astype(i32)


def route_places(routes):
    length = routes.shape[0]
    outs = [shape_of((length, LANES), i32), shape_of((8, length), i32)]
    return call(
        route_kernel,
        "places",
        (),
        [routes, routes.T],
        [whole((length, 2)), whole((2, length))],
        outs,
        [whole(o.shape) for o in outs],
    )


def gains_of(small_ref):
    return small_ref[...].astype(f32).T


def project_kernel(count, rows_ref, inputs_ref, *rest):
    pieces, (qkv_ref, dense_ref, gains_ref) = rest[:count], rest[count:]
    width = inputs_ref.shape[1]

    @pl.when(pl.program_id(0) == 0)
    def _():
        put_together(rows_ref, pieces, dense_ref)
        gains_ref[...] = dense_ref[:, 4 * width :].astype(f32).T

    xhat, _ = normalized(inputs_ref[...].astype(f32))
    normed = (gains_ref[0:1, :] * xhat).astype(bf16)
    qkv_ref[...] = dot_nn(normed, dense_ref[:, : 3 * width]).astype(bf16)


def project(rows, inputs, pieces):
    length, width = inputs.shape
    columns = pieces[0].shape[1]
    return call(
        functools.partial(project_kernel, len(pieces)),
        "project",
        (length // BLOCK,),
        [rows, inputs] + pieces,
        [SMEM, pl.BlockSpec((BLOCK, width), lambda i: (i, 0))]
        + gathered_specs(pieces, columns, lambda i: 0),
        [shape_of((length, 3 * width), bf16), shape_of((width, columns), bf16)],
        [pl.BlockSpec((BLOCK, 3 * width), lambda i: (i, 0)), whole((width, columns))],
        [pltpu.VMEM((LANES, width), f32)],
        flops=2 * length * width * 3 * width,
    )


def span_of(block):
    reach = MAX_DOC // BLOCK
    start = max(0, block - reach) * BLOCK
    return start, (block + 1) * BLOCK - start


def attend_kernel(doc_ref, doc_t_ref, q_ref, k_ref, v_ref, out_ref, log_ref, bias_ref):
    length = q_ref.shape[0]
    blocks = length // BLOCK

    @pl.when(pl.program_id(0) == 0)
    def _():
        for block in range(blocks):
            start, size = span_of(block)
            rows = slice(block * BLOCK, (block + 1) * BLOCK)
            row = iota((BLOCK, size), 0) + block * BLOCK
            col = iota((BLOCK, size), 1) + start
            kept = (row >= col) & (doc_ref[rows, :] == doc_t_ref[:, start : start + size])
            bias_ref[rows, :size] = jnp.where(kept, 0.0, -1e30)

    first = iota((BLOCK, PAIR), 1) < HEAD_DIM
    for block in range(blocks):
        start, size = span_of(block)
        rows = slice(block * BLOCK, (block + 1) * BLOCK)
        query = q_ref[rows, :] * 0.125
        keys, values = k_ref[start : start + size, :], v_ref[start : start + size, :]
        bias = bias_ref[rows, :size]
        parts, logs = [], []
        for own in (first, ~first):
            scores = dot_nt(jnp.where(own, query, 0).astype(bf16), keys) + bias
            peak = jnp.max(scores, axis=-1, keepdims=True)
            raised = jnp.exp(scores - peak)
            total = jnp.sum(raised, axis=-1, keepdims=True)
            parts.append(dot_nn(raised.astype(bf16), values) * (1.0 / total))
            logs.append(peak + jnp.log(total))
        out_ref[rows, :] = jnp.where(first, parts[0], parts[1]).astype(bf16)
        turned = jnp.where(first, logs[0], logs[1]).T
        log_ref[0, 0:1, rows] = turned[0:1, :]
        log_ref[0, 1:2, rows] = turned[HEAD_DIM : HEAD_DIM + 1, :]


def attend(docs, qkv):
    length, width = qkv.shape[0], qkv.shape[1] // 3
    pairs = width // PAIR
    heads = [pl.BlockSpec((length, PAIR), lambda i, k=k: (0, k * pairs + i)) for k in range(3)]
    return call(
        attend_kernel,
        "attend",
        (pairs,),
        [docs.reshape(length, 1), docs.reshape(1, length), qkv, qkv, qkv],
        [whole((length, 1)), whole((1, length))] + heads,
        [shape_of((length, width), bf16), shape_of((pairs, 8, length), f32)],
        [
            pl.BlockSpec((length, PAIR), lambda i: (0, i)),
            pl.BlockSpec((1, 8, length), lambda i: (i, 0, 0)),
        ],
        [pltpu.VMEM((length, MAX_DOC + BLOCK), f32)],
        flops=4 * length * 768 * width,
    )


def attend_back_kernel(
    doc_ref, doc_t_ref, q_ref, k_ref, v_ref, grad_ref, log_ref, dq_ref, dk_ref, dv_ref,
    bias_ref, dk_sum, dv_sum,
):
    length = q_ref.shape[0]
    blocks = length // BLOCK

    @pl.when(pl.program_id(0) == 0)
    def _():
        for block in range(blocks):
            start, size = span_of(block)
            cols = slice(block * BLOCK, (block + 1) * BLOCK)
            row = iota((size, BLOCK), 0) + start
            col = iota((size, BLOCK), 1) + block * BLOCK
            kept = (col >= row) & (doc_ref[start : start + size, :] == doc_t_ref[:, cols])
            bias_ref[:size, cols] = jnp.where(kept, 0.0, -1e30)

    dk_sum[...] = jnp.zeros_like(dk_sum)
    dv_sum[...] = jnp.zeros_like(dv_sum)
    first = iota((BLOCK, PAIR), 1) < HEAD_DIM
    for block in range(blocks):
        start, size = span_of(block)
        rows, span = slice(block * BLOCK, (block + 1) * BLOCK), slice(start, start + size)
        query, grad = q_ref[rows, :] * 0.125, grad_ref[rows, :]
        keys, values = k_ref[span, :], v_ref[span, :]
        bias = bias_ref[:size, rows]
        parts, dk, dv = [], 0.0, 0.0
        for head, own in enumerate((first, ~first)):
            own_query = jnp.where(own, query, 0).astype(bf16)
            own_grad = jnp.where(own, grad, 0).astype(bf16)
            scores = dot_nt(keys, own_query) + bias
            probs = jnp.exp(scores - log_ref[0, head : head + 1, rows])
            dv = dv + dot_nn(probs.astype(bf16), own_grad)
            weighted = probs * dot_nt(values, own_grad)
            mean = jnp.sum(weighted, axis=0, keepdims=True)
            grad_scores = (weighted - probs * mean).astype(bf16)
            dk = dk + dot_nn(grad_scores, own_query)
            parts.append(dot_tn(grad_scores, keys) * 0.125)
        dq_ref[rows, :] = jnp.where(first, parts[0], parts[1]).astype(bf16)
        dk_sum[span, :] += dk
        dv_sum[span, :] += dv
    dk_ref[...] = dk_sum[...].astype(bf16)
    dv_ref[...] = dv_sum[...].astype(bf16)


def attend_back(docs, qkv, grad, logs):
    length, width = qkv.shape[0], qkv.shape[1] // 3
    pairs = width // PAIR
    heads = [pl.BlockSpec((length, PAIR), lambda i, k=k: (0, k * pairs + i)) for k in range(3)]
    one = pl.BlockSpec((length, PAIR), lambda i: (0, i))
    return call(
        attend_back_kernel,
        "attend_back",
        (pairs,),
        [docs.reshape(length, 1), docs.reshape(1, length), qkv, qkv, qkv, grad, logs],
        [whole((length, 1)), whole((1, length))]
        + heads
        + [one, pl.BlockSpec((1, 8, length), lambda i: (i, 0, 0))],
        [shape_of((length, width), bf16)] * 3,
        [one] * 3,
        [
            pltpu.VMEM((MAX_DOC + BLOCK, length), f32),
            pltpu.VMEM((length, PAIR), f32),
            pltpu.VMEM((length, PAIR), f32),
        ],
        flops=10 * length * 768 * width,
    )


def middle_kernel(
    inputs_ref, attended_ref, place_ref, weight_ref, small_ref, hidden_ref, normed_ref, gate_ref,
    gains_ref,
):
    @pl.when(pl.program_id(0) == 0)
    def _():
        gains_ref[...] = gains_of(small_ref)

    hidden = inputs_ref[...].astype(f32) + dot_nn(attended_ref[...], weight_ref[...])
    hidden_ref[...] = hidden
    xhat, _ = normalized(hidden)
    normed = (gains_ref[1:2, :] * xhat).astype(bf16)
    normed_ref[...] = normed
    logits = dot_nn(normed, small_ref[...])
    mask = place_ref[...] >= 0
    logits = jnp.where(mask, pltpu.roll(logits, LANES - 2, 1), -1e30)
    peak = jnp.max(logits, axis=-1, keepdims=True)
    raised = jnp.where(mask, jnp.exp(logits - peak), 0.0)
    gate_ref[...] = raised / jnp.sum(raised, axis=-1, keepdims=True)


def middle(inputs, attended, place, dense):
    length, width = inputs.shape
    row = pl.BlockSpec((BLOCK, width), lambda i: (i, 0))
    thin = pl.BlockSpec((BLOCK, LANES), lambda i: (i, 0))
    return call(
        middle_kernel,
        "middle",
        (length // BLOCK,),
        [inputs, attended, place, dense, dense],
        [
            row,
            row,
            thin,
            pl.BlockSpec((width, width), lambda i: (0, 3)),
            pl.BlockSpec((width, LANES), lambda i: (0, 4 * width // LANES)),
        ],
        [
            shape_of((length, width), f32),
            shape_of((length, width), bf16),
            shape_of((length, LANES), f32),
        ],
        [row, row, thin],
        [pltpu.VMEM((LANES, width), f32)],
        flops=2 * length * width * width,
    )


def window_base(counts_ref, block, expert, experts):
    base = counts_ref[block * experts + expert]
    return pl.multiple_of(jnp.minimum(base // 128 * 128, CAP - WINDOW), 128)


def expert_kernel(
    expert, experts, train, count, rows_ref, order_ref, counts_ref, place_t_ref, gate_ref, normed_ref,
    cot_ref, *rest,
):
    in_pieces, out_pieces, rest = rest[:count], rest[count : 2 * count], rest[2 * count :]
    result_ref, back_ref, rest = rest[0], rest[1], rest[2:]
    if train:
        in_own, in_other, out_own, out_other = rest[:4]
        rest = rest[4:]
        turned_x, acts, grads, staged = rest[6:]
    rows_x, rows_g, sum_r, sum_b, in_ref, out_ref = rest[:6]
    length = normed_ref.shape[0]
    step = pl.program_id(0)
    load = counts_ref[length // BLOCK * experts + expert]

    @pl.when(step == 0)
    def _():
        rows_x[...] = jnp.zeros_like(rows_x)
        rows_g[...] = jnp.zeros_like(rows_g)
        sum_r[...] = jnp.zeros_like(sum_r)
        sum_b[...] = jnp.zeros_like(sum_b)
        for block in range(length // BLOCK):
            base = window_base(counts_ref, block, expert, experts)
            cols = slice(block * BLOCK, (block + 1) * BLOCK)
            pick = flag(iota((WINDOW, BLOCK), 0) + base == place_t_ref[expert : expert + 1, cols])
            window = pl.ds(base, WINDOW)
            rows_x[window, :] += dot_nn(pick, normed_ref[cols, :]).astype(bf16)
            scaled = gate_ref[cols, expert : expert + 1] * cot_ref[cols, :].astype(f32)
            rows_g[window, :] += dot_nn(pick, scaled.astype(bf16)).astype(bf16)
        if train:
            turned_x[...] = rows_x[...].T

    put_together(rows_ref, in_pieces, in_ref)
    put_together(rows_ref, out_pieces, out_ref)

    def tile(index, carry):
        rows = pl.ds(pl.multiple_of(index * ROW_TILE, ROW_TILE), ROW_TILE)
        pre = dot_nn(rows_x[rows, :], in_ref[...])
        grad_rows = rows_g[rows, :]
        square = pre * pre
        bend = jnp.tanh(0.7978845608028654 * pre * (1.0 + 0.044715 * square))
        half = 0.5 + 0.5 * bend
        slope = half + pre * (0.5 - 0.5 * bend * bend) * (
            0.7978845608028654 + 0.1070322243 * square
        )
        act = (pre * half).astype(bf16)
        grad = (dot_nt(grad_rows, out_ref[...]) * slope).astype(bf16)
        sum_r[rows, :] += dot_nn(act, out_ref[...])
        sum_b[rows, :] += dot_nt(grad, in_ref[...])
        if train:
            acts[rows, :] = act
            grads[rows, :] = grad
        return carry

    tiles = jnp.maximum((load + ROW_TILE - 1) // ROW_TILE, 1)
    lax.fori_loop(0, tiles, tile, 0)
    if train:
        for amount in range(1, CAP // ROW_TILE + 1):

            @pl.when(tiles == amount)
            def _(used=amount * ROW_TILE):
                staged[0] = dot_nn(turned_x[:, :used], grads[:used, :]).astype(bf16)
                staged[1] = dot_tn(acts[:used, :], rows_g[:used, :]).astype(bf16)

        lay_out(order_ref, staged.at[0], in_own, in_other)
        lay_out(order_ref, staged.at[1], out_own, out_other)

    @pl.when(step == pl.num_programs(0) - 1)
    def _():
        result_ref[...] = sum_r[...].astype(bf16)
        back_ref[...] = sum_b[...].astype(bf16)


def expert_pass(
    expert, experts, train, rows, order, counts, place_t, gates, normed, cot, pieces
):
    length, width = normed.shape
    hidden = pieces[0].shape[1] // 2
    steps = hidden // width
    half = width // 2
    slab = pl.BlockSpec((half, width), lambda i: (0, i))
    outs = [shape_of((CAP, width), bf16)] * 2
    out_specs = [whole((CAP, width))] * 2
    scratch = [
        pltpu.VMEM((CAP, width), bf16),
        pltpu.VMEM((CAP, width), bf16),
        pltpu.VMEM((CAP, width), f32),
        pltpu.VMEM((CAP, width), f32),
        pltpu.VMEM((width, width), bf16),
        pltpu.VMEM((width, width), bf16),
    ]
    if train:
        outs = outs + [shape_of((half, hidden), bf16)] * 4
        out_specs = out_specs + [slab] * 4
        scratch = scratch + [
            pltpu.VMEM((width, CAP), bf16),
            pltpu.VMEM((CAP, width), bf16),
            pltpu.VMEM((CAP, width), bf16),
            pltpu.VMEM((2, width, width), bf16),
        ]
    return call(
        functools.partial(expert_kernel, expert, experts, train, len(pieces)),
        "expert_%d" % expert,
        (steps,),
        [rows, order, counts, place_t, gates, normed, cot] + pieces + pieces,
        [
            SMEM,
            SMEM,
            SMEM,
            whole(place_t.shape),
            whole(gates.shape),
            whole(normed.shape),
            whole(cot.shape),
        ]
        + gathered_specs(pieces, width, lambda i: i)
        + gathered_specs(pieces, width, lambda i: i + steps),
        outs,
        out_specs,
        scratch,
        limit=56,
        flops=(12 if train else 8) * 600 * width * hidden,
    )


def combine_kernel(
    experts, order_ref, counts_ref, place_ref, gate_ref, hidden_ref, normed_ref, cot_ref, attended_ref,
    weight_ref, small_ref, *rest,
):
    result_refs, back_refs = rest[:experts], rest[experts : 2 * experts]
    (output_ref, grad_hidden_ref, grad_heads_ref, own_ref, other_ref,
     gains_ref, weight_sum, gain_sum, router_sum, staged) = rest[2 * experts :]
    step = pl.program_id(0)

    @pl.when(step == 0)
    def _():
        gains_ref[...] = gains_of(small_ref)
        weight_sum[...] = jnp.zeros_like(weight_sum)
        gain_sum[...] = jnp.zeros_like(gain_sum)
        router_sum[...] = jnp.zeros_like(router_sum)

    cot = cot_ref[...].astype(f32)
    hidden = hidden_ref[...]
    gates = gate_ref[...]
    lane = iota((BLOCK, LANES), 1)
    total, grad_normed = hidden, 0.0
    grad_gate = jnp.zeros((BLOCK, LANES), f32)
    for expert in range(experts):
        base = window_base(counts_ref, step, expert, experts)
        window = pl.ds(base, WINDOW)
        pick = flag(iota((BLOCK, WINDOW), 1) + base == place_ref[:, expert : expert + 1])
        picked = dot_nn(pick, result_refs[expert][window, :])
        total = total + gates[:, expert : expert + 1] * picked
        grad_gate = jnp.where(
            lane == expert, jnp.sum(cot * picked, axis=-1, keepdims=True), grad_gate
        )
        grad_normed = grad_normed + dot_nn(pick, back_refs[expert][window, :])
    output_ref[...] = total.astype(bf16)
    grad_logits = gates * (grad_gate - jnp.sum(gates * grad_gate, axis=-1, keepdims=True))
    high = grad_logits.astype(bf16)
    low = (grad_logits - high.astype(f32)).astype(bf16)
    gains = gains_ref[...]
    router = pltpu.roll(gains, LANES - 2, 0).astype(bf16)
    grad_normed = grad_normed + dot_nn(high, router) + dot_nn(low, router)
    normed = normed_ref[...]
    router_sum[...] += dot_tn(normed, high) + dot_tn(normed, low)
    xhat, inverse = normalized(hidden)
    gain_sum[...] += jnp.sum(grad_normed * xhat, axis=0, keepdims=True)
    grad_hidden = cot + norm_back(xhat, inverse, gains[1:2, :], grad_normed)
    grad_hidden_ref[...] = grad_hidden
    branch = grad_hidden.astype(bf16)
    grad_heads_ref[...] = dot_nt(branch, weight_ref[...]).astype(bf16)
    weight_sum[...] += dot_tn(attended_ref[...], branch)

    @pl.when(step == pl.num_programs(0) - 1)
    def _():
        width = weight_sum.shape[1]
        gain = jnp.broadcast_to(gain_sum[...], (LANES, width)).T
        small = jnp.where(iota((width, LANES), 1) == LANES - 1, gain, router_sum[...])
        staged[:, :width] = weight_sum[...].astype(bf16)
        staged[:, width:] = small.astype(bf16)
        lay_out(order_ref, staged, own_ref, other_ref)


def combine(
    experts, order, counts, place, gates, hidden, normed, cot, attended, dense, results, backs
):
    length, width = hidden.shape
    row = pl.BlockSpec((BLOCK, width), lambda i: (i, 0))
    thin = pl.BlockSpec((BLOCK, LANES), lambda i: (i, 0))
    term = (width // 2, width + LANES)
    return call(
        functools.partial(combine_kernel, experts),
        "combine",
        (length // BLOCK,),
        [order, counts, place, gates, hidden, normed, cot, attended, dense, dense]
        + results
        + backs,
        [
            SMEM,
            SMEM,
            thin,
            thin,
            row,
            row,
            row,
            row,
            pl.BlockSpec((width, width), lambda i: (0, 3)),
            pl.BlockSpec((width, LANES), lambda i: (0, 4 * width // LANES)),
        ]
        + [whole((CAP, width))] * (2 * experts),
        [
            shape_of((length, width), bf16),
            shape_of((length, width), f32),
            shape_of((length, width), bf16),
            shape_of(term, bf16),
            shape_of(term, bf16),
        ],
        [row, row, row, whole(term), whole(term)],
        [
            pltpu.VMEM((LANES, width), f32),
            pltpu.VMEM((width, width), f32),
            pltpu.VMEM((1, width), f32),
            pltpu.VMEM((width, LANES), f32),
            pltpu.VMEM((width, width + LANES), bf16),
        ],
        limit=56,
        flops=8 * length * width * width,
    )


def finish_kernel(
    order_ref, inputs_ref, dq_ref, dk_ref, dv_ref, grad_hidden_ref, weight_ref, small_ref, grad_ref,
    own_ref, other_ref, gains_ref, weight_sum, gain_sum, staged,
):
    step = pl.program_id(0)
    width = inputs_ref.shape[1]

    @pl.when(step == 0)
    def _():
        gains_ref[...] = gains_of(small_ref)
        weight_sum[...] = jnp.zeros_like(weight_sum)
        gain_sum[...] = jnp.zeros_like(gain_sum)

    gain = gains_ref[0:1, :]
    xhat, inverse = normalized(inputs_ref[...].astype(f32))
    normed = (gain * xhat).astype(bf16)
    grad = 0.0
    for k, ref in enumerate((dq_ref, dk_ref, dv_ref)):
        cols = slice(k * width, (k + 1) * width)
        grad = grad + dot_nt(ref[...], weight_ref[:, cols])
        weight_sum[:, cols] += dot_tn(normed, ref[...])
    gain_sum[...] += jnp.sum(grad * xhat, axis=0, keepdims=True)
    grad_ref[...] = grad_hidden_ref[...] + norm_back(xhat, inverse, gain, grad)

    @pl.when(step == pl.num_programs(0) - 1)
    def _():
        staged[:, : 3 * width] = weight_sum[...].astype(bf16)
        staged[:, 3 * width :] = jnp.broadcast_to(gain_sum[...], (LANES, width)).T.astype(bf16)
        lay_out(order_ref, staged, own_ref, other_ref)


def finish(order, inputs, dq, dk, dv, grad_hidden, dense):
    length, width = inputs.shape
    row = pl.BlockSpec((BLOCK, width), lambda i: (i, 0))
    term = (width // 2, 3 * width + LANES)
    return call(
        finish_kernel,
        "finish",
        (length // BLOCK,),
        [order, inputs, dq, dk, dv, grad_hidden, dense, dense],
        [
            SMEM,
            row,
            row,
            row,
            row,
            row,
            pl.BlockSpec((width, 3 * width), lambda i: (0, 0)),
            pl.BlockSpec((width, LANES), lambda i: (0, 4 * width // LANES)),
        ],
        [shape_of((length, width), f32), shape_of(term, bf16), shape_of(term, bf16)],
        [row, whole(term), whole(term)],
        [
            pltpu.VMEM((LANES, width), f32),
            pltpu.VMEM((width, 3 * width), f32),
            pltpu.VMEM((1, width), f32),
            pltpu.VMEM((width, 3 * width + LANES), bf16),
        ],
        limit=56,
        flops=4 * length * width * 3 * width,
    )


AXES = ("wide", "narrow")


class Links:
    def __init__(self, wide, narrow):
        self.wide, self.narrow = wide, narrow
        self.bits = [1 << b for b in range((wide // 2).bit_length() - 1)]
        index = lax.axis_index("wide")
        self.core, self.outer, self.place = index % 2, index // 2, lax.axis_index("narrow")

    def send(self, part, to):
        pairs = []
        for wide in range(self.wide):
            for narrow in range(self.narrow):
                outer, core, place = to(wide // 2, wide % 2, narrow)
                target = (outer * 2 + core) * self.narrow + place
                pairs.append((wide * self.narrow + narrow, target))
        return lax.ppermute(part, AXES, pairs)

    def flip(self, part, mask):
        return self.send(part, lambda o, c, z: (o ^ mask, c, z))

    def swap(self, part):
        return self.send(part, lambda o, c, z: (o, 1 - c, z))

    def shift(self, part, by):
        return self.send(part, lambda o, c, z: (o, c, (z + by) % self.narrow))


def after(values, *deps):
    flat, tree = jax.tree.flatten(values)
    more = jax.tree.leaves(deps)
    held = lax.optimization_barrier(tuple(flat) + tuple(more))
    return jax.tree.unflatten(tree, held[: len(flat)])


class Gather:
    def __init__(self, links, part):
        self.links, self.part = links, part

    def along(self):
        links, part = self.links, self.part
        self.got = [part] + [links.shift(part, -by) for by in range(1, links.narrow)]

    def first(self, *deps):
        links = self.links
        got, rows = self.got, self.part.shape[0]
        full = jnp.concatenate(got + got[:-1], axis=0)
        start = (links.narrow - links.place) % links.narrow * rows
        full = lax.dynamic_slice_in_dim(full, start, links.narrow * rows, 0)
        self.full = full = after(full, *deps) if deps else full
        low, high = links.bits[0], links.bits[1]
        self.low, self.high = links.flip(full, low), links.flip(full, high)
        self.full_over = links.swap(full)

    def second(self, *deps):
        links = self.links
        low, high = links.bits[0], links.bits[1]
        half = self.full.shape[0] // 2
        self.low, self.high = after((self.low, self.high), *deps)
        self.ends = [links.flip(self.low[:half], high), links.flip(self.high[half:], low)]
        self.over = [links.swap(self.low), links.swap(self.high)]

    def pieces(self):
        links = self.links
        low, high = links.bits[0], links.bits[1]
        own = [self.full, self.low, self.high] + self.ends
        over = [self.full_over] + self.over + [links.swap(e) for e in self.ends]
        for bit in links.bits[2:]:
            own = own + [links.flip(p, bit) for p in own]
            over = over + [links.flip(p, bit) for p in over]
        return own + over


def piece_rows(links, own_rows):
    height = links.narrow * own_rows
    low, high = links.bits[0], links.bits[1]
    marks = [(0, 0), (low, 0), (high, 0), (low | high, 0), (low | high, height // 2)]
    for bit in links.bits[2:]:
        marks = marks + [(mask | bit, extra) for mask, extra in marks]
    return jnp.stack(
        [
            ((links.outer ^ mask) * 2 + (links.core ^ over)) * height + extra
            for over in range(2)
            for mask, extra in marks
        ]
    ).astype(i32)


def part_rows(links, own_rows):
    height = links.narrow * own_rows
    return jnp.stack(
        [
            ((links.outer ^ mask) * 2 + (links.core ^ over)) * height
            for over in range(2)
            for mask in range(links.wide // 2)
        ]
    ).astype(i32)


def total(*terms):
    out = terms[0].astype(f32)
    for term in terms[1:]:
        out = out + term.astype(f32)
    return out


class Scatter:
    def __init__(self, links, own, other):
        self.links, self.own = links, own
        self.sent = links.swap(other)

    def first(self, *deps):
        links = self.links
        parts = links.wide // 2
        height = self.own.shape[0] // parts
        got = after(self.sent, *deps) if deps else self.sent
        blocks = [
            [a[m * height : (m + 1) * height] for a in (self.own, got)] for m in range(parts)
        ]
        for bit in links.bits[:1:-1]:
            sent = [links.flip(total(*blocks[m + bit]).astype(bf16), bit) for m in range(bit)]
            blocks = [blocks[m] + [sent[m]] for m in range(bit)]
        low, high = links.bits[0], links.bits[1]
        self.half = half = height // 2
        end = blocks[low | high]
        self.top = links.flip(total(*[b[:half] for b in end]).astype(bf16), low)
        self.bottom = links.flip(total(*[b[half:] for b in end]).astype(bf16), high)
        self.blocks = blocks

    def second(self, *deps):
        links, half, blocks = self.links, self.half, self.blocks
        low, high = links.bits[0], links.bits[1]
        top, bottom = after((self.top, self.bottom), *deps)
        to_high = [b[:half] for b in blocks[high]] + [top], [b[half:] for b in blocks[high]]
        to_low = [b[:half] for b in blocks[low]], [b[half:] for b in blocks[low]] + [bottom]
        to_high = jnp.concatenate([total(*t).astype(bf16) for t in to_high])
        to_low = jnp.concatenate([total(*t).astype(bf16) for t in to_low])
        self.kept = blocks[0] + [links.flip(to_low, low), links.flip(to_high, high)]

    def along(self, *deps):
        links = self.links
        kept = after(self.kept, *deps) if deps else self.kept
        rows = kept[0].shape[0] // links.narrow

        def share(by):
            start = (links.place + by) % links.narrow * rows
            return total(*[lax.dynamic_slice_in_dim(k, start, rows, 0) for k in kept])

        self.got = [share(0)] + [
            links.shift(share(by).astype(bf16), by) for by in range(1, links.narrow)
        ]

    def result(self):
        return total(*self.got)


def on_device(
    wide, narrow, inputs, segment_ids, routes, attention_gain, qkv_weight, output_weight,
    mixture_gain, router_train, router_frozen, expert_in, expert_out, frozen_in, frozen_out,
    cotangent,
):
    links = Links(wide, narrow)
    length, width = inputs.shape
    own_rows = qkv_weight.shape[0]
    train_count = expert_in.shape[1]
    experts = train_count + frozen_in.shape[1]
    groups = expert_in.shape[2] // width
    docs = segment_ids[0]
    small = jnp.concatenate(
        [attention_gain[:, None], mixture_gain[:, None], router_train, router_frozen], axis=1
    )
    small = jnp.pad(small, ((0, 0), (0, LANES - small.shape[1])))
    dense = Gather(links, jnp.concatenate([qkv_weight, output_weight, small], axis=1))
    rows, order = piece_rows(links, own_rows), part_rows(links, own_rows)

    weights = []
    for expert in range(experts):
        if expert < train_count:
            inner, outer = expert_in[:, expert], expert_out[:, expert]
        else:
            inner, outer = frozen_in[:, expert - train_count], frozen_out[:, expert - train_count]
        inner = inner.reshape(own_rows, width, groups).transpose(0, 2, 1).reshape(own_rows, -1)
        weights.append(
            Gather(links, jnp.concatenate([inner, outer.reshape(own_rows, -1)], axis=1))
        )

    chosen = (routes[:, :, None] == jnp.arange(experts, dtype=i32)).astype(i32)
    per_block = jnp.sum(chosen.reshape(length // BLOCK, 2 * BLOCK, experts), axis=1)
    counts = jnp.concatenate([jnp.zeros((1, experts), i32), jnp.cumsum(per_block, axis=0)])
    counts = counts.reshape(-1)
    place, place_t = route_places(routes)

    dense.along()
    chain = [dense] + weights
    for gather in weights:
        gather.along()
    dense.first()
    for before, gather in zip(chain, weights):
        gather.first(before.low, before.high)
        before.second()
    weights[-1].second()

    qkv, dense = project(rows, inputs, dense.pieces())
    attended, logs = attend(docs, qkv)
    hidden, normed, gates = middle(inputs, attended, place, dense)
    results, backs, terms = [], [], []
    for expert in range(experts):
        made = expert_pass(
            expert, experts, expert < train_count, rows, order, counts, place_t, gates, normed,
            cotangent, weights[expert].pieces(),
        )
        results.append(made[0])
        backs.append(made[1])
        if expert < train_count:
            terms.append(Scatter(links, made[2], made[3]))
            terms.append(Scatter(links, made[4], made[5]))
    for term in terms:
        term.first()
        term.second()
        term.along()
    block_output, grad_hidden, grad_heads, *made = combine(
        experts, order, counts, place, gates, hidden, normed, cotangent, attended, dense, results,
        backs,
    )
    out_term = Scatter(links, *made)
    out_term.first()
    out_term.second()
    out_term.along()
    dq, dk, dv = attend_back(docs, qkv, grad_heads, logs)
    input_grad, *made = finish(order, inputs, dq, dk, dv, grad_hidden, dense)
    qkv_term = Scatter(links, *made)
    qkv_term.first()
    qkv_term.second()
    qkv_term.along()
    terms = [t.result() for t in terms]
    out_term, qkv_term = out_term.result(), qkv_term.result()
    in_grad = jnp.stack(
        [
            t.reshape(own_rows, groups, width).transpose(0, 2, 1).reshape(own_rows, -1)
            for t in terms[::2]
        ],
        axis=1,
    )
    down_grad = jnp.stack([t.reshape(own_rows * groups, width) for t in terms[1::2]], axis=1)
    return (
        block_output,
        input_grad,
        qkv_term[:, 3 * width],
        qkv_term[:, : 3 * width],
        out_term[:, :width],
        out_term[:, width + LANES - 1],
        out_term[:, width : width + train_count],
        in_grad,
        down_grad,
    )


def solution(mesh):
    rows = P(AXES)
    return jax.shard_map(
        functools.partial(on_device, mesh.shape["wide"], mesh.shape["narrow"]),
        mesh=mesh,
        in_specs=(rows,) * 14,
        out_specs=(rows,) * 9,
        check_vma=False,
    )
```

time: 1430 us -> 734 us (0.51)
  matrix products: 356 us -> 0 us
  Pallas kernels: 0 us -> 220 us
  blocking collectives: 210 us -> 0 us
  local copies, waits for them, and re-layouts: 235 us -> 72 us
  waiting for transfers between devices: 408 us -> 248 us
  other arithmetic: 188 us -> 31 us
  starting transfers between devices: 0.41 us -> 153 us
    dot_general x33 -> x0, matrix products: 356 us -> none  [the longest x4 45 us: block_scores(): jnp.einsum('qhd,khd->hqk', query_block, key_rows, preferred_element_type=...]
    ppermute x0 -> x108, waiting for transfers between devices: none -> 248 us  [send(): return lax.ppermute(part, AXES, pairs)]
    reduce_scatter x2 -> x0, waiting for transfers between devices: 228 us -> none  [the longest x1 125 us: on_device(): lax.psum_scatter(qkv_term, ('wide', 'narrow'), scatter_dimension=0, tiled...]
    pallas_call x0 -> x11, Pallas kernels: none -> 220 us  [call(): pl.pallas_call(kernel, name=name, grid=grid, in_specs=in_specs, out_specs...]
    ppermute x0 -> x108, starting transfers between devices: none -> 153 us  [send(): return lax.ppermute(part, AXES, pairs)]
    all_gather x2 -> x0, blocking collectives: 129 us -> none  [the longest x1 65.6 us: on_device(): lax.all_gather(router_train, ('wide', 'narrow'), axis=0, tiled=True)]
    unnamed x12 -> x0, waiting for transfers between devices: 127 us -> none
    convert_element_type x9 -> x18, other arithmetic: 102 us -> 19.3 us  [the longest x6 8.29 us: second(): to_low = jnp.concatenate([total(*t).astype(bf16) for t in to_low])]
  transfers between devices with their start and end apart: 10 -> 108, of which waited for: 4 -> 34; matrix products, arithmetic and copies ran while one was open for 46% -> 12% of each run, Pallas kernels for 0% -> 30%
where the time goes in v1:
time: 734 us; the launch traced here: 725 us
  waiting for transfers between devices  248 us (34%)
  Pallas kernels  220 us (30%)
  starting transfers between devices  153 us (21%)
  local copies, waits for them, and re-layouts  72 us (10%)
  other arithmetic  31 us (4%)
    ppermute x108, waiting for transfers between devices, send(): return lax.ppermute(part, AXES, pairs)  248 us
    pallas_call x11, Pallas kernels, call(): pl.pallas_call(kernel, name=name, grid=grid, in_specs=in_specs, out_specs...  220 us
    ppermute x108, starting transfers between devices, send(): return lax.ppermute(part, AXES, pairs)  153 us
    unnamed x215, local copies, waits for them, and re-layouts  24.3 us
  transfers between devices with their start and end apart: 108, of which 34 were waited for; matrix products, arithmetic and copies ran while one was open for 12% of the time, Pallas kernels for 30%

profile of v1, /device:TPU:0, one launch (start us, length us, event | category | flops | bytes accessed | tf_op | source)
XLA Modules:
  0.0 725.3 jit_solution(3404166286384887749)
XLA Ops:
  6.2 5.0 collective-permute-start.12
  13.2 2.8 collective-permute-start
  32.2 2.8 collective-permute-done
  35.0 13.2 %collective-permute-start.2 = (bf16[24,3200]{1,0:T(8,128)(2,1)}, bf16[24,3200]{1,0:T(8,128)(2,1)S(1)}, u32[]{:S(2)}, u32[]{:S(2)}) collective-permute-start(bf16[24,3200]{1,0:T(8,128)(2,1)} %get-tuple-element.231), channel_id=1, source_target_pairs={{0,1},{1,2},{2,3},{3,0},{4,5},{5,6},{6,7},{7,4},{8,9},{9,10},{10,1... | collective-permute-start | bytes 460808 | tf_op jit(solution)/shard_map/ppermute | solution.py:665
  58.7 1.9 collective-permute-start.26
  60.7 2.4 collective-permute-start.36
  65.0 4.3 collective-permute-start.38
  69.3 18.3 %collective-permute-done.25 = bf16[24,6144]{1,0:T(8,128)(2,1)S(1)} collective-permute-done((bf16[24,6144]{1,0:T(8,128)(2,1)}, bf16[24,6144]{1,0:T(8,128)(2,1)S(1)}, u32[]{:S(2)}, u32[]{:S(2)}) %collective-permute-start.25) | collective-permute-done | bytes 294944 | tf_op jit(solution)/shard_map/ppermute | solution.py:665
  87.7 6.2 collective-permute-start.49
  94.2 14.8 %collective-permute-start.50 = (bf16[24,6144]{1,0:T(8,128)(2,1)S(1)}, bf16[24,6144]{1,0:T(8,128)(2,1)S(1)}, u32[]{:S(2)}, u32[]{:S(2)}) collective-permute-start(bf16[24,6144]{1,0:T(8,128)(2,1)S(1)} %copy-done.61), channel_id=1, source_target_pairs={{0,1},{1,2},{2,3},{3,0},{4,5},{5,6},{6,7},{7,4},{8,9},{9,10},{10,1... | collective-permute-start | bytes 884744 | tf_op jit(solution)/shard_map/ppermute | solution.py:665
  109.0 5.5 collective-permute-done.37
  117.7 9.8 %collective-permute-done.3.rest_1_ = bf16[96,3200]{1,0:T(8,128)(2,1)S(1)} collective-permute-done((bf16[96,3200]{1,0:T(8,128)(2,1)S(1)}, bf16[96,3200]{1,0:T(8,128)(2,1)S(1)}, u32[]{:S(2)}, u32[]{:S(2)}) %collective-permute-start.3) | collective-permute-done | bytes 614432 | tf_op jit(solution)/shard_map/ppermute | solution.py:665
  127.5 2.4 collective-permute-done.4.rest_2_
  133.2 1.9 collective-permute-start.6
  135.9 24.8 %collective-permute-done.5.rest_3_ = bf16[48,3200]{1,0:T(8,128)(2,1)S(1)} collective-permute-done((bf16[48,3200]{1,0:T(8,128)(2,1)S(1)}, bf16[48,3200]{1,0:T(8,128)(2,1)S(1)}, u32[]{:S(2)}, u32[]{:S(2)}) %collective-permute-start.5) | collective-permute-done | bytes 307232 | tf_op jit(solution)/shard_map/ppermute | solution.py:665
  168.0 12.1 %collective-permute-done.17.rest_3_.rest_13_ = bf16[48,6144]{1,0:T(8,128)(2,1)S(1)} collective-permute-done((bf16[48,6144]{1,0:T(8,128)(2,1)S(1)}, bf16[48,6144]{1,0:T(8,128)(2,1)S(1)}, u32[]{:S(2)}, u32[]{:S(2)}) %collective-permute-start.17) | collective-permute-done | bytes 589856 | tf_op jit(solution)/shard_map/ppermute | solution.py:665
  181.5 8.3 %project.1 = (bf16[1024,2304]{1,0:T(8,128)(2,1)}, bf16[768,3200]{1,0:T(8,128)(2,1)}) custom-call(s32[10]{0:T(128)S(1)} %stack.61.rows_ref, bf16[1024,768]{1,0:T(8,128)(2,1)} %inputs_ref.5, bf16[96,3200]{1,0:T(8,128)(2,1)S(1)} %constant_dynamic-slice_fusion.4.rest_0_, bf16[96,3200]{1,0:T(8,128)(2,1)S(1)} %collective-permute-done.3.rest_1_, ...), custom_call_target="tpu_custom_call" | custom-call | flops 3623878656 | bytes 16121896 | tf_op jit(solution)/shard_map/project/pallas_call | solution.py:70
  189.9 21.2 %attend.1 = (bf16[1024,768]{1,0:T(8,128)(2,1)S(1)}, f32[6,8,1024]{2,1,0:T(8,128)S(1)}) custom-call(s32[1024,1]{1,0:T(8,128)S(1)} %copy.83.doc_ref, s32[1,1024]{1,0:T(1,128)S(1)} %copy-done.6, bf16[1024,2304]{1,0:T(8,128)(2,1)} %get-tuple-element.74.q_ref.k_ref.v_ref, bf16[1024,2304]{1,0:T(8,128)(2,1)} %get-tuple-element.74.q_ref.k_ref.v_ref, ...), custom_call_target="tpu_custom_call" | custom-call | flops 2415919104 | bytes 15933440 | tf_op jit(solution)/shard_map/attend/pallas_call | solution.py:70
  211.1 7.9 %middle.1 = (f32[1024,768]{1,0:T(8,128)}, bf16[1024,768]{1,0:T(8,128)(2,1)S(1)}, f32[1024,128]{1,0:T(8,128)S(1)}) custom-call(bf16[1024,768]{1,0:T(8,128)(2,1)S(1)} %copy-done.2, bf16[1024,768]{1,0:T(8,128)(2,1)S(1)} %get-tuple-element.75.attended_ref, s32[1024,128]{1,0:T(8,128)S(1)} %get-tuple-element.71.place_ref, ...), custom_call_target="tpu_custom_call" | custom-call | flops 1207959552 | bytes 18743296 | tf_op jit(solution)/shard_map/middle/pallas_call | solution.py:70
  223.1 36.2 %expert_0.1 = (bf16[768,768]{1,0:T(8,128)(2,1)}, bf16[768,768]{1,0:T(8,128)(2,1)}, bf16[384,3072]{1,0:T(8,128)(2,1)}, bf16[384,3072]{1,0:T(8,128)(2,1)}, bf16[38...) custom-call(s32[10]{0:T(128)} %copy-done.7, s32[8]{0:T(128)} %stack.58.order_ref, s32[20]{0:T(128)} %reshape.43.counts_ref, ...), custom_call_target="tpu_custom_call" | custom-call | flops 16986931200 | bytes 34373784 | tf_op jit(solution)/shard_map/expert_0/pallas_call | solution.py:70
  262.1 2.1 collective-permute-start.40
  265.1 2.5 constant_dynamic-slice_fusion.rest_0_.rest_10_
  270.5 19.0 %collective-permute-done.39.rest_1_.rest_11_ = bf16[96,6144]{1,0:T(8,128)(2,1)S(1)} collective-permute-done((bf16[96,6144]{1,0:T(8,128)(2,1)}, bf16[96,6144]{1,0:T(8,128)(2,1)S(1)}, u32[]{:S(2)}, u32[]{:S(2)}) %collective-permute-start.39) | collective-permute-done | bytes 1179680 | tf_op jit(solution)/shard_map/ppermute | solution.py:665
  289.4 1.8 collective-permute-done.40.rest_2_.rest_12_
  292.1 10.9 %collective-permute-done.29.rest_3_.rest_13_ = bf16[48,6144]{1,0:T(8,128)(2,1)S(1)} collective-permute-done((bf16[48,6144]{1,0:T(8,128)(2,1)S(1)}, bf16[48,6144]{1,0:T(8,128)(2,1)S(1)}, u32[]{:S(2)}, u32[]{:S(2)}) %collective-permute-start.29) | collective-permute-done | bytes 589856 | tf_op jit(solution)/shard_map/ppermute | solution.py:665
  304.9 13.9 %collective-permute-done.30.rest_4_.rest_14_ = bf16[48,6144]{1,0:T(8,128)(2,1)S(1)} collective-permute-done((bf16[48,6144]{1,0:T(8,128)(2,1)S(1)}, bf16[48,6144]{1,0:T(8,128)(2,1)S(1)}, u32[]{:S(2)}, u32[]{:S(2)}) %collective-permute-start.30) | collective-permute-done | bytes 589856 | tf_op jit(solution)/shard_map/ppermute | solution.py:665
  327.2 35.8 %expert_1.1 = (bf16[768,768]{1,0:T(8,128)(2,1)}, bf16[768,768]{1,0:T(8,128)(2,1)}, bf16[384,3072]{1,0:T(8,128)(2,1)}, bf16[384,3072]{1,0:T(8,128)(2,1)}, bf16[38...) custom-call(s32[10]{0:T(128)} %copy-done.7, s32[8]{0:T(128)} %stack.58.order_ref, s32[20]{0:T(128)} %reshape.43.counts_ref, ...), custom_call_target="tpu_custom_call" | custom-call | flops 16986931200 | bytes 34373784 | tf_op jit(solution)/shard_map/expert_1/pallas_call | solution.py:70
  363.0 2.1 slice.522
  365.1 1.9 slice.494
  376.3 34.9 %collective-permute-done.42.rest_4_.rest_14_ = bf16[48,6144]{1,0:T(8,128)(2,1)S(1)} collective-permute-done((bf16[48,6144]{1,0:T(8,128)(2,1)S(1)}, bf16[48,6144]{1,0:T(8,128)(2,1)S(1)}, u32[]{:S(2)}, u32[]{:S(2)}) %collective-permute-start.42) | collective-permute-done | bytes 589856 | tf_op jit(solution)/shard_map/ppermute | solution.py:665
  411.9 3.1 collective-permute-done.47.rest_9_.rest_19_
  418.1 13.0 %collective-permute-done.95 = bf16[96,3072]{1,0:T(8,128)(2,1)S(1)} collective-permute-done((bf16[96,3072]{1,0:T(8,128)(2,1)S(1)}, bf16[96,3072]{1,0:T(8,128)(2,1)S(1)}, u32[]{:S(2)}, u32[]{:S(2)}) %collective-permute-start.95) | collective-permute-done | bytes 589856 | tf_op jit(solution)/shard_map/ppermute | solution.py:665
  431.6 25.9 %expert_2.1 = (bf16[768,768]{1,0:T(8,128)(2,1)}, bf16[768,768]{1,0:T(8,128)(2,1)}) custom-call(s32[10]{0:T(128)} %copy-done.7, s32[8]{0:T(128)} %stack.58.order_ref, s32[20]{0:T(128)} %reshape.43.counts_ref, s32[8,1024]{1,0:T(8,128)} %copy-done.8, f32[1024,128]{1,0:T(8,128)} %copy-done.4, bf16[1024,768]{1,0:T(8,128)(2,1)} %copy-done.3, ...), custom_call_target="tpu_custom_call" | custom-call | flops 11324620800 | bytes 24936600 | tf_op jit(solution)/shard_map/expert_2/pallas_call | solution.py:70
  457.5 2.1 slice.445
  460.8 2.7 collective-permute-start.98
  469.6 2.0 collective-permute-done.98
  471.6 2.4 collective-permute-start.56
  476.5 13.1 %collective-permute-done.53.rest_3_.rest_13_ = bf16[48,6144]{1,0:T(8,128)(2,1)} collective-permute-done((bf16[48,6144]{1,0:T(8,128)(2,1)}, bf16[48,6144]{1,0:T(8,128)(2,1)}, u32[]{:S(2)}, u32[]{:S(2)}) %collective-permute-start.53) | collective-permute-done | bytes 589856 | tf_op jit(solution)/shard_map/ppermute | solution.py:665
  489.7 2.9 collective-permute-start.54
  493.9 12.8 %collective-permute-done.54.rest_4_.rest_14_ = bf16[48,6144]{1,0:T(8,128)(2,1)S(1)} collective-permute-done((bf16[48,6144]{1,0:T(8,128)(2,1)}, bf16[48,6144]{1,0:T(8,128)(2,1)S(1)}, u32[]{:S(2)}, u32[]{:S(2)}) %collective-permute-start.54) | collective-permute-done | bytes 589856 | tf_op jit(solution)/shard_map/ppermute | solution.py:665
  507.2 2.0 add_convert_fusion.15
  515.0 13.5 %expert_3.1 = (bf16[768,768]{1,0:T(8,128)(2,1)}, bf16[768,768]{1,0:T(8,128)(2,1)}) custom-call(s32[10]{0:T(128)} %copy-done.7, s32[8]{0:T(128)} %stack.58.order_ref, s32[20]{0:T(128)} %reshape.43.counts_ref, s32[8,1024]{1,0:T(8,128)} %copy-done.8, f32[1024,128]{1,0:T(8,128)} %copy-done.4, bf16[1024,768]{1,0:T(8,128)(2,1)} %copy-done.3, ...), custom_call_target="tpu_custom_call" | custom-call | flops 11324620800 | bytes 24936600 | tf_op jit(solution)/shard_map/expert_3/pallas_call | solution.py:70
  528.5 21.9 %combine.1 = (bf16[1024,768]{1,0:T(8,128)(2,1)}, f32[1024,768]{1,0:T(8,128)}, bf16[1024,768]{1,0:T(8,128)(2,1)}, bf16[384,896]{1,0:T(8,128)(2,1)}, bf16[384,896]{1,0:T(8,128)(2,1)}) custom-call(s32[8]{0:T(128)} %stack.58.order_ref, s32[20]{0:T(128)} %reshape.43.counts_ref, s32[1024,128]{1,0:T(8,128)} %copy-done.1, f32[1024,128]{1,0:T(8,128)} %copy-done.4, ...), custom_call_target="tpu_custom_call" | custom-call | flops 4831838208 | bytes 35848304 | tf_op jit(solution)/shard_map/combine/pallas_call | solution.py:70
  550.4 5.6 collective-permute-start.68
  556.0 31.5 %attend_back.1 = (bf16[1024,768]{1,0:T(8,128)(2,1)S(1)}, bf16[1024,768]{1,0:T(8,128)(2,1)S(1)}, bf16[1024,768]{1,0:T(8,128)(2,1)S(1)}) custom-call(s32[1024,1]{1,0:T(8,128)S(1)} %copy.83.doc_ref, s32[1,1024]{1,0:T(1,128)S(1)} %copy-done.6, bf16[1024,2304]{1,0:T(8,128)(2,1)} %get-tuple-element.74.q_ref.k_ref.v_ref, ...), custom_call_target="tpu_custom_call" | custom-call | flops 6039797760 | bytes 20652032 | tf_op jit(solution)/shard_map/attend_back/pallas_call | solution.py:70
  591.1 16.4 %finish.1 = (f32[1024,768]{1,0:T(8,128)}, bf16[384,2432]{1,0:T(8,128)(2,1)}, bf16[384,2432]{1,0:T(8,128)(2,1)}) custom-call(s32[8]{0:T(128)} %stack.58.order_ref, bf16[1024,768]{1,0:T(8,128)(2,1)} %inputs_ref.5, bf16[1024,768]{1,0:T(8,128)(2,1)} %copy-done.9, bf16[1024,768]{1,0:T(8,128)(2,1)} %copy-done.10, bf16[1024,768]{1,0:T(8,128)(2,1)} %copy-done.11, ...), custom_call_target="tpu_custom_call" | custom-call | flops 7247757312 | bytes 26148896 | tf_op jit(solution)/shard_map/finish/pallas_call | solution.py:70
  613.0 2.1 collective-permute-start.103
  619.4 11.3 %collective-permute-done.69 = bf16[48,896]{1,0:T(8,128)(2,1)S(1)} collective-permute-done((bf16[48,896]{1,0:T(8,128)(2,1)S(1)}, bf16[48,896]{1,0:T(8,128)(2,1)S(1)}, u32[]{:S(2)}, u32[]{:S(2)}) %collective-permute-start.69) | collective-permute-done | bytes 86048 | tf_op jit(solution)/shard_map/ppermute | solution.py:665
  635.9 13.3 %collective-permute-done.71 = bf16[96,896]{1,0:T(8,128)(2,1)S(1)} collective-permute-done((bf16[96,896]{1,0:T(8,128)(2,1)S(1)}, bf16[96,896]{1,0:T(8,128)(2,1)S(1)}, u32[]{:S(2)}, u32[]{:S(2)}) %collective-permute-start.71) | collective-permute-done | bytes 172064 | tf_op jit(solution)/shard_map/ppermute | solution.py:665
  649.2 3.9 collective-permute-start.81
  654.5 3.0 collective-permute-start.74
  657.4 2.0 collective-permute-start.75
  662.8 1.9 collective-permute-start.89
  668.9 1.8 collective-permute-start.91
  671.9 4.3 collective-permute-done.82
  676.2 4.3 collective-permute-start.106
  680.5 3.4 collective-permute-start.107
  683.8 4.9 collective-permute-done.90
  689.6 1.8 collective-permute-start.62
  691.3 2.6 convert_add_fusion.2
  700.1 1.8 collective-permute-start.64
  710.3 3.6 collective-permute-start.65
  713.9 2.8 collective-permute-start.66
  719.0 3.4 collective-permute-done.66
  (492 shorter events, 153.3 us)
Async XLA Ops:
  6.2 52.5 %collective-permute-start.12 = (bf16[24,6144]{1,0:T(8,128)(2,1)}, bf16[24,6144]{1,0:T(8,128)(2,1)S(1)}, u32[]{:S(2)}, u32[]{:S(2)}) collective-permute-start(bf16[24,6144]{1,0:T(8,128)(2,1)} %get-tuple-element.245), channel_id=1, source_target_pairs={{0,3},{1,0},{2,1},{3,2},{4,7},{5,4},{6,5},{7,6},{8,11},{9,8},{10,9... | collective-permute-start | bytes 884744 | tf_op jit(solution)/shard_map/ppermute | solution.py:665
  11.3 49.4 %collective-permute-start.13 = (bf16[24,6144]{1,0:T(8,128)(2,1)}, bf16[24,6144]{1,0:T(8,128)(2,1)S(1)}, u32[]{:S(2)}, u32[]{:S(2)}) collective-permute-start(bf16[24,6144]{1,0:T(8,128)(2,1)} %get-tuple-element.245), channel_id=1, source_target_pairs={{0,2},{1,3},{2,0},{3,1},{4,6},{5,7},{6,4},{7,5},{8,10},{9,11},{10,... | collective-permute-start | bytes 884744 | tf_op jit(solution)/shard_map/ppermute | solution.py:665
  11.3 51.9 %collective-permute-start.14 = (bf16[24,6144]{1,0:T(8,128)(2,1)}, bf16[24,6144]{1,0:T(8,128)(2,1)}, u32[]{:S(2)}, u32[]{:S(2)}) collective-permute-start(bf16[24,6144]{1,0:T(8,128)(2,1)} %get-tuple-element.245), channel_id=1, source_target_pairs={{0,1},{1,2},{2,3},{3,0},{4,5},{5,6},{6,7},{7,4},{8,9},{9,10},{10,1... | collective-permute-start | bytes 884744 | tf_op jit(solution)/shard_map/ppermute | solution.py:665
  13.2 21.8 %collective-permute-start = (bf16[24,3200]{1,0:T(8,128)(2,1)}, bf16[24,3200]{1,0:T(8,128)(2,1)S(1)}, u32[]{:S(2)}, u32[]{:S(2)}) collective-permute-start(bf16[24,3200]{1,0:T(8,128)(2,1)} %get-tuple-element.231), channel_id=1, source_target_pairs={{0,3},{1,0},{2,1},{3,2},{4,7},{5,4},{6,5},{7,6},{8,11},{9,8},{10,9... | collective-permute-start | bytes 460808 | tf_op jit(solution)/shard_map/ppermute | solution.py:665
  16.0 34.1 %collective-permute-start.1 = (bf16[24,3200]{1,0:T(8,128)(2,1)}, bf16[24,3200]{1,0:T(8,128)(2,1)}, u32[]{:S(2)}, u32[]{:S(2)}) collective-permute-start(bf16[24,3200]{1,0:T(8,128)(2,1)} %get-tuple-element.231), channel_id=1, source_target_pairs={{0,2},{1,3},{2,0},{3,1},{4,6},{5,7},{6,4},{7,5},{8,10},{9,11},{10,... | collective-permute-start | bytes 460808 | tf_op jit(solution)/shard_map/ppermute | solution.py:665
  52.7 35.0 %collective-permute-start.25 = (bf16[24,6144]{1,0:T(8,128)(2,1)}, bf16[24,6144]{1,0:T(8,128)(2,1)S(1)}, u32[]{:S(2)}, u32[]{:S(2)}) collective-permute-start(bf16[24,6144]{1,0:T(8,128)(2,1)} %get-tuple-element.241), channel_id=1, source_target_pairs={{0,2},{1,3},{2,0},{3,1},{4,6},{5,7},{6,4},{7,5},{8,10},{9,11},{10,... | collective-permute-start | bytes 884744 | tf_op jit(solution)/shard_map/ppermute | solution.py:665
  58.7 29.0 %collective-permute-start.26 = (bf16[24,6144]{1,0:T(8,128)(2,1)}, bf16[24,6144]{1,0:T(8,128)(2,1)S(1)}, u32[]{:S(2)}, u32[]{:S(2)}) collective-permute-start(bf16[24,6144]{1,0:T(8,128)(2,1)} %get-tuple-element.241), channel_id=1, source_target_pairs={{0,1},{1,2},{2,3},{3,0},{4,5},{5,6},{6,7},{7,4},{8,9},{9,10},{10,1... | collective-permute-start | bytes 884744 | tf_op jit(solution)/shard_map/ppermute | solution.py:665
  60.7 33.5 %collective-permute-start.36 = (bf16[24,6144]{1,0:T(8,128)(2,1)}, bf16[24,6144]{1,0:T(8,128)(2,1)S(1)}, u32[]{:S(2)}, u32[]{:S(2)}) collective-permute-start(bf16[24,6144]{1,0:T(8,128)(2,1)} %get-tuple-element.237), channel_id=1, source_target_pairs={{0,3},{1,0},{2,1},{3,2},{4,7},{5,4},{6,5},{7,6},{8,11},{9,8},{10,9... | collective-permute-start | bytes 884744 | tf_op jit(solution)/shard_map/ppermute | solution.py:665
  63.2 51.3 %collective-permute-start.37 = (bf16[24,6144]{1,0:T(8,128)(2,1)S(1)}, bf16[24,6144]{1,0:T(8,128)(2,1)S(1)}, u32[]{:S(2)}, u32[]{:S(2)}) collective-permute-start(bf16[24,6144]{1,0:T(8,128)(2,1)S(1)} %copy-done.59), channel_id=1, source_target_pairs={{0,2},{1,3},{2,0},{3,1},{4,6},{5,7},{6,4},{7,5},{8,10},{9,11},{10,... | collective-permute-start | bytes 884744 | tf_op jit(solution)/shard_map/ppermute | solution.py:665
  65.0 51.0 %collective-permute-start.38 = (bf16[24,6144]{1,0:T(8,128)(2,1)S(1)}, bf16[24,6144]{1,0:T(8,128)(2,1)S(1)}, u32[]{:S(2)}, u32[]{:S(2)}) collective-permute-start(bf16[24,6144]{1,0:T(8,128)(2,1)S(1)} %copy-done.59), channel_id=1, source_target_pairs={{0,1},{1,2},{2,3},{3,0},{4,5},{5,6},{6,7},{7,4},{8,9},{9,10},{10,1... | collective-permute-start | bytes 884744 | tf_op jit(solution)/shard_map/ppermute | solution.py:665
  87.6 45.0 %collective-permute-start.48 = (bf16[24,6144]{1,0:T(8,128)(2,1)S(1)}, bf16[24,6144]{1,0:T(8,128)(2,1)S(1)}, u32[]{:S(2)}, u32[]{:S(2)}) collective-permute-start(bf16[24,6144]{1,0:T(8,128)(2,1)S(1)} %copy-done.61), channel_id=1, source_target_pairs={{0,3},{1,0},{2,1},{3,2},{4,7},{5,4},{6,5},{7,6},{8,11},{9,8},{10,9... | collective-permute-start | bytes 884744 | tf_op jit(solution)/shard_map/ppermute | solution.py:665
  87.7 45.5 %collective-permute-start.49 = (bf16[24,6144]{1,0:T(8,128)(2,1)S(1)}, bf16[24,6144]{1,0:T(8,128)(2,1)S(1)}, u32[]{:S(2)}, u32[]{:S(2)}) collective-permute-start(bf16[24,6144]{1,0:T(8,128)(2,1)S(1)} %copy-done.61), channel_id=1, source_target_pairs={{0,2},{1,3},{2,0},{3,1},{4,6},{5,7},{6,4},{7,5},{8,10},{9,11},{10,... | collective-permute-start | bytes 884744 | tf_op jit(solution)/shard_map/ppermute | solution.py:665
  94.2 41.7 %collective-permute-start.50 = (bf16[24,6144]{1,0:T(8,128)(2,1)S(1)}, bf16[24,6144]{1,0:T(8,128)(2,1)S(1)}, u32[]{:S(2)}, u32[]{:S(2)}) collective-permute-start(bf16[24,6144]{1,0:T(8,128)(2,1)S(1)} %copy-done.61), channel_id=1, source_target_pairs={{0,1},{1,2},{2,3},{3,0},{4,5},{5,6},{6,7},{7,4},{8,9},{9,10},{10,1... | collective-permute-start | bytes 884744 | tf_op jit(solution)/shard_map/ppermute | solution.py:665
  129.8 31.3 %collective-permute-start.15 = (bf16[96,6144]{1,0:T(8,128)(2,1)S(1)}, bf16[96,6144]{1,0:T(8,128)(2,1)S(1)}, u32[]{:S(2)}, u32[]{:S(2)}) collective-permute-start(bf16[96,6144]{1,0:T(8,128)(2,1)S(1)} %constant_dynamic-slice_fusion.3.rest_0_.rest_10_), channel_id=1, source_target_pairs={{0,8},{1,9},{2,10},{3,11},{4,12},{5,13},{6,14},{7,15},{8,0},{9,1},... | collective-permute-start | bytes 3538952 | tf_op jit(solution)/shard_map/ppermute | solution.py:665
  129.9 31.3 %collective-permute-start.16 = (bf16[96,6144]{1,0:T(8,128)(2,1)S(1)}, bf16[96,6144]{1,0:T(8,128)(2,1)S(1)}, u32[]{:S(2)}, u32[]{:S(2)}) collective-permute-start(bf16[96,6144]{1,0:T(8,128)(2,1)S(1)} %constant_dynamic-slice_fusion.3.rest_0_.rest_10_), channel_id=1, source_target_pairs={{0,16},{1,17},{2,18},{3,19},{4,20},{5,21},{6,22},{7,23},{8,24},{9,... | collective-permute-start | bytes 3538952 | tf_op jit(solution)/shard_map/ppermute | solution.py:665
  132.6 28.0 %collective-permute-start.5 = (bf16[48,3200]{1,0:T(8,128)(2,1)S(1)}, bf16[48,3200]{1,0:T(8,128)(2,1)S(1)}, u32[]{:S(2)}, u32[]{:S(2)}) collective-permute-start(bf16[48,3200]{1,0:T(8,128)(2,1)S(1)} %slice.429), channel_id=1, source_target_pairs={{0,16},{1,17},{2,18},{3,19},{4,20},{5,21},{6,22},{7,23},{8,24},{9,... | collective-permute-start | bytes 921608 | tf_op jit(solution)/shard_map/ppermute | solution.py:665
  133.2 27.4 %collective-permute-start.6 = (bf16[48,3200]{1,0:T(8,128)(2,1)S(1)}, bf16[48,3200]{1,0:T(8,128)(2,1)S(1)}, u32[]{:S(2)}, u32[]{:S(2)}) collective-permute-start(bf16[48,3200]{1,0:T(8,128)(2,1)S(1)} %slice.430), channel_id=1, source_target_pairs={{0,8},{1,9},{2,10},{3,11},{4,12},{5,13},{6,14},{7,15},{8,0},{9,1},... | collective-permute-start | bytes 921608 | tf_op jit(solution)/shard_map/ppermute | solution.py:665
  135.9 26.9 %collective-permute-start.7 = (bf16[96,3200]{1,0:T(8,128)(2,1)S(1)}, bf16[96,3200]{1,0:T(8,128)(2,1)S(1)}, u32[]{:S(2)}, u32[]{:S(2)}) collective-permute-start(bf16[96,3200]{1,0:T(8,128)(2,1)S(1)} %constant_dynamic-slice_fusion.4.rest_0_), channel_id=1, source_target_pairs={{0,4},{1,5},{2,6},{3,7},{4,0},{5,1},{6,2},{7,3},{8,12},{9,13},{10,... | collective-permute-start | bytes 1843208 | tf_op jit(solution)/shard_map/ppermute | solution.py:665
  162.7 58.2 %collective-permute-start.19 = (bf16[96,6144]{1,0:T(8,128)(2,1)S(1)}, bf16[96,6144]{1,0:T(8,128)(2,1)S(1)}, u32[]{:S(2)}, u32[]{:S(2)}) collective-permute-start(bf16[96,6144]{1,0:T(8,128)(2,1)S(1)} %constant_dynamic-slice_fusion.3.rest_0_.rest_10_), channel_id=1, source_target_pairs={{0,4},{1,5},{2,6},{3,7},{4,0},{5,1},{6,2},{7,3},{8,12},{9,13},{10,... | collective-permute-start | bytes 3538952 | tf_op jit(solution)/shard_map/ppermute | solution.py:665
  164.0 58.3 %collective-permute-start.20 = (bf16[96,6144]{1,0:T(8,128)(2,1)S(1)}, bf16[96,6144]{1,0:T(8,128)(2,1)}, u32[]{:S(2)}, u32[]{:S(2)}) collective-permute-start(bf16[96,6144]{1,0:T(8,128)(2,1)S(1)} %collective-permute-done.15.rest_1_.rest_11_), channel_id=1, source_target_pairs={{0,4},{1,5},{2,6},{3,7},{4,0},{5,1},{6,2},{7,3},{8,12},{9,13},{10,... | collective-permute-start | bytes 3538952 | tf_op jit(solution)/shard_map/ppermute | solution.py:665
  164.4 57.9 %collective-permute-start.21 = (bf16[96,6144]{1,0:T(8,128)(2,1)S(1)}, bf16[96,6144]{1,0:T(8,128)(2,1)}, u32[]{:S(2)}, u32[]{:S(2)}) collective-permute-start(bf16[96,6144]{1,0:T(8,128)(2,1)S(1)} %collective-permute-done.16.rest_2_.rest_12_), channel_id=1, source_target_pairs={{0,4},{1,5},{2,6},{3,7},{4,0},{5,1},{6,2},{7,3},{8,12},{9,13},{10,... | collective-permute-start | bytes 3538952 | tf_op jit(solution)/shard_map/ppermute | solution.py:665
  180.2 41.4 %collective-permute-start.22 = (bf16[48,6144]{1,0:T(8,128)(2,1)S(1)}, bf16[48,6144]{1,0:T(8,128)(2,1)S(1)}, u32[]{:S(2)}, u32[]{:S(2)}) collective-permute-start(bf16[48,6144]{1,0:T(8,128)(2,1)S(1)} %collective-permute-done.17.rest_3_.rest_13_), channel_id=1, source_target_pairs={{0,4},{1,5},{2,6},{3,7},{4,0},{5,1},{6,2},{7,3},{8,12},{9,13},{10,... | collective-permute-start | bytes 1769480 | tf_op jit(solution)/shard_map/ppermute | solution.py:665
  181.5 40.8 %collective-permute-start.23 = (bf16[48,6144]{1,0:T(8,128)(2,1)}, bf16[48,6144]{1,0:T(8,128)(2,1)S(1)}, u32[]{:S(2)}, u32[]{:S(2)}) collective-permute-start(bf16[48,6144]{1,0:T(8,128)(2,1)} %collective-permute-done.18.rest_4_.rest_14_), channel_id=1, source_target_pairs={{0,4},{1,5},{2,6},{3,7},{4,0},{5,1},{6,2},{7,3},{8,12},{9,13},{10,... | collective-permute-start | bytes 1769480 | tf_op jit(solution)/shard_map/ppermute | solution.py:665
  221.0 40.3 %collective-permute-start.27 = (bf16[96,6144]{1,0:T(8,128)(2,1)S(1)}, bf16[96,6144]{1,0:T(8,128)(2,1)S(1)}, u32[]{:S(2)}, u32[]{:S(2)}) collective-permute-start(bf16[96,6144]{1,0:T(8,128)(2,1)S(1)} %constant_dynamic-slice_fusion.2.rest_0_.rest_10_), channel_id=1, source_target_pairs={{0,8},{1,9},{2,10},{3,11},{4,12},{5,13},{6,14},{7,15},{8,0},{9,1},... | collective-permute-start | bytes 3538952 | tf_op jit(solution)/shard_map/ppermute | solution.py:665
  221.5 39.7 %collective-permute-start.28 = (bf16[96,6144]{1,0:T(8,128)(2,1)S(1)}, bf16[96,6144]{1,0:T(8,128)(2,1)}, u32[]{:S(2)}, u32[]{:S(2)}) collective-permute-start(bf16[96,6144]{1,0:T(8,128)(2,1)S(1)} %constant_dynamic-slice_fusion.2.rest_0_.rest_10_), channel_id=1, source_target_pairs={{0,16},{1,17},{2,18},{3,19},{4,20},{5,21},{6,22},{7,23},{8,24},{9,... | collective-permute-start | bytes 3538952 | tf_op jit(solution)/shard_map/ppermute | solution.py:665
  259.3 43.8 %collective-permute-start.92 = (bf16[384,3072]{1,0:T(8,128)(2,1)}, bf16[384,3072]{1,0:T(8,128)(2,1)S(1)}, u32[]{:S(2)}, u32[]{:S(2)}) collective-permute-start(bf16[384,3072]{1,0:T(8,128)(2,1)} %get-tuple-element.126), channel_id=1, source_target_pairs={{0,4},{1,5},{2,6},{3,7},{4,0},{5,1},{6,2},{7,3},{8,12},{9,13},{10,... | collective-permute-start | bytes 7077896 | tf_op jit(solution)/shard_map/ppermute | solution.py:665
  260.0 58.8 %collective-permute-start.76 = (bf16[384,3072]{1,0:T(8,128)(2,1)}, bf16[384,3072]{1,0:T(8,128)(2,1)S(1)}, u32[]{:S(2)}, u32[]{:S(2)}) collective-permute-start(bf16[384,3072]{1,0:T(8,128)(2,1)} %get-tuple-element.118), channel_id=1, source_target_pairs={{0,4},{1,5},{2,6},{3,7},{4,0},{5,1},{6,2},{7,3},{8,12},{9,13},{10,... | collective-permute-start | bytes 7077896 | tf_op jit(solution)/shard_map/ppermute | solution.py:665
  261.3 28.2 %collective-permute-start.39 = (bf16[96,6144]{1,0:T(8,128)(2,1)}, bf16[96,6144]{1,0:T(8,128)(2,1)S(1)}, u32[]{:S(2)}, u32[]{:S(2)}) collective-permute-start(bf16[96,6144]{1,0:T(8,128)(2,1)} %constant_dynamic-slice_fusion.1.rest_0_.rest_10_), channel_id=1, source_target_pairs={{0,8},{1,9},{2,10},{3,11},{4,12},{5,13},{6,14},{7,15},{8,0},{9,1},... | collective-permute-start | bytes 3538952 | tf_op jit(solution)/shard_map/ppermute | solution.py:665
  262.1 29.1 %collective-permute-start.40 = (bf16[96,6144]{1,0:T(8,128)(2,1)}, bf16[96,6144]{1,0:T(8,128)(2,1)S(1)}, u32[]{:S(2)}, u32[]{:S(2)}) collective-permute-start(bf16[96,6144]{1,0:T(8,128)(2,1)} %constant_dynamic-slice_fusion.1.rest_0_.rest_10_), channel_id=1, source_target_pairs={{0,16},{1,17},{2,18},{3,19},{4,20},{5,21},{6,22},{7,23},{8,24},{9,... | collective-permute-start | bytes 3538952 | tf_op jit(solution)/shard_map/ppermute | solution.py:665
  265.0 38.0 %collective-permute-start.29 = (bf16[48,6144]{1,0:T(8,128)(2,1)S(1)}, bf16[48,6144]{1,0:T(8,128)(2,1)S(1)}, u32[]{:S(2)}, u32[]{:S(2)}) collective-permute-start(bf16[48,6144]{1,0:T(8,128)(2,1)S(1)} %slice.437), channel_id=1, source_target_pairs={{0,16},{1,17},{2,18},{3,19},{4,20},{5,21},{6,22},{7,23},{8,24},{9,... | collective-permute-start | bytes 1769480 | tf_op jit(solution)/shard_map/ppermute | solution.py:665
  289.4 30.9 %collective-permute-start.31 = (bf16[96,6144]{1,0:T(8,128)(2,1)S(1)}, bf16[96,6144]{1,0:T(8,128)(2,1)S(1)}, u32[]{:S(2)}, u32[]{:S(2)}) collective-permute-start(bf16[96,6144]{1,0:T(8,128)(2,1)S(1)} %copy-done.28), channel_id=1, source_target_pairs={{0,4},{1,5},{2,6},{3,7},{4,0},{5,1},{6,2},{7,3},{8,12},{9,13},{10,... | collective-permute-start | bytes 3538952 | tf_op jit(solution)/shard_map/ppermute | solution.py:665
  291.2 32.0 %collective-permute-start.32 = (bf16[96,6144]{1,0:T(8,128)(2,1)S(1)}, bf16[96,6144]{1,0:T(8,128)(2,1)S(1)}, u32[]{:S(2)}, u32[]{:S(2)}) collective-permute-start(bf16[96,6144]{1,0:T(8,128)(2,1)S(1)} %copy-done.57), channel_id=1, source_target_pairs={{0,4},{1,5},{2,6},{3,7},{4,0},{5,1},{6,2},{7,3},{8,12},{9,13},{10,... | collective-permute-start | bytes 3538952 | tf_op jit(solution)/shard_map/ppermute | solution.py:665
  303.0 22.5 %collective-permute-start.33 = (bf16[96,6144]{1,0:T(8,128)(2,1)}, bf16[96,6144]{1,0:T(8,128)(2,1)}, u32[]{:S(2)}, u32[]{:S(2)}) collective-permute-start(bf16[96,6144]{1,0:T(8,128)(2,1)} %collective-permute-done.28.rest_2_.rest_12_), channel_id=1, source_target_pairs={{0,4},{1,5},{2,6},{3,7},{4,0},{5,1},{6,2},{7,3},{8,12},{9,13},{10,... | collective-permute-start | bytes 3538952 | tf_op jit(solution)/shard_map/ppermute | solution.py:665
  320.3 50.3 %collective-permute-start.41 = (bf16[48,6144]{1,0:T(8,128)(2,1)}, bf16[48,6144]{1,0:T(8,128)(2,1)}, u32[]{:S(2)}, u32[]{:S(2)}) collective-permute-start(bf16[48,6144]{1,0:T(8,128)(2,1)} %slice.441), channel_id=1, source_target_pairs={{0,16},{1,17},{2,18},{3,19},{4,20},{5,21},{6,22},{7,23},{8,24},{9,... | collective-permute-start | bytes 1769480 | tf_op jit(solution)/shard_map/ppermute | solution.py:665
  322.0 48.0 %collective-permute-start.93 = (bf16[48,3072]{1,0:T(8,128)(2,1)}, bf16[48,3072]{1,0:T(8,128)(2,1)S(1)}, u32[]{:S(2)}, u32[]{:S(2)}) collective-permute-start(bf16[48,3072]{1,0:T(8,128)(2,1)} %get-tuple-element.178), channel_id=1, source_target_pairs={{0,8},{1,9},{2,10},{3,11},{4,12},{5,13},{6,14},{7,15},{8,0},{9,1},... | collective-permute-start | bytes 884744 | tf_op jit(solution)/shard_map/ppermute | solution.py:665
  322.6 47.5 %collective-permute-start.94 = (bf16[48,3072]{1,0:T(8,128)(2,1)}, bf16[48,3072]{1,0:T(8,128)(2,1)}, u32[]{:S(2)}, u32[]{:S(2)}) collective-permute-start(bf16[48,3072]{1,0:T(8,128)(2,1)} %get-tuple-element.177), channel_id=1, source_target_pairs={{0,16},{1,17},{2,18},{3,19},{4,20},{5,21},{6,22},{7,23},{8,24},{9,... | collective-permute-start | bytes 884744 | tf_op jit(solution)/shard_map/ppermute | solution.py:665
  324.3 47.0 %collective-permute-start.77 = (bf16[48,3072]{1,0:T(8,128)(2,1)}, bf16[48,3072]{1,0:T(8,128)(2,1)}, u32[]{:S(2)}, u32[]{:S(2)}) collective-permute-start(bf16[48,3072]{1,0:T(8,128)(2,1)} %get-tuple-element.190), channel_id=1, source_target_pairs={{0,8},{1,9},{2,10},{3,11},{4,12},{5,13},{6,14},{7,15},{8,0},{9,1},... | collective-permute-start | bytes 884744 | tf_op jit(solution)/shard_map/ppermute | solution.py:665
  325.5 47.0 %collective-permute-start.78 = (bf16[48,3072]{1,0:T(8,128)(2,1)}, bf16[48,3072]{1,0:T(8,128)(2,1)}, u32[]{:S(2)}, u32[]{:S(2)}) collective-permute-start(bf16[48,3072]{1,0:T(8,128)(2,1)} %get-tuple-element.189), channel_id=1, source_target_pairs={{0,16},{1,17},{2,18},{3,19},{4,20},{5,21},{6,22},{7,23},{8,24},{9,... | collective-permute-start | bytes 884744 | tf_op jit(solution)/shard_map/ppermute | solution.py:665
  370.0 45.6 %collective-permute-start.51 = (bf16[96,6144]{1,0:T(8,128)(2,1)}, bf16[96,6144]{1,0:T(8,128)(2,1)}, u32[]{:S(2)}, u32[]{:S(2)}) collective-permute-start(bf16[96,6144]{1,0:T(8,128)(2,1)} %constant_dynamic-slice_fusion.rest_0_.rest_10_), channel_id=1, source_target_pairs={{0,8},{1,9},{2,10},{3,11},{4,12},{5,13},{6,14},{7,15},{8,0},{9,1},... | collective-permute-start | bytes 3538952 | tf_op jit(solution)/shard_map/ppermute | solution.py:665
  370.6 45.1 %collective-permute-start.52 = (bf16[96,6144]{1,0:T(8,128)(2,1)}, bf16[96,6144]{1,0:T(8,128)(2,1)S(1)}, u32[]{:S(2)}, u32[]{:S(2)}) collective-permute-start(bf16[96,6144]{1,0:T(8,128)(2,1)} %constant_dynamic-slice_fusion.rest_0_.rest_10_), channel_id=1, source_target_pairs={{0,16},{1,17},{2,18},{3,19},{4,20},{5,21},{6,22},{7,23},{8,24},{9,... | collective-permute-start | bytes 3538952 | tf_op jit(solution)/shard_map/ppermute | solution.py:665
  371.3 39.9 %collective-permute-start.42 = (bf16[48,6144]{1,0:T(8,128)(2,1)S(1)}, bf16[48,6144]{1,0:T(8,128)(2,1)S(1)}, u32[]{:S(2)}, u32[]{:S(2)}) collective-permute-start(bf16[48,6144]{1,0:T(8,128)(2,1)S(1)} %slice.442), channel_id=1, source_target_pairs={{0,8},{1,9},{2,10},{3,11},{4,12},{5,13},{6,14},{7,15},{8,0},{9,1},... | collective-permute-start | bytes 1769480 | tf_op jit(solution)/shard_map/ppermute | solution.py:665
  372.5 38.7 %collective-permute-start.46 = (bf16[48,6144]{1,0:T(8,128)(2,1)}, bf16[48,6144]{1,0:T(8,128)(2,1)S(1)}, u32[]{:S(2)}, u32[]{:S(2)}) collective-permute-start(bf16[48,6144]{1,0:T(8,128)(2,1)} %collective-permute-done.41.rest_3_.rest_13_), channel_id=1, source_target_pairs={{0,4},{1,5},{2,6},{3,7},{4,0},{5,1},{6,2},{7,3},{8,12},{9,13},{10,... | collective-permute-start | bytes 1769480 | tf_op jit(solution)/shard_map/ppermute | solution.py:665
  375.7 40.5 %collective-permute-start.44 = (bf16[96,6144]{1,0:T(8,128)(2,1)S(1)}, bf16[96,6144]{1,0:T(8,128)(2,1)S(1)}, u32[]{:S(2)}, u32[]{:S(2)}) collective-permute-start(bf16[96,6144]{1,0:T(8,128)(2,1)S(1)} %copy-done.51), channel_id=1, source_target_pairs={{0,4},{1,5},{2,6},{3,7},{4,0},{5,1},{6,2},{7,3},{8,12},{9,13},{10,... | collective-permute-start | bytes 3538952 | tf_op jit(solution)/shard_map/ppermute | solution.py:665
  415.6 74.0 %collective-permute-start.100 = (bf16[384,3072]{1,0:T(8,128)(2,1)}, bf16[384,3072]{1,0:T(8,128)(2,1)}, u32[]{:S(2)}, u32[]{:S(2)}) collective-permute-start(bf16[384,3072]{1,0:T(8,128)(2,1)} %get-tuple-element.130), channel_id=1, source_target_pairs={{0,4},{1,5},{2,6},{3,7},{4,0},{5,1},{6,2},{7,3},{8,12},{9,13},{10,... | collective-permute-start | bytes 7077896 | tf_op jit(solution)/shard_map/ppermute | solution.py:665
  415.7 91.0 %collective-permute-start.84 = (bf16[384,3072]{1,0:T(8,128)(2,1)}, bf16[384,3072]{1,0:T(8,128)(2,1)}, u32[]{:S(2)}, u32[]{:S(2)}) collective-permute-start(bf16[384,3072]{1,0:T(8,128)(2,1)} %get-tuple-element.122), channel_id=1, source_target_pairs={{0,4},{1,5},{2,6},{3,7},{4,0},{5,1},{6,2},{7,3},{8,12},{9,13},{10,... | collective-permute-start | bytes 7077896 | tf_op jit(solution)/shard_map/ppermute | solution.py:665
  416.2 44.3 %collective-permute-start.96 = (bf16[96,3072]{1,0:T(8,128)(2,1)S(1)}, bf16[96,3072]{1,0:T(8,128)(2,1)S(1)}, u32[]{:S(2)}, u32[]{:S(2)}) collective-permute-start(bf16[96,3072]{1,0:T(8,128)(2,1)S(1)} %pad_maximum_fusion.6), channel_id=1, source_target_pairs={{0,16},{1,17},{2,18},{3,19},{4,20},{5,21},{6,22},{7,23},{8,24},{9,... | collective-permute-start | bytes 1769480 | tf_op jit(solution)/shard_map/ppermute | solution.py:665
  416.9 43.9 %collective-permute-start.79 = (bf16[96,3072]{1,0:T(8,128)(2,1)S(1)}, bf16[96,3072]{1,0:T(8,128)(2,1)S(1)}, u32[]{:S(2)}, u32[]{:S(2)}) collective-permute-start(bf16[96,3072]{1,0:T(8,128)(2,1)S(1)} %pad_maximum_fusion), channel_id=1, source_target_pairs={{0,8},{1,9},{2,10},{3,11},{4,12},{5,13},{6,14},{7,15},{8,0},{9,1},... | collective-permute-start | bytes 1769480 | tf_op jit(solution)/shard_map/ppermute | solution.py:665
  431.1 32.4 %collective-permute-start.80 = (bf16[96,3072]{1,0:T(8,128)(2,1)S(1)}, bf16[96,3072]{1,0:T(8,128)(2,1)S(1)}, u32[]{:S(2)}, u32[]{:S(2)}) collective-permute-start(bf16[96,3072]{1,0:T(8,128)(2,1)S(1)} %pad_maximum_fusion.1), channel_id=1, source_target_pairs={{0,16},{1,17},{2,18},{3,19},{4,20},{5,21},{6,22},{7,23},{8,24},{9,... | collective-permute-start | bytes 1769480 | tf_op jit(solution)/shard_map/ppermute | solution.py:665
  467.9 41.3 %collective-permute-start.55 = (bf16[96,6144]{1,0:T(8,128)(2,1)}, bf16[96,6144]{1,0:T(8,128)(2,1)}, u32[]{:S(2)}, u32[]{:S(2)}) collective-permute-start(bf16[96,6144]{1,0:T(8,128)(2,1)} %constant_dynamic-slice_fusion.rest_0_.rest_10_), channel_id=1, source_target_pairs={{0,4},{1,5},{2,6},{3,7},{4,0},{5,1},{6,2},{7,3},{8,12},{9,13},{10,... | collective-permute-start | bytes 3538952 | tf_op jit(solution)/shard_map/ppermute | solution.py:665
  471.6 41.1 %collective-permute-start.56 = (bf16[96,6144]{1,0:T(8,128)(2,1)}, bf16[96,6144]{1,0:T(8,128)(2,1)}, u32[]{:S(2)}, u32[]{:S(2)}) collective-permute-start(bf16[96,6144]{1,0:T(8,128)(2,1)} %collective-permute-done.51.rest_1_.rest_11_), channel_id=1, source_target_pairs={{0,4},{1,5},{2,6},{3,7},{4,0},{5,1},{6,2},{7,3},{8,12},{9,13},{10,... | collective-permute-start | bytes 3538952 | tf_op jit(solution)/shard_map/ppermute | solution.py:665
  489.6 24.3 %collective-permute-start.57 = (bf16[96,6144]{1,0:T(8,128)(2,1)}, bf16[96,6144]{1,0:T(8,128)(2,1)S(1)}, u32[]{:S(2)}, u32[]{:S(2)}) collective-permute-start(bf16[96,6144]{1,0:T(8,128)(2,1)} %copy-done.48), channel_id=1, source_target_pairs={{0,4},{1,5},{2,6},{3,7},{4,0},{5,1},{6,2},{7,3},{8,12},{9,13},{10,... | collective-permute-start | bytes 3538952 | tf_op jit(solution)/shard_map/ppermute | solution.py:665
  509.2 101.9 %collective-permute-start.101 = (bf16[48,3072]{1,0:T(8,128)(2,1)S(1)}, bf16[48,3072]{1,0:T(8,128)(2,1)S(1)}, u32[]{:S(2)}, u32[]{:S(2)}) collective-permute-start(bf16[48,3072]{1,0:T(8,128)(2,1)S(1)} %get-tuple-element.184), channel_id=1, source_target_pairs={{0,8},{1,9},{2,10},{3,11},{4,12},{5,13},{6,14},{7,15},{8,0},{9,1},... | collective-permute-start | bytes 884744 | tf_op jit(solution)/shard_map/ppermute | solution.py:665
  511.0 100.3 %collective-permute-start.102 = (bf16[48,3072]{1,0:T(8,128)(2,1)S(1)}, bf16[48,3072]{1,0:T(8,128)(2,1)S(1)}, u32[]{:S(2)}, u32[]{:S(2)}) collective-permute-start(bf16[48,3072]{1,0:T(8,128)(2,1)S(1)} %get-tuple-element.183), channel_id=1, source_target_pairs={{0,16},{1,17},{2,18},{3,19},{4,20},{5,21},{6,22},{7,23},{8,24},{9,... | collective-permute-start | bytes 884744 | tf_op jit(solution)/shard_map/ppermute | solution.py:665
  512.3 102.9 %collective-permute-start.85 = (bf16[48,3072]{1,0:T(8,128)(2,1)S(1)}, bf16[48,3072]{1,0:T(8,128)(2,1)S(1)}, u32[]{:S(2)}, u32[]{:S(2)}) collective-permute-start(bf16[48,3072]{1,0:T(8,128)(2,1)S(1)} %get-tuple-element.196), channel_id=1, source_target_pairs={{0,8},{1,9},{2,10},{3,11},{4,12},{5,13},{6,14},{7,15},{8,0},{9,1},... | collective-permute-start | bytes 884744 | tf_op jit(solution)/shard_map/ppermute | solution.py:665
  513.2 103.4 %collective-permute-start.86 = (bf16[48,3072]{1,0:T(8,128)(2,1)}, bf16[48,3072]{1,0:T(8,128)(2,1)S(1)}, u32[]{:S(2)}, u32[]{:S(2)}) collective-permute-start(bf16[48,3072]{1,0:T(8,128)(2,1)} %get-tuple-element.195), channel_id=1, source_target_pairs={{0,16},{1,17},{2,18},{3,19},{4,20},{5,21},{6,22},{7,23},{8,24},{9,... | collective-permute-start | bytes 884744 | tf_op jit(solution)/shard_map/ppermute | solution.py:665
  550.4 67.9 %collective-permute-start.68 = (bf16[384,896]{1,0:T(8,128)(2,1)}, bf16[384,896]{1,0:T(8,128)(2,1)S(1)}, u32[]{:S(2)}, u32[]{:S(2)}) collective-permute-start(bf16[384,896]{1,0:T(8,128)(2,1)} %get-tuple-element.114), channel_id=1, source_target_pairs={{0,4},{1,5},{2,6},{3,7},{4,0},{5,1},{6,2},{7,3},{8,12},{9,13},{10,... | collective-permute-start | bytes 2064392 | tf_op jit(solution)/shard_map/ppermute | solution.py:665
  611.2 57.7 %collective-permute-start.60 = (bf16[384,2432]{1,0:T(8,128)(2,1)}, bf16[384,2432]{1,0:T(8,128)(2,1)}, u32[]{:S(2)}, u32[]{:S(2)}) collective-permute-start(bf16[384,2432]{1,0:T(8,128)(2,1)} %get-tuple-element.110), channel_id=1, source_target_pairs={{0,4},{1,5},{2,6},{3,7},{4,0},{5,1},{6,2},{7,3},{8,12},{9,13},{10,... | collective-permute-start | bytes 5603336 | tf_op jit(solution)/shard_map/ppermute | solution.py:665
  613.0 20.8 %collective-permute-start.103 = (bf16[96,3072]{1,0:T(8,128)(2,1)S(1)}, bf16[96,3072]{1,0:T(8,128)(2,1)S(1)}, u32[]{:S(2)}, u32[]{:S(2)}) collective-permute-start(bf16[96,3072]{1,0:T(8,128)(2,1)S(1)} %pad_maximum_fusion.7), channel_id=1, source_target_pairs={{0,8},{1,9},{2,10},{3,11},{4,12},{5,13},{6,14},{7,15},{8,0},{9,1},... | collective-permute-start | bytes 1769480 | tf_op jit(solution)/shard_map/ppermute | solution.py:665
  630.6 23.8 %collective-permute-start.87 = (bf16[96,3072]{1,0:T(8,128)(2,1)S(1)}, bf16[96,3072]{1,0:T(8,128)(2,1)S(1)}, u32[]{:S(2)}, u32[]{:S(2)}) collective-permute-start(bf16[96,3072]{1,0:T(8,128)(2,1)S(1)} %pad_maximum_fusion.2), channel_id=1, source_target_pairs={{0,8},{1,9},{2,10},{3,11},{4,12},{5,13},{6,14},{7,15},{8,0},{9,1},... | collective-permute-start | bytes 1769480 | tf_op jit(solution)/shard_map/ppermute | solution.py:665
  632.4 25.1 %collective-permute-start.88 = (bf16[96,3072]{1,0:T(8,128)(2,1)S(1)}, bf16[96,3072]{1,0:T(8,128)(2,1)S(1)}, u32[]{:S(2)}, u32[]{:S(2)}) collective-permute-start(bf16[96,3072]{1,0:T(8,128)(2,1)S(1)} %pad_maximum_fusion.3), channel_id=1, source_target_pairs={{0,16},{1,17},{2,18},{3,19},{4,20},{5,21},{6,22},{7,23},{8,24},{9,... | collective-permute-start | bytes 1769480 | tf_op jit(solution)/shard_map/ppermute | solution.py:665
  667.5 21.2 %collective-permute-start.90 = (bf16[24,3072]{1,0:T(8,128)(2,1)}, bf16[24,3072]{1,0:T(8,128)(2,1)S(1)}, u32[]{:S(2)}, u32[]{:S(2)}) collective-permute-start(bf16[24,3072]{1,0:T(8,128)(2,1)} %get-tuple-element.214), channel_id=1, source_target_pairs={{0,2},{1,3},{2,0},{3,1},{4,6},{5,7},{6,4},{7,5},{8,10},{9,11},{10,... | collective-permute-start | bytes 442376 | tf_op jit(solution)/shard_map/ppermute | solution.py:665
  676.2 25.7 %collective-permute-start.105 = (bf16[24,3072]{1,0:T(8,128)(2,1)}, bf16[24,3072]{1,0:T(8,128)(2,1)S(1)}, u32[]{:S(2)}, u32[]{:S(2)}) collective-permute-start(bf16[24,3072]{1,0:T(8,128)(2,1)} %get-tuple-element.206), channel_id=1, source_target_pairs={{0,1},{1,2},{2,3},{3,0},{4,5},{5,6},{6,7},{7,4},{8,9},{9,10},{10,1... | collective-permute-start | bytes 442376 | tf_op jit(solution)/shard_map/ppermute | solution.py:665
  676.2 25.7 %collective-permute-start.106 = (bf16[24,3072]{1,0:T(8,128)(2,1)}, bf16[24,3072]{1,0:T(8,128)(2,1)S(1)}, u32[]{:S(2)}, u32[]{:S(2)}) collective-permute-start(bf16[24,3072]{1,0:T(8,128)(2,1)} %get-tuple-element.208), channel_id=1, source_target_pairs={{0,2},{1,3},{2,0},{3,1},{4,6},{5,7},{6,4},{7,5},{8,10},{9,11},{10,... | collective-permute-start | bytes 442376 | tf_op jit(solution)/shard_map/ppermute | solution.py:665
  680.5 21.4 %collective-permute-start.107 = (bf16[24,3072]{1,0:T(8,128)(2,1)}, bf16[24,3072]{1,0:T(8,128)(2,1)S(1)}, u32[]{:S(2)}, u32[]{:S(2)}) collective-permute-start(bf16[24,3072]{1,0:T(8,128)(2,1)} %get-tuple-element.207), channel_id=1, source_target_pairs={{0,3},{1,0},{2,1},{3,2},{4,7},{5,4},{6,5},{7,6},{8,11},{9,8},{10,9... | collective-permute-start | bytes 442376 | tf_op jit(solution)/shard_map/ppermute | solution.py:665
  (132 other events, 2089.1 us)

commit v2 on v1

--- a/solution.py
+++ b/solution.py
@@ -85,7 +85,10 @@
 
 
 def gathered_specs(pieces, columns, index):
-    return [pl.BlockSpec((p.shape[0], columns), lambda *i: (0, index(*i))) for p in pieces]
+    return [
+        pl.BlockSpec((height, columns), lambda *i, at=at: (at, index(*i)))
+        for _, height, at in pieces
+    ]
 
 
 def put_together(rows_ref, piece_refs, whole_ref):
@@ -139,13 +142,14 @@
 
 
 def project_kernel(count, rows_ref, inputs_ref, *rest):
-    pieces, (qkv_ref, dense_ref, gains_ref) = rest[:count], rest[count:]
+    pieces, (qkv_ref, dense_ref, rows_out_ref, gains_ref) = rest[:count], rest[count:]
     width = inputs_ref.shape[1]
 
     @pl.when(pl.program_id(0) == 0)
     def _():
         put_together(rows_ref, pieces, dense_ref)
         gains_ref[...] = dense_ref[:, 4 * width :].astype(f32).T
+        rows_out_ref[...] = gains_ref[:16, :].astype(bf16)
 
     xhat, _ = normalized(inputs_ref[...].astype(f32))
     normed = (gains_ref[0:1, :] * xhat).astype(bf16)
@@ -154,16 +158,24 @@
 
 def project(rows, inputs, pieces):
     length, width = inputs.shape
-    columns = pieces[0].shape[1]
+    columns = pieces[0][0].shape[1]
     return call(
         functools.partial(project_kernel, len(pieces)),
         "project",
         (length // BLOCK,),
-        [rows, inputs] + pieces,
+        [rows, inputs] + [p[0] for p in pieces],
         [SMEM, pl.BlockSpec((BLOCK, width), lambda i: (i, 0))]
         + gathered_specs(pieces, columns, lambda i: 0),
-        [shape_of((length, 3 * width), bf16), shape_of((width, columns), bf16)],
-        [pl.BlockSpec((BLOCK, 3 * width), lambda i: (i, 0)), whole((width, columns))],
+        [
+            shape_of((length, 3 * width), bf16),
+            shape_of((width, columns), bf16),
+            shape_of((16, width), bf16),
+        ],
+        [
+            pl.BlockSpec((BLOCK, 3 * width), lambda i: (i, 0)),
+            whole((width, columns)),
+            whole((16, width)),
+        ],
         [pltpu.VMEM((LANES, width), f32)],
         flops=2 * length * width * 3 * width,
     )
@@ -363,7 +375,8 @@
         rest = rest[4:]
         turned_x, acts, grads, staged = rest[6:]
     rows_x, rows_g, sum_r, sum_b, in_ref, out_ref = rest[:6]
-    length = normed_ref.shape[0]
+    length, width = normed_ref.shape
+    half = width // 2
     step = pl.program_id(0)
     load = counts_ref[length // BLOCK * experts + expert]
 
@@ -382,7 +395,8 @@
             scaled = gate_ref[cols, expert : expert + 1] * cot_ref[cols, :].astype(f32)
             rows_g[window, :] += dot_nn(pick, scaled.astype(bf16)).astype(bf16)
         if train:
-            turned_x[...] = rows_x[...].T
+            staged[...] = rows_x[...].T
+            lay_out(order_ref, staged, turned_x.at[:half], turned_x.at[half:])
 
     put_together(rows_ref, in_pieces, in_ref)
     put_together(rows_ref, out_pieces, out_ref)
@@ -413,11 +427,12 @@
 
             @pl.when(tiles == amount)
             def _(used=amount * ROW_TILE):
-                staged[0] = dot_nn(turned_x[:, :used], grads[:used, :]).astype(bf16)
-                staged[1] = dot_tn(acts[:used, :], rows_g[:used, :]).astype(bf16)
-
-        lay_out(order_ref, staged.at[0], in_own, in_other)
-        lay_out(order_ref, staged.at[1], out_own, out_other)
+                inner = dot_nn(turned_x[:, :used], grads[:used, :]).astype(bf16)
+                in_own[...] = inner[:half]
+                in_other[...] = inner[half:]
+                staged[...] = dot_tn(acts[:used, :], rows_g[:used, :]).astype(bf16)
+
+        lay_out(order_ref, staged, out_own, out_other)
 
     @pl.when(step == pl.num_programs(0) - 1)
     def _():
@@ -429,7 +444,8 @@
     expert, experts, train, rows, order, counts, place_t, gates, normed, cot, pieces
 ):
     length, width = normed.shape
-    hidden = pieces[0].shape[1] // 2
+    hidden = pieces[0][0].shape[1] // 2
+    arrays = [p[0] for p in pieces]
     steps = hidden // width
     half = width // 2
     slab = pl.BlockSpec((half, width), lambda i: (0, i))
@@ -450,13 +466,13 @@
             pltpu.VMEM((width, CAP), bf16),
             pltpu.VMEM((CAP, width), bf16),
             pltpu.VMEM((CAP, width), bf16),
-            pltpu.VMEM((2, width, width), bf16),
+            pltpu.VMEM((width, width), bf16),
         ]
     return call(
         functools.partial(expert_kernel, expert, experts, train, len(pieces)),
         "expert_%d" % expert,
         (steps,),
-        [rows, order, counts, place_t, gates, normed, cot] + pieces + pieces,
+        [rows, order, counts, place_t, gates, normed, cot] + arrays + arrays,
         [
             SMEM,
             SMEM,
@@ -582,78 +598,186 @@
     )
 
 
-def finish_kernel(
-    order_ref, inputs_ref, dq_ref, dk_ref, dv_ref, grad_hidden_ref, weight_ref, small_ref, grad_ref,
-    own_ref, other_ref, gains_ref, weight_sum, gain_sum, staged,
-):
-    step = pl.program_id(0)
+def weigh_kernel(order_ref, inputs_ref, gain_ref, dq_ref, dk_ref, dv_ref, own_ref, other_ref, turned,
+                 staged):
+    half = inputs_ref.shape[1] // 2
+
+    @pl.when(pl.program_id(0) == 0)
+    def _():
+        xhat, _ = normalized(inputs_ref[...].astype(f32))
+        staged[...] = (gain_ref[0:1, :].astype(f32) * xhat).astype(bf16).T
+        lay_out(order_ref, staged, turned.at[:half], turned.at[half:])
+
+    for k, ref in enumerate((dq_ref, dk_ref, dv_ref)):
+
+        @pl.when(pl.program_id(0) == k)
+        def _(ref=ref):
+            grad = dot_nn(turned[...], ref[...]).astype(bf16)
+            own_ref[...] = grad[:half]
+            other_ref[...] = grad[half:]
+
+
+def weigh(order, inputs, gains, dq, dk, dv):
+    length, width = inputs.shape
+    outs = [shape_of((width // 2, 3 * width), bf16)] * 2
+    return call(
+        weigh_kernel,
+        "weigh",
+        (3,),
+        [order, inputs, gains, dq, dk, dv],
+        [SMEM, whole((length, width)), whole(gains.shape)] + [whole((length, width))] * 3,
+        outs,
+        [pl.BlockSpec((width // 2, width), lambda i: (0, i))] * 2,
+        [pltpu.VMEM((width, length), bf16), pltpu.VMEM((width, length), bf16)],
+        limit=56,
+        flops=2 * length * width * 3 * width,
+    )
+
+
+def finish_kernel(inputs_ref, gain_ref, dq_ref, dk_ref, dv_ref, grad_hidden_ref, weight_ref, grad_ref):
     width = inputs_ref.shape[1]
-
-    @pl.when(step == 0)
-    def _():
-        gains_ref[...] = gains_of(small_ref)
-        weight_sum[...] = jnp.zeros_like(weight_sum)
-        gain_sum[...] = jnp.zeros_like(gain_sum)
-
-    gain = gains_ref[0:1, :]
     xhat, inverse = normalized(inputs_ref[...].astype(f32))
-    normed = (gain * xhat).astype(bf16)
     grad = 0.0
     for k, ref in enumerate((dq_ref, dk_ref, dv_ref)):
-        cols = slice(k * width, (k + 1) * width)
-        grad = grad + dot_nt(ref[...], weight_ref[:, cols])
-        weight_sum[:, cols] += dot_tn(normed, ref[...])
-    gain_sum[...] += jnp.sum(grad * xhat, axis=0, keepdims=True)
+        grad = grad + dot_nt(ref[...], weight_ref[:, k * width : (k + 1) * width])
+    gain = gain_ref[0:1, :].astype(f32)
     grad_ref[...] = grad_hidden_ref[...] + norm_back(xhat, inverse, gain, grad)
 
-    @pl.when(step == pl.num_programs(0) - 1)
-    def _():
-        staged[:, : 3 * width] = weight_sum[...].astype(bf16)
-        staged[:, 3 * width :] = jnp.broadcast_to(gain_sum[...], (LANES, width)).T.astype(bf16)
-        lay_out(order_ref, staged, own_ref, other_ref)
-
-
-def finish(order, inputs, dq, dk, dv, grad_hidden, dense):
+
+def finish(inputs, gains, dq, dk, dv, grad_hidden, dense):
     length, width = inputs.shape
     row = pl.BlockSpec((BLOCK, width), lambda i: (i, 0))
-    term = (width // 2, 3 * width + LANES)
     return call(
         finish_kernel,
         "finish",
         (length // BLOCK,),
-        [order, inputs, dq, dk, dv, grad_hidden, dense, dense],
-        [
-            SMEM,
+        [inputs, gains, dq, dk, dv, grad_hidden, dense],
+        [
             row,
+            whole(gains.shape),
             row,
             row,
             row,
             row,
             pl.BlockSpec((width, 3 * width), lambda i: (0, 0)),
-            pl.BlockSpec((width, LANES), lambda i: (0, 4 * width // LANES)),
         ],
-        [shape_of((length, width), f32), shape_of(term, bf16), shape_of(term, bf16)],
-        [row, whole(term), whole(term)],
-        [
-            pltpu.VMEM((LANES, width), f32),
-            pltpu.VMEM((width, 3 * width), f32),
-            pltpu.VMEM((1, width), f32),
-            pltpu.VMEM((width, 3 * width + LANES), bf16),
-        ],
+        [shape_of((length, width), f32)],
+        [row],
         limit=56,
-        flops=4 * length * width * 3 * width,
-    )
-
-
-AXES = ("wide", "narrow")
+        flops=2 * length * width * 3 * width,
+    )[0]
+
+
+def wide_slices(refs):
+    edges = [sum(r.shape[1] for r in refs[:i]) for i in range(len(refs) + 1)]
+    return [slice(a, b) for a, b in zip(edges, edges[1:])]
+
+
+def end_kernel(count, *refs):
+    own, got, (top, bottom) = refs[:count], refs[count : 2 * count], refs[2 * count :]
+    half = top.shape[0]
+    for one, other, cols in zip(own, got, wide_slices(own)):
+        both = one[...].astype(f32) + other[...].astype(f32)
+        top[:, cols] = both[:half].astype(bf16)
+        bottom[:, cols] = both[half:].astype(bf16)
+
+
+def middle_sums_kernel(count, *refs):
+    own, got = refs[: 2 * count], refs[2 * count : 4 * count]
+    top, bottom, to_low, to_high = refs[4 * count :]
+    half = top.shape[0]
+    for k, cols in enumerate(wide_slices(own[:count])):
+        both = own[k][...].astype(f32) + got[k][...].astype(f32)
+        to_low[:half, cols] = both[:half].astype(bf16)
+        to_low[half:, cols] = (both[half:] + bottom[:, cols].astype(f32)).astype(bf16)
+        both = own[count + k][...].astype(f32) + got[count + k][...].astype(f32)
+        to_high[:half, cols] = (both[:half] + top[:, cols].astype(f32)).astype(bf16)
+        to_high[half:, cols] = both[half:].astype(bf16)
+
+
+def line_sums_kernel(count, narrow, place_ref, *refs):
+    own, got = refs[:count], refs[count : 2 * count]
+    low, high, mine, *sums, whole_ref = refs[2 * count :]
+    rows = mine.shape[0]
+    for one, other, cols in zip(own, got, wide_slices(own)):
+        whole_ref[:, cols] = (
+            one[...].astype(f32)
+            + other[...].astype(f32)
+            + low[:, cols].astype(f32)
+            + high[:, cols].astype(f32)
+        )
+    for by, ref in enumerate([mine] + sums):
+        number = lax.rem(place_ref[0] + by, narrow)
+        if rows % 8 == 0:
+            start = pl.multiple_of(number * rows, 8)
+            ref[...] = whole_ref[pl.ds(start, rows), :].astype(ref.dtype)
+        else:
+            for other in range(narrow):
+
+                @pl.when(number == other)
+                def _(ref=ref, at=other * rows):
+                    ref[...] = whole_ref[at : at + rows, :].astype(ref.dtype)
+
+
+def blocks_at(arrays, number):
+    return [pl.BlockSpec((a.shape[0] // 4, a.shape[1]), lambda *_: (number, 0)) for a in arrays]
+
+
+def end_sums(own, got):
+    count, columns = len(own), sum(a.shape[1] for a in own)
+    outs = [shape_of((own[0].shape[0] // 8, columns), bf16)] * 2
+    return call(
+        functools.partial(end_kernel, count),
+        "end_sums",
+        (1,),
+        own + got,
+        blocks_at(own + got, 3),
+        outs,
+        [whole(o.shape) for o in outs],
+    )
+
+
+def middle_sums(own, got, ends):
+    count, columns = len(own), sum(a.shape[1] for a in own)
+    outs = [shape_of((own[0].shape[0] // 4, columns), bf16)] * 2
+    return call(
+        functools.partial(middle_sums_kernel, count),
+        "middle_sums",
+        (1,),
+        own + own + got + got + ends,
+        blocks_at(own, 1) + blocks_at(own, 2) + blocks_at(got, 1) + blocks_at(got, 2)
+        + [whole(e.shape) for e in ends],
+        outs,
+        [whole(o.shape) for o in outs],
+    )
+
+
+def line_sums(place, narrow, own, got, sides):
+    count, columns = len(own), sum(a.shape[1] for a in own)
+    height = own[0].shape[0] // 4
+    outs = [shape_of((height // narrow, columns), f32)]
+    outs = outs + [shape_of((height // narrow, columns), bf16)] * (narrow - 1)
+    made = call(
+        functools.partial(line_sums_kernel, count, narrow),
+        "line_sums",
+        (1,),
+        [place] + own + got + sides,
+        [SMEM] + blocks_at(own + got, 0) + [whole(s.shape) for s in sides],
+        outs,
+        [whole(o.shape) for o in outs],
+        [pltpu.VMEM((height, columns), f32)],
+    )
+    return made[0], made[1:]
+
+
+AXES = ("outer", "core", "narrow")
 
 
 class Links:
     def __init__(self, wide, narrow):
         self.wide, self.narrow = wide, narrow
         self.bits = [1 << b for b in range((wide // 2).bit_length() - 1)]
-        index = lax.axis_index("wide")
-        self.core, self.outer, self.place = index % 2, index // 2, lax.axis_index("narrow")
+        self.outer, self.core, self.place = (lax.axis_index(axis) for axis in AXES)
 
     def send(self, part, to):
         pairs = []
@@ -681,42 +805,58 @@
     return jax.tree.unflatten(tree, held[: len(flat)])
 
 
+def together(always, step):
+    shapes = jax.eval_shape(step)
+    return lax.cond(
+        always, step, lambda: jax.tree.map(lambda s: jnp.zeros(s.shape, s.dtype), shapes)
+    )
+
+
 class Gather:
     def __init__(self, links, part):
         self.links, self.part = links, part
 
-    def along(self):
-        links, part = self.links, self.part
-        self.got = [part] + [links.shift(part, -by) for by in range(1, links.narrow)]
-
-    def first(self, *deps):
-        links = self.links
-        got, rows = self.got, self.part.shape[0]
-        full = jnp.concatenate(got + got[:-1], axis=0)
-        start = (links.narrow - links.place) % links.narrow * rows
-        full = lax.dynamic_slice_in_dim(full, start, links.narrow * rows, 0)
-        self.full = full = after(full, *deps) if deps else full
-        low, high = links.bits[0], links.bits[1]
-        self.low, self.high = links.flip(full, low), links.flip(full, high)
-        self.full_over = links.swap(full)
-
-    def second(self, *deps):
+    def send_along(self, which=None):
+        which = range(1, self.links.narrow) if which is None else which
+        return [self.links.shift(self.part, -by) for by in which]
+
+    def take_along(self, got):
+        links, rows = self.links, self.part.shape[0]
+        full = jnp.zeros((links.narrow * rows, self.part.shape[1]), self.part.dtype)
+        for by, part in enumerate([self.part] + got):
+            start = (links.place + by) % links.narrow * rows
+            full = lax.dynamic_update_slice_in_dim(full, part, start, 0)
+        self.full = full
+
+    def send_first(self):
+        links, full = self.links, self.full
+        return [links.flip(full, bit) for bit in links.bits[:2]] + [links.swap(full)]
+
+    def take_first(self, got):
+        self.low, self.high, self.full_over = got
+        half = self.full.shape[0] // 2
+        self.sent = [self.low[:half], self.high[half:]]
+
+    def send_second(self):
         links = self.links
         low, high = links.bits[0], links.bits[1]
-        half = self.full.shape[0] // 2
-        self.low, self.high = after((self.low, self.high), *deps)
-        self.ends = [links.flip(self.low[:half], high), links.flip(self.high[half:], low)]
-        self.over = [links.swap(self.low), links.swap(self.high)]
-
-    def pieces(self):
+        ends = [links.flip(self.sent[0], high), links.flip(self.sent[1], low)]
+        return ends + [links.swap(self.low), links.swap(self.high)]
+
+    def take_second(self, got):
+        self.ends, self.over = got[:2], got[2:]
+
+    def send_third(self):
+        return [self.links.swap(e) for e in self.ends]
+
+    def take_third(self, got):
         links = self.links
-        low, high = links.bits[0], links.bits[1]
         own = [self.full, self.low, self.high] + self.ends
-        over = [self.full_over] + self.over + [links.swap(e) for e in self.ends]
+        over = [self.full_over] + self.over + got
         for bit in links.bits[2:]:
             own = own + [links.flip(p, bit) for p in own]
             over = over + [links.flip(p, bit) for p in over]
-        return own + over
+        self.pieces = [(p, p.shape[0], 0) for p in own + over]
 
 
 def piece_rows(links, own_rows):
@@ -754,52 +894,43 @@
 
 class Scatter:
     def __init__(self, links, own, other):
-        self.links, self.own = links, own
-        self.sent = links.swap(other)
-
-    def first(self, *deps):
+        self.links, self.own, self.other = links, own, other
+
+    def send_over(self):
+        return [self.links.swap(part) for part in self.other]
+
+    def take_over(self, got):
+        links, own = self.links, self.own
+        for bit in links.bits[:1:-1]:
+            height = own[0].shape[0] // 2
+            sums = [total(a, b).astype(bf16) for a, b in zip(own, got)]
+            own = [s[:height] for s in sums]
+            got = [links.flip(s[height:], bit) for s in sums]
+        self.near, self.got = own, got
+        self.sums = end_sums(own, got)
+
+    def send_first(self):
+        low, high = self.links.bits[0], self.links.bits[1]
+        return [self.links.flip(self.sums[0], low), self.links.flip(self.sums[1], high)]
+
+    def take_first(self, got):
+        self.sums = middle_sums(self.near, self.got, list(got))
+
+    def send_second(self):
+        low, high = self.links.bits[0], self.links.bits[1]
+        return [self.links.flip(self.sums[0], low), self.links.flip(self.sums[1], high)]
+
+    def take_second(self, got):
         links = self.links
-        parts = links.wide // 2
-        height = self.own.shape[0] // parts
-        got = after(self.sent, *deps) if deps else self.sent
-        blocks = [
-            [a[m * height : (m + 1) * height] for a in (self.own, got)] for m in range(parts)
-        ]
-        for bit in links.bits[:1:-1]:
-            sent = [links.flip(total(*blocks[m + bit]).astype(bf16), bit) for m in range(bit)]
-            blocks = [blocks[m] + [sent[m]] for m in range(bit)]
-        low, high = links.bits[0], links.bits[1]
-        self.half = half = height // 2
-        end = blocks[low | high]
-        self.top = links.flip(total(*[b[:half] for b in end]).astype(bf16), low)
-        self.bottom = links.flip(total(*[b[half:] for b in end]).astype(bf16), high)
-        self.blocks = blocks
-
-    def second(self, *deps):
-        links, half, blocks = self.links, self.half, self.blocks
-        low, high = links.bits[0], links.bits[1]
-        top, bottom = after((self.top, self.bottom), *deps)
-        to_high = [b[:half] for b in blocks[high]] + [top], [b[half:] for b in blocks[high]]
-        to_low = [b[:half] for b in blocks[low]], [b[half:] for b in blocks[low]] + [bottom]
-        to_high = jnp.concatenate([total(*t).astype(bf16) for t in to_high])
-        to_low = jnp.concatenate([total(*t).astype(bf16) for t in to_low])
-        self.kept = blocks[0] + [links.flip(to_low, low), links.flip(to_high, high)]
-
-    def along(self, *deps):
-        links = self.links
-        kept = after(self.kept, *deps) if deps else self.kept
-        rows = kept[0].shape[0] // links.narrow
-
-        def share(by):
-            start = (links.place + by) % links.narrow * rows
-            return total(*[lax.dynamic_slice_in_dim(k, start, rows, 0) for k in kept])
-
-        self.got = [share(0)] + [
-            links.shift(share(by).astype(bf16), by) for by in range(1, links.narrow)
-        ]
-
-    def result(self):
-        return total(*self.got)
+        place = links.place.astype(i32).reshape(1)
+        self.mine, self.sums = line_sums(place, links.narrow, self.near, self.got, list(got))
+
+    def send_along(self, which=None):
+        which = range(1, self.links.narrow) if which is None else which
+        return [self.links.shift(self.sums[by - 1], by) for by in which]
+
+    def take_along(self, got):
+        self.result = total(self.mine, *got)
 
 
 def on_device(
@@ -821,80 +952,168 @@
     dense = Gather(links, jnp.concatenate([qkv_weight, output_weight, small], axis=1))
     rows, order = piece_rows(links, own_rows), part_rows(links, own_rows)
 
-    weights = []
-    for expert in range(experts):
-        if expert < train_count:
-            inner, outer = expert_in[:, expert], expert_out[:, expert]
-        else:
-            inner, outer = frozen_in[:, expert - train_count], frozen_out[:, expert - train_count]
+    def packed(inner, outer):
         inner = inner.reshape(own_rows, width, groups).transpose(0, 2, 1).reshape(own_rows, -1)
-        weights.append(
-            Gather(links, jnp.concatenate([inner, outer.reshape(own_rows, -1)], axis=1))
-        )
-
+        return jnp.concatenate([inner, outer.reshape(own_rows, -1)], axis=1)
+
+    def part_of(e):
+        if e < train_count:
+            return packed(expert_in[:, e], expert_out[:, e])
+        return packed(frozen_in[:, e - train_count], frozen_out[:, e - train_count])
+
+    weights = [Gather(links, part_of(e)) for e in range(experts)]
+    always = segment_ids[0, 0] >= 0
     chosen = (routes[:, :, None] == jnp.arange(experts, dtype=i32)).astype(i32)
     per_block = jnp.sum(chosen.reshape(length // BLOCK, 2 * BLOCK, experts), axis=1)
     counts = jnp.concatenate([jnp.zeros((1, experts), i32), jnp.cumsum(per_block, axis=0)])
     counts = counts.reshape(-1)
     place, place_t = route_places(routes)
 
-    dense.along()
-    chain = [dense] + weights
-    for gather in weights:
-        gather.along()
-    dense.first()
-    for before, gather in zip(chain, weights):
-        gather.first(before.low, before.high)
-        before.second()
-    weights[-1].second()
-
-    qkv, dense = project(rows, inputs, dense.pieces())
-    attended, logs = attend(docs, qkv)
-    hidden, normed, gates = middle(inputs, attended, place, dense)
-    results, backs, terms = [], [], []
-    for expert in range(experts):
-        made = expert_pass(
+    def run(expert, normed):
+        return expert_pass(
             expert, experts, expert < train_count, rows, order, counts, place_t, gates, normed,
-            cotangent, weights[expert].pieces(),
+            cotangent, weights[expert].pieces,
         )
-        results.append(made[0])
-        backs.append(made[1])
-        if expert < train_count:
-            terms.append(Scatter(links, made[2], made[3]))
-            terms.append(Scatter(links, made[4], made[5]))
-    for term in terms:
-        term.first()
-        term.second()
-        term.along()
-    block_output, grad_hidden, grad_heads, *made = combine(
-        experts, order, counts, place, gates, hidden, normed, cotangent, attended, dense, results,
-        backs,
-    )
-    out_term = Scatter(links, *made)
-    out_term.first()
-    out_term.second()
-    out_term.along()
-    dq, dk, dv = attend_back(docs, qkv, grad_heads, logs)
-    input_grad, *made = finish(order, inputs, dq, dk, dv, grad_hidden, dense)
-    qkv_term = Scatter(links, *made)
-    qkv_term.first()
-    qkv_term.second()
-    qkv_term.along()
-    terms = [t.result() for t in terms]
-    out_term, qkv_term = out_term.result(), qkv_term.result()
-    in_grad = jnp.stack(
-        [
-            t.reshape(own_rows, groups, width).transpose(0, 2, 1).reshape(own_rows, -1)
-            for t in terms[::2]
-        ],
-        axis=1,
-    )
-    down_grad = jnp.stack([t.reshape(own_rows * groups, width) for t in terms[1::2]], axis=1)
+
+    shifts = list(range(1, narrow))
+
+    def line(gather, *deps):
+        part = after(gather.part, *deps) if deps else gather.part
+        gather.full = lax.all_gather(part, "narrow", axis=0, tiled=True)
+
+    w0, w1, w2, w3 = weights
+    w0.part = after(w0.part, dense.part)
+    line(w0)
+    dense.take_along(dense.send_along())
+    line(w1, dense.full)
+    dense.take_first(dense.send_first())
+    line(w2, dense.low)
+    dense.take_second(dense.send_second())
+    line(w3, dense.ends)
+    dense.take_third(dense.send_third())
+
+    def step():
+        qkv, full, gains = project(rows, inputs, dense.pieces)
+        attended, logs = attend(docs, qkv)
+        return w0.send_first(), (qkv, full, gains, attended, logs)
+
+    got, (qkv, dense, gains, attended, logs) = together(always, step)
+    w0.take_first(got)
+    got, (hidden, normed, gates) = together(
+        always, lambda: (w0.send_second(), middle(inputs, attended, place, dense))
+    )
+    w0.take_second(got)
+    w0.take_third(w0.send_third())
+    got, one = together(always, lambda: (w1.send_first(), run(0, normed)))
+    w1.take_first(got)
+    w1.take_second(w1.send_second())
+    w1.take_third(w1.send_third())
+    term0 = Scatter(links, [one[2], one[4]], [one[3], one[5]])
+    w2.full = after(w2.full, one[0])
+    got, more, two = together(
+        always, lambda: (w2.send_first(), term0.send_over(), run(1, normed))
+    )
+    w2.take_first(got)
+
+    def step():
+        term0.take_over(more)
+        return w2.send_second(), (term0.near, term0.got, term0.sums)
+
+    got, (term0.near, term0.got, term0.sums) = together(always, step)
+    w2.take_second(got)
+    w2.take_third(w2.send_third())
+    term1 = Scatter(links, [two[2], two[4]], [two[3], two[5]])
+    w3.full = after(w3.full, two[0])
+    got, more, three = together(
+        always, lambda: (w3.send_first(), term1.send_over(), run(2, normed))
+    )
+    w3.take_first(got)
+
+    def step():
+        term1.take_over(more)
+        return w3.send_second(), (term1.near, term1.got, term1.sums)
+
+    got, (term1.near, term1.got, term1.sums) = together(always, step)
+    w3.take_second(got)
+    w3.take_third(w3.send_third())
+    got, more, four = together(
+        always, lambda: (term0.send_first(), term1.send_first(), run(3, normed))
+    )
+    term0.take_first(got)
+    results, backs = [[m[i] for m in (one, two, three, four)] for i in range(2)]
+
+    def step():
+        made = combine(
+            experts, order, counts, place, gates, hidden, normed, cotangent, attended, dense,
+            results, backs,
+        )
+        term1.take_first(more)
+        return term0.send_second(), term1.sums, made
+
+    got, term1.sums, (block_output, grad_hidden, grad_heads, *made) = together(always, step)
+    term0.take_second(got)
+    out_term = Scatter(links, *[[m] for m in made])
+    got, more, (dq, dk, dv) = together(
+        always,
+        lambda: (
+            term1.send_second(), term0.send_along(), attend_back(docs, qkv, grad_heads, logs)
+        ),
+    )
+    term1.take_second(got)
+    over, one, made = together(
+        always,
+        lambda: (
+            out_term.send_over(), term1.send_along(shifts[:1]),
+            weigh(order, inputs, gains, dq, dk, dv),
+        ),
+    )
+    out_term.take_over(over)
+    qkv_term = Scatter(links, *[[m] for m in made])
+    over, got, last, input_grad = together(
+        always,
+        lambda: (
+            qkv_term.send_over(), out_term.send_first(), term1.send_along(shifts[2:]),
+            finish(inputs, gains, dq, dk, dv, grad_hidden, dense),
+        ),
+    )
+    qkv_term.take_over(over)
+    out_term.take_first(got)
+
+    def unpacked(parts):
+        full = total(*parts)
+        inner = groups * width
+        inner, outer = full[:, :inner], full[:, inner:]
+        inner = inner.reshape(own_rows, groups, width).transpose(0, 2, 1).reshape(own_rows, -1)
+        return inner, outer.reshape(own_rows * groups, width)
+
+    got, two, first = together(
+        always,
+        lambda: (
+            qkv_term.send_first(), out_term.send_second(), unpacked([term0.mine] + more)
+        ),
+    )
+    qkv_term.take_first(got)
+    out_term.take_second(two)
+    got, middle_part = together(
+        always, lambda: (qkv_term.send_second(), term1.send_along(shifts[1:2]))
+    )
+    qkv_term.take_second(got)
+
+    def step():
+        second = unpacked([term1.mine] + one + middle_part + last)
+        in_grad, down_grad = [jnp.stack(pair, axis=1) for pair in zip(first, second)]
+        return qkv_term.send_along(), out_term.send_along(), in_grad, down_grad
+
+    got, two, in_grad, down_grad = together(always, step)
+    qkv_term.take_along(got)
+    out_term.take_along(two)
+    out_term, qkv_grad = out_term.result, qkv_term.result
+    gain_grad = jnp.sum(qkv_weight.astype(f32) * qkv_grad, axis=1) / attention_gain.astype(f32)
     return (
         block_output,
         input_grad,
-        qkv_term[:, 3 * width],
-        qkv_term[:, : 3 * width],
+        gain_grad,
+        qkv_grad,
         out_term[:, :width],
         out_term[:, width + LANES - 1],
         out_term[:, width : width + train_count],
@@ -904,9 +1123,11 @@
 
 
 def solution(mesh):
+    wide, narrow = mesh.shape["wide"], mesh.shape["narrow"]
+    mesh = Mesh(mesh.devices.reshape(wide // 2, 2, narrow), AXES)
     rows = P(AXES)
     return jax.shard_map(
-        functools.partial(on_device, mesh.shape["wide"], mesh.shape["narrow"]),
+        functools.partial(on_device, wide, narrow),
         mesh=mesh,
         in_specs=(rows,) * 14,
         out_specs=(rows,) * 9,

time: 734 us -> 492 us (0.67)
  waiting for transfers between devices: 248 us -> 88.6 us
  starting transfers between devices: 153 us -> 64.1 us
  Pallas kernels: 220 us -> 251 us
  local copies, waits for them, and re-layouts: 72 us -> 50.2 us
  other arithmetic: 31 us -> 11.6 us
  between operations: 2.4 us -> 15.3 us
    ppermute x108 -> x82, waiting for transfers between devices: 248 us -> 88.5 us  [send(): return lax.ppermute(part, AXES, pairs)]
    ppermute x108 -> x82, starting transfers between devices: 153 us -> 63.9 us  [send(): return lax.ppermute(part, AXES, pairs)]
    pallas_call x11 -> x24, Pallas kernels: 220 us -> 251 us  [call(): pl.pallas_call(kernel, name=name, grid=grid, in_specs=in_specs, out_specs...]
    unnamed x215 -> x67, local copies, waits for them, and re-layouts: 24.3 us -> 4.36 us
    convert_element_type x18 -> x6, other arithmetic: 19.3 us -> 2.76 us  [total(): out = out + term.astype(f32)]
    cond x0 -> x28, local copies, waits for them, and re-layouts: none -> 13.4 us
    slice x32 -> x21, local copies, waits for them, and re-layouts: 26.5 us -> 22.6 us  [the longest x10 12.4 us: take_first(): self.sent = [self.low[:half], self.high[half:]]]
  transfers between devices with their start and end apart: 108 -> 86, of which waited for: 34 -> 29; matrix products, arithmetic and copies ran while one was open for 12% -> 11% of each run, Pallas kernels for 30% -> 47%
where the time goes in v2:
time: 492 us; the launch traced here: 484 us
  Pallas kernels  251 us (51%)
  waiting for transfers between devices  88.6 us (18%)
  starting transfers between devices  64.1 us (13%)
  local copies, waits for them, and re-layouts  50.2 us (10%)
  between operations  15.3 us (3%)
  other arithmetic  11.6 us (2%)
    pallas_call x24, Pallas kernels, call(): pl.pallas_call(kernel, name=name, grid=grid, in_specs=in_specs, out_specs...  251 us
    ppermute x82, waiting for transfers between devices, send(): return lax.ppermute(part, AXES, pairs)  88.5 us
    ppermute x82, starting transfers between devices, send(): return lax.ppermute(part, AXES, pairs)  63.9 us
    cond x28, local copies, waits for them, and re-layouts  13.4 us
    slice x10, local copies, waits for them, and re-layouts, take_first(): self.sent = [self.low[:half], self.high[half:]]  12.4 us
  transfers between devices with their start and end apart: 86, of which 29 were waited for; matrix products, arithmetic and copies ran while one was open for 11% of the time, Pallas kernels for 47%

profile of v2, /device:TPU:0, one launch (start us, length us, event | category | flops | bytes accessed | tf_op | source)
XLA Modules:
  0.0 483.5 jit_solution(4519791701947909922)
XLA Ops:
  9.1 5.1 %collective-permute-start.58 = (bf16[24,3200]{1,0:T(8,128)(2,1)S(1)}, bf16[24,3200]{1,0:T(8,128)(2,1)S(1)}, u32[]{:S(2)}, u32[]{:S(2)}) collective-permute-start(bf16[24,3200]{1,0:T(8,128)(2,1)S(1)} %get-tuple-element.1027), channel_id=1, source_target_pairs={{0,3},{1,0},{2,1},{3,2},{4,7},{5,4},{6,5},{7,6},{8,11},{9,8},{10,9... | collective-permute-start | bytes 460808 | tf_op jit(solution)/shard_map/ppermute | solution.py:789
  22.0 5.1 %collective-permute-done.59 = bf16[24,3200]{1,0:T(8,128)(2,1)S(1)} collective-permute-done((bf16[24,3200]{1,0:T(8,128)(2,1)S(1)}, bf16[24,3200]{1,0:T(8,128)(2,1)S(1)}, u32[]{:S(2)}, u32[]{:S(2)}) %collective-permute-start.59) | collective-permute-done | bytes 153632 | tf_op jit(solution)/shard_map/ppermute | solution.py:789
  32.7 1.9 slice_reduce_fusion
  34.7 7.9 %collective-permute-done.61 = bf16[96,3200]{1,0:T(8,128)(2,1)S(1)} collective-permute-done((bf16[96,3200]{1,0:T(8,128)(2,1)S(1)}, bf16[96,3200]{1,0:T(8,128)(2,1)S(1)}, u32[]{:S(2)}, u32[]{:S(2)}) %collective-permute-start.61) | collective-permute-done | bytes 614432 | tf_op jit(solution)/shard_map/ppermute | solution.py:789
  48.1 2.4 collective-permute-done.63
  50.5 2.4 collective-permute-done.64
  55.6 37.6 %conditional.15 = (bf16[96,6144]{1,0:T(8,128)(2,1)}, bf16[96,6144]{1,0:T(8,128)(2,1)}, bf16[96,6144]{1,0:T(8,128)(2,1)}, bf16[1024,2304]{1,0:T(8,128)(2,1)}, bf1...) conditional(s32[]{:T(128)} %bitcast.10, () %tuple.165, ...), branch_computations={%region_2.3_spmd, %region_3.4_spmd} | conditional | flops 6039797760 | bytes 56123688 | solution.py:810
  58.2 9.6 %project.1 = (bf16[1024,2304]{1,0:T(8,128)(2,1)}, bf16[768,3200]{1,0:T(8,128)(2,1)}, bf16[16,768]{1,0:T(8,128)(2,1)}) custom-call(s32[10]{0:T(128)S(1)} %get-tuple-element.399.rows_ref, bf16[1024,768]{1,0:T(8,128)(2,1)} %get-tuple-element.400.inputs_ref, bf16[96,3200]{1,0:T(8,128)(2,1)S(1)} %get-tuple-element.401.rest_0_, ...), custom_call_target="tpu_custom_call" | custom-call | flops 3623878656 | bytes 16146472 | tf_op jit(solution)/shard_map/cond/branch_1_fun/project/pallas_call | solution.py:70
  67.8 21.5 %attend.1 = (bf16[1024,768]{1,0:T(8,128)(2,1)}, f32[6,8,1024]{2,1,0:T(8,128)}) custom-call(s32[1024,1]{1,0:T(8,128)S(1)} %copy.95.doc_ref, s32[1,1024]{1,0:T(1,128)S(1)} %get-tuple-element.414.doc_t_ref, bf16[1024,2304]{1,0:T(8,128)(2,1)} %get-tuple-element.1042.q_ref.k_ref.v_ref, bf16[1024,2304]{1,0:T(8,128)(2,1)} %get-tuple-element.1042.q_ref.k_ref.v_ref, ...), custom_call_target="tpu_custom_call" | custom-call | flops 2415919104 | bytes 15933440 | tf_op jit(solution)/shard_map/cond/branch_1_fun/attend/pallas_call | solution.py:70
  89.3 2.1 slice.112
  91.4 1.9 slice.113
  94.4 17.8 %conditional.16 = (bf16[48,6144]{1,0:T(8,128)(2,1)}, bf16[48,6144]{1,0:T(8,128)(2,1)}, bf16[96,6144]{1,0:T(8,128)(2,1)}, bf16[96,6144]{1,0:T(8,128)(2,1)}, f32[1...) conditional(s32[]{:T(128)} %bitcast.10, () %tuple.164, (bf16[48,6144]{1,0:T(8,128)(2,1)}, ...), branch_computations={%region_4.5_spmd, %region_5.6_spmd} | conditional | flops 1207959552 | bytes 32899288 | solution.py:810
  97.0 7.3 %middle.1 = (f32[1024,768]{1,0:T(8,128)}, bf16[1024,768]{1,0:T(8,128)(2,1)}, f32[1024,128]{1,0:T(8,128)S(1)}) custom-call(bf16[1024,768]{1,0:T(8,128)(2,1)} %get-tuple-element.421.inputs_ref, bf16[1024,768]{1,0:T(8,128)(2,1)S(1)} %get-tuple-element.422.attended_ref, s32[1024,128]{1,0:T(8,128)S(1)} %get-tuple-element.423.place_ref, ...), custom_call_target="tpu_custom_call" | custom-call | flops 1207959552 | bytes 18743296 | tf_op jit(solution)/shard_map/cond/branch_1_fun/middle/pallas_call | solution.py:70
  104.4 6.6 %collective-permute-done.3 = bf16[48,6144]{1,0:T(8,128)(2,1)} collective-permute-done((bf16[48,6144]{1,0:T(8,128)(2,1)}, bf16[48,6144]{1,0:T(8,128)(2,1)}, u32[]{:S(2)}, u32[]{:S(2)}) %collective-permute-start.3) | collective-permute-done | bytes 589856 | tf_op jit(solution)/shard_map/cond/branch_1_fun/ppermute | solution.py:789
  115.7 29.1 %conditional.17 = (bf16[96,6144]{1,0:T(8,128)(2,1)}, bf16[96,6144]{1,0:T(8,128)(2,1)}, bf16[96,6144]{1,0:T(8,128)(2,1)}, bf16[768,768]{1,0:T(8,128)(2,1)}, bf16[...) conditional(s32[]{:T(128)} %bitcast.10, () %tuple.162, ...), branch_computations={%region_6.7_spmd, %region_7.8_spmd} | conditional | flops 16986931200 | bytes 48529752 | solution.py:810
  117.8 25.7 %expert_0.1 = (bf16[768,768]{1,0:T(8,128)(2,1)}, bf16[768,768]{1,0:T(8,128)(2,1)}, bf16[384,3072]{1,0:T(8,128)(2,1)}, bf16[384,3072]{1,0:T(8,128)(2,1)}, bf16[38...) custom-call(s32[10]{0:T(128)S(1)} %get-tuple-element.429.rows_ref, s32[8]{0:T(128)S(1)} %get-tuple-element.430.order_ref, ...), custom_call_target="tpu_custom_call" | custom-call | flops 16986931200 | bytes 34373784 | tf_op jit(solution)/shard_map/cond/branch_1_fun/expert_0/pallas_call | solution.py:70
  144.7 1.9 slice.105
  151.0 12.9 %collective-permute-done.72 = bf16[48,6144]{1,0:T(8,128)(2,1)} collective-permute-done((bf16[48,6144]{1,0:T(8,128)(2,1)}, bf16[48,6144]{1,0:T(8,128)(2,1)}, u32[]{:S(2)}, u32[]{:S(2)}) %collective-permute-start.72) | collective-permute-done | bytes 589856 | tf_op jit(solution)/shard_map/ppermute | solution.py:789
  164.5 1.8 collective-permute-done.76
  167.0 39.4 %conditional.18 = (bf16[96,6144]{1,0:T(8,128)(2,1)}, bf16[96,6144]{1,0:T(8,128)(2,1)}, bf16[96,6144]{1,0:T(8,128)(2,1)}, bf16[384,3072]{1,0:T(8,128)(2,1)}, bf16...) conditional(s32[]{:T(128)} %bitcast.10, () %tuple.160, ...), branch_computations={%region_8.9_spmd, %region_9.10_spmd} | conditional | flops 16986931200 | bytes 80642616 | solution.py:810
  170.0 34.2 %expert_1.1 = (bf16[768,768]{1,0:T(8,128)(2,1)S(1)}, bf16[768,768]{1,0:T(8,128)(2,1)}, bf16[384,3072]{1,0:T(8,128)(2,1)S(1)}, bf16[384,3072]{1,0:T(8,128)(2,1)},...) custom-call(s32[10]{0:T(128)S(1)} %get-tuple-element.455.rows_ref, s32[8]{0:T(128)S(1)} %get-tuple-element.456.order_ref, ...), custom_call_target="tpu_custom_call" | custom-call | flops 16986931200 | bytes 34373784 | tf_op jit(solution)/shard_map/cond/branch_1_fun/expert_1/pallas_call | solution.py:70
  206.4 17.5 %conditional.19 = (bf16[48,6144]{1,0:T(8,128)(2,1)}, bf16[48,6144]{1,0:T(8,128)(2,1)}, bf16[96,6144]{1,0:T(8,128)(2,1)}, bf16[96,6144]{1,0:T(8,128)(2,1)}, bf16[...) conditional(s32[]{:T(128)} %bitcast.10, () %tuple.159, ...), branch_computations={%region_10.11_spmd, %region_11.12_spmd} | conditional | bytes 53084456 | solution.py:810
  209.0 3.3 copy.222
  212.3 3.5 copy.223
  215.7 2.5 end_sums.4
  218.2 4.7 collective-permute-done.15
  224.5 1.8 collective-permute-done.78
  227.2 31.3 %conditional.20 = (bf16[96,6144]{1,0:T(8,128)(2,1)}, bf16[96,6144]{1,0:T(8,128)(2,1)}, bf16[96,6144]{1,0:T(8,128)(2,1)}, bf16[384,3072]{1,0:T(8,128)(2,1)}, bf16...) conditional(s32[]{:T(128)} %bitcast.10, () %tuple.175, ...), branch_computations={%region_12.13_spmd, %region_13.14_spmd} | conditional | flops 11324620800 | bytes 60326312 | solution.py:810
  229.5 24.9 %expert_2.1 = (bf16[768,768]{1,0:T(8,128)(2,1)}, bf16[768,768]{1,0:T(8,128)(2,1)}) custom-call(s32[10]{0:T(128)S(1)} %get-tuple-element.491.rows_ref, s32[8]{0:T(128)S(1)} %get-tuple-element.492.order_ref, s32[20]{0:T(128)S(1)} %get-tuple-element.493.counts_ref, s32[8,1024]{1,0:T(8,128)} %get-tuple-element.494.place_t_ref, ...), custom_call_target="tpu_custom_call" | custom-call | flops 11324620800 | bytes 24936600 | tf_op jit(solution)/shard_map/cond/branch_1_fun/expert_2/pallas_call | solution.py:70
  254.4 1.9 collective-permute-done.19
  258.5 16.4 %conditional.21 = (bf16[48,6144]{1,0:T(8,128)(2,1)}, bf16[48,6144]{1,0:T(8,128)(2,1)}, bf16[96,6144]{1,0:T(8,128)(2,1)}, bf16[96,6144]{1,0:T(8,128)(2,1)}, bf16[...) conditional(s32[]{:T(128)} %bitcast.10, () %tuple.174, ...), branch_computations={%region_14.15_spmd, %region_15.16_spmd} | conditional | bytes 43647244 | solution.py:810
  262.3 1.8 copy.261
  264.7 2.5 end_sums.5
  267.2 7.3 %collective-permute-done.24 = bf16[48,6144]{1,0:T(8,128)(2,1)} collective-permute-done((bf16[48,6144]{1,0:T(8,128)(2,1)S(1)}, bf16[48,6144]{1,0:T(8,128)(2,1)}, u32[]{:S(2)}, u32[]{:S(2)}) %collective-permute-start.24) | collective-permute-done | bytes 589856 | tf_op jit(solution)/shard_map/cond/branch_1_fun/ppermute | solution.py:789
  275.5 1.7 collective-permute-done.80
  278.0 29.0 %conditional.22 = (bf16[48,6144]{1,0:T(8,128)(2,1)}, bf16[48,6144]{1,0:T(8,128)(2,1)}, bf16[48,6144]{1,0:T(8,128)(2,1)}, bf16[48,6144]{1,0:T(8,128)(2,1)}, bf16[...) conditional(s32[]{:T(128)} %bitcast.10, () %tuple.173, (bf16[48,6144]{1,0:T(8,128)(2,1)}, ...), branch_computations={%region_16.17_spmd, %region_17.18_spmd} | conditional | flops 11324620800 | bytes 34373992 | solution.py:810
  282.1 24.9 %expert_3.1 = (bf16[768,768]{1,0:T(8,128)(2,1)}, bf16[768,768]{1,0:T(8,128)(2,1)}) custom-call(s32[10]{0:T(128)S(1)} %get-tuple-element.524.rows_ref, s32[8]{0:T(128)S(1)} %get-tuple-element.525.order_ref, s32[20]{0:T(128)S(1)} %get-tuple-element.526.counts_ref, s32[8,1024]{1,0:T(8,128)} %get-tuple-element.527.place_t_ref, ...), custom_call_target="tpu_custom_call" | custom-call | flops 11324620800 | bytes 24936600 | tf_op jit(solution)/shard_map/cond/branch_1_fun/expert_3/pallas_call | solution.py:70
  307.1 4.7 middle_sums.5
  313.9 28.4 %conditional.23 = (bf16[96,6144]{1,0:T(8,128)(2,1)}, bf16[96,6144]{1,0:T(8,128)(2,1)}, bf16[96,6144]{1,0:T(8,128)(2,1)}, bf16[96,6144]{1,0:T(8,128)(2,1)}, bf16[...) conditional(s32[]{:T(128)} %bitcast.10, () %tuple.158, ...), branch_computations={%region_18.19_spmd, %region_19.20_spmd} | conditional | flops 4831838208 | bytes 67698952 | solution.py:810
  316.8 3.2 middle_sums.4
  320.0 20.5 %combine.1 = (bf16[1024,768]{1,0:T(8,128)(2,1)}, f32[1024,768]{1,0:T(8,128)}, bf16[1024,768]{1,0:T(8,128)(2,1)}, bf16[384,896]{1,0:T(8,128)(2,1)}, bf16[384,896]{1,0:T(8,128)(2,1)}) custom-call(s32[8]{0:T(128)S(1)} %get-tuple-element.553.order_ref, s32[20]{0:T(128)S(1)} %get-tuple-element.554.counts_ref, s32[1024,128]{1,0:T(8,128)S(1)} %get-tuple-element.555.place_ref, ...), custom_call_target="tpu_custom_call" | custom-call | flops 4831838208 | bytes 35848304 | tf_op jit(solution)/shard_map/cond/branch_1_fun/combine/pallas_call | solution.py:70
  342.3 4.4 line_sums.4
  346.8 39.4 %conditional.24 = (bf16[96,6144]{1,0:T(8,128)(2,1)}, bf16[96,6144]{1,0:T(8,128)(2,1)}, bf16[24,6144]{1,0:T(8,128)(2,1)}, bf16[24,6144]{1,0:T(8,128)(2,1)}, bf16[...) conditional(s32[]{:T(128)} %bitcast.10, () %tuple.184, ...), branch_computations={%region_20.21_spmd, %region_21.22_spmd} | conditional | flops 6039797760 | bytes 33636616 | solution.py:810
  349.2 2.3 collective-permute-start.37
  351.5 2.9 collective-permute-start.38
  354.6 31.3 %attend_back.1 = (bf16[1024,768]{1,0:T(8,128)(2,1)}, bf16[1024,768]{1,0:T(8,128)(2,1)}, bf16[1024,768]{1,0:T(8,128)(2,1)}) custom-call(s32[1024,1]{1,0:T(8,128)S(1)} %copy.96.doc_ref, s32[1,1024]{1,0:T(1,128)S(1)} %get-tuple-element.580.doc_t_ref, bf16[1024,2304]{1,0:T(8,128)(2,1)} %get-tuple-element.581.q_ref.k_ref.v_ref, ...), custom_call_target="tpu_custom_call" | custom-call | flops 6039797760 | bytes 20652032 | tf_op jit(solution)/shard_map/cond/branch_1_fun/attend_back/pallas_call | solution.py:70
  386.2 4.3 line_sums.5
  390.5 11.4 %conditional.25 = (bf16[384,896]{1,0:T(8,128)(2,1)}, bf16[24,6144]{1,0:T(8,128)(2,1)}, bf16[384,2304]{1,0:T(8,128)(2,1)S(1)}, bf16[384,2304]{1,0:T(8,128)(2,1)}) conditional(s32[]{:T(128)} %bitcast.10, () %tuple.183, (bf16[384,896]{1,0:T(8,128)(2,1)}, bf16[24,6144]{1,0:T(8,128)(2,1)S(1)}, s32[8]{0:T(128)S(1)}, bf16[1024,768]{1,0:T(8,128)(2,1)S(1)}, ...), branch_computations={%region_22.23_spmd, %region_23.24_spmd} | conditional | flops 3623878656 | bytes 13787280 | solution.py:810
  390.7 8.8 %weigh.1 = (bf16[384,2304]{1,0:T(8,128)(2,1)S(1)}, bf16[384,2304]{1,0:T(8,128)(2,1)}) custom-call(s32[8]{0:T(128)S(1)} %get-tuple-element.589.order_ref, bf16[1024,768]{1,0:T(8,128)(2,1)S(1)} %get-tuple-element.590.inputs_ref, bf16[16,768]{1,0:T(8,128)(2,1)S(1)} %get-tuple-element.591.gain_ref, bf16[1024,768]{1,0:T(8,128)(2,1)} %get-tuple-element.592.dq_ref, ...), custom_call_target="tpu_custom_call" | custom-call | flops 3623878656 | bytes 9855008 | tf_op jit(solution)/shard_map/cond/branch_1_fun/weigh/pallas_call | solution.py:70
  399.4 2.5 collective-permute-done.40
  402.9 12.1 %conditional.26 = (bf16[384,2304]{1,0:T(8,128)(2,1)}, bf16[48,896]{1,0:T(8,128)(2,1)}, bf16[48,896]{1,0:T(8,128)(2,1)}, bf16[24,6144]{1,0:T(8,128)(2,1)}, f32[1024,768]{1,0:T(8,128)S(1)}) conditional(s32[]{:T(128)} %bitcast.10, () %tuple.182, (bf16[384,2304]{1,0:T(8,128)(2,1)}, bf16[48,896]{1,0:T(8,128)(2,1)S(1)}, bf16[48,896]{1,0:T(8,128)(2,1)S(1)}, ...), branch_computations={%region_24.25_spmd, %region_25.26_spmd} | conditional | flops 3623878656 | bytes 26468552 | solution.py:810
  406.1 8.8 %finish.1 = f32[1024,768]{1,0:T(8,128)S(1)} custom-call(bf16[1024,768]{1,0:T(8,128)(2,1)} %get-tuple-element.601.inputs_ref, bf16[16,768]{1,0:T(8,128)(2,1)S(1)} %get-tuple-element.602.gain_ref, bf16[1024,768]{1,0:T(8,128)(2,1)} %get-tuple-element.603.dq_ref, bf16[1024,768]{1,0:T(8,128)(2,1)} %get-tuple-element.604.dk_ref, ...), custom_call_target="tpu_custom_call" | custom-call | flops 3623878656 | bytes 17522688 | tf_op jit(solution)/shard_map/cond/branch_1_fun/finish/pallas_call | solution.py:70
  415.0 2.4 middle_sums.6
  417.4 1.9 end_sums.7
  419.3 11.6 %conditional.27 = (bf16[48,2304]{1,0:T(8,128)(2,1)}, bf16[48,2304]{1,0:T(8,128)(2,1)}, bf16[96,896]{1,0:T(8,128)(2,1)}, bf16[96,896]{1,0:T(8,128)(2,1)}, f32[24,3072]{0,1:T(8,128)}, /*index=5*/f32[96,768]{1,0:T(8,128)S(1)}) conditional(s32[]{:T(128)} %bitcast.10, () %tuple.189, (bf16[48,2304]{1,0:T(8,128)(2,1)}, bf16[48,2304]{1,0:T(8,128)(2,1)}, ...), branch_computations={%region_26.27_spmd, %region_27.28_spmd} | conditional | flops 884736 | bytes 9339116 | solution.py:810
  427.1 3.0 collective-permute-done.50
  430.9 1.8 line_sums.7
  434.3 16.5 %conditional.28 = (bf16[96,2304]{1,0:T(8,128)(2,1)}, bf16[96,2304]{1,0:T(8,128)(2,1)}, bf16[24,6144]{1,0:T(8,128)(2,1)}) conditional(s32[]{:T(128)} %bitcast.10, () %tuple.188, (bf16[96,2304]{1,0:T(8,128)(2,1)S(1)}, bf16[96,2304]{1,0:T(8,128)(2,1)S(1)}, bf16[24,6144]{1,0:T(8,128)(2,1)S(1)}) %tuple.272), branch_computations={%region_28.29_spmd, %region_29.30_spmd} | conditional | bytes 4718736 | solution.py:810
  436.8 14.0 %collective-permute-done.47 = bf16[24,6144]{1,0:T(8,128)(2,1)} collective-permute-done((bf16[24,6144]{1,0:T(8,128)(2,1)S(1)}, bf16[24,6144]{1,0:T(8,128)(2,1)}, u32[]{:S(2)}, u32[]{:S(2)}) %collective-permute-start.47) | collective-permute-done | bytes 294944 | tf_op jit(solution)/shard_map/cond/branch_1_fun/ppermute | solution.py:789
  450.8 2.4 line_sums.6
  453.3 20.0 %conditional.29 = (f32[24,2304]{1,0:T(8,128)S(1)}, f32[24,2304]{1,0:T(8,128)S(1)}, f32[24,2304]{1,0:T(8,128)S(1)}, f32[24,896]{1,0:T(8,128)S(1)}, f32[24,896]{1,...) conditional(s32[]{:T(128)} %bitcast.10, () %tuple.192, ...), branch_computations={%region_30.31_spmd, %region_31.32_spmd} | conditional | flops 1410048 | bytes 14309708 | solution.py:810
  454.5 2.7 collective-permute-start.54
  462.0 1.9 copy.111
  464.0 2.2 collective-permute-done.55
  (318 shorter events, 108.7 us)
Async XLA Ops:
  7.2 48.5 %all-gather.9.cloned.1.call-start = ((), (), s32[]{:S(2)}) async-start(), calls=%async_computation.2 | async-start | bytes 1474560 | tf_op jit(solution)/shard_map/all_gather | solution.py:982
  9.1 13.0 %collective-permute-start.58 = (bf16[24,3200]{1,0:T(8,128)(2,1)S(1)}, bf16[24,3200]{1,0:T(8,128)(2,1)S(1)}, u32[]{:S(2)}, u32[]{:S(2)}) collective-permute-start(bf16[24,3200]{1,0:T(8,128)(2,1)S(1)} %get-tuple-element.1027), channel_id=1, source_target_pairs={{0,3},{1,0},{2,1},{3,2},{4,7},{5,4},{6,5},{7,6},{8,11},{9,8},{10,9... | collective-permute-start | bytes 460808 | tf_op jit(solution)/shard_map/ppermute | solution.py:789
  14.2 13.0 %collective-permute-start.59 = (bf16[24,3200]{1,0:T(8,128)(2,1)S(1)}, bf16[24,3200]{1,0:T(8,128)(2,1)S(1)}, u32[]{:S(2)}, u32[]{:S(2)}) collective-permute-start(bf16[24,3200]{1,0:T(8,128)(2,1)S(1)} %get-tuple-element.1027), channel_id=1, source_target_pairs={{0,2},{1,3},{2,0},{3,1},{4,6},{5,7},{6,4},{7,5},{8,10},{9,11},{10,... | collective-permute-start | bytes 460808 | tf_op jit(solution)/shard_map/ppermute | solution.py:789
  14.2 13.0 %collective-permute-start.60 = (bf16[24,3200]{1,0:T(8,128)(2,1)S(1)}, bf16[24,3200]{1,0:T(8,128)(2,1)S(1)}, u32[]{:S(2)}, u32[]{:S(2)}) collective-permute-start(bf16[24,3200]{1,0:T(8,128)(2,1)S(1)} %get-tuple-element.1027), channel_id=1, source_target_pairs={{0,1},{1,2},{2,3},{3,0},{4,5},{5,6},{6,7},{7,4},{8,9},{9,10},{10,1... | collective-permute-start | bytes 460808 | tf_op jit(solution)/shard_map/ppermute | solution.py:789
  20.0 95.6 %all-gather.7.cloned.1.call-start = ((), (), s32[]{:S(2)}) async-start(), calls=%async_computation.1 | async-start | bytes 1474560 | tf_op jit(solution)/shard_map/all_gather | solution.py:982
  27.3 137.2 %all-gather.5.cloned.1.call-start = ((), (), s32[]{:S(2)}) async-start(), calls=%async_computation | async-start | bytes 1474560 | tf_op jit(solution)/shard_map/all_gather | solution.py:982
  27.3 15.3 %collective-permute-start.61 = (bf16[96,3200]{1,0:T(8,128)(2,1)S(1)}, bf16[96,3200]{1,0:T(8,128)(2,1)S(1)}, u32[]{:S(2)}, u32[]{:S(2)}) collective-permute-start(bf16[96,3200]{1,0:T(8,128)(2,1)S(1)} %constant_dynamic-update-slice_fusion), channel_id=1, source_target_pairs={{0,8},{1,9},{2,10},{3,11},{4,12},{5,13},{6,14},{7,15},{8,0},{9,1},... | collective-permute-start | bytes 1843208 | tf_op jit(solution)/shard_map/ppermute | solution.py:789
  28.9 15.3 %collective-permute-start.62 = (bf16[96,3200]{1,0:T(8,128)(2,1)S(1)}, bf16[96,3200]{1,0:T(8,128)(2,1)}, u32[]{:S(2)}, u32[]{:S(2)}) collective-permute-start(bf16[96,3200]{1,0:T(8,128)(2,1)S(1)} %constant_dynamic-update-slice_fusion), channel_id=1, source_target_pairs={{0,16},{1,17},{2,18},{3,19},{4,20},{5,21},{6,22},{7,23},{8,24},{9,... | collective-permute-start | bytes 1843208 | tf_op jit(solution)/shard_map/ppermute | solution.py:789
  34.6 21.0 %collective-permute-start.65 = (bf16[96,3200]{1,0:T(8,128)(2,1)S(1)}, bf16[96,3200]{1,0:T(8,128)(2,1)}, u32[]{:S(2)}, u32[]{:S(2)}) collective-permute-start(bf16[96,3200]{1,0:T(8,128)(2,1)S(1)} %constant_dynamic-update-slice_fusion), channel_id=1, source_target_pairs={{0,4},{1,5},{2,6},{3,7},{4,0},{5,1},{6,2},{7,3},{8,12},{9,13},{10,... | collective-permute-start | bytes 1843208 | tf_op jit(solution)/shard_map/ppermute | solution.py:789
  48.1 176.4 %all-gather.11.cloned.1.call-start = ((), (), s32[]{:S(2)}) async-start(), calls=%async_computation.3 | async-start | bytes 1474560 | tf_op jit(solution)/shard_map/all_gather | solution.py:982
  55.9 33.4 %collective-permute-start = (bf16[96,6144]{1,0:T(8,128)(2,1)}, bf16[96,6144]{1,0:T(8,128)(2,1)}, u32[]{:S(2)}, u32[]{:S(2)}) collective-permute-start(bf16[96,6144]{1,0:T(8,128)(2,1)} %get-tuple-element.398), channel_id=1, source_target_pairs={{0,8},{1,9},{2,10},{3,11},{4,12},{5,13},{6,14},{7,15},{8,0},{9,1},... | collective-permute-start | bytes 3538952 | tf_op jit(solution)/shard_map/cond/branch_1_fun/ppermute | solution.py:789
  57.4 33.9 %collective-permute-start.1 = (bf16[96,6144]{1,0:T(8,128)(2,1)}, bf16[96,6144]{1,0:T(8,128)(2,1)}, u32[]{:S(2)}, u32[]{:S(2)}) collective-permute-start(bf16[96,6144]{1,0:T(8,128)(2,1)} %get-tuple-element.398), channel_id=1, source_target_pairs={{0,16},{1,17},{2,18},{3,19},{4,20},{5,21},{6,22},{7,23},{8,24},{9,... | collective-permute-start | bytes 3538952 | tf_op jit(solution)/shard_map/cond/branch_1_fun/ppermute | solution.py:789
  58.0 35.3 %collective-permute-start.2 = (bf16[96,6144]{1,0:T(8,128)(2,1)}, bf16[96,6144]{1,0:T(8,128)(2,1)}, u32[]{:S(2)}, u32[]{:S(2)}) collective-permute-start(bf16[96,6144]{1,0:T(8,128)(2,1)} %get-tuple-element.398), channel_id=1, source_target_pairs={{0,4},{1,5},{2,6},{3,7},{4,0},{5,1},{6,2},{7,3},{8,12},{9,13},{10,... | collective-permute-start | bytes 3538952 | tf_op jit(solution)/shard_map/cond/branch_1_fun/ppermute | solution.py:789
  94.4 17.8 %collective-permute-start.5 = (bf16[96,6144]{1,0:T(8,128)(2,1)}, bf16[96,6144]{1,0:T(8,128)(2,1)}, u32[]{:S(2)}, u32[]{:S(2)}) collective-permute-start(bf16[96,6144]{1,0:T(8,128)(2,1)} %get-tuple-element.419), channel_id=1, source_target_pairs={{0,4},{1,5},{2,6},{3,7},{4,0},{5,1},{6,2},{7,3},{8,12},{9,13},{10,... | collective-permute-start | bytes 3538952 | tf_op jit(solution)/shard_map/cond/branch_1_fun/ppermute | solution.py:789
  94.9 17.3 %collective-permute-start.6 = (bf16[96,6144]{1,0:T(8,128)(2,1)}, bf16[96,6144]{1,0:T(8,128)(2,1)}, u32[]{:S(2)}, u32[]{:S(2)}) collective-permute-start(bf16[96,6144]{1,0:T(8,128)(2,1)} %get-tuple-element.420), channel_id=1, source_target_pairs={{0,4},{1,5},{2,6},{3,7},{4,0},{5,1},{6,2},{7,3},{8,12},{9,13},{10,... | collective-permute-start | bytes 3538952 | tf_op jit(solution)/shard_map/cond/branch_1_fun/ppermute | solution.py:789
  94.9 16.1 %collective-permute-start.3 = (bf16[48,6144]{1,0:T(8,128)(2,1)}, bf16[48,6144]{1,0:T(8,128)(2,1)}, u32[]{:S(2)}, u32[]{:S(2)}) collective-permute-start(bf16[48,6144]{1,0:T(8,128)(2,1)} %get-tuple-element.417), channel_id=1, source_target_pairs={{0,16},{1,17},{2,18},{3,19},{4,20},{5,21},{6,22},{7,23},{8,24},{9,... | collective-permute-start | bytes 1769480 | tf_op jit(solution)/shard_map/cond/branch_1_fun/ppermute | solution.py:789
  96.5 15.8 %collective-permute-start.4 = (bf16[48,6144]{1,0:T(8,128)(2,1)}, bf16[48,6144]{1,0:T(8,128)(2,1)}, u32[]{:S(2)}, u32[]{:S(2)}) collective-permute-start(bf16[48,6144]{1,0:T(8,128)(2,1)} %get-tuple-element.418), channel_id=1, source_target_pairs={{0,8},{1,9},{2,10},{3,11},{4,12},{5,13},{6,14},{7,15},{8,0},{9,1},... | collective-permute-start | bytes 1769480 | tf_op jit(solution)/shard_map/cond/branch_1_fun/ppermute | solution.py:789
  116.1 28.3 %collective-permute-start.7 = (bf16[96,6144]{1,0:T(8,128)(2,1)}, bf16[96,6144]{1,0:T(8,128)(2,1)}, u32[]{:S(2)}, u32[]{:S(2)}) collective-permute-start(bf16[96,6144]{1,0:T(8,128)(2,1)} %get-tuple-element.428), channel_id=1, source_target_pairs={{0,8},{1,9},{2,10},{3,11},{4,12},{5,13},{6,14},{7,15},{8,0},{9,1},... | collective-permute-start | bytes 3538952 | tf_op jit(solution)/shard_map/cond/branch_1_fun/ppermute | solution.py:789
  116.7 28.0 %collective-permute-start.8 = (bf16[96,6144]{1,0:T(8,128)(2,1)}, bf16[96,6144]{1,0:T(8,128)(2,1)}, u32[]{:S(2)}, u32[]{:S(2)}) collective-permute-start(bf16[96,6144]{1,0:T(8,128)(2,1)} %get-tuple-element.428), channel_id=1, source_target_pairs={{0,16},{1,17},{2,18},{3,19},{4,20},{5,21},{6,22},{7,23},{8,24},{9,... | collective-permute-start | bytes 3538952 | tf_op jit(solution)/shard_map/cond/branch_1_fun/ppermute | solution.py:789
  117.8 27.0 %collective-permute-start.9 = (bf16[96,6144]{1,0:T(8,128)(2,1)}, bf16[96,6144]{1,0:T(8,128)(2,1)}, u32[]{:S(2)}, u32[]{:S(2)}) collective-permute-start(bf16[96,6144]{1,0:T(8,128)(2,1)} %get-tuple-element.428), channel_id=1, source_target_pairs={{0,4},{1,5},{2,6},{3,7},{4,0},{5,1},{6,2},{7,3},{8,12},{9,13},{10,... | collective-permute-start | bytes 3538952 | tf_op jit(solution)/shard_map/cond/branch_1_fun/ppermute | solution.py:789
  146.6 20.4 %collective-permute-start.74 = (bf16[96,6144]{1,0:T(8,128)(2,1)}, bf16[96,6144]{1,0:T(8,128)(2,1)}, u32[]{:S(2)}, u32[]{:S(2)}) collective-permute-start(bf16[96,6144]{1,0:T(8,128)(2,1)} %get-tuple-element.813), channel_id=1, source_target_pairs={{0,4},{1,5},{2,6},{3,7},{4,0},{5,1},{6,2},{7,3},{8,12},{9,13},{10,... | collective-permute-start | bytes 3538952 | tf_op jit(solution)/shard_map/ppermute | solution.py:789
  147.7 19.3 %collective-permute-start.75 = (bf16[96,6144]{1,0:T(8,128)(2,1)}, bf16[96,6144]{1,0:T(8,128)(2,1)}, u32[]{:S(2)}, u32[]{:S(2)}) collective-permute-start(bf16[96,6144]{1,0:T(8,128)(2,1)} %get-tuple-element.814), channel_id=1, source_target_pairs={{0,4},{1,5},{2,6},{3,7},{4,0},{5,1},{6,2},{7,3},{8,12},{9,13},{10,... | collective-permute-start | bytes 3538952 | tf_op jit(solution)/shard_map/ppermute | solution.py:789
  148.3 15.6 %collective-permute-start.72 = (bf16[48,6144]{1,0:T(8,128)(2,1)}, bf16[48,6144]{1,0:T(8,128)(2,1)}, u32[]{:S(2)}, u32[]{:S(2)}) collective-permute-start(bf16[48,6144]{1,0:T(8,128)(2,1)} %slice.105), channel_id=1, source_target_pairs={{0,16},{1,17},{2,18},{3,19},{4,20},{5,21},{6,22},{7,23},{8,24},{9,... | collective-permute-start | bytes 1769480 | tf_op jit(solution)/shard_map/ppermute | solution.py:789
  149.3 15.1 %collective-permute-start.73 = (bf16[48,6144]{1,0:T(8,128)(2,1)S(1)}, bf16[48,6144]{1,0:T(8,128)(2,1)}, u32[]{:S(2)}, u32[]{:S(2)}) collective-permute-start(bf16[48,6144]{1,0:T(8,128)(2,1)S(1)} %slice.106), channel_id=1, source_target_pairs={{0,8},{1,9},{2,10},{3,11},{4,12},{5,13},{6,14},{7,15},{8,0},{9,1},... | collective-permute-start | bytes 1769480 | tf_op jit(solution)/shard_map/ppermute | solution.py:789
  167.3 39.2 %collective-permute-start.13 = (bf16[384,3072]{1,0:T(8,128)(2,1)}, bf16[384,3072]{1,0:T(8,128)(2,1)}, u32[]{:S(2)}, u32[]{:S(2)}) collective-permute-start(bf16[384,3072]{1,0:T(8,128)(2,1)} %get-tuple-element.453), channel_id=1, source_target_pairs={{0,4},{1,5},{2,6},{3,7},{4,0},{5,1},{6,2},{7,3},{8,12},{9,13},{10,... | collective-permute-start | bytes 7077896 | tf_op jit(solution)/shard_map/cond/branch_1_fun/ppermute | solution.py:789
  167.5 39.0 %collective-permute-start.14 = (bf16[384,3072]{1,0:T(8,128)(2,1)}, bf16[384,3072]{1,0:T(8,128)(2,1)}, u32[]{:S(2)}, u32[]{:S(2)}) collective-permute-start(bf16[384,3072]{1,0:T(8,128)(2,1)} %get-tuple-element.454), channel_id=1, source_target_pairs={{0,4},{1,5},{2,6},{3,7},{4,0},{5,1},{6,2},{7,3},{8,12},{9,13},{10,... | collective-permute-start | bytes 7077896 | tf_op jit(solution)/shard_map/cond/branch_1_fun/ppermute | solution.py:789
  167.8 36.3 %collective-permute-start.10 = (bf16[96,6144]{1,0:T(8,128)(2,1)}, bf16[96,6144]{1,0:T(8,128)(2,1)}, u32[]{:S(2)}, u32[]{:S(2)}) collective-permute-start(bf16[96,6144]{1,0:T(8,128)(2,1)} %get-tuple-element.452), channel_id=1, source_target_pairs={{0,8},{1,9},{2,10},{3,11},{4,12},{5,13},{6,14},{7,15},{8,0},{9,1},... | collective-permute-start | bytes 3538952 | tf_op jit(solution)/shard_map/cond/branch_1_fun/ppermute | solution.py:789
  169.3 35.9 %collective-permute-start.11 = (bf16[96,6144]{1,0:T(8,128)(2,1)}, bf16[96,6144]{1,0:T(8,128)(2,1)}, u32[]{:S(2)}, u32[]{:S(2)}) collective-permute-start(bf16[96,6144]{1,0:T(8,128)(2,1)} %get-tuple-element.452), channel_id=1, source_target_pairs={{0,16},{1,17},{2,18},{3,19},{4,20},{5,21},{6,22},{7,23},{8,24},{9,... | collective-permute-start | bytes 3538952 | tf_op jit(solution)/shard_map/cond/branch_1_fun/ppermute | solution.py:789
  170.0 36.4 %collective-permute-start.12 = (bf16[96,6144]{1,0:T(8,128)(2,1)}, bf16[96,6144]{1,0:T(8,128)(2,1)}, u32[]{:S(2)}, u32[]{:S(2)}) collective-permute-start(bf16[96,6144]{1,0:T(8,128)(2,1)} %get-tuple-element.452), channel_id=1, source_target_pairs={{0,4},{1,5},{2,6},{3,7},{4,0},{5,1},{6,2},{7,3},{8,12},{9,13},{10,... | collective-permute-start | bytes 3538952 | tf_op jit(solution)/shard_map/cond/branch_1_fun/ppermute | solution.py:789
  206.5 17.5 %collective-permute-start.17 = (bf16[96,6144]{1,0:T(8,128)(2,1)}, bf16[96,6144]{1,0:T(8,128)(2,1)}, u32[]{:S(2)}, u32[]{:S(2)}) collective-permute-start(bf16[96,6144]{1,0:T(8,128)(2,1)} %get-tuple-element.480), channel_id=1, source_target_pairs={{0,4},{1,5},{2,6},{3,7},{4,0},{5,1},{6,2},{7,3},{8,12},{9,13},{10,... | collective-permute-start | bytes 3538952 | tf_op jit(solution)/shard_map/cond/branch_1_fun/ppermute | solution.py:789
  207.0 17.0 %collective-permute-start.18 = (bf16[96,6144]{1,0:T(8,128)(2,1)}, bf16[96,6144]{1,0:T(8,128)(2,1)}, u32[]{:S(2)}, u32[]{:S(2)}) collective-permute-start(bf16[96,6144]{1,0:T(8,128)(2,1)} %get-tuple-element.481), channel_id=1, source_target_pairs={{0,4},{1,5},{2,6},{3,7},{4,0},{5,1},{6,2},{7,3},{8,12},{9,13},{10,... | collective-permute-start | bytes 3538952 | tf_op jit(solution)/shard_map/cond/branch_1_fun/ppermute | solution.py:789
  207.1 15.8 %collective-permute-start.15 = (bf16[48,6144]{1,0:T(8,128)(2,1)S(1)}, bf16[48,6144]{1,0:T(8,128)(2,1)}, u32[]{:S(2)}, u32[]{:S(2)}) collective-permute-start(bf16[48,6144]{1,0:T(8,128)(2,1)S(1)} %get-tuple-element.478), channel_id=1, source_target_pairs={{0,16},{1,17},{2,18},{3,19},{4,20},{5,21},{6,22},{7,23},{8,24},{9,... | collective-permute-start | bytes 1769480 | tf_op jit(solution)/shard_map/cond/branch_1_fun/ppermute | solution.py:789
  208.5 15.5 %collective-permute-start.16 = (bf16[48,6144]{1,0:T(8,128)(2,1)S(1)}, bf16[48,6144]{1,0:T(8,128)(2,1)}, u32[]{:S(2)}, u32[]{:S(2)}) collective-permute-start(bf16[48,6144]{1,0:T(8,128)(2,1)S(1)} %get-tuple-element.479), channel_id=1, source_target_pairs={{0,8},{1,9},{2,10},{3,11},{4,12},{5,13},{6,14},{7,15},{8,0},{9,1},... | collective-permute-start | bytes 1769480 | tf_op jit(solution)/shard_map/cond/branch_1_fun/ppermute | solution.py:789
  227.4 31.1 %collective-permute-start.22 = (bf16[384,3072]{1,0:T(8,128)(2,1)}, bf16[384,3072]{1,0:T(8,128)(2,1)}, u32[]{:S(2)}, u32[]{:S(2)}) collective-permute-start(bf16[384,3072]{1,0:T(8,128)(2,1)} %get-tuple-element.489), channel_id=1, source_target_pairs={{0,4},{1,5},{2,6},{3,7},{4,0},{5,1},{6,2},{7,3},{8,12},{9,13},{10,... | collective-permute-start | bytes 7077896 | tf_op jit(solution)/shard_map/cond/branch_1_fun/ppermute | solution.py:789
  227.6 30.9 %collective-permute-start.23 = (bf16[384,3072]{1,0:T(8,128)(2,1)}, bf16[384,3072]{1,0:T(8,128)(2,1)}, u32[]{:S(2)}, u32[]{:S(2)}) collective-permute-start(bf16[384,3072]{1,0:T(8,128)(2,1)} %get-tuple-element.490), channel_id=1, source_target_pairs={{0,4},{1,5},{2,6},{3,7},{4,0},{5,1},{6,2},{7,3},{8,12},{9,13},{10,... | collective-permute-start | bytes 7077896 | tf_op jit(solution)/shard_map/cond/branch_1_fun/ppermute | solution.py:789
  227.9 28.3 %collective-permute-start.19 = (bf16[96,6144]{1,0:T(8,128)(2,1)}, bf16[96,6144]{1,0:T(8,128)(2,1)}, u32[]{:S(2)}, u32[]{:S(2)}) collective-permute-start(bf16[96,6144]{1,0:T(8,128)(2,1)} %get-tuple-element.488), channel_id=1, source_target_pairs={{0,8},{1,9},{2,10},{3,11},{4,12},{5,13},{6,14},{7,15},{8,0},{9,1},... | collective-permute-start | bytes 3538952 | tf_op jit(solution)/shard_map/cond/branch_1_fun/ppermute | solution.py:789
  228.5 28.9 %collective-permute-start.20 = (bf16[96,6144]{1,0:T(8,128)(2,1)}, bf16[96,6144]{1,0:T(8,128)(2,1)}, u32[]{:S(2)}, u32[]{:S(2)}) collective-permute-start(bf16[96,6144]{1,0:T(8,128)(2,1)} %get-tuple-element.488), channel_id=1, source_target_pairs={{0,16},{1,17},{2,18},{3,19},{4,20},{5,21},{6,22},{7,23},{8,24},{9,... | collective-permute-start | bytes 3538952 | tf_op jit(solution)/shard_map/cond/branch_1_fun/ppermute | solution.py:789
  229.5 29.0 %collective-permute-start.21 = (bf16[96,6144]{1,0:T(8,128)(2,1)}, bf16[96,6144]{1,0:T(8,128)(2,1)}, u32[]{:S(2)}, u32[]{:S(2)}) collective-permute-start(bf16[96,6144]{1,0:T(8,128)(2,1)} %get-tuple-element.488), channel_id=1, source_target_pairs={{0,4},{1,5},{2,6},{3,7},{4,0},{5,1},{6,2},{7,3},{8,12},{9,13},{10,... | collective-permute-start | bytes 3538952 | tf_op jit(solution)/shard_map/cond/branch_1_fun/ppermute | solution.py:789
  258.5 16.4 %collective-permute-start.26 = (bf16[96,6144]{1,0:T(8,128)(2,1)}, bf16[96,6144]{1,0:T(8,128)(2,1)}, u32[]{:S(2)}, u32[]{:S(2)}) collective-permute-start(bf16[96,6144]{1,0:T(8,128)(2,1)} %get-tuple-element.512), channel_id=1, source_target_pairs={{0,4},{1,5},{2,6},{3,7},{4,0},{5,1},{6,2},{7,3},{8,12},{9,13},{10,... | collective-permute-start | bytes 3538952 | tf_op jit(solution)/shard_map/cond/branch_1_fun/ppermute | solution.py:789
  258.6 16.3 %collective-permute-start.27 = (bf16[96,6144]{1,0:T(8,128)(2,1)}, bf16[96,6144]{1,0:T(8,128)(2,1)}, u32[]{:S(2)}, u32[]{:S(2)}) collective-permute-start(bf16[96,6144]{1,0:T(8,128)(2,1)} %get-tuple-element.513), channel_id=1, source_target_pairs={{0,4},{1,5},{2,6},{3,7},{4,0},{5,1},{6,2},{7,3},{8,12},{9,13},{10,... | collective-permute-start | bytes 3538952 | tf_op jit(solution)/shard_map/cond/branch_1_fun/ppermute | solution.py:789
  259.1 15.4 %collective-permute-start.24 = (bf16[48,6144]{1,0:T(8,128)(2,1)S(1)}, bf16[48,6144]{1,0:T(8,128)(2,1)}, u32[]{:S(2)}, u32[]{:S(2)}) collective-permute-start(bf16[48,6144]{1,0:T(8,128)(2,1)S(1)} %get-tuple-element.510), channel_id=1, source_target_pairs={{0,16},{1,17},{2,18},{3,19},{4,20},{5,21},{6,22},{7,23},{8,24},{9,... | collective-permute-start | bytes 1769480 | tf_op jit(solution)/shard_map/cond/branch_1_fun/ppermute | solution.py:789
  259.8 15.1 %collective-permute-start.25 = (bf16[48,6144]{1,0:T(8,128)(2,1)S(1)}, bf16[48,6144]{1,0:T(8,128)(2,1)}, u32[]{:S(2)}, u32[]{:S(2)}) collective-permute-start(bf16[48,6144]{1,0:T(8,128)(2,1)S(1)} %get-tuple-element.511), channel_id=1, source_target_pairs={{0,8},{1,9},{2,10},{3,11},{4,12},{5,13},{6,14},{7,15},{8,0},{9,1},... | collective-permute-start | bytes 1769480 | tf_op jit(solution)/shard_map/cond/branch_1_fun/ppermute | solution.py:789
  278.0 29.0 %collective-permute-start.28 = (bf16[48,6144]{1,0:T(8,128)(2,1)}, bf16[48,6144]{1,0:T(8,128)(2,1)}, u32[]{:S(2)}, u32[]{:S(2)}) collective-permute-start(bf16[48,6144]{1,0:T(8,128)(2,1)} %get-tuple-element.520), channel_id=1, source_target_pairs={{0,8},{1,9},{2,10},{3,11},{4,12},{5,13},{6,14},{7,15},{8,0},{9,1},... | collective-permute-start | bytes 1769480 | tf_op jit(solution)/shard_map/cond/branch_1_fun/ppermute | solution.py:789
  279.0 28.1 %collective-permute-start.29 = (bf16[48,6144]{1,0:T(8,128)(2,1)}, bf16[48,6144]{1,0:T(8,128)(2,1)}, u32[]{:S(2)}, u32[]{:S(2)}) collective-permute-start(bf16[48,6144]{1,0:T(8,128)(2,1)} %get-tuple-element.521), channel_id=1, source_target_pairs={{0,16},{1,17},{2,18},{3,19},{4,20},{5,21},{6,22},{7,23},{8,24},{9,... | collective-permute-start | bytes 1769480 | tf_op jit(solution)/shard_map/cond/branch_1_fun/ppermute | solution.py:789
  280.1 27.0 %collective-permute-start.30 = (bf16[48,6144]{1,0:T(8,128)(2,1)}, bf16[48,6144]{1,0:T(8,128)(2,1)}, u32[]{:S(2)}, u32[]{:S(2)}) collective-permute-start(bf16[48,6144]{1,0:T(8,128)(2,1)} %get-tuple-element.522), channel_id=1, source_target_pairs={{0,8},{1,9},{2,10},{3,11},{4,12},{5,13},{6,14},{7,15},{8,0},{9,1},... | collective-permute-start | bytes 1769480 | tf_op jit(solution)/shard_map/cond/branch_1_fun/ppermute | solution.py:789
  281.5 25.6 %collective-permute-start.31 = (bf16[48,6144]{1,0:T(8,128)(2,1)}, bf16[48,6144]{1,0:T(8,128)(2,1)}, u32[]{:S(2)}, u32[]{:S(2)}) collective-permute-start(bf16[48,6144]{1,0:T(8,128)(2,1)} %get-tuple-element.523), channel_id=1, source_target_pairs={{0,16},{1,17},{2,18},{3,19},{4,20},{5,21},{6,22},{7,23},{8,24},{9,... | collective-permute-start | bytes 1769480 | tf_op jit(solution)/shard_map/cond/branch_1_fun/ppermute | solution.py:789
  314.3 27.3 %collective-permute-start.32 = (bf16[96,6144]{1,0:T(8,128)(2,1)}, bf16[96,6144]{1,0:T(8,128)(2,1)}, u32[]{:S(2)}, u32[]{:S(2)}) collective-permute-start(bf16[96,6144]{1,0:T(8,128)(2,1)} %get-tuple-element.543), channel_id=1, source_target_pairs={{0,8},{1,9},{2,10},{3,11},{4,12},{5,13},{6,14},{7,15},{8,0},{9,1},... | collective-permute-start | bytes 3538952 | tf_op jit(solution)/shard_map/cond/branch_1_fun/ppermute | solution.py:789
  315.4 26.9 %collective-permute-start.33 = (bf16[96,6144]{1,0:T(8,128)(2,1)}, bf16[96,6144]{1,0:T(8,128)(2,1)}, u32[]{:S(2)}, u32[]{:S(2)}) collective-permute-start(bf16[96,6144]{1,0:T(8,128)(2,1)} %get-tuple-element.544), channel_id=1, source_target_pairs={{0,16},{1,17},{2,18},{3,19},{4,20},{5,21},{6,22},{7,23},{8,24},{9,... | collective-permute-start | bytes 3538952 | tf_op jit(solution)/shard_map/cond/branch_1_fun/ppermute | solution.py:789
  346.8 39.2 %collective-permute-start.34 = (bf16[96,6144]{1,0:T(8,128)(2,1)}, bf16[96,6144]{1,0:T(8,128)(2,1)}, u32[]{:S(2)}, u32[]{:S(2)}) collective-permute-start(bf16[96,6144]{1,0:T(8,128)(2,1)} %get-tuple-element.575), channel_id=1, source_target_pairs={{0,8},{1,9},{2,10},{3,11},{4,12},{5,13},{6,14},{7,15},{8,0},{9,1},... | collective-permute-start | bytes 3538952 | tf_op jit(solution)/shard_map/cond/branch_1_fun/ppermute | solution.py:789
  347.8 38.2 %collective-permute-start.35 = (bf16[96,6144]{1,0:T(8,128)(2,1)}, bf16[96,6144]{1,0:T(8,128)(2,1)}, u32[]{:S(2)}, u32[]{:S(2)}) collective-permute-start(bf16[96,6144]{1,0:T(8,128)(2,1)} %get-tuple-element.576), channel_id=1, source_target_pairs={{0,16},{1,17},{2,18},{3,19},{4,20},{5,21},{6,22},{7,23},{8,24},{9,... | collective-permute-start | bytes 3538952 | tf_op jit(solution)/shard_map/cond/branch_1_fun/ppermute | solution.py:789
  348.8 37.1 %collective-permute-start.36 = (bf16[24,6144]{1,0:T(8,128)(2,1)S(1)}, bf16[24,6144]{1,0:T(8,128)(2,1)}, u32[]{:S(2)}, u32[]{:S(2)}) collective-permute-start(bf16[24,6144]{1,0:T(8,128)(2,1)S(1)} %get-tuple-element.577), channel_id=1, source_target_pairs={{0,1},{1,2},{2,3},{3,0},{4,5},{5,6},{6,7},{7,4},{8,9},{9,10},{10,1... | collective-permute-start | bytes 884744 | tf_op jit(solution)/shard_map/cond/branch_1_fun/ppermute | solution.py:789
  349.2 36.8 %collective-permute-start.37 = (bf16[24,6144]{1,0:T(8,128)(2,1)}, bf16[24,6144]{1,0:T(8,128)(2,1)}, u32[]{:S(2)}, u32[]{:S(2)}) collective-permute-start(bf16[24,6144]{1,0:T(8,128)(2,1)} %get-tuple-element.578), channel_id=1, source_target_pairs={{0,2},{1,3},{2,0},{3,1},{4,6},{5,7},{6,4},{7,5},{8,10},{9,11},{10,... | collective-permute-start | bytes 884744 | tf_op jit(solution)/shard_map/cond/branch_1_fun/ppermute | solution.py:789
  351.5 34.5 %collective-permute-start.38 = (bf16[24,6144]{1,0:T(8,128)(2,1)}, bf16[24,6144]{1,0:T(8,128)(2,1)}, u32[]{:S(2)}, u32[]{:S(2)}) collective-permute-start(bf16[24,6144]{1,0:T(8,128)(2,1)} %get-tuple-element.579), channel_id=1, source_target_pairs={{0,3},{1,0},{2,1},{3,2},{4,7},{5,4},{6,5},{7,6},{8,11},{9,8},{10,9... | collective-permute-start | bytes 884744 | tf_op jit(solution)/shard_map/cond/branch_1_fun/ppermute | solution.py:789
  390.5 11.4 %collective-permute-start.39 = (bf16[384,896]{1,0:T(8,128)(2,1)}, bf16[384,896]{1,0:T(8,128)(2,1)}, u32[]{:S(2)}, u32[]{:S(2)}) collective-permute-start(bf16[384,896]{1,0:T(8,128)(2,1)} %get-tuple-element.587), channel_id=1, source_target_pairs={{0,4},{1,5},{2,6},{3,7},{4,0},{5,1},{6,2},{7,3},{8,12},{9,13},{10,... | collective-permute-start | bytes 2064392 | tf_op jit(solution)/shard_map/cond/branch_1_fun/ppermute | solution.py:789
  402.9 12.0 %collective-permute-start.41 = (bf16[384,2304]{1,0:T(8,128)(2,1)}, bf16[384,2304]{1,0:T(8,128)(2,1)}, u32[]{:S(2)}, u32[]{:S(2)}) collective-permute-start(bf16[384,2304]{1,0:T(8,128)(2,1)} %get-tuple-element.597), channel_id=1, source_target_pairs={{0,4},{1,5},{2,6},{3,7},{4,0},{5,1},{6,2},{7,3},{8,12},{9,13},{10,... | collective-permute-start | bytes 5308424 | tf_op jit(solution)/shard_map/cond/branch_1_fun/ppermute | solution.py:789
  403.0 11.9 %collective-permute-start.44 = (bf16[24,6144]{1,0:T(8,128)(2,1)S(1)}, bf16[24,6144]{1,0:T(8,128)(2,1)}, u32[]{:S(2)}, u32[]{:S(2)}) collective-permute-start(bf16[24,6144]{1,0:T(8,128)(2,1)S(1)} %get-tuple-element.600), channel_id=1, source_target_pairs={{0,3},{1,0},{2,1},{3,2},{4,7},{5,4},{6,5},{7,6},{8,11},{9,8},{10,9... | collective-permute-start | bytes 884744 | tf_op jit(solution)/shard_map/cond/branch_1_fun/ppermute | solution.py:789
  419.3 11.6 %collective-permute-start.48 = (bf16[48,2304]{1,0:T(8,128)(2,1)}, bf16[48,2304]{1,0:T(8,128)(2,1)}, u32[]{:S(2)}, u32[]{:S(2)}) collective-permute-start(bf16[48,2304]{1,0:T(8,128)(2,1)} %get-tuple-element.608), channel_id=1, source_target_pairs={{0,8},{1,9},{2,10},{3,11},{4,12},{5,13},{6,14},{7,15},{8,0},{9,1},... | collective-permute-start | bytes 663560 | tf_op jit(solution)/shard_map/cond/branch_1_fun/ppermute | solution.py:789
  434.3 16.5 %collective-permute-start.45 = (bf16[96,2304]{1,0:T(8,128)(2,1)S(1)}, bf16[96,2304]{1,0:T(8,128)(2,1)}, u32[]{:S(2)}, u32[]{:S(2)}) collective-permute-start(bf16[96,2304]{1,0:T(8,128)(2,1)S(1)} %get-tuple-element.616), channel_id=1, source_target_pairs={{0,8},{1,9},{2,10},{3,11},{4,12},{5,13},{6,14},{7,15},{8,0},{9,1},... | collective-permute-start | bytes 1327112 | tf_op jit(solution)/shard_map/cond/branch_1_fun/ppermute | solution.py:789
  435.4 15.4 %collective-permute-start.46 = (bf16[96,2304]{1,0:T(8,128)(2,1)S(1)}, bf16[96,2304]{1,0:T(8,128)(2,1)}, u32[]{:S(2)}, u32[]{:S(2)}) collective-permute-start(bf16[96,2304]{1,0:T(8,128)(2,1)S(1)} %get-tuple-element.617), channel_id=1, source_target_pairs={{0,16},{1,17},{2,18},{3,19},{4,20},{5,21},{6,22},{7,23},{8,24},{9,... | collective-permute-start | bytes 1327112 | tf_op jit(solution)/shard_map/cond/branch_1_fun/ppermute | solution.py:789
  436.8 14.0 %collective-permute-start.47 = (bf16[24,6144]{1,0:T(8,128)(2,1)S(1)}, bf16[24,6144]{1,0:T(8,128)(2,1)}, u32[]{:S(2)}, u32[]{:S(2)}) collective-permute-start(bf16[24,6144]{1,0:T(8,128)(2,1)S(1)} %get-tuple-element.618), channel_id=1, source_target_pairs={{0,2},{1,3},{2,0},{3,1},{4,6},{5,7},{6,4},{7,5},{8,10},{9,11},{10,... | collective-permute-start | bytes 884744 | tf_op jit(solution)/shard_map/cond/branch_1_fun/ppermute | solution.py:789
  453.3 17.0 %collective-permute-start.52 = (bf16[24,2304]{1,0:T(8,128)(2,1)}, bf16[24,2304]{1,0:T(8,128)(2,1)}, u32[]{:S(2)}, u32[]{:S(2)}) collective-permute-start(bf16[24,2304]{1,0:T(8,128)(2,1)} %get-tuple-element.625), channel_id=1, source_target_pairs={{0,1},{1,2},{2,3},{3,0},{4,5},{5,6},{6,7},{7,4},{8,9},{9,10},{10,1... | collective-permute-start | bytes 331784 | tf_op jit(solution)/shard_map/cond/branch_1_fun/ppermute | solution.py:789
  453.3 17.9 %collective-permute-start.53 = (bf16[24,2304]{1,0:T(8,128)(2,1)}, bf16[24,2304]{1,0:T(8,128)(2,1)}, u32[]{:S(2)}, u32[]{:S(2)}) collective-permute-start(bf16[24,2304]{1,0:T(8,128)(2,1)} %get-tuple-element.626), channel_id=1, source_target_pairs={{0,2},{1,3},{2,0},{3,1},{4,6},{5,7},{6,4},{7,5},{8,10},{9,11},{10,... | collective-permute-start | bytes 331784 | tf_op jit(solution)/shard_map/cond/branch_1_fun/ppermute | solution.py:789
  454.5 17.7 %collective-permute-start.54 = (bf16[24,2304]{1,0:T(8,128)(2,1)}, bf16[24,2304]{1,0:T(8,128)(2,1)}, u32[]{:S(2)}, u32[]{:S(2)}) collective-permute-start(bf16[24,2304]{1,0:T(8,128)(2,1)} %get-tuple-element.627), channel_id=1, source_target_pairs={{0,3},{1,0},{2,1},{3,2},{4,7},{5,4},{6,5},{7,6},{8,11},{9,8},{10,9... | collective-permute-start | bytes 331784 | tf_op jit(solution)/shard_map/cond/branch_1_fun/ppermute | solution.py:789
  457.9 11.7 %collective-permute-start.56 = (bf16[24,896]{1,0:T(8,128)(2,1)}, bf16[24,896]{1,0:T(8,128)(2,1)S(1)}, u32[]{:S(2)}, u32[]{:S(2)}) collective-permute-start(bf16[24,896]{1,0:T(8,128)(2,1)} %get-tuple-element.629), channel_id=1, source_target_pairs={{0,2},{1,3},{2,0},{3,1},{4,6},{5,7},{6,4},{7,5},{8,10},{9,11},{10,... | collective-permute-start | bytes 129032 | tf_op jit(solution)/shard_map/cond/branch_1_fun/ppermute | solution.py:789
  (63 other events, 551.3 us)
Sparse Core Ops, SparseCore 0:
  20.1 30.8 all-gather.8
  52.6 29.5 all-gather.6
  83.8 29.5 all-gather.4
  151.2 29.4 all-gather.10

commit v3 on v2

--- a/solution.py
+++ b/solution.py
@@ -364,39 +364,65 @@
     return pl.multiple_of(jnp.minimum(base // 128 * 128, CAP - WINDOW), 128)
 
 
-def expert_kernel(
-    expert, experts, train, count, rows_ref, order_ref, counts_ref, place_t_ref, gate_ref, normed_ref,
-    cot_ref, *rest,
+def dispatch_kernel(
+    expert, experts, order_ref, counts_ref, place_t_ref, gate_ref, normed_ref, cot_ref, x_ref, g_ref,
+    *rest,
 ):
+    length = normed_ref.shape[0]
+    x_ref[...] = jnp.zeros_like(x_ref)
+    g_ref[...] = jnp.zeros_like(g_ref)
+    for block in range(length // BLOCK):
+        base = window_base(counts_ref, block, expert, experts)
+        cols = slice(block * BLOCK, (block + 1) * BLOCK)
+        pick = flag(iota((WINDOW, BLOCK), 0) + base == place_t_ref[expert : expert + 1, cols])
+        window = pl.ds(base, WINDOW)
+        x_ref[window, :] += dot_nn(pick, normed_ref[cols, :]).astype(bf16)
+        scaled = gate_ref[cols, expert : expert + 1] * cot_ref[cols, :].astype(f32)
+        g_ref[window, :] += dot_nn(pick, scaled.astype(bf16)).astype(bf16)
+    if rest:
+        turned_ref, staged = rest
+        half = turned_ref.shape[0] // 2
+        staged[...] = x_ref[...].T
+        lay_out(order_ref, staged, turned_ref.at[:half], turned_ref.at[half:])
+
+
+def dispatch(expert, experts, train, order, counts, place_t, gates, normed, cot):
+    width = normed.shape[1]
+    outs = [shape_of((CAP, width), bf16)] * 2
+    outs = outs + ([shape_of((width, CAP), bf16)] if train else [])
+    ins = [place_t, gates, normed, cot]
+    return call(
+        functools.partial(dispatch_kernel, expert, experts),
+        "dispatch_%d" % expert,
+        (1,),
+        [order, counts] + ins,
+        [SMEM, SMEM] + [whole(a.shape) for a in ins],
+        outs,
+        [whole(o.shape) for o in outs],
+        [pltpu.VMEM((width, CAP), bf16)] if train else [],
+        flops=4 * CAP * WINDOW * width,
+    )
+
+
+def expert_kernel(slot, train, count, rows_ref, order_ref, counts_ref, *rest):
+    rows_x, rows_g, rest = rest[0], rest[1], rest[2:]
+    if train:
+        turned_x, rest = rest[0], rest[1:]
     in_pieces, out_pieces, rest = rest[:count], rest[count : 2 * count], rest[2 * count :]
     result_ref, back_ref, rest = rest[0], rest[1], rest[2:]
     if train:
         in_own, in_other, out_own, out_other = rest[:4]
         rest = rest[4:]
-        turned_x, acts, grads, staged = rest[6:]
-    rows_x, rows_g, sum_r, sum_b, in_ref, out_ref = rest[:6]
-    length, width = normed_ref.shape
-    half = width // 2
+        acts, grads, staged = rest[4:]
+    sum_r, sum_b, in_ref, out_ref = rest[:4]
+    half = rows_x.shape[1] // 2
     step = pl.program_id(0)
-    load = counts_ref[length // BLOCK * experts + expert]
+    load = counts_ref[slot]
 
     @pl.when(step == 0)
     def _():
-        rows_x[...] = jnp.zeros_like(rows_x)
-        rows_g[...] = jnp.zeros_like(rows_g)
         sum_r[...] = jnp.zeros_like(sum_r)
         sum_b[...] = jnp.zeros_like(sum_b)
-        for block in range(length // BLOCK):
-            base = window_base(counts_ref, block, expert, experts)
-            cols = slice(block * BLOCK, (block + 1) * BLOCK)
-            pick = flag(iota((WINDOW, BLOCK), 0) + base == place_t_ref[expert : expert + 1, cols])
-            window = pl.ds(base, WINDOW)
-            rows_x[window, :] += dot_nn(pick, normed_ref[cols, :]).astype(bf16)
-            scaled = gate_ref[cols, expert : expert + 1] * cot_ref[cols, :].astype(f32)
-            rows_g[window, :] += dot_nn(pick, scaled.astype(bf16)).astype(bf16)
-        if train:
-            staged[...] = rows_x[...].T
-            lay_out(order_ref, staged, turned_x.at[:half], turned_x.at[half:])
 
     put_together(rows_ref, in_pieces, in_ref)
     put_together(rows_ref, out_pieces, out_ref)
@@ -440,10 +466,8 @@
         back_ref[...] = sum_b[...].astype(bf16)
 
 
-def expert_pass(
-    expert, experts, train, rows, order, counts, place_t, gates, normed, cot, pieces
-):
-    length, width = normed.shape
+def expert_pass(expert, slot, train, rows, order, counts, picked, pieces):
+    width = picked[0].shape[1]
     hidden = pieces[0][0].shape[1] // 2
     arrays = [p[0] for p in pieces]
     steps = hidden // width
@@ -452,8 +476,6 @@
     outs = [shape_of((CAP, width), bf16)] * 2
     out_specs = [whole((CAP, width))] * 2
     scratch = [
-        pltpu.VMEM((CAP, width), bf16),
-        pltpu.VMEM((CAP, width), bf16),
         pltpu.VMEM((CAP, width), f32),
         pltpu.VMEM((CAP, width), f32),
         pltpu.VMEM((width, width), bf16),
@@ -463,25 +485,17 @@
         outs = outs + [shape_of((half, hidden), bf16)] * 4
         out_specs = out_specs + [slab] * 4
         scratch = scratch + [
-            pltpu.VMEM((width, CAP), bf16),
             pltpu.VMEM((CAP, width), bf16),
             pltpu.VMEM((CAP, width), bf16),
             pltpu.VMEM((width, width), bf16),
         ]
     return call(
-        functools.partial(expert_kernel, expert, experts, train, len(pieces)),
+        functools.partial(expert_kernel, slot, train, len(pieces)),
         "expert_%d" % expert,
         (steps,),
-        [rows, order, counts, place_t, gates, normed, cot] + arrays + arrays,
-        [
-            SMEM,
-            SMEM,
-            SMEM,
-            whole(place_t.shape),
-            whole(gates.shape),
-            whole(normed.shape),
-            whole(cot.shape),
-        ]
+        [rows, order, counts] + list(picked) + arrays + arrays,
+        [SMEM, SMEM, SMEM]
+        + [whole(p.shape) for p in picked]
         + gathered_specs(pieces, width, lambda i: i)
         + gathered_specs(pieces, width, lambda i: i + steps),
         outs,
@@ -723,6 +737,30 @@
     return [pl.BlockSpec((a.shape[0] // 4, a.shape[1]), lambda *_: (number, 0)) for a in arrays]
 
 
+def halves_kernel(low, high, top, bottom):
+    top[...] = low[...]
+    bottom[...] = high[...]
+
+
+def halves(low, high):
+    half, columns = low.shape[0] // 2, low.shape[1]
+    if half % 8:
+        return [low[:half], high[half:]]
+    outs = [shape_of((half, columns), bf16)] * 2
+    return call(
+        halves_kernel,
+        "halves",
+        (1,),
+        [low, high],
+        [
+            pl.BlockSpec((half, columns), lambda *_: (0, 0)),
+            pl.BlockSpec((half, columns), lambda *_: (1, 0)),
+        ],
+        outs,
+        [whole(o.shape) for o in outs],
+    )
+
+
 def end_sums(own, got):
     count, columns = len(own), sum(a.shape[1] for a in own)
     outs = [shape_of((own[0].shape[0] // 8, columns), bf16)] * 2
@@ -834,8 +872,7 @@
 
     def take_first(self, got):
         self.low, self.high, self.full_over = got
-        half = self.full.shape[0] // 2
-        self.sent = [self.low[:half], self.high[half:]]
+        self.sent = halves(self.low, self.high)
 
     def send_second(self):
         links = self.links
@@ -857,6 +894,37 @@
             own = own + [links.flip(p, bit) for p in own]
             over = over + [links.flip(p, bit) for p in over]
         self.pieces = [(p, p.shape[0], 0) for p in own + over]
+
+
+class PlaneFirst:
+    def __init__(self, links, part):
+        self.links, self.part = links, part
+
+    def send_first(self):
+        return [self.links.flip(self.part, bit) for bit in self.links.bits[:2]]
+
+    def take_first(self, got):
+        self.low, self.high = got
+        half = self.part.shape[0] // 2
+        self.sent = [self.low[:half], self.high[half:]]
+
+    def send_second(self):
+        low, high = self.links.bits[0], self.links.bits[1]
+        return [self.links.flip(self.sent[0], high), self.links.flip(self.sent[1], low)]
+
+    def take_second(self, got):
+        self.end = jnp.concatenate(got)
+
+    def take_lines(self, own):
+        for bit in self.links.bits[2:]:
+            own = own + [self.links.flip(p, bit) for p in own]
+        self.own = own
+
+    def send_over(self, which):
+        return [self.links.swap(self.own[number]) for number in which]
+
+    def take_over(self, got):
+        self.pieces = [(p, p.shape[0], 0) for p in self.own + got]
 
 
 def piece_rows(links, own_rows):
@@ -907,7 +975,9 @@
             own = [s[:height] for s in sums]
             got = [links.flip(s[height:], bit) for s in sums]
         self.near, self.got = own, got
-        self.sums = end_sums(own, got)
+
+    def end(self):
+        return end_sums(self.near, self.got)
 
     def send_first(self):
         low, high = self.links.bits[0], self.links.bits[1]
@@ -961,7 +1031,8 @@
             return packed(expert_in[:, e], expert_out[:, e])
         return packed(frozen_in[:, e - train_count], frozen_out[:, e - train_count])
 
-    weights = [Gather(links, part_of(e)) for e in range(experts)]
+    last = experts - 1
+    weights = [Gather(links, part_of(e)) for e in range(last)] + [PlaneFirst(links, part_of(last))]
     always = segment_ids[0, 0] >= 0
     chosen = (routes[:, :, None] == jnp.arange(experts, dtype=i32)).astype(i32)
     per_block = jnp.sum(chosen.reshape(length // BLOCK, 2 * BLOCK, experts), axis=1)
@@ -969,75 +1040,85 @@
     counts = counts.reshape(-1)
     place, place_t = route_places(routes)
 
-    def run(expert, normed):
+    def pick(expert, normed, gates):
+        return dispatch(
+            expert, experts, expert < train_count, order, counts, place_t, gates, normed, cotangent
+        )
+
+    def run(expert, picked):
         return expert_pass(
-            expert, experts, expert < train_count, rows, order, counts, place_t, gates, normed,
-            cotangent, weights[expert].pieces,
+            expert, length // BLOCK * experts + expert, expert < train_count,
+            order if expert == last else rows, order, counts, picked, weights[expert].pieces,
         )
 
     shifts = list(range(1, narrow))
 
-    def line(gather, *deps):
-        part = after(gather.part, *deps) if deps else gather.part
-        gather.full = lax.all_gather(part, "narrow", axis=0, tiled=True)
+    def line(part, *deps):
+        part = after(part, *deps) if deps else part
+        return lax.all_gather(part, "narrow", axis=0, tiled=True)
 
     w0, w1, w2, w3 = weights
     w0.part = after(w0.part, dense.part)
-    line(w0)
+    w0.full = line(w0.part)
     dense.take_along(dense.send_along())
-    line(w1, dense.full)
-    dense.take_first(dense.send_first())
-    line(w2, dense.low)
-    dense.take_second(dense.send_second())
-    line(w3, dense.ends)
+    w1.full = line(w1.part, dense.full)
+    dense.take_first(together(always, dense.send_first))
+    w2.full = line(w2.part, dense.low)
+    dense.take_second(together(always, dense.send_second))
     dense.take_third(dense.send_third())
 
     def step():
         qkv, full, gains = project(rows, inputs, dense.pieces)
         attended, logs = attend(docs, qkv)
-        return w0.send_first(), (qkv, full, gains, attended, logs)
-
-    got, (qkv, dense, gains, attended, logs) = together(always, step)
+        return w0.send_first(), w3.send_first(), (qkv, full, gains, attended, logs)
+
+    got, ahead, (qkv, dense, gains, attended, logs) = together(always, step)
     w0.take_first(got)
-    got, (hidden, normed, gates) = together(
-        always, lambda: (w0.send_second(), middle(inputs, attended, place, dense))
-    )
+    w3.take_first(ahead)
+    w3.own = [line(shard, qkv) for shard in (w3.part, w3.low, w3.high)]
+    def step():
+        made = middle(inputs, attended, place, dense)
+        return w0.send_second(), made, pick(0, *made[1:])
+
+    got, (hidden, normed, gates), picked = together(always, step)
     w0.take_second(got)
     w0.take_third(w0.send_third())
-    got, one = together(always, lambda: (w1.send_first(), run(0, normed)))
+    got, ahead, one = together(
+        always, lambda: (w1.send_first(), w3.send_second(), run(0, picked))
+    )
     w1.take_first(got)
-    w1.take_second(w1.send_second())
+    w3.take_second(ahead)
+    got, picked = together(
+        always,
+        lambda: (w1.send_second(), [pick(e, normed, gates) for e in range(1, experts)]),
+    )
+    w1.take_second(got)
     w1.take_third(w1.send_third())
+    end = line(w3.end, w1.ends)
     term0 = Scatter(links, [one[2], one[4]], [one[3], one[5]])
     w2.full = after(w2.full, one[0])
     got, more, two = together(
-        always, lambda: (w2.send_first(), term0.send_over(), run(1, normed))
+        always, lambda: (w2.send_first(), term0.send_over(), run(1, picked[0]))
     )
     w2.take_first(got)
 
-    def step():
-        term0.take_over(more)
-        return w2.send_second(), (term0.near, term0.got, term0.sums)
-
-    got, (term0.near, term0.got, term0.sums) = together(always, step)
+    term0.take_over(more)
+    got, ahead, term0.sums = together(
+        always, lambda: (w2.send_second(), w3.send_over([0]), term0.end())
+    )
     w2.take_second(got)
     w2.take_third(w2.send_third())
+    w3.take_lines(w3.own + [end])
     term1 = Scatter(links, [two[2], two[4]], [two[3], two[5]])
-    w3.full = after(w3.full, two[0])
+    count = len(w3.own)
     got, more, three = together(
-        always, lambda: (w3.send_first(), term1.send_over(), run(2, normed))
-    )
-    w3.take_first(got)
-
-    def step():
-        term1.take_over(more)
-        return w3.send_second(), (term1.near, term1.got, term1.sums)
-
-    got, (term1.near, term1.got, term1.sums) = together(always, step)
-    w3.take_second(got)
-    w3.take_third(w3.send_third())
+        always, lambda: (w3.send_over(range(1, count)), term1.send_over(), run(2, picked[1]))
+    )
+    w3.take_over(ahead + got)
+    term1.take_over(more)
+    term1.sums = term1.end()
     got, more, four = together(
-        always, lambda: (term0.send_first(), term1.send_first(), run(3, normed))
+        always, lambda: (term0.send_first(), term1.send_first(), run(3, picked[2]))
     )
     term0.take_first(got)
     results, backs = [[m[i] for m in (one, two, three, four)] for i in range(2)]
@@ -1068,6 +1149,7 @@
         ),
     )
     out_term.take_over(over)
+    out_term.sums = out_term.end()
     qkv_term = Scatter(links, *[[m] for m in made])
     over, got, last, input_grad = together(
         always,
@@ -1077,6 +1159,7 @@
         ),
     )
     qkv_term.take_over(over)
+    qkv_term.sums = qkv_term.end()
     out_term.take_first(got)
 
     def unpacked(parts):
@@ -1086,37 +1169,41 @@
         inner = inner.reshape(own_rows, groups, width).transpose(0, 2, 1).reshape(own_rows, -1)
         return inner, outer.reshape(own_rows * groups, width)
 
-    got, two, first = together(
+    got, two, middle_part, first = together(
         always,
         lambda: (
-            qkv_term.send_first(), out_term.send_second(), unpacked([term0.mine] + more)
+            qkv_term.send_first(), out_term.send_second(), term1.send_along(shifts[1:2]),
+            unpacked([term0.mine] + more),
         ),
     )
     qkv_term.take_first(got)
     out_term.take_second(two)
-    got, middle_part = together(
-        always, lambda: (qkv_term.send_second(), term1.send_along(shifts[1:2]))
-    )
-    qkv_term.take_second(got)
 
     def step():
         second = unpacked([term1.mine] + one + middle_part + last)
         in_grad, down_grad = [jnp.stack(pair, axis=1) for pair in zip(first, second)]
-        return qkv_term.send_along(), out_term.send_along(), in_grad, down_grad
+        return qkv_term.send_second(), out_term.send_along(), in_grad, down_grad
 
     got, two, in_grad, down_grad = together(always, step)
+    qkv_term.take_second(got)
+
+    def step():
+        out_term.take_along(two)
+        out = out_term.result
+        return qkv_term.send_along(), (
+            out[:, :width], out[:, width + LANES - 1], out[:, width : width + train_count]
+        )
+
+    got, outs = together(always, step)
     qkv_term.take_along(got)
-    out_term.take_along(two)
-    out_term, qkv_grad = out_term.result, qkv_term.result
+    qkv_grad = qkv_term.result
     gain_grad = jnp.sum(qkv_weight.astype(f32) * qkv_grad, axis=1) / attention_gain.astype(f32)
     return (
         block_output,
         input_grad,
         gain_grad,
         qkv_grad,
-        out_term[:, :width],
-        out_term[:, width + LANES - 1],
-        out_term[:, width : width + train_count],
+        *outs,
         in_grad,
         down_grad,
     )

time: 492 us -> 474 us (0.963)
  local copies, waits for them, and re-layouts: 50.2 us -> 28.7 us
  Pallas kernels: 251 us -> 262 us
  waiting for transfers between devices: 88.6 us -> 79.2 us
    cond x28 -> x21, local copies, waits for them, and re-layouts: 13.4 us -> 2.71 us
    slice x10 -> x2, local copies, waits for them, and re-layouts: 12.4 us -> 1.92 us  [take_first(): self.sent = [self.low[:half], self.high[half:]]]
    ppermute x82 -> x81, waiting for transfers between devices: 88.5 us -> 78 us  [send(): return lax.ppermute(part, AXES, pairs)]
    pallas_call x24 -> x32, Pallas kernels: 251 us -> 262 us  [call(): pl.pallas_call(kernel, name=name, grid=grid, in_specs=in_specs, out_specs...]
    ppermute x82 -> x81, starting transfers between devices: 63.9 us -> 68 us  [send(): return lax.ppermute(part, AXES, pairs)]
  transfers between devices with their start and end apart: 86 -> 88, of which waited for: 29 -> 27; matrix products, arithmetic and copies ran while one was open for 11% -> 7% of each run, Pallas kernels for 47% -> 50%
where the time goes in v3:
time: 474 us; the launch traced here: 465 us
  Pallas kernels  262 us (55%)
  waiting for transfers between devices  79.2 us (17%)
  starting transfers between devices  68.3 us (14%)
  local copies, waits for them, and re-layouts  28.7 us (6%)
  between operations  15.6 us (3%)
  other arithmetic  10.1 us (2%)
    pallas_call x32, Pallas kernels, call(): pl.pallas_call(kernel, name=name, grid=grid, in_specs=in_specs, out_specs...  262 us
    ppermute x81, waiting for transfers between devices, send(): return lax.ppermute(part, AXES, pairs)  78 us
    ppermute x81, starting transfers between devices, send(): return lax.ppermute(part, AXES, pairs)  68 us
  transfers between devices with their start and end apart: 88, of which 27 were waited for; matrix products, arithmetic and copies ran while one was open for 7% of the time, Pallas kernels for 50%

profile of v3, /device:TPU:0, one launch (start us, length us, event | category | flops | bytes accessed | tf_op | source)
XLA Modules:
  0.0 465.4 jit_solution(14367798434089385024)
XLA Ops:
  9.1 5.1 %collective-permute-start.70 = (bf16[24,3200]{1,0:T(8,128)(2,1)S(1)}, bf16[24,3200]{1,0:T(8,128)(2,1)S(1)}, u32[]{:S(2)}, u32[]{:S(2)}) collective-permute-start(bf16[24,3200]{1,0:T(8,128)(2,1)S(1)} %get-tuple-element.1142), channel_id=1, source_target_pairs={{0,3},{1,0},{2,1},{3,2},{4,7},{5,4},{6,5},{7,6},{8,11},{9,8},{10,9... | collective-permute-start | bytes 460808 | tf_op jit(solution)/shard_map/ppermute | solution.py:827
  20.9 6.3 %collective-permute-done.71 = bf16[24,3200]{1,0:T(8,128)(2,1)S(1)} collective-permute-done((bf16[24,3200]{1,0:T(8,128)(2,1)S(1)}, bf16[24,3200]{1,0:T(8,128)(2,1)S(1)}, u32[]{:S(2)}, u32[]{:S(2)}) %collective-permute-start.71) | collective-permute-done | bytes 153632 | tf_op jit(solution)/shard_map/ppermute | solution.py:827
  32.2 16.5 %conditional.17 = (bf16[96,3200]{1,0:T(8,128)(2,1)}, bf16[96,3200]{1,0:T(8,128)(2,1)}, bf16[96,3200]{1,0:T(8,128)(2,1)}) conditional(s32[]{:T(128)} %bitcast.11, () %tuple.167, bf16[96,3200]{1,0:T(8,128)(2,1)S(1)} %constant_dynamic-update-slice_fusion.2), branch_computations={%region_2.3_spmd, %region_3.4_spmd} | conditional | bytes 7372944 | solution.py:848
  35.2 12.3 %collective-permute-done = bf16[96,3200]{1,0:T(8,128)(2,1)} collective-permute-done((bf16[96,3200]{1,0:T(8,128)(2,1)S(1)}, bf16[96,3200]{1,0:T(8,128)(2,1)}, u32[]{:S(2)}, u32[]{:S(2)}) %collective-permute-start) | collective-permute-done | bytes 614432 | tf_op jit(solution)/shard_map/cond/branch_1_fun/ppermute | solution.py:827
  51.3 11.2 %conditional.18 = (bf16[48,3200]{1,0:T(8,128)(2,1)}, bf16[48,3200]{1,0:T(8,128)(2,1)}, bf16[96,3200]{1,0:T(8,128)(2,1)}, bf16[96,3200]{1,0:T(8,128)(2,1)}) conditional(s32[]{:T(128)} %bitcast.11, () %tuple.168, (bf16[48,3200]{1,0:T(8,128)(2,1)S(1)}, bf16[48,3200]{1,0:T(8,128)(2,1)S(1)}, bf16[96,3200]{1,0:T(8,128)(2,1)}, ...), branch_computations={%region_4.5_spmd, %region_5.6_spmd} | conditional | bytes 7372992 | solution.py:848
  53.9 7.3 %collective-permute-done.3 = bf16[48,3200]{1,0:T(8,128)(2,1)} collective-permute-done((bf16[48,3200]{1,0:T(8,128)(2,1)S(1)}, bf16[48,3200]{1,0:T(8,128)(2,1)}, u32[]{:S(2)}, u32[]{:S(2)}) %collective-permute-start.3) | collective-permute-done | bytes 307232 | tf_op jit(solution)/shard_map/cond/branch_1_fun/ppermute | solution.py:827
  64.7 37.5 %conditional.19 = (bf16[96,6144]{1,0:T(8,128)(2,1)}, bf16[96,6144]{1,0:T(8,128)(2,1)}, bf16[96,6144]{1,0:T(8,128)(2,1)}, bf16[24,6144]{1,0:T(8,128)(2,1)}, bf16[...) conditional(s32[]{:T(128)} %bitcast.11, () %tuple.165, ...), branch_computations={%region_6.7_spmd, %region_7.8_spmd} | conditional | flops 6039797760 | bytes 49193296 | solution.py:848
  69.1 9.4 %project.1 = (bf16[1024,2304]{1,0:T(8,128)(2,1)}, bf16[768,3200]{1,0:T(8,128)(2,1)}, bf16[16,768]{1,0:T(8,128)(2,1)}) custom-call(s32[10]{0:T(128)S(1)} %get-tuple-element.420.rows_ref, bf16[1024,768]{1,0:T(8,128)(2,1)S(1)} %get-tuple-element.421.inputs_ref, bf16[96,3200]{1,0:T(8,128)(2,1)S(1)} %get-tuple-element.422.rest_0_, ...), custom_call_target="tpu_custom_call" | custom-call | flops 3623878656 | bytes 16146472 | tf_op jit(solution)/shard_map/cond/branch_1_fun/project/pallas_call | solution.py:70
  78.7 21.5 %attend.1 = (bf16[1024,768]{1,0:T(8,128)(2,1)S(1)}, f32[6,8,1024]{2,1,0:T(8,128)}) custom-call(s32[1024,1]{1,0:T(8,128)S(1)} %copy.111.doc_ref, s32[1,1024]{1,0:T(1,128)S(1)} %get-tuple-element.435.doc_t_ref, bf16[1024,2304]{1,0:T(8,128)(2,1)} %get-tuple-element.1175.q_ref.k_ref.v_ref, bf16[1024,2304]{1,0:T(8,128)(2,1)} %get-tuple-element.1175.q_ref.k_ref.v_ref, ...), custom_call_target="tpu_custom_call" | custom-call | flops 2415919104 | bytes 15933440 | tf_op jit(solution)/shard_map/cond/branch_1_fun/attend/pallas_call | solution.py:70
  107.4 16.2 %conditional.20 = (bf16[48,6144]{1,0:T(8,128)(2,1)}, bf16[48,6144]{1,0:T(8,128)(2,1)}, bf16[96,6144]{1,0:T(8,128)(2,1)}, bf16[96,6144]{1,0:T(8,128)(2,1)}, f32[1...) conditional(s32[]{:T(128)} %bitcast.11, () %tuple.171, ...), branch_computations={%region_8.9_spmd, %region_9.10_spmd} | conditional | flops 2113929216 | bytes 40141152 | solution.py:848
  109.0 7.4 %middle.1 = (f32[1024,768]{1,0:T(8,128)}, bf16[1024,768]{1,0:T(8,128)(2,1)}, f32[1024,128]{1,0:T(8,128)}) custom-call(bf16[1024,768]{1,0:T(8,128)(2,1)} %get-tuple-element.442.inputs_ref, bf16[1024,768]{1,0:T(8,128)(2,1)S(1)} %get-tuple-element.443.attended_ref, s32[1024,128]{1,0:T(8,128)S(1)} %get-tuple-element.444.place_ref, ...), custom_call_target="tpu_custom_call" | custom-call | flops 1207959552 | bytes 18743296 | tf_op jit(solution)/shard_map/cond/branch_1_fun/middle/pallas_call | solution.py:70
  116.5 4.8 %dispatch_0.1 = (bf16[768,768]{1,0:T(8,128)(2,1)}, bf16[768,768]{1,0:T(8,128)(2,1)}, bf16[768,768]{1,0:T(8,128)(2,1)}) custom-call(s32[8]{0:T(128)S(1)} %get-tuple-element.449.order_ref, s32[20]{0:T(128)S(1)} %get-tuple-element.450.counts_ref, s32[8,1024]{1,0:T(8,128)S(1)} %get-tuple-element.451.place_t_ref, f32[1024,128]{1,0:T(8,128)} %get-tuple-element.1198.gate_ref, ...), custom_call_target="tpu_custom_call" | custom-call | flops 905969664 | bytes 7241840 | tf_op jit(solution)/shard_map/cond/branch_1_fun/dispatch_0/pallas_call | solution.py:70
  121.3 2.0 collective-permute-done.12
  126.7 33.4 %conditional.21 = (bf16[96,6144]{1,0:T(8,128)(2,1)}, bf16[96,6144]{1,0:T(8,128)(2,1)}, bf16[96,6144]{1,0:T(8,128)(2,1)}, bf16[12,6144]{1,0:T(8,128)(2,1)}, bf16[...) conditional(s32[]{:T(128)} %bitcast.11, () %tuple.163, ...), branch_computations={%region_10.11_spmd, %region_11.12_spmd} | conditional | flops 16986931200 | bytes 54264304 | solution.py:848
  131.3 24.2 %expert_0.1 = (bf16[768,768]{1,0:T(8,128)(2,1)}, bf16[768,768]{1,0:T(8,128)(2,1)}, bf16[384,3072]{1,0:T(8,128)(2,1)S(1)}, bf16[384,3072]{1,0:T(8,128)(2,1)}, bf1...) custom-call(s32[10]{0:T(128)S(1)} %get-tuple-element.459.rows_ref, s32[8]{0:T(128)S(1)} %get-tuple-element.460.order_ref, ...), custom_call_target="tpu_custom_call" | custom-call | flops 16986931200 | bytes 34209944 | tf_op jit(solution)/shard_map/cond/branch_1_fun/expert_0/pallas_call | solution.py:70
  155.5 4.5 collective-permute-done.19
  161.8 20.9 %conditional.22 = (bf16[48,6144]{1,0:T(8,128)(2,1)}, bf16[48,6144]{1,0:T(8,128)(2,1)}, bf16[96,6144]{1,0:T(8,128)(2,1)}, bf16[96,6144]{1,0:T(8,128)(2,1)}, bf16[...) conditional(s32[]{:T(128)} %bitcast.11, () %tuple.177, ...), branch_computations={%region_12.13_spmd, %region_13.14_spmd} | conditional | flops 2717908992 | bytes 33784448 | solution.py:848
  162.3 5.3 %collective-permute-start.21 = (bf16[48,6144]{1,0:T(8,128)(2,1)S(1)}, bf16[48,6144]{1,0:T(8,128)(2,1)}, u32[]{:S(2)}, u32[]{:S(2)}) collective-permute-start(bf16[48,6144]{1,0:T(8,128)(2,1)S(1)} %get-tuple-element.481), channel_id=1, source_target_pairs={{0,16},{1,17},{2,18},{3,19},{4,20},{5,21},{6,22},{7,23},{8,24},{9,... | collective-permute-start | bytes 1769480 | tf_op jit(solution)/shard_map/cond/branch_1_fun/ppermute | solution.py:827
  168.2 4.6 dispatch_1.1
  172.8 4.5 dispatch_2.1
  177.4 4.5 dispatch_3.1
  182.7 1.8 pad_maximum_fusion.5
  185.1 1.8 collective-permute-done.77
  187.8 29.5 %conditional.23 = (bf16[96,6144]{1,0:T(8,128)(2,1)}, bf16[96,6144]{1,0:T(8,128)(2,1)}, bf16[96,6144]{1,0:T(8,128)(2,1)}, bf16[384,3072]{1,0:T(8,128)(2,1)}, bf16...) conditional(s32[]{:T(128)} %bitcast.11, () %tuple.174, ...), branch_computations={%region_14.15_spmd, %region_15.16_spmd} | conditional | flops 16986931200 | bytes 67240376 | solution.py:848
  189.4 24.0 %expert_1.1 = (bf16[768,768]{1,0:T(8,128)(2,1)}, bf16[768,768]{1,0:T(8,128)(2,1)}, bf16[384,3072]{1,0:T(8,128)(2,1)}, bf16[384,3072]{1,0:T(8,128)(2,1)}, bf16[38...) custom-call(s32[10]{0:T(128)S(1)} %get-tuple-element.501.rows_ref, s32[8]{0:T(128)S(1)} %get-tuple-element.502.order_ref, ...), custom_call_target="tpu_custom_call" | custom-call | flops 16986931200 | bytes 34209944 | tf_op jit(solution)/shard_map/cond/branch_1_fun/expert_1/pallas_call | solution.py:70
  213.3 3.5 collective-permute-done.25
  217.3 2.3 halves.7
  219.6 16.6 %conditional.24 = (bf16[48,6144]{1,0:T(8,128)(2,1)}, bf16[48,6144]{1,0:T(8,128)(2,1)}, bf16[96,6144]{1,0:T(8,128)(2,1)}, bf16[96,6144]{1,0:T(8,128)(2,1)}, bf16[...) conditional(s32[]{:T(128)} %bitcast.11, () %tuple.181, ...), branch_computations={%region_16.17_spmd, %region_17.18_spmd} | conditional | bytes 29491456 | solution.py:848
  223.5 12.7 %collective-permute-done.30 = bf16[48,6144]{1,0:T(8,128)(2,1)} collective-permute-done((bf16[48,6144]{1,0:T(8,128)(2,1)}, bf16[48,6144]{1,0:T(8,128)(2,1)}, u32[]{:S(2)}, u32[]{:S(2)}) %collective-permute-start.30) | collective-permute-done | bytes 589856 | tf_op jit(solution)/shard_map/cond/branch_1_fun/ppermute | solution.py:827
  236.8 1.8 collective-permute-done.79
  239.5 24.2 %conditional.25 = (bf16[96,6144]{1,0:T(8,128)(2,1)}, bf16[96,6144]{1,0:T(8,128)(2,1)}, bf16[96,6144]{1,0:T(8,128)(2,1)}, bf16[384,3072]{1,0:T(8,128)(2,1)}, bf16...) conditional(s32[]{:T(128)} %bitcast.11, () %tuple.184, ...), branch_computations={%region_18.19_spmd, %region_19.20_spmd} | conditional | flops 11324620800 | bytes 56623512 | solution.py:848
  240.7 23.0 %expert_2.1 = (bf16[768,768]{1,0:T(8,128)(2,1)}, bf16[768,768]{1,0:T(8,128)(2,1)}) custom-call(s32[10]{0:T(128)S(1)} %get-tuple-element.539.rows_ref, s32[8]{0:T(128)S(1)} %get-tuple-element.540.order_ref, s32[20]{0:T(128)S(1)} %get-tuple-element.541.counts_ref, bf16[768,768]{1,0:T(8,128)(2,1)} %get-tuple-element.542.rest_0_, ...), custom_call_target="tpu_custom_call" | custom-call | flops 11324620800 | bytes 23593112 | tf_op jit(solution)/shard_map/cond/branch_1_fun/expert_2/pallas_call | solution.py:70
  263.7 3.0 end_sums.5
  267.0 29.8 %conditional.26 = (bf16[48,6144]{1,0:T(8,128)(2,1)}, bf16[48,6144]{1,0:T(8,128)(2,1)}, bf16[48,6144]{1,0:T(8,128)(2,1)}, bf16[48,6144]{1,0:T(8,128)(2,1)}, bf16[...) conditional(s32[]{:T(128)} %bitcast.11, () %tuple.180, (bf16[48,6144]{1,0:T(8,128)(2,1)S(1)}, ...), branch_computations={%region_20.21_spmd, %region_21.22_spmd} | conditional | flops 11324620800 | bytes 33030496 | solution.py:848
  271.5 22.8 %expert_3.1 = (bf16[768,768]{1,0:T(8,128)(2,1)}, bf16[768,768]{1,0:T(8,128)(2,1)}) custom-call(s32[8]{0:T(128)S(1)} %get-tuple-element.560.rows_ref.order_ref, s32[8]{0:T(128)S(1)} %get-tuple-element.560.rows_ref.order_ref, s32[20]{0:T(128)S(1)} %get-tuple-element.561.counts_ref, bf16[768,768]{1,0:T(8,128)(2,1)} %get-tuple-element.562.rest_0_, ...), custom_call_target="tpu_custom_call" | custom-call | flops 11324620800 | bytes 23593104 | tf_op jit(solution)/shard_map/cond/branch_1_fun/expert_3/pallas_call | solution.py:70
  294.3 2.5 collective-permute-done.43
  296.8 4.4 middle_sums.5
  301.3 28.6 %conditional.27 = (bf16[96,6144]{1,0:T(8,128)(2,1)}, bf16[96,6144]{1,0:T(8,128)(2,1)}, bf16[96,6144]{1,0:T(8,128)(2,1)}, bf16[96,6144]{1,0:T(8,128)(2,1)}, bf16[...) conditional(s32[]{:T(128)} %bitcast.11, () %tuple.162, ...), branch_computations={%region_22.23_spmd, %region_23.24_spmd} | conditional | flops 4831838208 | bytes 67698952 | solution.py:848
  302.1 1.7 collective-permute-start.45
  303.8 4.6 middle_sums.4
  308.4 20.8 %combine.1 = (bf16[1024,768]{1,0:T(8,128)(2,1)}, f32[1024,768]{1,0:T(8,128)}, bf16[1024,768]{1,0:T(8,128)(2,1)}, bf16[384,896]{1,0:T(8,128)(2,1)S(1)}, bf16[384,896]{1,0:T(8,128)(2,1)}) custom-call(s32[8]{0:T(128)S(1)} %get-tuple-element.584.order_ref, s32[20]{0:T(128)S(1)} %get-tuple-element.585.counts_ref, s32[1024,128]{1,0:T(8,128)} %get-tuple-element.586.place_ref, ...), custom_call_target="tpu_custom_call" | custom-call | flops 4831838208 | bytes 35848304 | tf_op jit(solution)/shard_map/cond/branch_1_fun/combine/pallas_call | solution.py:70
  329.9 4.2 line_sums.4
  334.1 39.7 %conditional.28 = (bf16[96,6144]{1,0:T(8,128)(2,1)}, bf16[96,6144]{1,0:T(8,128)(2,1)}, bf16[24,6144]{1,0:T(8,128)(2,1)}, bf16[24,6144]{1,0:T(8,128)(2,1)}, bf16[...) conditional(s32[]{:T(128)} %bitcast.11, () %tuple.193, ...), branch_computations={%region_24.25_spmd, %region_25.26_spmd} | conditional | flops 6039797760 | bytes 33636616 | solution.py:848
  339.1 2.9 collective-permute-start.50
  342.2 31.3 %attend_back.1 = (bf16[1024,768]{1,0:T(8,128)(2,1)}, bf16[1024,768]{1,0:T(8,128)(2,1)}, bf16[1024,768]{1,0:T(8,128)(2,1)}) custom-call(s32[1024,1]{1,0:T(8,128)S(1)} %copy.112.doc_ref, s32[1,1024]{1,0:T(1,128)S(1)} %get-tuple-element.611.doc_t_ref, bf16[1024,2304]{1,0:T(8,128)(2,1)} %get-tuple-element.612.q_ref.k_ref.v_ref, ...), custom_call_target="tpu_custom_call" | custom-call | flops 6039797760 | bytes 20652032 | tf_op jit(solution)/shard_map/cond/branch_1_fun/attend_back/pallas_call | solution.py:70
  373.8 4.5 line_sums.5
  378.3 11.4 %conditional.29 = (bf16[384,896]{1,0:T(8,128)(2,1)}, bf16[24,6144]{1,0:T(8,128)(2,1)}, bf16[384,2304]{1,0:T(8,128)(2,1)S(1)}, bf16[384,2304]{1,0:T(8,128)(2,1)}) conditional(s32[]{:T(128)} %bitcast.11, () %tuple.192, (bf16[384,896]{1,0:T(8,128)(2,1)}, bf16[24,6144]{1,0:T(8,128)(2,1)S(1)}, s32[8]{0:T(128)S(1)}, bf16[1024,768]{1,0:T(8,128)(2,1)S(1)}, ...), branch_computations={%region_26.27_spmd, %region_27.28_spmd} | conditional | flops 3623878656 | bytes 13787280 | solution.py:848
  378.4 8.8 %weigh.1 = (bf16[384,2304]{1,0:T(8,128)(2,1)S(1)}, bf16[384,2304]{1,0:T(8,128)(2,1)}) custom-call(s32[8]{0:T(128)S(1)} %get-tuple-element.620.order_ref, bf16[1024,768]{1,0:T(8,128)(2,1)S(1)} %get-tuple-element.621.inputs_ref, bf16[16,768]{1,0:T(8,128)(2,1)S(1)} %get-tuple-element.622.gain_ref, bf16[1024,768]{1,0:T(8,128)(2,1)} %get-tuple-element.623.dq_ref, ...), custom_call_target="tpu_custom_call" | custom-call | flops 3623878656 | bytes 9855008 | tf_op jit(solution)/shard_map/cond/branch_1_fun/weigh/pallas_call | solution.py:70
  387.2 2.5 collective-permute-done.52
  390.7 11.8 %conditional.30 = (bf16[384,2304]{1,0:T(8,128)(2,1)}, bf16[48,896]{1,0:T(8,128)(2,1)}, bf16[48,896]{1,0:T(8,128)(2,1)}, bf16[24,6144]{1,0:T(8,128)(2,1)}, f32[1024,768]{1,0:T(8,128)S(1)}) conditional(s32[]{:T(128)} %bitcast.11, () %tuple.191, (bf16[384,2304]{1,0:T(8,128)(2,1)}, bf16[48,896]{1,0:T(8,128)(2,1)S(1)}, bf16[48,896]{1,0:T(8,128)(2,1)S(1)}, ...), branch_computations={%region_28.29_spmd, %region_29.30_spmd} | conditional | flops 3623878656 | bytes 26468552 | solution.py:848
  393.6 8.8 %finish.1 = f32[1024,768]{1,0:T(8,128)S(1)} custom-call(bf16[1024,768]{1,0:T(8,128)(2,1)} %get-tuple-element.632.inputs_ref, bf16[16,768]{1,0:T(8,128)(2,1)S(1)} %get-tuple-element.633.gain_ref, bf16[1024,768]{1,0:T(8,128)(2,1)} %get-tuple-element.634.dq_ref, bf16[1024,768]{1,0:T(8,128)(2,1)} %get-tuple-element.635.dk_ref, ...), custom_call_target="tpu_custom_call" | custom-call | flops 3623878656 | bytes 17522688 | tf_op jit(solution)/shard_map/cond/branch_1_fun/finish/pallas_call | solution.py:70
  402.5 2.4 middle_sums.6
  404.9 1.9 end_sums.7
  406.8 16.0 %conditional.31 = (bf16[48,2304]{1,0:T(8,128)(2,1)}, bf16[48,2304]{1,0:T(8,128)(2,1)}, bf16[96,896]{1,0:T(8,128)(2,1)}, bf16[96,896]{1,0:T(8,128)(2,1)}, bf16[24...) conditional(s32[]{:T(128)} %bitcast.11, () %tuple.198, (bf16[48,2304]{1,0:T(8,128)(2,1)}, ...), branch_computations={%region_30.31_spmd, %region_31.32_spmd} | conditional | flops 884736 | bytes 10518812 | solution.py:848
  414.7 3.0 collective-permute-done.62
  419.2 3.6 collective-permute-done.64
  422.8 1.8 line_sums.6
  424.6 2.4 middle_sums.7
  427.0 16.8 %conditional.32 = (bf16[96,2304]{1,0:T(8,128)(2,1)}, bf16[96,2304]{1,0:T(8,128)(2,1)}, bf16[24,896]{1,0:T(8,128)(2,1)}, bf16[24,896]{1,0:T(8,128)(2,1)}, bf16[24...) conditional(s32[]{:T(128)} %bitcast.11, () %tuple.197, ...), branch_computations={%region_32.33_spmd, %region_33.34_spmd} | conditional | flops 1179648 | bytes 19685744 | solution.py:848
  430.7 2.8 collective-permute-start.69
  439.1 1.9 copy.127
  446.4 10.5 %conditional.33 = (f32[24]{0:T(128)S(1)}, f32[24,2]{0,1:T(2,128)S(1)}, f32[24,2304]{1,0:T(8,128)S(1)}, f32[24,2304]{1,0:T(8,128)S(1)}, f32[24,2304]{1,0:T(8,128)S(1)}, /*index=5*/f32[24,768]{1,0:T(8,128)S(1)}) conditional(s32[]{:T(128)} %bitcast.11, () %tuple.201, (bf16[24,896]{1,0:T(8,128)(2,1)}, f32[24,896]{1,0:T(8,128)S(1)}, ...), branch_computations={%region_34.35_spmd, %region_35.36_spmd} | conditional | flops 294912 | bytes 3349224 | solution.py:848
  448.5 2.8 collective-permute-start.59
  454.8 2.0 collective-permute-done.58
  (324 shorter events, 105.2 us)
Async XLA Ops:
  7.2 57.5 %all-gather.10.cloned.1.call-start = ((), (), s32[]{:S(2)}) async-start(), calls=%async_computation.1 | async-start | bytes 1474560 | tf_op jit(solution)/shard_map/all_gather | solution.py:1058
  9.1 11.8 %collective-permute-start.70 = (bf16[24,3200]{1,0:T(8,128)(2,1)S(1)}, bf16[24,3200]{1,0:T(8,128)(2,1)S(1)}, u32[]{:S(2)}, u32[]{:S(2)}) collective-permute-start(bf16[24,3200]{1,0:T(8,128)(2,1)S(1)} %get-tuple-element.1142), channel_id=1, source_target_pairs={{0,3},{1,0},{2,1},{3,2},{4,7},{5,4},{6,5},{7,6},{8,11},{9,8},{10,9... | collective-permute-start | bytes 460808 | tf_op jit(solution)/shard_map/ppermute | solution.py:827
  14.2 13.0 %collective-permute-start.71 = (bf16[24,3200]{1,0:T(8,128)(2,1)S(1)}, bf16[24,3200]{1,0:T(8,128)(2,1)S(1)}, u32[]{:S(2)}, u32[]{:S(2)}) collective-permute-start(bf16[24,3200]{1,0:T(8,128)(2,1)S(1)} %get-tuple-element.1142), channel_id=1, source_target_pairs={{0,2},{1,3},{2,0},{3,1},{4,6},{5,7},{6,4},{7,5},{8,10},{9,11},{10,... | collective-permute-start | bytes 460808 | tf_op jit(solution)/shard_map/ppermute | solution.py:827
  14.2 13.0 %collective-permute-start.72 = (bf16[24,3200]{1,0:T(8,128)(2,1)S(1)}, bf16[24,3200]{1,0:T(8,128)(2,1)S(1)}, u32[]{:S(2)}, u32[]{:S(2)}) collective-permute-start(bf16[24,3200]{1,0:T(8,128)(2,1)S(1)} %get-tuple-element.1142), channel_id=1, source_target_pairs={{0,1},{1,2},{2,3},{3,0},{4,5},{5,6},{6,7},{7,4},{8,9},{9,10},{10,1... | collective-permute-start | bytes 460808 | tf_op jit(solution)/shard_map/ppermute | solution.py:827
  18.9 105.2 %all-gather.8.cloned.1.call-start = ((), (), s32[]{:S(2)}) async-start(), calls=%async_computation | async-start | bytes 1474560 | tf_op jit(solution)/shard_map/all_gather | solution.py:1058
  27.3 157.9 %all-gather.12.cloned.1.call-start = ((), (), s32[]{:S(2)}) async-start(), calls=%async_computation.2 | async-start | bytes 1474560 | tf_op jit(solution)/shard_map/all_gather | solution.py:1058
  32.2 15.3 %collective-permute-start = (bf16[96,3200]{1,0:T(8,128)(2,1)S(1)}, bf16[96,3200]{1,0:T(8,128)(2,1)}, u32[]{:S(2)}, u32[]{:S(2)}) collective-permute-start(bf16[96,3200]{1,0:T(8,128)(2,1)S(1)} %param.1), channel_id=1, source_target_pairs={{0,8},{1,9},{2,10},{3,11},{4,12},{5,13},{6,14},{7,15},{8,0},{9,1},... | collective-permute-start | bytes 1843208 | tf_op jit(solution)/shard_map/cond/branch_1_fun/ppermute | solution.py:827
  33.7 15.0 %collective-permute-start.1 = (bf16[96,3200]{1,0:T(8,128)(2,1)S(1)}, bf16[96,3200]{1,0:T(8,128)(2,1)}, u32[]{:S(2)}, u32[]{:S(2)}) collective-permute-start(bf16[96,3200]{1,0:T(8,128)(2,1)S(1)} %param.1), channel_id=1, source_target_pairs={{0,16},{1,17},{2,18},{3,19},{4,20},{5,21},{6,22},{7,23},{8,24},{9,... | collective-permute-start | bytes 1843208 | tf_op jit(solution)/shard_map/cond/branch_1_fun/ppermute | solution.py:827
  35.2 13.5 %collective-permute-start.2 = (bf16[96,3200]{1,0:T(8,128)(2,1)S(1)}, bf16[96,3200]{1,0:T(8,128)(2,1)}, u32[]{:S(2)}, u32[]{:S(2)}) collective-permute-start(bf16[96,3200]{1,0:T(8,128)(2,1)S(1)} %param.1), channel_id=1, source_target_pairs={{0,4},{1,5},{2,6},{3,7},{4,0},{5,1},{6,2},{7,3},{8,12},{9,13},{10,... | collective-permute-start | bytes 1843208 | tf_op jit(solution)/shard_map/cond/branch_1_fun/ppermute | solution.py:827
  48.8 170.9 %all-gather.14.cloned.1.call-start = ((), (), s32[]{:S(2)}) async-start(), calls=%async_computation.3 | async-start | bytes 1474560 | tf_op jit(solution)/shard_map/all_gather | solution.py:1058
  65.0 37.2 %collective-permute-start.7 = (bf16[96,6144]{1,0:T(8,128)(2,1)}, bf16[96,6144]{1,0:T(8,128)(2,1)}, u32[]{:S(2)}, u32[]{:S(2)}) collective-permute-start(bf16[96,6144]{1,0:T(8,128)(2,1)} %get-tuple-element.418), channel_id=1, source_target_pairs={{0,8},{1,9},{2,10},{3,11},{4,12},{5,13},{6,14},{7,15},{8,0},{9,1},... | collective-permute-start | bytes 3538952 | tf_op jit(solution)/shard_map/cond/branch_1_fun/ppermute | solution.py:827
  65.6 36.6 %collective-permute-start.8 = (bf16[96,6144]{1,0:T(8,128)(2,1)}, bf16[96,6144]{1,0:T(8,128)(2,1)}, u32[]{:S(2)}, u32[]{:S(2)}) collective-permute-start(bf16[96,6144]{1,0:T(8,128)(2,1)} %get-tuple-element.418), channel_id=1, source_target_pairs={{0,16},{1,17},{2,18},{3,19},{4,20},{5,21},{6,22},{7,23},{8,24},{9,... | collective-permute-start | bytes 3538952 | tf_op jit(solution)/shard_map/cond/branch_1_fun/ppermute | solution.py:827
  66.1 36.1 %collective-permute-start.9 = (bf16[96,6144]{1,0:T(8,128)(2,1)}, bf16[96,6144]{1,0:T(8,128)(2,1)}, u32[]{:S(2)}, u32[]{:S(2)}) collective-permute-start(bf16[96,6144]{1,0:T(8,128)(2,1)} %get-tuple-element.418), channel_id=1, source_target_pairs={{0,4},{1,5},{2,6},{3,7},{4,0},{5,1},{6,2},{7,3},{8,12},{9,13},{10,... | collective-permute-start | bytes 3538952 | tf_op jit(solution)/shard_map/cond/branch_1_fun/ppermute | solution.py:827
  66.1 34.1 %collective-permute-start.10 = (bf16[24,6144]{1,0:T(8,128)(2,1)S(1)}, bf16[24,6144]{1,0:T(8,128)(2,1)}, u32[]{:S(2)}, u32[]{:S(2)}) collective-permute-start(bf16[24,6144]{1,0:T(8,128)(2,1)S(1)} %get-tuple-element.419), channel_id=1, source_target_pairs={{0,8},{1,9},{2,10},{3,11},{4,12},{5,13},{6,14},{7,15},{8,0},{9,1},... | collective-permute-start | bytes 884744 | tf_op jit(solution)/shard_map/cond/branch_1_fun/ppermute | solution.py:827
  67.6 33.6 %collective-permute-start.11 = (bf16[24,6144]{1,0:T(8,128)(2,1)S(1)}, bf16[24,6144]{1,0:T(8,128)(2,1)}, u32[]{:S(2)}, u32[]{:S(2)}) collective-permute-start(bf16[24,6144]{1,0:T(8,128)(2,1)S(1)} %get-tuple-element.419), channel_id=1, source_target_pairs={{0,16},{1,17},{2,18},{3,19},{4,20},{5,21},{6,22},{7,23},{8,24},{9,... | collective-permute-start | bytes 884744 | tf_op jit(solution)/shard_map/cond/branch_1_fun/ppermute | solution.py:827
  102.2 134.6 %all-gather.16.cloned.1.call-start = ((), (), s32[]{:S(2)}) async-start(), calls=%async_computation.4 | async-start | bytes 1474560 | tf_op jit(solution)/shard_map/all_gather | solution.py:1058
  102.8 134.0 %all-gather.18.cloned.1.call-start = ((), (), s32[]{:S(2)}) async-start(), calls=%async_computation.5 | async-start | bytes 1474560 | tf_op jit(solution)/shard_map/all_gather | solution.py:1058
  103.4 136.1 %all-gather.20.cloned.1.call-start = ((), (), s32[]{:S(2)}) async-start(), calls=%async_computation.6 | async-start | bytes 1474560 | tf_op jit(solution)/shard_map/all_gather | solution.py:1058
  107.4 16.2 %collective-permute-start.14 = (bf16[96,6144]{1,0:T(8,128)(2,1)}, bf16[96,6144]{1,0:T(8,128)(2,1)}, u32[]{:S(2)}, u32[]{:S(2)}) collective-permute-start(bf16[96,6144]{1,0:T(8,128)(2,1)} %get-tuple-element.440), channel_id=1, source_target_pairs={{0,4},{1,5},{2,6},{3,7},{4,0},{5,1},{6,2},{7,3},{8,12},{9,13},{10,... | collective-permute-start | bytes 3538952 | tf_op jit(solution)/shard_map/cond/branch_1_fun/ppermute | solution.py:827
  107.5 16.2 %collective-permute-start.15 = (bf16[96,6144]{1,0:T(8,128)(2,1)}, bf16[96,6144]{1,0:T(8,128)(2,1)}, u32[]{:S(2)}, u32[]{:S(2)}) collective-permute-start(bf16[96,6144]{1,0:T(8,128)(2,1)} %get-tuple-element.441), channel_id=1, source_target_pairs={{0,4},{1,5},{2,6},{3,7},{4,0},{5,1},{6,2},{7,3},{8,12},{9,13},{10,... | collective-permute-start | bytes 3538952 | tf_op jit(solution)/shard_map/cond/branch_1_fun/ppermute | solution.py:827
  108.0 15.4 %collective-permute-start.12 = (bf16[48,6144]{1,0:T(8,128)(2,1)S(1)}, bf16[48,6144]{1,0:T(8,128)(2,1)}, u32[]{:S(2)}, u32[]{:S(2)}) collective-permute-start(bf16[48,6144]{1,0:T(8,128)(2,1)S(1)} %get-tuple-element.438), channel_id=1, source_target_pairs={{0,16},{1,17},{2,18},{3,19},{4,20},{5,21},{6,22},{7,23},{8,24},{9,... | collective-permute-start | bytes 1769480 | tf_op jit(solution)/shard_map/cond/branch_1_fun/ppermute | solution.py:827
  108.5 15.1 %collective-permute-start.13 = (bf16[48,6144]{1,0:T(8,128)(2,1)S(1)}, bf16[48,6144]{1,0:T(8,128)(2,1)}, u32[]{:S(2)}, u32[]{:S(2)}) collective-permute-start(bf16[48,6144]{1,0:T(8,128)(2,1)S(1)} %get-tuple-element.439), channel_id=1, source_target_pairs={{0,8},{1,9},{2,10},{3,11},{4,12},{5,13},{6,14},{7,15},{8,0},{9,1},... | collective-permute-start | bytes 1769480 | tf_op jit(solution)/shard_map/cond/branch_1_fun/ppermute | solution.py:827
  127.2 32.9 %collective-permute-start.16 = (bf16[96,6144]{1,0:T(8,128)(2,1)}, bf16[96,6144]{1,0:T(8,128)(2,1)}, u32[]{:S(2)}, u32[]{:S(2)}) collective-permute-start(bf16[96,6144]{1,0:T(8,128)(2,1)} %get-tuple-element.456), channel_id=1, source_target_pairs={{0,8},{1,9},{2,10},{3,11},{4,12},{5,13},{6,14},{7,15},{8,0},{9,1},... | collective-permute-start | bytes 3538952 | tf_op jit(solution)/shard_map/cond/branch_1_fun/ppermute | solution.py:827
  127.8 32.3 %collective-permute-start.17 = (bf16[96,6144]{1,0:T(8,128)(2,1)}, bf16[96,6144]{1,0:T(8,128)(2,1)}, u32[]{:S(2)}, u32[]{:S(2)}) collective-permute-start(bf16[96,6144]{1,0:T(8,128)(2,1)} %get-tuple-element.456), channel_id=1, source_target_pairs={{0,16},{1,17},{2,18},{3,19},{4,20},{5,21},{6,22},{7,23},{8,24},{9,... | collective-permute-start | bytes 3538952 | tf_op jit(solution)/shard_map/cond/branch_1_fun/ppermute | solution.py:827
  129.3 30.8 %collective-permute-start.18 = (bf16[96,6144]{1,0:T(8,128)(2,1)}, bf16[96,6144]{1,0:T(8,128)(2,1)}, u32[]{:S(2)}, u32[]{:S(2)}) collective-permute-start(bf16[96,6144]{1,0:T(8,128)(2,1)} %get-tuple-element.456), channel_id=1, source_target_pairs={{0,4},{1,5},{2,6},{3,7},{4,0},{5,1},{6,2},{7,3},{8,12},{9,13},{10,... | collective-permute-start | bytes 3538952 | tf_op jit(solution)/shard_map/cond/branch_1_fun/ppermute | solution.py:827
  129.3 30.8 %collective-permute-start.19 = (bf16[12,6144]{1,0:T(8,128)(2,1)S(1)}, bf16[12,6144]{1,0:T(8,128)(2,1)}, u32[]{:S(2)}, u32[]{:S(2)}) collective-permute-start(bf16[12,6144]{1,0:T(8,128)(2,1)S(1)} %get-tuple-element.457), channel_id=1, source_target_pairs={{0,16},{1,17},{2,18},{3,19},{4,20},{5,21},{6,22},{7,23},{8,24},{9,... | collective-permute-start | bytes 442376 | tf_op jit(solution)/shard_map/cond/branch_1_fun/ppermute | solution.py:827
  129.8 30.2 %collective-permute-start.20 = (bf16[12,6144]{1,0:T(8,128)(2,1)S(1)}, bf16[12,6144]{1,0:T(8,128)(2,1)}, u32[]{:S(2)}, u32[]{:S(2)}) collective-permute-start(bf16[12,6144]{1,0:T(8,128)(2,1)S(1)} %get-tuple-element.458), channel_id=1, source_target_pairs={{0,8},{1,9},{2,10},{3,11},{4,12},{5,13},{6,14},{7,15},{8,0},{9,1},... | collective-permute-start | bytes 442376 | tf_op jit(solution)/shard_map/cond/branch_1_fun/ppermute | solution.py:827
  161.8 20.9 %collective-permute-start.23 = (bf16[96,6144]{1,0:T(8,128)(2,1)}, bf16[96,6144]{1,0:T(8,128)(2,1)}, u32[]{:S(2)}, u32[]{:S(2)}) collective-permute-start(bf16[96,6144]{1,0:T(8,128)(2,1)} %get-tuple-element.483), channel_id=1, source_target_pairs={{0,4},{1,5},{2,6},{3,7},{4,0},{5,1},{6,2},{7,3},{8,12},{9,13},{10,... | collective-permute-start | bytes 3538952 | tf_op jit(solution)/shard_map/cond/branch_1_fun/ppermute | solution.py:827
  161.8 20.9 %collective-permute-start.24 = (bf16[96,6144]{1,0:T(8,128)(2,1)}, bf16[96,6144]{1,0:T(8,128)(2,1)}, u32[]{:S(2)}, u32[]{:S(2)}) collective-permute-start(bf16[96,6144]{1,0:T(8,128)(2,1)} %get-tuple-element.484), channel_id=1, source_target_pairs={{0,4},{1,5},{2,6},{3,7},{4,0},{5,1},{6,2},{7,3},{8,12},{9,13},{10,... | collective-permute-start | bytes 3538952 | tf_op jit(solution)/shard_map/cond/branch_1_fun/ppermute | solution.py:827
  162.3 19.6 %collective-permute-start.21 = (bf16[48,6144]{1,0:T(8,128)(2,1)S(1)}, bf16[48,6144]{1,0:T(8,128)(2,1)}, u32[]{:S(2)}, u32[]{:S(2)}) collective-permute-start(bf16[48,6144]{1,0:T(8,128)(2,1)S(1)} %get-tuple-element.481), channel_id=1, source_target_pairs={{0,16},{1,17},{2,18},{3,19},{4,20},{5,21},{6,22},{7,23},{8,24},{9,... | collective-permute-start | bytes 1769480 | tf_op jit(solution)/shard_map/cond/branch_1_fun/ppermute | solution.py:827
  167.7 15.1 %collective-permute-start.22 = (bf16[48,6144]{1,0:T(8,128)(2,1)S(1)}, bf16[48,6144]{1,0:T(8,128)(2,1)}, u32[]{:S(2)}, u32[]{:S(2)}) collective-permute-start(bf16[48,6144]{1,0:T(8,128)(2,1)S(1)} %get-tuple-element.482), channel_id=1, source_target_pairs={{0,8},{1,9},{2,10},{3,11},{4,12},{5,13},{6,14},{7,15},{8,0},{9,1},... | collective-permute-start | bytes 1769480 | tf_op jit(solution)/shard_map/cond/branch_1_fun/ppermute | solution.py:827
  188.0 29.3 %collective-permute-start.28 = (bf16[384,3072]{1,0:T(8,128)(2,1)}, bf16[384,3072]{1,0:T(8,128)(2,1)}, u32[]{:S(2)}, u32[]{:S(2)}) collective-permute-start(bf16[384,3072]{1,0:T(8,128)(2,1)} %get-tuple-element.499), channel_id=1, source_target_pairs={{0,4},{1,5},{2,6},{3,7},{4,0},{5,1},{6,2},{7,3},{8,12},{9,13},{10,... | collective-permute-start | bytes 7077896 | tf_op jit(solution)/shard_map/cond/branch_1_fun/ppermute | solution.py:827
  188.2 29.1 %collective-permute-start.29 = (bf16[384,3072]{1,0:T(8,128)(2,1)}, bf16[384,3072]{1,0:T(8,128)(2,1)}, u32[]{:S(2)}, u32[]{:S(2)}) collective-permute-start(bf16[384,3072]{1,0:T(8,128)(2,1)} %get-tuple-element.500), channel_id=1, source_target_pairs={{0,4},{1,5},{2,6},{3,7},{4,0},{5,1},{6,2},{7,3},{8,12},{9,13},{10,... | collective-permute-start | bytes 7077896 | tf_op jit(solution)/shard_map/cond/branch_1_fun/ppermute | solution.py:827
  188.6 28.3 %collective-permute-start.25 = (bf16[96,6144]{1,0:T(8,128)(2,1)}, bf16[96,6144]{1,0:T(8,128)(2,1)}, u32[]{:S(2)}, u32[]{:S(2)}) collective-permute-start(bf16[96,6144]{1,0:T(8,128)(2,1)} %get-tuple-element.498), channel_id=1, source_target_pairs={{0,8},{1,9},{2,10},{3,11},{4,12},{5,13},{6,14},{7,15},{8,0},{9,1},... | collective-permute-start | bytes 3538952 | tf_op jit(solution)/shard_map/cond/branch_1_fun/ppermute | solution.py:827
  189.3 28.0 %collective-permute-start.26 = (bf16[96,6144]{1,0:T(8,128)(2,1)}, bf16[96,6144]{1,0:T(8,128)(2,1)}, u32[]{:S(2)}, u32[]{:S(2)}) collective-permute-start(bf16[96,6144]{1,0:T(8,128)(2,1)} %get-tuple-element.498), channel_id=1, source_target_pairs={{0,16},{1,17},{2,18},{3,19},{4,20},{5,21},{6,22},{7,23},{8,24},{9,... | collective-permute-start | bytes 3538952 | tf_op jit(solution)/shard_map/cond/branch_1_fun/ppermute | solution.py:827
  189.4 27.9 %collective-permute-start.27 = (bf16[96,6144]{1,0:T(8,128)(2,1)}, bf16[96,6144]{1,0:T(8,128)(2,1)}, u32[]{:S(2)}, u32[]{:S(2)}) collective-permute-start(bf16[96,6144]{1,0:T(8,128)(2,1)} %get-tuple-element.498), channel_id=1, source_target_pairs={{0,4},{1,5},{2,6},{3,7},{4,0},{5,1},{6,2},{7,3},{8,12},{9,13},{10,... | collective-permute-start | bytes 3538952 | tf_op jit(solution)/shard_map/cond/branch_1_fun/ppermute | solution.py:827
  219.6 16.6 %collective-permute-start.32 = (bf16[96,6144]{1,0:T(8,128)(2,1)}, bf16[96,6144]{1,0:T(8,128)(2,1)}, u32[]{:S(2)}, u32[]{:S(2)}) collective-permute-start(bf16[96,6144]{1,0:T(8,128)(2,1)} %get-tuple-element.525), channel_id=1, source_target_pairs={{0,4},{1,5},{2,6},{3,7},{4,0},{5,1},{6,2},{7,3},{8,12},{9,13},{10,... | collective-permute-start | bytes 3538952 | tf_op jit(solution)/shard_map/cond/branch_1_fun/ppermute | solution.py:827
  219.6 16.6 %collective-permute-start.33 = (bf16[96,6144]{1,0:T(8,128)(2,1)}, bf16[96,6144]{1,0:T(8,128)(2,1)}, u32[]{:S(2)}, u32[]{:S(2)}) collective-permute-start(bf16[96,6144]{1,0:T(8,128)(2,1)} %get-tuple-element.526), channel_id=1, source_target_pairs={{0,4},{1,5},{2,6},{3,7},{4,0},{5,1},{6,2},{7,3},{8,12},{9,13},{10,... | collective-permute-start | bytes 3538952 | tf_op jit(solution)/shard_map/cond/branch_1_fun/ppermute | solution.py:827
  220.1 16.1 %collective-permute-start.34 = (bf16[96,6144]{1,0:T(8,128)(2,1)}, bf16[96,6144]{1,0:T(8,128)(2,1)}, u32[]{:S(2)}, u32[]{:S(2)}) collective-permute-start(bf16[96,6144]{1,0:T(8,128)(2,1)} %get-tuple-element.527), channel_id=1, source_target_pairs={{0,4},{1,5},{2,6},{3,7},{4,0},{5,1},{6,2},{7,3},{8,12},{9,13},{10,... | collective-permute-start | bytes 3538952 | tf_op jit(solution)/shard_map/cond/branch_1_fun/ppermute | solution.py:827
  220.2 16.0 %collective-permute-start.30 = (bf16[48,6144]{1,0:T(8,128)(2,1)}, bf16[48,6144]{1,0:T(8,128)(2,1)}, u32[]{:S(2)}, u32[]{:S(2)}) collective-permute-start(bf16[48,6144]{1,0:T(8,128)(2,1)} %get-tuple-element.523), channel_id=1, source_target_pairs={{0,16},{1,17},{2,18},{3,19},{4,20},{5,21},{6,22},{7,23},{8,24},{9,... | collective-permute-start | bytes 1769480 | tf_op jit(solution)/shard_map/cond/branch_1_fun/ppermute | solution.py:827
  220.5 15.8 %collective-permute-start.31 = (bf16[48,6144]{1,0:T(8,128)(2,1)}, bf16[48,6144]{1,0:T(8,128)(2,1)}, u32[]{:S(2)}, u32[]{:S(2)}) collective-permute-start(bf16[48,6144]{1,0:T(8,128)(2,1)} %get-tuple-element.524), channel_id=1, source_target_pairs={{0,8},{1,9},{2,10},{3,11},{4,12},{5,13},{6,14},{7,15},{8,0},{9,1},... | collective-permute-start | bytes 1769480 | tf_op jit(solution)/shard_map/cond/branch_1_fun/ppermute | solution.py:827
  239.5 24.1 %collective-permute-start.38 = (bf16[384,3072]{1,0:T(8,128)(2,1)}, bf16[384,3072]{1,0:T(8,128)(2,1)}, u32[]{:S(2)}, u32[]{:S(2)}) collective-permute-start(bf16[384,3072]{1,0:T(8,128)(2,1)} %get-tuple-element.537), channel_id=1, source_target_pairs={{0,4},{1,5},{2,6},{3,7},{4,0},{5,1},{6,2},{7,3},{8,12},{9,13},{10,... | collective-permute-start | bytes 7077896 | tf_op jit(solution)/shard_map/cond/branch_1_fun/ppermute | solution.py:827
  239.6 24.0 %collective-permute-start.39 = (bf16[384,3072]{1,0:T(8,128)(2,1)}, bf16[384,3072]{1,0:T(8,128)(2,1)}, u32[]{:S(2)}, u32[]{:S(2)}) collective-permute-start(bf16[384,3072]{1,0:T(8,128)(2,1)} %get-tuple-element.538), channel_id=1, source_target_pairs={{0,4},{1,5},{2,6},{3,7},{4,0},{5,1},{6,2},{7,3},{8,12},{9,13},{10,... | collective-permute-start | bytes 7077896 | tf_op jit(solution)/shard_map/cond/branch_1_fun/ppermute | solution.py:827
  240.0 23.6 %collective-permute-start.35 = (bf16[96,6144]{1,0:T(8,128)(2,1)}, bf16[96,6144]{1,0:T(8,128)(2,1)}, u32[]{:S(2)}, u32[]{:S(2)}) collective-permute-start(bf16[96,6144]{1,0:T(8,128)(2,1)} %get-tuple-element.534), channel_id=1, source_target_pairs={{0,4},{1,5},{2,6},{3,7},{4,0},{5,1},{6,2},{7,3},{8,12},{9,13},{10,... | collective-permute-start | bytes 3538952 | tf_op jit(solution)/shard_map/cond/branch_1_fun/ppermute | solution.py:827
  240.2 23.5 %collective-permute-start.36 = (bf16[96,6144]{1,0:T(8,128)(2,1)}, bf16[96,6144]{1,0:T(8,128)(2,1)}, u32[]{:S(2)}, u32[]{:S(2)}) collective-permute-start(bf16[96,6144]{1,0:T(8,128)(2,1)} %get-tuple-element.535), channel_id=1, source_target_pairs={{0,4},{1,5},{2,6},{3,7},{4,0},{5,1},{6,2},{7,3},{8,12},{9,13},{10,... | collective-permute-start | bytes 3538952 | tf_op jit(solution)/shard_map/cond/branch_1_fun/ppermute | solution.py:827
  240.5 23.1 %collective-permute-start.37 = (bf16[96,6144]{1,0:T(8,128)(2,1)}, bf16[96,6144]{1,0:T(8,128)(2,1)}, u32[]{:S(2)}, u32[]{:S(2)}) collective-permute-start(bf16[96,6144]{1,0:T(8,128)(2,1)} %get-tuple-element.536), channel_id=1, source_target_pairs={{0,4},{1,5},{2,6},{3,7},{4,0},{5,1},{6,2},{7,3},{8,12},{9,13},{10,... | collective-permute-start | bytes 3538952 | tf_op jit(solution)/shard_map/cond/branch_1_fun/ppermute | solution.py:827
  267.4 26.9 %collective-permute-start.40 = (bf16[48,6144]{1,0:T(8,128)(2,1)S(1)}, bf16[48,6144]{1,0:T(8,128)(2,1)}, u32[]{:S(2)}, u32[]{:S(2)}) collective-permute-start(bf16[48,6144]{1,0:T(8,128)(2,1)S(1)} %get-tuple-element.556), channel_id=1, source_target_pairs={{0,8},{1,9},{2,10},{3,11},{4,12},{5,13},{6,14},{7,15},{8,0},{9,1},... | collective-permute-start | bytes 1769480 | tf_op jit(solution)/shard_map/cond/branch_1_fun/ppermute | solution.py:827
  268.8 25.5 %collective-permute-start.41 = (bf16[48,6144]{1,0:T(8,128)(2,1)S(1)}, bf16[48,6144]{1,0:T(8,128)(2,1)}, u32[]{:S(2)}, u32[]{:S(2)}) collective-permute-start(bf16[48,6144]{1,0:T(8,128)(2,1)S(1)} %get-tuple-element.557), channel_id=1, source_target_pairs={{0,16},{1,17},{2,18},{3,19},{4,20},{5,21},{6,22},{7,23},{8,24},{9,... | collective-permute-start | bytes 1769480 | tf_op jit(solution)/shard_map/cond/branch_1_fun/ppermute | solution.py:827
  270.5 23.8 %collective-permute-start.42 = (bf16[48,6144]{1,0:T(8,128)(2,1)}, bf16[48,6144]{1,0:T(8,128)(2,1)}, u32[]{:S(2)}, u32[]{:S(2)}) collective-permute-start(bf16[48,6144]{1,0:T(8,128)(2,1)} %get-tuple-element.558), channel_id=1, source_target_pairs={{0,8},{1,9},{2,10},{3,11},{4,12},{5,13},{6,14},{7,15},{8,0},{9,1},... | collective-permute-start | bytes 1769480 | tf_op jit(solution)/shard_map/cond/branch_1_fun/ppermute | solution.py:827
  270.6 26.2 %collective-permute-start.43 = (bf16[48,6144]{1,0:T(8,128)(2,1)}, bf16[48,6144]{1,0:T(8,128)(2,1)}, u32[]{:S(2)}, u32[]{:S(2)}) collective-permute-start(bf16[48,6144]{1,0:T(8,128)(2,1)} %get-tuple-element.559), channel_id=1, source_target_pairs={{0,16},{1,17},{2,18},{3,19},{4,20},{5,21},{6,22},{7,23},{8,24},{9,... | collective-permute-start | bytes 1769480 | tf_op jit(solution)/shard_map/cond/branch_1_fun/ppermute | solution.py:827
  301.3 28.0 %collective-permute-start.44 = (bf16[96,6144]{1,0:T(8,128)(2,1)}, bf16[96,6144]{1,0:T(8,128)(2,1)}, u32[]{:S(2)}, u32[]{:S(2)}) collective-permute-start(bf16[96,6144]{1,0:T(8,128)(2,1)} %get-tuple-element.574), channel_id=1, source_target_pairs={{0,8},{1,9},{2,10},{3,11},{4,12},{5,13},{6,14},{7,15},{8,0},{9,1},... | collective-permute-start | bytes 3538952 | tf_op jit(solution)/shard_map/cond/branch_1_fun/ppermute | solution.py:827
  302.1 27.8 %collective-permute-start.45 = (bf16[96,6144]{1,0:T(8,128)(2,1)}, bf16[96,6144]{1,0:T(8,128)(2,1)}, u32[]{:S(2)}, u32[]{:S(2)}) collective-permute-start(bf16[96,6144]{1,0:T(8,128)(2,1)} %get-tuple-element.575), channel_id=1, source_target_pairs={{0,16},{1,17},{2,18},{3,19},{4,20},{5,21},{6,22},{7,23},{8,24},{9,... | collective-permute-start | bytes 3538952 | tf_op jit(solution)/shard_map/cond/branch_1_fun/ppermute | solution.py:827
  334.1 39.5 %collective-permute-start.46 = (bf16[96,6144]{1,0:T(8,128)(2,1)}, bf16[96,6144]{1,0:T(8,128)(2,1)}, u32[]{:S(2)}, u32[]{:S(2)}) collective-permute-start(bf16[96,6144]{1,0:T(8,128)(2,1)} %get-tuple-element.606), channel_id=1, source_target_pairs={{0,8},{1,9},{2,10},{3,11},{4,12},{5,13},{6,14},{7,15},{8,0},{9,1},... | collective-permute-start | bytes 3538952 | tf_op jit(solution)/shard_map/cond/branch_1_fun/ppermute | solution.py:827
  334.9 38.7 %collective-permute-start.47 = (bf16[96,6144]{1,0:T(8,128)(2,1)}, bf16[96,6144]{1,0:T(8,128)(2,1)}, u32[]{:S(2)}, u32[]{:S(2)}) collective-permute-start(bf16[96,6144]{1,0:T(8,128)(2,1)} %get-tuple-element.607), channel_id=1, source_target_pairs={{0,16},{1,17},{2,18},{3,19},{4,20},{5,21},{6,22},{7,23},{8,24},{9,... | collective-permute-start | bytes 3538952 | tf_op jit(solution)/shard_map/cond/branch_1_fun/ppermute | solution.py:827
  336.5 37.0 %collective-permute-start.48 = (bf16[24,6144]{1,0:T(8,128)(2,1)S(1)}, bf16[24,6144]{1,0:T(8,128)(2,1)}, u32[]{:S(2)}, u32[]{:S(2)}) collective-permute-start(bf16[24,6144]{1,0:T(8,128)(2,1)S(1)} %get-tuple-element.608), channel_id=1, source_target_pairs={{0,1},{1,2},{2,3},{3,0},{4,5},{5,6},{6,7},{7,4},{8,9},{9,10},{10,1... | collective-permute-start | bytes 884744 | tf_op jit(solution)/shard_map/cond/branch_1_fun/ppermute | solution.py:827
  337.4 36.2 %collective-permute-start.49 = (bf16[24,6144]{1,0:T(8,128)(2,1)}, bf16[24,6144]{1,0:T(8,128)(2,1)}, u32[]{:S(2)}, u32[]{:S(2)}) collective-permute-start(bf16[24,6144]{1,0:T(8,128)(2,1)} %get-tuple-element.609), channel_id=1, source_target_pairs={{0,2},{1,3},{2,0},{3,1},{4,6},{5,7},{6,4},{7,5},{8,10},{9,11},{10,... | collective-permute-start | bytes 884744 | tf_op jit(solution)/shard_map/cond/branch_1_fun/ppermute | solution.py:827
  339.1 34.5 %collective-permute-start.50 = (bf16[24,6144]{1,0:T(8,128)(2,1)}, bf16[24,6144]{1,0:T(8,128)(2,1)}, u32[]{:S(2)}, u32[]{:S(2)}) collective-permute-start(bf16[24,6144]{1,0:T(8,128)(2,1)} %get-tuple-element.610), channel_id=1, source_target_pairs={{0,3},{1,0},{2,1},{3,2},{4,7},{5,4},{6,5},{7,6},{8,11},{9,8},{10,9... | collective-permute-start | bytes 884744 | tf_op jit(solution)/shard_map/cond/branch_1_fun/ppermute | solution.py:827
  406.8 16.0 %collective-permute-start.64 = (bf16[24,6144]{1,0:T(8,128)(2,1)}, bf16[24,6144]{1,0:T(8,128)(2,1)}, u32[]{:S(2)}, u32[]{:S(2)}) collective-permute-start(bf16[24,6144]{1,0:T(8,128)(2,1)} %get-tuple-element.643), channel_id=1, source_target_pairs={{0,2},{1,3},{2,0},{3,1},{4,6},{5,7},{6,4},{7,5},{8,10},{9,11},{10,... | collective-permute-start | bytes 884744 | tf_op jit(solution)/shard_map/cond/branch_1_fun/ppermute | solution.py:827
  406.9 12.3 %collective-permute-start.60 = (bf16[48,2304]{1,0:T(8,128)(2,1)}, bf16[48,2304]{1,0:T(8,128)(2,1)}, u32[]{:S(2)}, u32[]{:S(2)}) collective-permute-start(bf16[48,2304]{1,0:T(8,128)(2,1)} %get-tuple-element.639), channel_id=1, source_target_pairs={{0,8},{1,9},{2,10},{3,11},{4,12},{5,13},{6,14},{7,15},{8,0},{9,1},... | collective-permute-start | bytes 663560 | tf_op jit(solution)/shard_map/cond/branch_1_fun/ppermute | solution.py:827
  427.0 16.8 %collective-permute-start.65 = (bf16[96,2304]{1,0:T(8,128)(2,1)}, bf16[96,2304]{1,0:T(8,128)(2,1)}, u32[]{:S(2)}, u32[]{:S(2)}) collective-permute-start(bf16[96,2304]{1,0:T(8,128)(2,1)} %get-tuple-element.648), channel_id=1, source_target_pairs={{0,8},{1,9},{2,10},{3,11},{4,12},{5,13},{6,14},{7,15},{8,0},{9,1},... | collective-permute-start | bytes 1327112 | tf_op jit(solution)/shard_map/cond/branch_1_fun/ppermute | solution.py:827
  428.7 15.1 %collective-permute-start.66 = (bf16[96,2304]{1,0:T(8,128)(2,1)}, bf16[96,2304]{1,0:T(8,128)(2,1)}, u32[]{:S(2)}, u32[]{:S(2)}) collective-permute-start(bf16[96,2304]{1,0:T(8,128)(2,1)} %get-tuple-element.649), channel_id=1, source_target_pairs={{0,16},{1,17},{2,18},{3,19},{4,20},{5,21},{6,22},{7,23},{8,24},{9,... | collective-permute-start | bytes 1327112 | tf_op jit(solution)/shard_map/cond/branch_1_fun/ppermute | solution.py:827
  429.7 14.1 %collective-permute-start.67 = (bf16[24,896]{1,0:T(8,128)(2,1)S(1)}, bf16[24,896]{1,0:T(8,128)(2,1)}, u32[]{:S(2)}, u32[]{:S(2)}) collective-permute-start(bf16[24,896]{1,0:T(8,128)(2,1)S(1)} %get-tuple-element.650), channel_id=1, source_target_pairs={{0,1},{1,2},{2,3},{3,0},{4,5},{5,6},{6,7},{7,4},{8,9},{9,10},{10,1... | collective-permute-start | bytes 129032 | tf_op jit(solution)/shard_map/cond/branch_1_fun/ppermute | solution.py:827
  429.7 14.1 %collective-permute-start.68 = (bf16[24,896]{1,0:T(8,128)(2,1)S(1)}, bf16[24,896]{1,0:T(8,128)(2,1)}, u32[]{:S(2)}, u32[]{:S(2)}) collective-permute-start(bf16[24,896]{1,0:T(8,128)(2,1)S(1)} %get-tuple-element.651), channel_id=1, source_target_pairs={{0,2},{1,3},{2,0},{3,1},{4,6},{5,7},{6,4},{7,5},{8,10},{9,11},{10,... | collective-permute-start | bytes 129032 | tf_op jit(solution)/shard_map/cond/branch_1_fun/ppermute | solution.py:827
  430.7 13.1 %collective-permute-start.69 = (bf16[24,896]{1,0:T(8,128)(2,1)}, bf16[24,896]{1,0:T(8,128)(2,1)}, u32[]{:S(2)}, u32[]{:S(2)}) collective-permute-start(bf16[24,896]{1,0:T(8,128)(2,1)} %get-tuple-element.652), channel_id=1, source_target_pairs={{0,3},{1,0},{2,1},{3,2},{4,7},{5,4},{6,5},{7,6},{8,11},{9,8},{10,9... | collective-permute-start | bytes 129032 | tf_op jit(solution)/shard_map/cond/branch_1_fun/ppermute | solution.py:827
  (64 other events, 370.8 us)
Sparse Core Ops, SparseCore 0:
  19.0 30.8 all-gather.9
  52.1 29.5 all-gather.7
  83.3 29.4 all-gather.11
  114.2 29.6 all-gather.13
  145.3 29.5 all-gather.15
  176.3 29.5 all-gather.17
  207.5 29.5 all-gather.19

commit v4 on v3

--- a/solution.py
+++ b/solution.py
@@ -243,7 +243,7 @@
 
 
 def attend_back_kernel(
-    doc_ref, doc_t_ref, q_ref, k_ref, v_ref, grad_ref, log_ref, dq_ref, dk_ref, dv_ref,
+    doc_ref, doc_t_ref, q_ref, k_ref, v_ref, grad_ref, out_ref, log_ref, dq_ref, dk_ref, dv_ref,
     bias_ref, dk_sum, dv_sum,
 ):
     length = q_ref.shape[0]
@@ -259,6 +259,7 @@
             kept = (col >= row) & (doc_ref[start : start + size, :] == doc_t_ref[:, cols])
             bias_ref[:size, cols] = jnp.where(kept, 0.0, -1e30)
 
+    turned_keys = k_ref[...].T
     dk_sum[...] = jnp.zeros_like(dk_sum)
     dv_sum[...] = jnp.zeros_like(dv_sum)
     first = iota((BLOCK, PAIR), 1) < HEAD_DIM
@@ -268,6 +269,7 @@
         query, grad = q_ref[rows, :] * 0.125, grad_ref[rows, :]
         keys, values = k_ref[span, :], v_ref[span, :]
         bias = bias_ref[:size, rows]
+        turned = (grad.astype(f32) * out_ref[rows, :].astype(f32)).T
         parts, dk, dv = [], 0.0, 0.0
         for head, own in enumerate((first, ~first)):
             own_query = jnp.where(own, query, 0).astype(bf16)
@@ -275,19 +277,19 @@
             scores = dot_nt(keys, own_query) + bias
             probs = jnp.exp(scores - log_ref[0, head : head + 1, rows])
             dv = dv + dot_nn(probs.astype(bf16), own_grad)
-            weighted = probs * dot_nt(values, own_grad)
-            mean = jnp.sum(weighted, axis=0, keepdims=True)
-            grad_scores = (weighted - probs * mean).astype(bf16)
+            lanes = slice(head * HEAD_DIM, (head + 1) * HEAD_DIM)
+            mean = jnp.sum(turned[lanes, :], axis=0, keepdims=True)
+            grad_scores = (probs * (dot_nt(values, own_grad) - mean)).astype(bf16)
             dk = dk + dot_nn(grad_scores, own_query)
-            parts.append(dot_tn(grad_scores, keys) * 0.125)
-        dq_ref[rows, :] = jnp.where(first, parts[0], parts[1]).astype(bf16)
+            parts.append(dot_nn(turned_keys[lanes, span], grad_scores))
+        dq_ref[rows, :] = (jnp.concatenate(parts).T * 0.125).astype(bf16)
         dk_sum[span, :] += dk
         dv_sum[span, :] += dv
     dk_ref[...] = dk_sum[...].astype(bf16)
     dv_ref[...] = dv_sum[...].astype(bf16)
 
 
-def attend_back(docs, qkv, grad, logs):
+def attend_back(docs, qkv, grad, attended, logs):
     length, width = qkv.shape[0], qkv.shape[1] // 3
     pairs = width // PAIR
     heads = [pl.BlockSpec((length, PAIR), lambda i, k=k: (0, k * pairs + i)) for k in range(3)]
@@ -296,10 +298,10 @@
         attend_back_kernel,
         "attend_back",
         (pairs,),
-        [docs.reshape(length, 1), docs.reshape(1, length), qkv, qkv, qkv, grad, logs],
+        [docs.reshape(length, 1), docs.reshape(1, length), qkv, qkv, qkv, grad, attended, logs],
         [whole((length, 1)), whole((1, length))]
         + heads
-        + [one, pl.BlockSpec((1, 8, length), lambda i: (i, 0, 0))],
+        + [one, one, pl.BlockSpec((1, 8, length), lambda i: (i, 0, 0))],
         [shape_of((length, width), bf16)] * 3,
         [one] * 3,
         [
@@ -544,9 +546,10 @@
     low = (grad_logits - high.astype(f32)).astype(bf16)
     gains = gains_ref[...]
     router = pltpu.roll(gains, LANES - 2, 0).astype(bf16)
-    grad_normed = grad_normed + dot_nn(high, router) + dot_nn(low, router)
-    normed = normed_ref[...]
-    router_sum[...] += dot_tn(normed, high) + dot_tn(normed, low)
+    both = jnp.concatenate([high, low], axis=1)
+    grad_normed = grad_normed + dot_nn(both, jnp.concatenate([router, router]))
+    made = dot_tn(normed_ref[...], both)
+    router_sum[...] += made[:, :LANES] + made[:, LANES:]
     xhat, inverse = normalized(hidden)
     gain_sum[...] += jnp.sum(grad_normed * xhat, axis=0, keepdims=True)
     grad_hidden = cot + norm_back(xhat, inverse, gains[1:2, :], grad_normed)
@@ -737,6 +740,30 @@
     return [pl.BlockSpec((a.shape[0] // 4, a.shape[1]), lambda *_: (number, 0)) for a in arrays]
 
 
+def line_up_kernel(place_ref, *refs):
+    *parts, full_ref, staged = refs
+    rows = parts[0].shape[0]
+    for by, part in enumerate(parts):
+        start = pl.multiple_of(lax.rem(place_ref[0] + by, len(parts)) * rows, 8)
+        staged[pl.ds(start, rows), :] = part[...].astype(f32)
+    full_ref[...] = staged[...].astype(bf16)
+
+
+def line_up(place, parts):
+    rows, columns = parts[0].shape
+    full = (len(parts) * rows, columns)
+    return call(
+        line_up_kernel,
+        "line_up",
+        (1,),
+        [place] + parts,
+        [SMEM] + [whole(p.shape) for p in parts],
+        [shape_of(full, bf16)],
+        [whole(full)],
+        [pltpu.VMEM(full, f32)],
+    )[0]
+
+
 def halves_kernel(low, high, top, bottom):
     top[...] = low[...]
     bottom[...] = high[...]
@@ -860,6 +887,9 @@
 
     def take_along(self, got):
         links, rows = self.links, self.part.shape[0]
+        if rows % 8 == 0:
+            self.full = line_up(links.place.astype(i32).reshape(1), [self.part] + got)
+            return
         full = jnp.zeros((links.narrow * rows, self.part.shape[1]), self.part.dtype)
         for by, part in enumerate([self.part] + got):
             start = (links.place + by) % links.narrow * rows
@@ -1059,12 +1089,12 @@
 
     w0, w1, w2, w3 = weights
     w0.part = after(w0.part, dense.part)
-    w0.full = line(w0.part)
     dense.take_along(dense.send_along())
-    w1.full = line(w1.part, dense.full)
+    w0.full = line(w0.part, dense.full)
     dense.take_first(together(always, dense.send_first))
-    w2.full = line(w2.part, dense.low)
+    w1.full = line(w1.part, dense.low)
     dense.take_second(together(always, dense.send_second))
+    w2.full = line(w2.part, dense.ends)
     dense.take_third(dense.send_third())
 
     def step():
@@ -1137,7 +1167,7 @@
     got, more, (dq, dk, dv) = together(
         always,
         lambda: (
-            term1.send_second(), term0.send_along(), attend_back(docs, qkv, grad_heads, logs)
+            term1.send_second(), term0.send_along(), attend_back(docs, qkv, grad_heads, attended, logs)
         ),
     )
     term1.take_second(got)

time: 474 us -> 471 us (level)
  Pallas kernels: 262 us -> 254 us
  waiting for transfers between devices: 79.2 us -> 85.1 us
    pallas_call x32 -> x33, Pallas kernels: 262 us -> 254 us  [call(): pl.pallas_call(kernel, name=name, grid=grid, in_specs=in_specs, out_specs...]
    ppermute x81, waiting for transfers between devices: 78 us -> 83.4 us  [send(): return lax.ppermute(part, AXES, pairs)]
  transfers between devices with their start and end apart: 88 -> 88, of which waited for: 27 -> 28; matrix products, arithmetic and copies ran while one was open for 7% -> 7% of each run, Pallas kernels for 50% -> 49%
where the time goes in v4:
time: 471 us; the launch traced here: 463 us
  Pallas kernels  254 us (54%)
  waiting for transfers between devices  85.1 us (18%)
  starting transfers between devices  66.4 us (14%)
  local copies, waits for them, and re-layouts  29.8 us (6%)
  between operations  15.6 us (3%)
  other arithmetic  9.96 us (2%)
    pallas_call x33, Pallas kernels, call(): pl.pallas_call(kernel, name=name, grid=grid, in_specs=in_specs, out_specs...  254 us
    ppermute x81, waiting for transfers between devices, send(): return lax.ppermute(part, AXES, pairs)  83.4 us
    ppermute x81, starting transfers between devices, send(): return lax.ppermute(part, AXES, pairs)  66.1 us
  transfers between devices with their start and end apart: 88, of which 28 were waited for; matrix products, arithmetic and copies ran while one was open for 7% of the time, Pallas kernels for 49%

profile of v4, /device:TPU:0, one launch (start us, length us, event | category | flops | bytes accessed | tf_op | source)
XLA Modules:
  0.0 462.9 jit_solution(14604139484567906916)
XLA Ops:
  9.0 5.1 %collective-permute-start.70 = (bf16[24,3200]{1,0:T(8,128)(2,1)S(1)}, bf16[24,3200]{1,0:T(8,128)(2,1)S(1)}, u32[]{:S(2)}, u32[]{:S(2)}) collective-permute-start(bf16[24,3200]{1,0:T(8,128)(2,1)S(1)} %fusion.1.refs_0_), channel_id=1, source_target_pairs={{0,3},{1,0},{2,1},{3,2},{4,7},{5,4},{6,5},{7,6},{8,11},{9,8},{10,9... | collective-permute-start | bytes 460808 | tf_op jit(solution)/shard_map/ppermute | solution.py:854
  15.1 1.7 fusion.5
  20.0 7.1 %collective-permute-done.71.refs_2_ = bf16[24,3200]{1,0:T(8,128)(2,1)S(1)} collective-permute-done((bf16[24,3200]{1,0:T(8,128)(2,1)S(1)}, bf16[24,3200]{1,0:T(8,128)(2,1)S(1)}, u32[]{:S(2)}, u32[]{:S(2)}) %collective-permute-start.71) | collective-permute-done | bytes 153632 | tf_op jit(solution)/shard_map/ppermute | solution.py:854
  30.4 16.5 %conditional.17 = (bf16[96,3200]{1,0:T(8,128)(2,1)}, bf16[96,3200]{1,0:T(8,128)(2,1)}, bf16[96,3200]{1,0:T(8,128)(2,1)}) conditional(s32[]{:T(128)} %bitcast.11, () %tuple.165, bf16[96,3200]{1,0:T(8,128)(2,1)S(1)} %line_up.1), branch_computations={%region_2.3_spmd, %region_3.4_spmd} | conditional | bytes 7372944 | solution.py:875
  33.5 12.3 %collective-permute-done = bf16[96,3200]{1,0:T(8,128)(2,1)} collective-permute-done((bf16[96,3200]{1,0:T(8,128)(2,1)S(1)}, bf16[96,3200]{1,0:T(8,128)(2,1)}, u32[]{:S(2)}, u32[]{:S(2)}) %collective-permute-start) | collective-permute-done | bytes 614432 | tf_op jit(solution)/shard_map/cond/branch_1_fun/ppermute | solution.py:854
  51.8 11.2 %conditional.18 = (bf16[48,3200]{1,0:T(8,128)(2,1)}, bf16[48,3200]{1,0:T(8,128)(2,1)}, bf16[96,3200]{1,0:T(8,128)(2,1)}, bf16[96,3200]{1,0:T(8,128)(2,1)}) conditional(s32[]{:T(128)} %bitcast.11, () %tuple.170, (bf16[48,3200]{1,0:T(8,128)(2,1)S(1)}, bf16[48,3200]{1,0:T(8,128)(2,1)S(1)}, bf16[96,3200]{1,0:T(8,128)(2,1)}, ...), branch_computations={%region_4.5_spmd, %region_5.6_spmd} | conditional | bytes 7372992 | solution.py:875
  54.5 7.3 %collective-permute-done.3 = bf16[48,3200]{1,0:T(8,128)(2,1)} collective-permute-done((bf16[48,3200]{1,0:T(8,128)(2,1)S(1)}, bf16[48,3200]{1,0:T(8,128)(2,1)}, u32[]{:S(2)}, u32[]{:S(2)}) %collective-permute-start.3) | collective-permute-done | bytes 307232 | tf_op jit(solution)/shard_map/cond/branch_1_fun/ppermute | solution.py:854
  66.8 37.5 %conditional.19 = (bf16[96,6144]{1,0:T(8,128)(2,1)}, bf16[96,6144]{1,0:T(8,128)(2,1)}, bf16[96,6144]{1,0:T(8,128)(2,1)}, bf16[24,6144]{1,0:T(8,128)(2,1)}, bf16[...) conditional(s32[]{:T(128)} %bitcast.11, () %tuple.167, ...), branch_computations={%region_6.7_spmd, %region_7.8_spmd} | conditional | flops 6039797760 | bytes 49193296 | solution.py:875
  71.2 9.4 %project.1 = (bf16[1024,2304]{1,0:T(8,128)(2,1)}, bf16[768,3200]{1,0:T(8,128)(2,1)}, bf16[16,768]{1,0:T(8,128)(2,1)}) custom-call(s32[10]{0:T(128)S(1)} %get-tuple-element.422.rows_ref, bf16[1024,768]{1,0:T(8,128)(2,1)S(1)} %get-tuple-element.423.inputs_ref, bf16[96,3200]{1,0:T(8,128)(2,1)S(1)} %get-tuple-element.424.rest_0_, ...), custom_call_target="tpu_custom_call" | custom-call | flops 3623878656 | bytes 16146472 | tf_op jit(solution)/shard_map/cond/branch_1_fun/project/pallas_call | solution.py:70
  80.8 21.5 %attend.1 = (bf16[1024,768]{1,0:T(8,128)(2,1)S(1)}, f32[6,8,1024]{2,1,0:T(8,128)}) custom-call(s32[1024,1]{1,0:T(8,128)S(1)} %copy.111.doc_ref, s32[1,1024]{1,0:T(1,128)S(1)} %get-tuple-element.437.doc_t_ref, bf16[1024,2304]{1,0:T(8,128)(2,1)} %get-tuple-element.1178.q_ref.k_ref.v_ref, bf16[1024,2304]{1,0:T(8,128)(2,1)} %get-tuple-element.1178.q_ref.k_ref.v_ref, ...), custom_call_target="tpu_custom_call" | custom-call | flops 2415919104 | bytes 15933440 | tf_op jit(solution)/shard_map/cond/branch_1_fun/attend/pallas_call | solution.py:70
  109.5 16.1 %conditional.20 = (bf16[48,6144]{1,0:T(8,128)(2,1)}, bf16[48,6144]{1,0:T(8,128)(2,1)}, bf16[96,6144]{1,0:T(8,128)(2,1)}, bf16[96,6144]{1,0:T(8,128)(2,1)}, f32[1...) conditional(s32[]{:T(128)} %bitcast.11, () %tuple.173, ...), branch_computations={%region_8.9_spmd, %region_9.10_spmd} | conditional | flops 2113929216 | bytes 40141152 | solution.py:875
  111.1 7.4 %middle.1 = (f32[1024,768]{1,0:T(8,128)}, bf16[1024,768]{1,0:T(8,128)(2,1)}, f32[1024,128]{1,0:T(8,128)}) custom-call(bf16[1024,768]{1,0:T(8,128)(2,1)} %get-tuple-element.444.inputs_ref, bf16[1024,768]{1,0:T(8,128)(2,1)S(1)} %get-tuple-element.445.attended_ref, s32[1024,128]{1,0:T(8,128)S(1)} %get-tuple-element.446.place_ref, ...), custom_call_target="tpu_custom_call" | custom-call | flops 1207959552 | bytes 18743296 | tf_op jit(solution)/shard_map/cond/branch_1_fun/middle/pallas_call | solution.py:70
  118.5 4.9 %dispatch_0.1 = (bf16[768,768]{1,0:T(8,128)(2,1)}, bf16[768,768]{1,0:T(8,128)(2,1)}, bf16[768,768]{1,0:T(8,128)(2,1)}) custom-call(s32[8]{0:T(128)S(1)} %get-tuple-element.451.order_ref, s32[20]{0:T(128)S(1)} %get-tuple-element.452.counts_ref, s32[8,1024]{1,0:T(8,128)S(1)} %get-tuple-element.453.place_t_ref, f32[1024,128]{1,0:T(8,128)} %get-tuple-element.1201.gate_ref, ...), custom_call_target="tpu_custom_call" | custom-call | flops 905969664 | bytes 7241840 | tf_op jit(solution)/shard_map/cond/branch_1_fun/dispatch_0/pallas_call | solution.py:70
  123.4 2.0 collective-permute-done.12
  126.2 1.7 collective-permute-done.75
  128.7 33.4 %conditional.21 = (bf16[96,6144]{1,0:T(8,128)(2,1)}, bf16[96,6144]{1,0:T(8,128)(2,1)}, bf16[96,6144]{1,0:T(8,128)(2,1)}, bf16[12,6144]{1,0:T(8,128)(2,1)}, bf16[...) conditional(s32[]{:T(128)} %bitcast.11, () %tuple.164, ...), branch_computations={%region_10.11_spmd, %region_11.12_spmd} | conditional | flops 16986931200 | bytes 54264304 | solution.py:875
  133.3 16.1 %expert_0.1 = (bf16[768,768]{1,0:T(8,128)(2,1)}, bf16[768,768]{1,0:T(8,128)(2,1)}, bf16[384,3072]{1,0:T(8,128)(2,1)S(1)}, bf16[384,3072]{1,0:T(8,128)(2,1)}, bf1...) custom-call(s32[10]{0:T(128)S(1)} %get-tuple-element.461.rows_ref, s32[8]{0:T(128)S(1)} %get-tuple-element.462.order_ref, ...), custom_call_target="tpu_custom_call" | custom-call | flops 16986931200 | bytes 34209944 | tf_op jit(solution)/shard_map/cond/branch_1_fun/expert_0/pallas_call | solution.py:70
  149.4 12.6 %collective-permute-done.19 = bf16[12,6144]{1,0:T(8,128)(2,1)} collective-permute-done((bf16[12,6144]{1,0:T(8,128)(2,1)S(1)}, bf16[12,6144]{1,0:T(8,128)(2,1)}, u32[]{:S(2)}, u32[]{:S(2)}) %collective-permute-start.19) | collective-permute-done | bytes 147488 | tf_op jit(solution)/shard_map/cond/branch_1_fun/ppermute | solution.py:854
  163.9 17.1 %conditional.22 = (bf16[48,6144]{1,0:T(8,128)(2,1)}, bf16[48,6144]{1,0:T(8,128)(2,1)}, bf16[96,6144]{1,0:T(8,128)(2,1)}, bf16[96,6144]{1,0:T(8,128)(2,1)}, bf16[...) conditional(s32[]{:T(128)} %bitcast.11, () %tuple.179, ...), branch_computations={%region_12.13_spmd, %region_13.14_spmd} | conditional | flops 2717908992 | bytes 33784448 | solution.py:875
  167.4 4.6 dispatch_1.1
  172.0 4.5 dispatch_2.1
  176.5 4.5 dispatch_3.1
  181.0 1.8 pad_maximum_fusion.5
  183.3 1.8 collective-permute-done.77
  186.0 35.4 %conditional.23 = (bf16[96,6144]{1,0:T(8,128)(2,1)}, bf16[96,6144]{1,0:T(8,128)(2,1)}, bf16[96,6144]{1,0:T(8,128)(2,1)}, bf16[384,3072]{1,0:T(8,128)(2,1)}, bf16...) conditional(s32[]{:T(128)} %bitcast.11, () %tuple.176, ...), branch_computations={%region_14.15_spmd, %region_15.16_spmd} | conditional | flops 16986931200 | bytes 67240376 | solution.py:875
  188.8 32.6 %expert_1.1 = (bf16[768,768]{1,0:T(8,128)(2,1)}, bf16[768,768]{1,0:T(8,128)(2,1)}, bf16[384,3072]{1,0:T(8,128)(2,1)}, bf16[384,3072]{1,0:T(8,128)(2,1)}, bf16[38...) custom-call(s32[10]{0:T(128)S(1)} %get-tuple-element.503.rows_ref, s32[8]{0:T(128)S(1)} %get-tuple-element.504.order_ref, ...), custom_call_target="tpu_custom_call" | custom-call | flops 16986931200 | bytes 34209944 | tf_op jit(solution)/shard_map/cond/branch_1_fun/expert_1/pallas_call | solution.py:70
  221.4 2.3 halves.7
  223.8 17.8 %conditional.24 = (bf16[48,6144]{1,0:T(8,128)(2,1)}, bf16[48,6144]{1,0:T(8,128)(2,1)}, bf16[96,6144]{1,0:T(8,128)(2,1)}, bf16[96,6144]{1,0:T(8,128)(2,1)}, bf16[...) conditional(s32[]{:T(128)} %bitcast.11, () %tuple.183, ...), branch_computations={%region_16.17_spmd, %region_17.18_spmd} | conditional | bytes 29491456 | solution.py:875
  226.7 1.7 end_sums.4
  228.4 12.0 %collective-permute-done.30 = bf16[48,6144]{1,0:T(8,128)(2,1)} collective-permute-done((bf16[48,6144]{1,0:T(8,128)(2,1)}, bf16[48,6144]{1,0:T(8,128)(2,1)}, u32[]{:S(2)}, u32[]{:S(2)}) %collective-permute-start.30) | collective-permute-done | bytes 589856 | tf_op jit(solution)/shard_map/cond/branch_1_fun/ppermute | solution.py:854
  242.2 1.8 collective-permute-done.79
  245.4 24.0 %conditional.25 = (bf16[96,6144]{1,0:T(8,128)(2,1)}, bf16[96,6144]{1,0:T(8,128)(2,1)}, bf16[96,6144]{1,0:T(8,128)(2,1)}, bf16[384,3072]{1,0:T(8,128)(2,1)}, bf16...) conditional(s32[]{:T(128)} %bitcast.11, () %tuple.186, ...), branch_computations={%region_18.19_spmd, %region_19.20_spmd} | conditional | flops 11324620800 | bytes 56623512 | solution.py:875
  246.4 23.0 %expert_2.1 = (bf16[768,768]{1,0:T(8,128)(2,1)}, bf16[768,768]{1,0:T(8,128)(2,1)}) custom-call(s32[10]{0:T(128)S(1)} %get-tuple-element.541.rows_ref, s32[8]{0:T(128)S(1)} %get-tuple-element.542.order_ref, s32[20]{0:T(128)S(1)} %get-tuple-element.543.counts_ref, bf16[768,768]{1,0:T(8,128)(2,1)} %get-tuple-element.544.rest_0_, ...), custom_call_target="tpu_custom_call" | custom-call | flops 11324620800 | bytes 23593112 | tf_op jit(solution)/shard_map/cond/branch_1_fun/expert_2/pallas_call | solution.py:70
  269.5 3.0 end_sums.5
  272.8 30.1 %conditional.26 = (bf16[48,6144]{1,0:T(8,128)(2,1)}, bf16[48,6144]{1,0:T(8,128)(2,1)}, bf16[48,6144]{1,0:T(8,128)(2,1)}, bf16[48,6144]{1,0:T(8,128)(2,1)}, bf16[...) conditional(s32[]{:T(128)} %bitcast.11, () %tuple.182, (bf16[48,6144]{1,0:T(8,128)(2,1)S(1)}, ...), branch_computations={%region_20.21_spmd, %region_21.22_spmd} | conditional | flops 11324620800 | bytes 33030496 | solution.py:875
  277.3 22.8 %expert_3.1 = (bf16[768,768]{1,0:T(8,128)(2,1)}, bf16[768,768]{1,0:T(8,128)(2,1)}) custom-call(s32[8]{0:T(128)S(1)} %get-tuple-element.562.rows_ref.order_ref, s32[8]{0:T(128)S(1)} %get-tuple-element.562.rows_ref.order_ref, s32[20]{0:T(128)S(1)} %get-tuple-element.563.counts_ref, bf16[768,768]{1,0:T(8,128)(2,1)} %get-tuple-element.564.rest_0_, ...), custom_call_target="tpu_custom_call" | custom-call | flops 11324620800 | bytes 23593104 | tf_op jit(solution)/shard_map/cond/branch_1_fun/expert_3/pallas_call | solution.py:70
  303.0 4.4 middle_sums.5
  307.3 28.0 %conditional.27 = (bf16[96,6144]{1,0:T(8,128)(2,1)}, bf16[96,6144]{1,0:T(8,128)(2,1)}, bf16[96,6144]{1,0:T(8,128)(2,1)}, bf16[96,6144]{1,0:T(8,128)(2,1)}, bf16[...) conditional(s32[]{:T(128)} %bitcast.11, () %tuple.163, ...), branch_computations={%region_22.23_spmd, %region_23.24_spmd} | conditional | flops 4831838208 | bytes 67698952 | solution.py:875
  309.5 4.6 middle_sums.4
  314.1 20.2 %combine.1 = (bf16[1024,768]{1,0:T(8,128)(2,1)}, f32[1024,768]{1,0:T(8,128)}, bf16[1024,768]{1,0:T(8,128)(2,1)}, bf16[384,896]{1,0:T(8,128)(2,1)S(1)}, bf16[384,896]{1,0:T(8,128)(2,1)}) custom-call(s32[8]{0:T(128)S(1)} %get-tuple-element.586.order_ref, s32[20]{0:T(128)S(1)} %get-tuple-element.587.counts_ref, s32[1024,128]{1,0:T(8,128)} %get-tuple-element.588.place_ref, ...), custom_call_target="tpu_custom_call" | custom-call | flops 4831838208 | bytes 35848304 | tf_op jit(solution)/shard_map/cond/branch_1_fun/combine/pallas_call | solution.py:70
  335.4 4.2 line_sums.4
  339.6 31.7 %conditional.28 = (bf16[96,6144]{1,0:T(8,128)(2,1)}, bf16[96,6144]{1,0:T(8,128)(2,1)}, bf16[24,6144]{1,0:T(8,128)(2,1)}, bf16[24,6144]{1,0:T(8,128)(2,1)}, bf16[...) conditional(s32[]{:T(128)} %bitcast.11, () %tuple.195, ...), branch_computations={%region_24.25_spmd, %region_25.26_spmd} | conditional | flops 6039797760 | bytes 35209480 | solution.py:875
  344.0 2.9 collective-permute-start.50
  347.2 23.9 %attend_back.1 = (bf16[1024,768]{1,0:T(8,128)(2,1)}, bf16[1024,768]{1,0:T(8,128)(2,1)}, bf16[1024,768]{1,0:T(8,128)(2,1)}) custom-call(s32[1024,1]{1,0:T(8,128)S(1)} %copy.112.doc_ref, s32[1,1024]{1,0:T(1,128)S(1)} %get-tuple-element.613.doc_t_ref, bf16[1024,2304]{1,0:T(8,128)(2,1)} %get-tuple-element.614.q_ref.k_ref.v_ref, ...), custom_call_target="tpu_custom_call" | custom-call | flops 6039797760 | bytes 22224896 | tf_op jit(solution)/shard_map/cond/branch_1_fun/attend_back/pallas_call | solution.py:70
  371.3 4.5 line_sums.5
  375.8 11.4 %conditional.29 = (bf16[384,896]{1,0:T(8,128)(2,1)}, bf16[24,6144]{1,0:T(8,128)(2,1)}, bf16[384,2304]{1,0:T(8,128)(2,1)S(1)}, bf16[384,2304]{1,0:T(8,128)(2,1)}) conditional(s32[]{:T(128)} %bitcast.11, () %tuple.194, (bf16[384,896]{1,0:T(8,128)(2,1)}, bf16[24,6144]{1,0:T(8,128)(2,1)S(1)}, s32[8]{0:T(128)S(1)}, bf16[1024,768]{1,0:T(8,128)(2,1)S(1)}, ...), branch_computations={%region_26.27_spmd, %region_27.28_spmd} | conditional | flops 3623878656 | bytes 13787280 | solution.py:875
  376.0 8.8 %weigh.1 = (bf16[384,2304]{1,0:T(8,128)(2,1)S(1)}, bf16[384,2304]{1,0:T(8,128)(2,1)}) custom-call(s32[8]{0:T(128)S(1)} %get-tuple-element.623.order_ref, bf16[1024,768]{1,0:T(8,128)(2,1)S(1)} %get-tuple-element.624.inputs_ref, bf16[16,768]{1,0:T(8,128)(2,1)S(1)} %get-tuple-element.625.gain_ref, bf16[1024,768]{1,0:T(8,128)(2,1)} %get-tuple-element.626.dq_ref, ...), custom_call_target="tpu_custom_call" | custom-call | flops 3623878656 | bytes 9855008 | tf_op jit(solution)/shard_map/cond/branch_1_fun/weigh/pallas_call | solution.py:70
  384.7 2.5 collective-permute-done.52
  388.2 11.9 %conditional.30 = (bf16[384,2304]{1,0:T(8,128)(2,1)}, bf16[48,896]{1,0:T(8,128)(2,1)}, bf16[48,896]{1,0:T(8,128)(2,1)}, bf16[24,6144]{1,0:T(8,128)(2,1)}, f32[1024,768]{1,0:T(8,128)S(1)}) conditional(s32[]{:T(128)} %bitcast.11, () %tuple.193, (bf16[384,2304]{1,0:T(8,128)(2,1)}, bf16[48,896]{1,0:T(8,128)(2,1)S(1)}, bf16[48,896]{1,0:T(8,128)(2,1)S(1)}, ...), branch_computations={%region_28.29_spmd, %region_29.30_spmd} | conditional | flops 3623878656 | bytes 26468552 | solution.py:875
  391.3 8.8 %finish.1 = f32[1024,768]{1,0:T(8,128)S(1)} custom-call(bf16[1024,768]{1,0:T(8,128)(2,1)} %get-tuple-element.635.inputs_ref, bf16[16,768]{1,0:T(8,128)(2,1)S(1)} %get-tuple-element.636.gain_ref, bf16[1024,768]{1,0:T(8,128)(2,1)} %get-tuple-element.637.dq_ref, bf16[1024,768]{1,0:T(8,128)(2,1)} %get-tuple-element.638.dk_ref, ...), custom_call_target="tpu_custom_call" | custom-call | flops 3623878656 | bytes 17522688 | tf_op jit(solution)/shard_map/cond/branch_1_fun/finish/pallas_call | solution.py:70
  400.2 2.4 middle_sums.6
  402.6 1.9 end_sums.7
  404.5 16.0 %conditional.31 = (bf16[48,2304]{1,0:T(8,128)(2,1)}, bf16[48,2304]{1,0:T(8,128)(2,1)}, bf16[96,896]{1,0:T(8,128)(2,1)}, bf16[96,896]{1,0:T(8,128)(2,1)}, bf16[24...) conditional(s32[]{:T(128)} %bitcast.11, () %tuple.200, (bf16[48,2304]{1,0:T(8,128)(2,1)}, ...), branch_computations={%region_30.31_spmd, %region_31.32_spmd} | conditional | flops 884736 | bytes 10518812 | solution.py:875
  412.4 3.0 collective-permute-done.62
  416.2 4.3 collective-permute-done.64
  420.5 1.8 line_sums.6
  422.3 2.4 middle_sums.7
  424.6 16.7 %conditional.32 = (bf16[96,2304]{1,0:T(8,128)(2,1)}, bf16[96,2304]{1,0:T(8,128)(2,1)}, bf16[24,896]{1,0:T(8,128)(2,1)}, bf16[24,896]{1,0:T(8,128)(2,1)}, bf16[24...) conditional(s32[]{:T(128)} %bitcast.11, () %tuple.199, ...), branch_computations={%region_32.33_spmd, %region_33.34_spmd} | conditional | flops 1179648 | bytes 19685744 | solution.py:875
  428.2 2.8 collective-permute-start.69
  436.6 1.9 copy.127
  442.1 1.7 line_sums.7
  443.9 10.5 %conditional.33 = (f32[24]{0:T(128)S(1)}, f32[24,2]{0,1:T(2,128)S(1)}, f32[24,2304]{1,0:T(8,128)S(1)}, f32[24,2304]{1,0:T(8,128)S(1)}, f32[24,2304]{1,0:T(8,128)S(1)}, /*index=5*/f32[24,768]{1,0:T(8,128)S(1)}) conditional(s32[]{:T(128)} %bitcast.11, () %tuple.203, (bf16[24,896]{1,0:T(8,128)(2,1)}, f32[24,896]{1,0:T(8,128)S(1)}, ...), branch_computations={%region_34.35_spmd, %region_35.36_spmd} | conditional | flops 294912 | bytes 3349224 | solution.py:875
  446.0 2.8 collective-permute-start.59
  452.3 2.0 collective-permute-done.58
  (319 shorter events, 108.0 us)
Async XLA Ops:
  7.2 59.6 %all-gather.10.cloned.1.call-start = ((), (), s32[]{:S(2)}) async-start(), calls=%async_computation.1 | async-start | bytes 1474560 | tf_op jit(solution)/shard_map/all_gather | solution.py:1088
  14.1 13.0 %collective-permute-start.71 = (bf16[24,3200]{1,0:T(8,128)(2,1)S(1)}, bf16[24,3200]{1,0:T(8,128)(2,1)S(1)}, u32[]{:S(2)}, u32[]{:S(2)}) collective-permute-start(bf16[24,3200]{1,0:T(8,128)(2,1)S(1)} %fusion.1.refs_0_), channel_id=1, source_target_pairs={{0,2},{1,3},{2,0},{3,1},{4,6},{5,7},{6,4},{7,5},{8,10},{9,11},{10,... | collective-permute-start | bytes 460808 | tf_op jit(solution)/shard_map/ppermute | solution.py:854
  14.1 13.0 %collective-permute-start.72 = (bf16[24,3200]{1,0:T(8,128)(2,1)S(1)}, bf16[24,3200]{1,0:T(8,128)(2,1)S(1)}, u32[]{:S(2)}, u32[]{:S(2)}) collective-permute-start(bf16[24,3200]{1,0:T(8,128)(2,1)S(1)} %fusion.1.refs_0_), channel_id=1, source_target_pairs={{0,1},{1,2},{2,3},{3,0},{4,5},{5,6},{6,7},{7,4},{8,9},{9,10},{10,1... | collective-permute-start | bytes 460808 | tf_op jit(solution)/shard_map/ppermute | solution.py:854
  27.3 98.9 %all-gather.8.cloned.1.call-start = ((), (), s32[]{:S(2)}) async-start(), calls=%async_computation | async-start | bytes 1474560 | tf_op jit(solution)/shard_map/all_gather | solution.py:1088
  30.4 15.3 %collective-permute-start = (bf16[96,3200]{1,0:T(8,128)(2,1)S(1)}, bf16[96,3200]{1,0:T(8,128)(2,1)}, u32[]{:S(2)}, u32[]{:S(2)}) collective-permute-start(bf16[96,3200]{1,0:T(8,128)(2,1)S(1)} %param.1), channel_id=1, source_target_pairs={{0,8},{1,9},{2,10},{3,11},{4,12},{5,13},{6,14},{7,15},{8,0},{9,1},... | collective-permute-start | bytes 1843208 | tf_op jit(solution)/shard_map/cond/branch_1_fun/ppermute | solution.py:854
  31.9 15.0 %collective-permute-start.1 = (bf16[96,3200]{1,0:T(8,128)(2,1)S(1)}, bf16[96,3200]{1,0:T(8,128)(2,1)}, u32[]{:S(2)}, u32[]{:S(2)}) collective-permute-start(bf16[96,3200]{1,0:T(8,128)(2,1)S(1)} %param.1), channel_id=1, source_target_pairs={{0,16},{1,17},{2,18},{3,19},{4,20},{5,21},{6,22},{7,23},{8,24},{9,... | collective-permute-start | bytes 1843208 | tf_op jit(solution)/shard_map/cond/branch_1_fun/ppermute | solution.py:854
  33.5 13.5 %collective-permute-start.2 = (bf16[96,3200]{1,0:T(8,128)(2,1)S(1)}, bf16[96,3200]{1,0:T(8,128)(2,1)}, u32[]{:S(2)}, u32[]{:S(2)}) collective-permute-start(bf16[96,3200]{1,0:T(8,128)(2,1)S(1)} %param.1), channel_id=1, source_target_pairs={{0,4},{1,5},{2,6},{3,7},{4,0},{5,1},{6,2},{7,3},{8,12},{9,13},{10,... | collective-permute-start | bytes 1843208 | tf_op jit(solution)/shard_map/cond/branch_1_fun/ppermute | solution.py:854
  47.0 136.3 %all-gather.12.cloned.1.call-start = ((), (), s32[]{:S(2)}) async-start(), calls=%async_computation.2 | async-start | bytes 1474560 | tf_op jit(solution)/shard_map/all_gather | solution.py:1088
  63.1 160.7 %all-gather.14.cloned.1.call-start = ((), (), s32[]{:S(2)}) async-start(), calls=%async_computation.3 | async-start | bytes 1474560 | tf_op jit(solution)/shard_map/all_gather | solution.py:1088
  67.0 37.2 %collective-permute-start.7 = (bf16[96,6144]{1,0:T(8,128)(2,1)}, bf16[96,6144]{1,0:T(8,128)(2,1)}, u32[]{:S(2)}, u32[]{:S(2)}) collective-permute-start(bf16[96,6144]{1,0:T(8,128)(2,1)} %get-tuple-element.420), channel_id=1, source_target_pairs={{0,8},{1,9},{2,10},{3,11},{4,12},{5,13},{6,14},{7,15},{8,0},{9,1},... | collective-permute-start | bytes 3538952 | tf_op jit(solution)/shard_map/cond/branch_1_fun/ppermute | solution.py:854
  67.6 36.6 %collective-permute-start.8 = (bf16[96,6144]{1,0:T(8,128)(2,1)}, bf16[96,6144]{1,0:T(8,128)(2,1)}, u32[]{:S(2)}, u32[]{:S(2)}) collective-permute-start(bf16[96,6144]{1,0:T(8,128)(2,1)} %get-tuple-element.420), channel_id=1, source_target_pairs={{0,16},{1,17},{2,18},{3,19},{4,20},{5,21},{6,22},{7,23},{8,24},{9,... | collective-permute-start | bytes 3538952 | tf_op jit(solution)/shard_map/cond/branch_1_fun/ppermute | solution.py:854
  68.1 36.1 %collective-permute-start.9 = (bf16[96,6144]{1,0:T(8,128)(2,1)}, bf16[96,6144]{1,0:T(8,128)(2,1)}, u32[]{:S(2)}, u32[]{:S(2)}) collective-permute-start(bf16[96,6144]{1,0:T(8,128)(2,1)} %get-tuple-element.420), channel_id=1, source_target_pairs={{0,4},{1,5},{2,6},{3,7},{4,0},{5,1},{6,2},{7,3},{8,12},{9,13},{10,... | collective-permute-start | bytes 3538952 | tf_op jit(solution)/shard_map/cond/branch_1_fun/ppermute | solution.py:854
  68.1 34.2 %collective-permute-start.10 = (bf16[24,6144]{1,0:T(8,128)(2,1)S(1)}, bf16[24,6144]{1,0:T(8,128)(2,1)}, u32[]{:S(2)}, u32[]{:S(2)}) collective-permute-start(bf16[24,6144]{1,0:T(8,128)(2,1)S(1)} %get-tuple-element.421), channel_id=1, source_target_pairs={{0,8},{1,9},{2,10},{3,11},{4,12},{5,13},{6,14},{7,15},{8,0},{9,1},... | collective-permute-start | bytes 884744 | tf_op jit(solution)/shard_map/cond/branch_1_fun/ppermute | solution.py:854
  69.6 33.6 %collective-permute-start.11 = (bf16[24,6144]{1,0:T(8,128)(2,1)S(1)}, bf16[24,6144]{1,0:T(8,128)(2,1)}, u32[]{:S(2)}, u32[]{:S(2)}) collective-permute-start(bf16[24,6144]{1,0:T(8,128)(2,1)S(1)} %get-tuple-element.421), channel_id=1, source_target_pairs={{0,16},{1,17},{2,18},{3,19},{4,20},{5,21},{6,22},{7,23},{8,24},{9,... | collective-permute-start | bytes 884744 | tf_op jit(solution)/shard_map/cond/branch_1_fun/ppermute | solution.py:854
  104.3 137.9 %all-gather.16.cloned.1.call-start = ((), (), s32[]{:S(2)}) async-start(), calls=%async_computation.4 | async-start | bytes 1474560 | tf_op jit(solution)/shard_map/all_gather | solution.py:1088
  104.9 137.3 %all-gather.18.cloned.1.call-start = ((), (), s32[]{:S(2)}) async-start(), calls=%async_computation.5 | async-start | bytes 1474560 | tf_op jit(solution)/shard_map/all_gather | solution.py:1088
  105.5 140.0 %all-gather.20.cloned.1.call-start = ((), (), s32[]{:S(2)}) async-start(), calls=%async_computation.6 | async-start | bytes 1474560 | tf_op jit(solution)/shard_map/all_gather | solution.py:1088
  109.5 16.1 %collective-permute-start.14 = (bf16[96,6144]{1,0:T(8,128)(2,1)}, bf16[96,6144]{1,0:T(8,128)(2,1)}, u32[]{:S(2)}, u32[]{:S(2)}) collective-permute-start(bf16[96,6144]{1,0:T(8,128)(2,1)} %get-tuple-element.442), channel_id=1, source_target_pairs={{0,4},{1,5},{2,6},{3,7},{4,0},{5,1},{6,2},{7,3},{8,12},{9,13},{10,... | collective-permute-start | bytes 3538952 | tf_op jit(solution)/shard_map/cond/branch_1_fun/ppermute | solution.py:854
  109.5 16.1 %collective-permute-start.15 = (bf16[96,6144]{1,0:T(8,128)(2,1)}, bf16[96,6144]{1,0:T(8,128)(2,1)}, u32[]{:S(2)}, u32[]{:S(2)}) collective-permute-start(bf16[96,6144]{1,0:T(8,128)(2,1)} %get-tuple-element.443), channel_id=1, source_target_pairs={{0,4},{1,5},{2,6},{3,7},{4,0},{5,1},{6,2},{7,3},{8,12},{9,13},{10,... | collective-permute-start | bytes 3538952 | tf_op jit(solution)/shard_map/cond/branch_1_fun/ppermute | solution.py:854
  110.0 15.4 %collective-permute-start.12 = (bf16[48,6144]{1,0:T(8,128)(2,1)S(1)}, bf16[48,6144]{1,0:T(8,128)(2,1)}, u32[]{:S(2)}, u32[]{:S(2)}) collective-permute-start(bf16[48,6144]{1,0:T(8,128)(2,1)S(1)} %get-tuple-element.440), channel_id=1, source_target_pairs={{0,16},{1,17},{2,18},{3,19},{4,20},{5,21},{6,22},{7,23},{8,24},{9,... | collective-permute-start | bytes 1769480 | tf_op jit(solution)/shard_map/cond/branch_1_fun/ppermute | solution.py:854
  110.5 15.1 %collective-permute-start.13 = (bf16[48,6144]{1,0:T(8,128)(2,1)S(1)}, bf16[48,6144]{1,0:T(8,128)(2,1)}, u32[]{:S(2)}, u32[]{:S(2)}) collective-permute-start(bf16[48,6144]{1,0:T(8,128)(2,1)S(1)} %get-tuple-element.441), channel_id=1, source_target_pairs={{0,8},{1,9},{2,10},{3,11},{4,12},{5,13},{6,14},{7,15},{8,0},{9,1},... | collective-permute-start | bytes 1769480 | tf_op jit(solution)/shard_map/cond/branch_1_fun/ppermute | solution.py:854
  129.2 32.9 %collective-permute-start.16 = (bf16[96,6144]{1,0:T(8,128)(2,1)}, bf16[96,6144]{1,0:T(8,128)(2,1)}, u32[]{:S(2)}, u32[]{:S(2)}) collective-permute-start(bf16[96,6144]{1,0:T(8,128)(2,1)} %get-tuple-element.458), channel_id=1, source_target_pairs={{0,8},{1,9},{2,10},{3,11},{4,12},{5,13},{6,14},{7,15},{8,0},{9,1},... | collective-permute-start | bytes 3538952 | tf_op jit(solution)/shard_map/cond/branch_1_fun/ppermute | solution.py:854
  129.8 32.3 %collective-permute-start.17 = (bf16[96,6144]{1,0:T(8,128)(2,1)}, bf16[96,6144]{1,0:T(8,128)(2,1)}, u32[]{:S(2)}, u32[]{:S(2)}) collective-permute-start(bf16[96,6144]{1,0:T(8,128)(2,1)} %get-tuple-element.458), channel_id=1, source_target_pairs={{0,16},{1,17},{2,18},{3,19},{4,20},{5,21},{6,22},{7,23},{8,24},{9,... | collective-permute-start | bytes 3538952 | tf_op jit(solution)/shard_map/cond/branch_1_fun/ppermute | solution.py:854
  131.3 30.8 %collective-permute-start.18 = (bf16[96,6144]{1,0:T(8,128)(2,1)}, bf16[96,6144]{1,0:T(8,128)(2,1)}, u32[]{:S(2)}, u32[]{:S(2)}) collective-permute-start(bf16[96,6144]{1,0:T(8,128)(2,1)} %get-tuple-element.458), channel_id=1, source_target_pairs={{0,4},{1,5},{2,6},{3,7},{4,0},{5,1},{6,2},{7,3},{8,12},{9,13},{10,... | collective-permute-start | bytes 3538952 | tf_op jit(solution)/shard_map/cond/branch_1_fun/ppermute | solution.py:854
  131.3 30.7 %collective-permute-start.19 = (bf16[12,6144]{1,0:T(8,128)(2,1)S(1)}, bf16[12,6144]{1,0:T(8,128)(2,1)}, u32[]{:S(2)}, u32[]{:S(2)}) collective-permute-start(bf16[12,6144]{1,0:T(8,128)(2,1)S(1)} %get-tuple-element.459), channel_id=1, source_target_pairs={{0,16},{1,17},{2,18},{3,19},{4,20},{5,21},{6,22},{7,23},{8,24},{9,... | collective-permute-start | bytes 442376 | tf_op jit(solution)/shard_map/cond/branch_1_fun/ppermute | solution.py:854
  131.8 30.2 %collective-permute-start.20 = (bf16[12,6144]{1,0:T(8,128)(2,1)S(1)}, bf16[12,6144]{1,0:T(8,128)(2,1)}, u32[]{:S(2)}, u32[]{:S(2)}) collective-permute-start(bf16[12,6144]{1,0:T(8,128)(2,1)S(1)} %get-tuple-element.460), channel_id=1, source_target_pairs={{0,8},{1,9},{2,10},{3,11},{4,12},{5,13},{6,14},{7,15},{8,0},{9,1},... | collective-permute-start | bytes 442376 | tf_op jit(solution)/shard_map/cond/branch_1_fun/ppermute | solution.py:854
  163.9 17.1 %collective-permute-start.23 = (bf16[96,6144]{1,0:T(8,128)(2,1)}, bf16[96,6144]{1,0:T(8,128)(2,1)}, u32[]{:S(2)}, u32[]{:S(2)}) collective-permute-start(bf16[96,6144]{1,0:T(8,128)(2,1)} %get-tuple-element.485), channel_id=1, source_target_pairs={{0,4},{1,5},{2,6},{3,7},{4,0},{5,1},{6,2},{7,3},{8,12},{9,13},{10,... | collective-permute-start | bytes 3538952 | tf_op jit(solution)/shard_map/cond/branch_1_fun/ppermute | solution.py:854
  163.9 17.1 %collective-permute-start.24 = (bf16[96,6144]{1,0:T(8,128)(2,1)}, bf16[96,6144]{1,0:T(8,128)(2,1)}, u32[]{:S(2)}, u32[]{:S(2)}) collective-permute-start(bf16[96,6144]{1,0:T(8,128)(2,1)} %get-tuple-element.486), channel_id=1, source_target_pairs={{0,4},{1,5},{2,6},{3,7},{4,0},{5,1},{6,2},{7,3},{8,12},{9,13},{10,... | collective-permute-start | bytes 3538952 | tf_op jit(solution)/shard_map/cond/branch_1_fun/ppermute | solution.py:854
  164.4 16.6 %collective-permute-start.21 = (bf16[48,6144]{1,0:T(8,128)(2,1)S(1)}, bf16[48,6144]{1,0:T(8,128)(2,1)}, u32[]{:S(2)}, u32[]{:S(2)}) collective-permute-start(bf16[48,6144]{1,0:T(8,128)(2,1)S(1)} %get-tuple-element.483), channel_id=1, source_target_pairs={{0,16},{1,17},{2,18},{3,19},{4,20},{5,21},{6,22},{7,23},{8,24},{9,... | collective-permute-start | bytes 1769480 | tf_op jit(solution)/shard_map/cond/branch_1_fun/ppermute | solution.py:854
  165.9 15.1 %collective-permute-start.22 = (bf16[48,6144]{1,0:T(8,128)(2,1)S(1)}, bf16[48,6144]{1,0:T(8,128)(2,1)}, u32[]{:S(2)}, u32[]{:S(2)}) collective-permute-start(bf16[48,6144]{1,0:T(8,128)(2,1)S(1)} %get-tuple-element.484), channel_id=1, source_target_pairs={{0,8},{1,9},{2,10},{3,11},{4,12},{5,13},{6,14},{7,15},{8,0},{9,1},... | collective-permute-start | bytes 1769480 | tf_op jit(solution)/shard_map/cond/branch_1_fun/ppermute | solution.py:854
  186.2 35.2 %collective-permute-start.28 = (bf16[384,3072]{1,0:T(8,128)(2,1)}, bf16[384,3072]{1,0:T(8,128)(2,1)}, u32[]{:S(2)}, u32[]{:S(2)}) collective-permute-start(bf16[384,3072]{1,0:T(8,128)(2,1)} %get-tuple-element.501), channel_id=1, source_target_pairs={{0,4},{1,5},{2,6},{3,7},{4,0},{5,1},{6,2},{7,3},{8,12},{9,13},{10,... | collective-permute-start | bytes 7077896 | tf_op jit(solution)/shard_map/cond/branch_1_fun/ppermute | solution.py:854
  186.4 35.0 %collective-permute-start.29 = (bf16[384,3072]{1,0:T(8,128)(2,1)}, bf16[384,3072]{1,0:T(8,128)(2,1)}, u32[]{:S(2)}, u32[]{:S(2)}) collective-permute-start(bf16[384,3072]{1,0:T(8,128)(2,1)} %get-tuple-element.502), channel_id=1, source_target_pairs={{0,4},{1,5},{2,6},{3,7},{4,0},{5,1},{6,2},{7,3},{8,12},{9,13},{10,... | collective-permute-start | bytes 7077896 | tf_op jit(solution)/shard_map/cond/branch_1_fun/ppermute | solution.py:854
  186.8 34.6 %collective-permute-start.25 = (bf16[96,6144]{1,0:T(8,128)(2,1)}, bf16[96,6144]{1,0:T(8,128)(2,1)}, u32[]{:S(2)}, u32[]{:S(2)}) collective-permute-start(bf16[96,6144]{1,0:T(8,128)(2,1)} %get-tuple-element.500), channel_id=1, source_target_pairs={{0,8},{1,9},{2,10},{3,11},{4,12},{5,13},{6,14},{7,15},{8,0},{9,1},... | collective-permute-start | bytes 3538952 | tf_op jit(solution)/shard_map/cond/branch_1_fun/ppermute | solution.py:854
  188.3 33.1 %collective-permute-start.26 = (bf16[96,6144]{1,0:T(8,128)(2,1)}, bf16[96,6144]{1,0:T(8,128)(2,1)}, u32[]{:S(2)}, u32[]{:S(2)}) collective-permute-start(bf16[96,6144]{1,0:T(8,128)(2,1)} %get-tuple-element.500), channel_id=1, source_target_pairs={{0,16},{1,17},{2,18},{3,19},{4,20},{5,21},{6,22},{7,23},{8,24},{9,... | collective-permute-start | bytes 3538952 | tf_op jit(solution)/shard_map/cond/branch_1_fun/ppermute | solution.py:854
  188.8 32.6 %collective-permute-start.27 = (bf16[96,6144]{1,0:T(8,128)(2,1)}, bf16[96,6144]{1,0:T(8,128)(2,1)}, u32[]{:S(2)}, u32[]{:S(2)}) collective-permute-start(bf16[96,6144]{1,0:T(8,128)(2,1)} %get-tuple-element.500), channel_id=1, source_target_pairs={{0,4},{1,5},{2,6},{3,7},{4,0},{5,1},{6,2},{7,3},{8,12},{9,13},{10,... | collective-permute-start | bytes 3538952 | tf_op jit(solution)/shard_map/cond/branch_1_fun/ppermute | solution.py:854
  223.8 17.8 %collective-permute-start.32 = (bf16[96,6144]{1,0:T(8,128)(2,1)}, bf16[96,6144]{1,0:T(8,128)(2,1)}, u32[]{:S(2)}, u32[]{:S(2)}) collective-permute-start(bf16[96,6144]{1,0:T(8,128)(2,1)} %get-tuple-element.527), channel_id=1, source_target_pairs={{0,4},{1,5},{2,6},{3,7},{4,0},{5,1},{6,2},{7,3},{8,12},{9,13},{10,... | collective-permute-start | bytes 3538952 | tf_op jit(solution)/shard_map/cond/branch_1_fun/ppermute | solution.py:854
  224.3 17.3 %collective-permute-start.33 = (bf16[96,6144]{1,0:T(8,128)(2,1)}, bf16[96,6144]{1,0:T(8,128)(2,1)}, u32[]{:S(2)}, u32[]{:S(2)}) collective-permute-start(bf16[96,6144]{1,0:T(8,128)(2,1)} %get-tuple-element.528), channel_id=1, source_target_pairs={{0,4},{1,5},{2,6},{3,7},{4,0},{5,1},{6,2},{7,3},{8,12},{9,13},{10,... | collective-permute-start | bytes 3538952 | tf_op jit(solution)/shard_map/cond/branch_1_fun/ppermute | solution.py:854
  224.3 17.3 %collective-permute-start.34 = (bf16[96,6144]{1,0:T(8,128)(2,1)}, bf16[96,6144]{1,0:T(8,128)(2,1)}, u32[]{:S(2)}, u32[]{:S(2)}) collective-permute-start(bf16[96,6144]{1,0:T(8,128)(2,1)} %get-tuple-element.529), channel_id=1, source_target_pairs={{0,4},{1,5},{2,6},{3,7},{4,0},{5,1},{6,2},{7,3},{8,12},{9,13},{10,... | collective-permute-start | bytes 3538952 | tf_op jit(solution)/shard_map/cond/branch_1_fun/ppermute | solution.py:854
  224.8 15.6 %collective-permute-start.30 = (bf16[48,6144]{1,0:T(8,128)(2,1)}, bf16[48,6144]{1,0:T(8,128)(2,1)}, u32[]{:S(2)}, u32[]{:S(2)}) collective-permute-start(bf16[48,6144]{1,0:T(8,128)(2,1)} %get-tuple-element.525), channel_id=1, source_target_pairs={{0,16},{1,17},{2,18},{3,19},{4,20},{5,21},{6,22},{7,23},{8,24},{9,... | collective-permute-start | bytes 1769480 | tf_op jit(solution)/shard_map/cond/branch_1_fun/ppermute | solution.py:854
  226.3 15.3 %collective-permute-start.31 = (bf16[48,6144]{1,0:T(8,128)(2,1)}, bf16[48,6144]{1,0:T(8,128)(2,1)}, u32[]{:S(2)}, u32[]{:S(2)}) collective-permute-start(bf16[48,6144]{1,0:T(8,128)(2,1)} %get-tuple-element.526), channel_id=1, source_target_pairs={{0,8},{1,9},{2,10},{3,11},{4,12},{5,13},{6,14},{7,15},{8,0},{9,1},... | collective-permute-start | bytes 1769480 | tf_op jit(solution)/shard_map/cond/branch_1_fun/ppermute | solution.py:854
  245.4 24.0 %collective-permute-start.38 = (bf16[384,3072]{1,0:T(8,128)(2,1)}, bf16[384,3072]{1,0:T(8,128)(2,1)}, u32[]{:S(2)}, u32[]{:S(2)}) collective-permute-start(bf16[384,3072]{1,0:T(8,128)(2,1)} %get-tuple-element.539), channel_id=1, source_target_pairs={{0,4},{1,5},{2,6},{3,7},{4,0},{5,1},{6,2},{7,3},{8,12},{9,13},{10,... | collective-permute-start | bytes 7077896 | tf_op jit(solution)/shard_map/cond/branch_1_fun/ppermute | solution.py:854
  245.4 24.0 %collective-permute-start.39 = (bf16[384,3072]{1,0:T(8,128)(2,1)}, bf16[384,3072]{1,0:T(8,128)(2,1)}, u32[]{:S(2)}, u32[]{:S(2)}) collective-permute-start(bf16[384,3072]{1,0:T(8,128)(2,1)} %get-tuple-element.540), channel_id=1, source_target_pairs={{0,4},{1,5},{2,6},{3,7},{4,0},{5,1},{6,2},{7,3},{8,12},{9,13},{10,... | collective-permute-start | bytes 7077896 | tf_op jit(solution)/shard_map/cond/branch_1_fun/ppermute | solution.py:854
  245.9 23.5 %collective-permute-start.35 = (bf16[96,6144]{1,0:T(8,128)(2,1)}, bf16[96,6144]{1,0:T(8,128)(2,1)}, u32[]{:S(2)}, u32[]{:S(2)}) collective-permute-start(bf16[96,6144]{1,0:T(8,128)(2,1)} %get-tuple-element.536), channel_id=1, source_target_pairs={{0,4},{1,5},{2,6},{3,7},{4,0},{5,1},{6,2},{7,3},{8,12},{9,13},{10,... | collective-permute-start | bytes 3538952 | tf_op jit(solution)/shard_map/cond/branch_1_fun/ppermute | solution.py:854
  245.9 23.5 %collective-permute-start.36 = (bf16[96,6144]{1,0:T(8,128)(2,1)}, bf16[96,6144]{1,0:T(8,128)(2,1)}, u32[]{:S(2)}, u32[]{:S(2)}) collective-permute-start(bf16[96,6144]{1,0:T(8,128)(2,1)} %get-tuple-element.537), channel_id=1, source_target_pairs={{0,4},{1,5},{2,6},{3,7},{4,0},{5,1},{6,2},{7,3},{8,12},{9,13},{10,... | collective-permute-start | bytes 3538952 | tf_op jit(solution)/shard_map/cond/branch_1_fun/ppermute | solution.py:854
  246.4 23.0 %collective-permute-start.37 = (bf16[96,6144]{1,0:T(8,128)(2,1)}, bf16[96,6144]{1,0:T(8,128)(2,1)}, u32[]{:S(2)}, u32[]{:S(2)}) collective-permute-start(bf16[96,6144]{1,0:T(8,128)(2,1)} %get-tuple-element.538), channel_id=1, source_target_pairs={{0,4},{1,5},{2,6},{3,7},{4,0},{5,1},{6,2},{7,3},{8,12},{9,13},{10,... | collective-permute-start | bytes 3538952 | tf_op jit(solution)/shard_map/cond/branch_1_fun/ppermute | solution.py:854
  273.2 26.9 %collective-permute-start.40 = (bf16[48,6144]{1,0:T(8,128)(2,1)S(1)}, bf16[48,6144]{1,0:T(8,128)(2,1)}, u32[]{:S(2)}, u32[]{:S(2)}) collective-permute-start(bf16[48,6144]{1,0:T(8,128)(2,1)S(1)} %get-tuple-element.558), channel_id=1, source_target_pairs={{0,8},{1,9},{2,10},{3,11},{4,12},{5,13},{6,14},{7,15},{8,0},{9,1},... | collective-permute-start | bytes 1769480 | tf_op jit(solution)/shard_map/cond/branch_1_fun/ppermute | solution.py:854
  274.8 25.4 %collective-permute-start.41 = (bf16[48,6144]{1,0:T(8,128)(2,1)S(1)}, bf16[48,6144]{1,0:T(8,128)(2,1)}, u32[]{:S(2)}, u32[]{:S(2)}) collective-permute-start(bf16[48,6144]{1,0:T(8,128)(2,1)S(1)} %get-tuple-element.559), channel_id=1, source_target_pairs={{0,16},{1,17},{2,18},{3,19},{4,20},{5,21},{6,22},{7,23},{8,24},{9,... | collective-permute-start | bytes 1769480 | tf_op jit(solution)/shard_map/cond/branch_1_fun/ppermute | solution.py:854
  276.2 25.5 %collective-permute-start.42 = (bf16[48,6144]{1,0:T(8,128)(2,1)}, bf16[48,6144]{1,0:T(8,128)(2,1)}, u32[]{:S(2)}, u32[]{:S(2)}) collective-permute-start(bf16[48,6144]{1,0:T(8,128)(2,1)} %get-tuple-element.560), channel_id=1, source_target_pairs={{0,8},{1,9},{2,10},{3,11},{4,12},{5,13},{6,14},{7,15},{8,0},{9,1},... | collective-permute-start | bytes 1769480 | tf_op jit(solution)/shard_map/cond/branch_1_fun/ppermute | solution.py:854
  276.8 26.2 %collective-permute-start.43 = (bf16[48,6144]{1,0:T(8,128)(2,1)}, bf16[48,6144]{1,0:T(8,128)(2,1)}, u32[]{:S(2)}, u32[]{:S(2)}) collective-permute-start(bf16[48,6144]{1,0:T(8,128)(2,1)} %get-tuple-element.561), channel_id=1, source_target_pairs={{0,16},{1,17},{2,18},{3,19},{4,20},{5,21},{6,22},{7,23},{8,24},{9,... | collective-permute-start | bytes 1769480 | tf_op jit(solution)/shard_map/cond/branch_1_fun/ppermute | solution.py:854
  307.4 27.7 %collective-permute-start.44 = (bf16[96,6144]{1,0:T(8,128)(2,1)}, bf16[96,6144]{1,0:T(8,128)(2,1)}, u32[]{:S(2)}, u32[]{:S(2)}) collective-permute-start(bf16[96,6144]{1,0:T(8,128)(2,1)} %get-tuple-element.576), channel_id=1, source_target_pairs={{0,8},{1,9},{2,10},{3,11},{4,12},{5,13},{6,14},{7,15},{8,0},{9,1},... | collective-permute-start | bytes 3538952 | tf_op jit(solution)/shard_map/cond/branch_1_fun/ppermute | solution.py:854
  308.0 27.4 %collective-permute-start.45 = (bf16[96,6144]{1,0:T(8,128)(2,1)}, bf16[96,6144]{1,0:T(8,128)(2,1)}, u32[]{:S(2)}, u32[]{:S(2)}) collective-permute-start(bf16[96,6144]{1,0:T(8,128)(2,1)} %get-tuple-element.577), channel_id=1, source_target_pairs={{0,16},{1,17},{2,18},{3,19},{4,20},{5,21},{6,22},{7,23},{8,24},{9,... | collective-permute-start | bytes 3538952 | tf_op jit(solution)/shard_map/cond/branch_1_fun/ppermute | solution.py:854
  339.6 31.5 %collective-permute-start.46 = (bf16[96,6144]{1,0:T(8,128)(2,1)}, bf16[96,6144]{1,0:T(8,128)(2,1)}, u32[]{:S(2)}, u32[]{:S(2)}) collective-permute-start(bf16[96,6144]{1,0:T(8,128)(2,1)} %get-tuple-element.608), channel_id=1, source_target_pairs={{0,8},{1,9},{2,10},{3,11},{4,12},{5,13},{6,14},{7,15},{8,0},{9,1},... | collective-permute-start | bytes 3538952 | tf_op jit(solution)/shard_map/cond/branch_1_fun/ppermute | solution.py:854
  341.0 30.1 %collective-permute-start.47 = (bf16[96,6144]{1,0:T(8,128)(2,1)}, bf16[96,6144]{1,0:T(8,128)(2,1)}, u32[]{:S(2)}, u32[]{:S(2)}) collective-permute-start(bf16[96,6144]{1,0:T(8,128)(2,1)} %get-tuple-element.609), channel_id=1, source_target_pairs={{0,16},{1,17},{2,18},{3,19},{4,20},{5,21},{6,22},{7,23},{8,24},{9,... | collective-permute-start | bytes 3538952 | tf_op jit(solution)/shard_map/cond/branch_1_fun/ppermute | solution.py:854
  342.5 28.6 %collective-permute-start.48 = (bf16[24,6144]{1,0:T(8,128)(2,1)S(1)}, bf16[24,6144]{1,0:T(8,128)(2,1)}, u32[]{:S(2)}, u32[]{:S(2)}) collective-permute-start(bf16[24,6144]{1,0:T(8,128)(2,1)S(1)} %get-tuple-element.610), channel_id=1, source_target_pairs={{0,1},{1,2},{2,3},{3,0},{4,5},{5,6},{6,7},{7,4},{8,9},{9,10},{10,1... | collective-permute-start | bytes 884744 | tf_op jit(solution)/shard_map/cond/branch_1_fun/ppermute | solution.py:854
  343.3 27.8 %collective-permute-start.49 = (bf16[24,6144]{1,0:T(8,128)(2,1)}, bf16[24,6144]{1,0:T(8,128)(2,1)}, u32[]{:S(2)}, u32[]{:S(2)}) collective-permute-start(bf16[24,6144]{1,0:T(8,128)(2,1)} %get-tuple-element.611), channel_id=1, source_target_pairs={{0,2},{1,3},{2,0},{3,1},{4,6},{5,7},{6,4},{7,5},{8,10},{9,11},{10,... | collective-permute-start | bytes 884744 | tf_op jit(solution)/shard_map/cond/branch_1_fun/ppermute | solution.py:854
  344.0 27.0 %collective-permute-start.50 = (bf16[24,6144]{1,0:T(8,128)(2,1)}, bf16[24,6144]{1,0:T(8,128)(2,1)}, u32[]{:S(2)}, u32[]{:S(2)}) collective-permute-start(bf16[24,6144]{1,0:T(8,128)(2,1)} %get-tuple-element.612), channel_id=1, source_target_pairs={{0,3},{1,0},{2,1},{3,2},{4,7},{5,4},{6,5},{7,6},{8,11},{9,8},{10,9... | collective-permute-start | bytes 884744 | tf_op jit(solution)/shard_map/cond/branch_1_fun/ppermute | solution.py:854
  388.2 11.9 %collective-permute-start.53 = (bf16[384,2304]{1,0:T(8,128)(2,1)}, bf16[384,2304]{1,0:T(8,128)(2,1)}, u32[]{:S(2)}, u32[]{:S(2)}) collective-permute-start(bf16[384,2304]{1,0:T(8,128)(2,1)} %get-tuple-element.631), channel_id=1, source_target_pairs={{0,4},{1,5},{2,6},{3,7},{4,0},{5,1},{6,2},{7,3},{8,12},{9,13},{10,... | collective-permute-start | bytes 5308424 | tf_op jit(solution)/shard_map/cond/branch_1_fun/ppermute | solution.py:854
  388.3 11.8 %collective-permute-start.56 = (bf16[24,6144]{1,0:T(8,128)(2,1)S(1)}, bf16[24,6144]{1,0:T(8,128)(2,1)}, u32[]{:S(2)}, u32[]{:S(2)}) collective-permute-start(bf16[24,6144]{1,0:T(8,128)(2,1)S(1)} %get-tuple-element.634), channel_id=1, source_target_pairs={{0,3},{1,0},{2,1},{3,2},{4,7},{5,4},{6,5},{7,6},{8,11},{9,8},{10,9... | collective-permute-start | bytes 884744 | tf_op jit(solution)/shard_map/cond/branch_1_fun/ppermute | solution.py:854
  404.5 16.0 %collective-permute-start.64 = (bf16[24,6144]{1,0:T(8,128)(2,1)}, bf16[24,6144]{1,0:T(8,128)(2,1)}, u32[]{:S(2)}, u32[]{:S(2)}) collective-permute-start(bf16[24,6144]{1,0:T(8,128)(2,1)} %get-tuple-element.646), channel_id=1, source_target_pairs={{0,2},{1,3},{2,0},{3,1},{4,6},{5,7},{6,4},{7,5},{8,10},{9,11},{10,... | collective-permute-start | bytes 884744 | tf_op jit(solution)/shard_map/cond/branch_1_fun/ppermute | solution.py:854
  424.7 16.7 %collective-permute-start.65 = (bf16[96,2304]{1,0:T(8,128)(2,1)}, bf16[96,2304]{1,0:T(8,128)(2,1)}, u32[]{:S(2)}, u32[]{:S(2)}) collective-permute-start(bf16[96,2304]{1,0:T(8,128)(2,1)} %get-tuple-element.651), channel_id=1, source_target_pairs={{0,8},{1,9},{2,10},{3,11},{4,12},{5,13},{6,14},{7,15},{8,0},{9,1},... | collective-permute-start | bytes 1327112 | tf_op jit(solution)/shard_map/cond/branch_1_fun/ppermute | solution.py:854
  425.7 15.6 %collective-permute-start.66 = (bf16[96,2304]{1,0:T(8,128)(2,1)}, bf16[96,2304]{1,0:T(8,128)(2,1)}, u32[]{:S(2)}, u32[]{:S(2)}) collective-permute-start(bf16[96,2304]{1,0:T(8,128)(2,1)} %get-tuple-element.652), channel_id=1, source_target_pairs={{0,16},{1,17},{2,18},{3,19},{4,20},{5,21},{6,22},{7,23},{8,24},{9,... | collective-permute-start | bytes 1327112 | tf_op jit(solution)/shard_map/cond/branch_1_fun/ppermute | solution.py:854
  427.2 14.1 %collective-permute-start.67 = (bf16[24,896]{1,0:T(8,128)(2,1)S(1)}, bf16[24,896]{1,0:T(8,128)(2,1)}, u32[]{:S(2)}, u32[]{:S(2)}) collective-permute-start(bf16[24,896]{1,0:T(8,128)(2,1)S(1)} %get-tuple-element.653), channel_id=1, source_target_pairs={{0,1},{1,2},{2,3},{3,0},{4,5},{5,6},{6,7},{7,4},{8,9},{9,10},{10,1... | collective-permute-start | bytes 129032 | tf_op jit(solution)/shard_map/cond/branch_1_fun/ppermute | solution.py:854
  427.2 14.1 %collective-permute-start.68 = (bf16[24,896]{1,0:T(8,128)(2,1)S(1)}, bf16[24,896]{1,0:T(8,128)(2,1)}, u32[]{:S(2)}, u32[]{:S(2)}) collective-permute-start(bf16[24,896]{1,0:T(8,128)(2,1)S(1)} %get-tuple-element.654), channel_id=1, source_target_pairs={{0,2},{1,3},{2,0},{3,1},{4,6},{5,7},{6,4},{7,5},{8,10},{9,11},{10,... | collective-permute-start | bytes 129032 | tf_op jit(solution)/shard_map/cond/branch_1_fun/ppermute | solution.py:854
  428.2 13.1 %collective-permute-start.69 = (bf16[24,896]{1,0:T(8,128)(2,1)}, bf16[24,896]{1,0:T(8,128)(2,1)}, u32[]{:S(2)}, u32[]{:S(2)}) collective-permute-start(bf16[24,896]{1,0:T(8,128)(2,1)} %get-tuple-element.655), channel_id=1, source_target_pairs={{0,3},{1,0},{2,1},{3,2},{4,7},{5,4},{6,5},{7,6},{8,11},{9,8},{10,9... | collective-permute-start | bytes 129032 | tf_op jit(solution)/shard_map/cond/branch_1_fun/ppermute | solution.py:854
  (63 other events, 356.9 us)
Sparse Core Ops, SparseCore 0:
  27.4 30.8 all-gather.9
  60.5 29.5 all-gather.7
  91.6 29.5 all-gather.11
  122.7 29.5 all-gather.13
  153.6 29.5 all-gather.15
  184.7 29.5 all-gather.17
  215.8 29.5 all-gather.19

commit v5 on v4

--- a/solution.py
+++ b/solution.py
@@ -1089,7 +1089,8 @@
 
     w0, w1, w2, w3 = weights
     w0.part = after(w0.part, dense.part)
-    dense.take_along(dense.send_along())
+    got = dense.send_along()
+    dense.take_along(after(got, [w.part for w in weights]))
     w0.full = line(w0.part, dense.full)
     dense.take_first(together(always, dense.send_first))
     w1.full = line(w1.part, dense.low)
@@ -1142,9 +1143,10 @@
     term1 = Scatter(links, [two[2], two[4]], [two[3], two[5]])
     count = len(w3.own)
     got, more, three = together(
-        always, lambda: (w3.send_over(range(1, count)), term1.send_over(), run(2, picked[1]))
-    )
-    w3.take_over(ahead + got)
+        always, lambda: (w3.send_over(range(1, count - 1)), term1.send_over(), run(2, picked[1]))
+    )
+    w3.own = w3.own[:-1] + [after(w3.own[-1], three[0])]
+    w3.take_over(ahead + got + w3.send_over([count - 1]))
     term1.take_over(more)
     term1.sums = term1.end()
     got, more, four = together(

time: 471 us -> 469 us (level)
  waiting for transfers between devices: 85.1 us -> 77.7 us
  starting transfers between devices: 66.4 us -> 72.5 us
    ppermute x81, waiting for transfers between devices: 83.4 us -> 76.6 us  [send(): return lax.ppermute(part, AXES, pairs)]
    ppermute x81, starting transfers between devices: 66.1 us -> 72.2 us  [send(): return lax.ppermute(part, AXES, pairs)]
  transfers between devices with their start and end apart: 88 -> 88, of which waited for: 28 -> 29; matrix products, arithmetic and copies ran while one was open for 7% -> 7% of each run, Pallas kernels for 49% -> 50%
where the time goes in v5:
time: 469 us; the launch traced here: 461 us
  Pallas kernels  254 us (54%)
  waiting for transfers between devices  77.7 us (17%)
  starting transfers between devices  72.5 us (15%)
  local copies, waits for them, and re-layouts  30 us (6%)
  between operations  15.6 us (3%)
  other arithmetic  8.52 us (2%)
    pallas_call x33, Pallas kernels, call(): pl.pallas_call(kernel, name=name, grid=grid, in_specs=in_specs, out_specs...  254 us
    ppermute x81, waiting for transfers between devices, send(): return lax.ppermute(part, AXES, pairs)  76.6 us
    ppermute x81, starting transfers between devices, send(): return lax.ppermute(part, AXES, pairs)  72.2 us
  transfers between devices with their start and end apart: 88, of which 29 were waited for; matrix products, arithmetic and copies ran while one was open for 7% of the time, Pallas kernels for 50%

profile of v5, /device:TPU:0, one launch (start us, length us, event | category | flops | bytes accessed | tf_op | source)
XLA Modules:
  0.0 460.8 jit_solution(8253421021891371452)
XLA Ops:
  9.0 5.1 %collective-permute-start.69 = (bf16[24,3200]{1,0:T(8,128)(2,1)S(1)}, bf16[24,3200]{1,0:T(8,128)(2,1)S(1)}, u32[]{:S(2)}, u32[]{:S(2)}) collective-permute-start(bf16[24,3200]{1,0:T(8,128)(2,1)S(1)} %fusion.1.refs_0_), channel_id=1, source_target_pairs={{0,3},{1,0},{2,1},{3,2},{4,7},{5,4},{6,5},{7,6},{8,11},{9,8},{10,9... | collective-permute-start | bytes 460808 | tf_op jit(solution)/shard_map/ppermute | solution.py:854
  29.3 16.9 %conditional.17 = (bf16[96,3200]{1,0:T(8,128)(2,1)}, bf16[96,3200]{1,0:T(8,128)(2,1)}, bf16[96,3200]{1,0:T(8,128)(2,1)}) conditional(s32[]{:T(128)} %bitcast.11, () %tuple.167, bf16[96,3200]{1,0:T(8,128)(2,1)} %line_up.1), branch_computations={%region_2.3_spmd, %region_3.4_spmd} | conditional | bytes 7372944 | solution.py:875
  32.4 12.5 %collective-permute-done = bf16[96,3200]{1,0:T(8,128)(2,1)} collective-permute-done((bf16[96,3200]{1,0:T(8,128)(2,1)}, bf16[96,3200]{1,0:T(8,128)(2,1)}, u32[]{:S(2)}, u32[]{:S(2)}) %collective-permute-start) | collective-permute-done | bytes 614432 | tf_op jit(solution)/shard_map/cond/branch_1_fun/ppermute | solution.py:854
  47.4 11.2 %conditional.18 = (bf16[48,3200]{1,0:T(8,128)(2,1)}, bf16[48,3200]{1,0:T(8,128)(2,1)}, bf16[96,3200]{1,0:T(8,128)(2,1)}, bf16[96,3200]{1,0:T(8,128)(2,1)}) conditional(s32[]{:T(128)} %bitcast.11, () %tuple.173, (bf16[48,3200]{1,0:T(8,128)(2,1)S(1)}, bf16[48,3200]{1,0:T(8,128)(2,1)S(1)}, bf16[96,3200]{1,0:T(8,128)(2,1)}, ...), branch_computations={%region_4.5_spmd, %region_5.6_spmd} | conditional | bytes 7372992 | solution.py:875
  50.0 7.3 %collective-permute-done.3 = bf16[48,3200]{1,0:T(8,128)(2,1)} collective-permute-done((bf16[48,3200]{1,0:T(8,128)(2,1)S(1)}, bf16[48,3200]{1,0:T(8,128)(2,1)}, u32[]{:S(2)}, u32[]{:S(2)}) %collective-permute-start.3) | collective-permute-done | bytes 307232 | tf_op jit(solution)/shard_map/cond/branch_1_fun/ppermute | solution.py:854
  61.0 37.7 %conditional.19 = (bf16[96,6144]{1,0:T(8,128)(2,1)}, bf16[96,6144]{1,0:T(8,128)(2,1)}, bf16[96,6144]{1,0:T(8,128)(2,1)}, bf16[24,6144]{1,0:T(8,128)(2,1)}, bf16[...) conditional(s32[]{:T(128)} %bitcast.11, () %tuple.171, ...), branch_computations={%region_6.7_spmd, %region_7.8_spmd} | conditional | flops 6039797760 | bytes 49193296 | solution.py:875
  65.3 9.7 %project.1 = (bf16[1024,2304]{1,0:T(8,128)(2,1)}, bf16[768,3200]{1,0:T(8,128)(2,1)}, bf16[16,768]{1,0:T(8,128)(2,1)}) custom-call(s32[10]{0:T(128)S(1)} %get-tuple-element.420.rows_ref, bf16[1024,768]{1,0:T(8,128)(2,1)S(1)} %get-tuple-element.421.inputs_ref, bf16[96,3200]{1,0:T(8,128)(2,1)} %get-tuple-element.422.rest_0_, ...), custom_call_target="tpu_custom_call" | custom-call | flops 3623878656 | bytes 16146472 | tf_op jit(solution)/shard_map/cond/branch_1_fun/project/pallas_call | solution.py:70
  75.2 21.5 %attend.1 = (bf16[1024,768]{1,0:T(8,128)(2,1)S(1)}, f32[6,8,1024]{2,1,0:T(8,128)}) custom-call(s32[1024,1]{1,0:T(8,128)S(1)} %copy.111.doc_ref, s32[1,1024]{1,0:T(1,128)S(1)} %get-tuple-element.435.doc_t_ref, bf16[1024,2304]{1,0:T(8,128)(2,1)} %get-tuple-element.1183.q_ref.k_ref.v_ref, bf16[1024,2304]{1,0:T(8,128)(2,1)} %get-tuple-element.1183.q_ref.k_ref.v_ref, ...), custom_call_target="tpu_custom_call" | custom-call | flops 2415919104 | bytes 15933440 | tf_op jit(solution)/shard_map/cond/branch_1_fun/attend/pallas_call | solution.py:70
  104.0 16.0 %conditional.20 = (bf16[48,6144]{1,0:T(8,128)(2,1)}, bf16[48,6144]{1,0:T(8,128)(2,1)}, bf16[96,6144]{1,0:T(8,128)(2,1)}, bf16[96,6144]{1,0:T(8,128)(2,1)}, f32[1...) conditional(s32[]{:T(128)} %bitcast.11, () %tuple.176, ...), branch_computations={%region_8.9_spmd, %region_9.10_spmd} | conditional | flops 2113929216 | bytes 40141152 | solution.py:875
  105.4 7.4 %middle.1 = (f32[1024,768]{1,0:T(8,128)}, bf16[1024,768]{1,0:T(8,128)(2,1)}, f32[1024,128]{1,0:T(8,128)}) custom-call(bf16[1024,768]{1,0:T(8,128)(2,1)} %get-tuple-element.442.inputs_ref, bf16[1024,768]{1,0:T(8,128)(2,1)S(1)} %get-tuple-element.443.attended_ref, s32[1024,128]{1,0:T(8,128)S(1)} %get-tuple-element.444.place_ref, ...), custom_call_target="tpu_custom_call" | custom-call | flops 1207959552 | bytes 18743296 | tf_op jit(solution)/shard_map/cond/branch_1_fun/middle/pallas_call | solution.py:70
  112.9 4.9 %dispatch_0.1 = (bf16[768,768]{1,0:T(8,128)(2,1)}, bf16[768,768]{1,0:T(8,128)(2,1)}, bf16[768,768]{1,0:T(8,128)(2,1)}) custom-call(s32[8]{0:T(128)S(1)} %get-tuple-element.449.order_ref, s32[20]{0:T(128)S(1)} %get-tuple-element.450.counts_ref, s32[8,1024]{1,0:T(8,128)S(1)} %get-tuple-element.451.place_t_ref, f32[1024,128]{1,0:T(8,128)} %get-tuple-element.1206.gate_ref, ...), custom_call_target="tpu_custom_call" | custom-call | flops 905969664 | bytes 7241840 | tf_op jit(solution)/shard_map/cond/branch_1_fun/dispatch_0/pallas_call | solution.py:70
  117.7 2.2 collective-permute-done.12
  123.1 33.3 %conditional.21 = (bf16[96,6144]{1,0:T(8,128)(2,1)}, bf16[96,6144]{1,0:T(8,128)(2,1)}, bf16[96,6144]{1,0:T(8,128)(2,1)}, bf16[12,6144]{1,0:T(8,128)(2,1)}, bf16[...) conditional(s32[]{:T(128)} %bitcast.11, () %tuple.166, ...), branch_computations={%region_10.11_spmd, %region_11.12_spmd} | conditional | flops 16986931200 | bytes 54264304 | solution.py:875
  127.7 24.4 %expert_0.1 = (bf16[768,768]{1,0:T(8,128)(2,1)}, bf16[768,768]{1,0:T(8,128)(2,1)}, bf16[384,3072]{1,0:T(8,128)(2,1)S(1)}, bf16[384,3072]{1,0:T(8,128)(2,1)}, bf1...) custom-call(s32[10]{0:T(128)S(1)} %get-tuple-element.459.rows_ref, s32[8]{0:T(128)S(1)} %get-tuple-element.460.order_ref, ...), custom_call_target="tpu_custom_call" | custom-call | flops 16986931200 | bytes 34209944 | tf_op jit(solution)/shard_map/cond/branch_1_fun/expert_0/pallas_call | solution.py:70
  152.1 4.3 collective-permute-done.19
  158.2 17.2 %conditional.22 = (bf16[48,6144]{1,0:T(8,128)(2,1)}, bf16[48,6144]{1,0:T(8,128)(2,1)}, bf16[96,6144]{1,0:T(8,128)(2,1)}, bf16[96,6144]{1,0:T(8,128)(2,1)}, bf16[...) conditional(s32[]{:T(128)} %bitcast.11, () %tuple.182, ...), branch_computations={%region_12.13_spmd, %region_13.14_spmd} | conditional | flops 2717908992 | bytes 33784448 | solution.py:875
  161.8 4.6 dispatch_1.1
  166.4 4.5 dispatch_2.1
  170.9 4.5 dispatch_3.1
  175.4 1.8 pad_maximum_fusion.3
  177.8 1.8 collective-permute-done.76
  180.5 30.3 %conditional.23 = (bf16[96,6144]{1,0:T(8,128)(2,1)}, bf16[96,6144]{1,0:T(8,128)(2,1)}, bf16[96,6144]{1,0:T(8,128)(2,1)}, bf16[384,3072]{1,0:T(8,128)(2,1)}, bf16...) conditional(s32[]{:T(128)} %bitcast.11, () %tuple.179, ...), branch_computations={%region_14.15_spmd, %region_15.16_spmd} | conditional | flops 16986931200 | bytes 67240376 | solution.py:875
  183.1 24.0 %expert_1.1 = (bf16[768,768]{1,0:T(8,128)(2,1)}, bf16[768,768]{1,0:T(8,128)(2,1)}, bf16[384,3072]{1,0:T(8,128)(2,1)}, bf16[384,3072]{1,0:T(8,128)(2,1)}, bf16[38...) custom-call(s32[10]{0:T(128)S(1)} %get-tuple-element.501.rows_ref, s32[8]{0:T(128)S(1)} %get-tuple-element.502.order_ref, ...), custom_call_target="tpu_custom_call" | custom-call | flops 16986931200 | bytes 34209944 | tf_op jit(solution)/shard_map/cond/branch_1_fun/expert_1/pallas_call | solution.py:70
  207.1 2.4 collective-permute-done.25
  210.8 2.3 halves.7
  213.1 22.6 %conditional.24 = (bf16[48,6144]{1,0:T(8,128)(2,1)}, bf16[48,6144]{1,0:T(8,128)(2,1)}, bf16[96,6144]{1,0:T(8,128)(2,1)}, bf16[96,6144]{1,0:T(8,128)(2,1)}, bf16[...) conditional(s32[]{:T(128)} %bitcast.11, () %tuple.186, ...), branch_computations={%region_16.17_spmd, %region_17.18_spmd} | conditional | bytes 29491456 | solution.py:875
  213.1 5.2 %collective-permute-start.32 = (bf16[96,6144]{1,0:T(8,128)(2,1)}, bf16[96,6144]{1,0:T(8,128)(2,1)}, u32[]{:S(2)}, u32[]{:S(2)}) collective-permute-start(bf16[96,6144]{1,0:T(8,128)(2,1)} %get-tuple-element.525), channel_id=1, source_target_pairs={{0,4},{1,5},{2,6},{3,7},{4,0},{5,1},{6,2},{7,3},{8,12},{9,13},{10,... | collective-permute-start | bytes 3538952 | tf_op jit(solution)/shard_map/cond/branch_1_fun/ppermute | solution.py:854
  222.0 12.3 %collective-permute-done.30 = bf16[48,6144]{1,0:T(8,128)(2,1)} collective-permute-done((bf16[48,6144]{1,0:T(8,128)(2,1)}, bf16[48,6144]{1,0:T(8,128)(2,1)}, u32[]{:S(2)}, u32[]{:S(2)}) %collective-permute-start.30) | collective-permute-done | bytes 589856 | tf_op jit(solution)/shard_map/cond/branch_1_fun/ppermute | solution.py:854
  236.2 1.8 collective-permute-done.78
  238.9 24.1 %conditional.25 = (bf16[96,6144]{1,0:T(8,128)(2,1)}, bf16[96,6144]{1,0:T(8,128)(2,1)}, bf16[384,3072]{1,0:T(8,128)(2,1)}, bf16[384,3072]{1,0:T(8,128)(2,1)}, bf1...) conditional(s32[]{:T(128)} %bitcast.11, () %tuple.189, (bf16[96,6144]{1,0:T(8,128)(2,1)}, ...), branch_computations={%region_18.19_spmd, %region_19.20_spmd} | conditional | flops 11324620800 | bytes 51904872 | solution.py:875
  239.9 23.0 %expert_2.1 = (bf16[768,768]{1,0:T(8,128)(2,1)}, bf16[768,768]{1,0:T(8,128)(2,1)}) custom-call(s32[10]{0:T(128)S(1)} %get-tuple-element.538.rows_ref, s32[8]{0:T(128)S(1)} %get-tuple-element.539.order_ref, s32[20]{0:T(128)S(1)} %get-tuple-element.540.counts_ref, bf16[768,768]{1,0:T(8,128)(2,1)} %get-tuple-element.541.rest_0_, ...), custom_call_target="tpu_custom_call" | custom-call | flops 11324620800 | bytes 23593112 | tf_op jit(solution)/shard_map/cond/branch_1_fun/expert_2/pallas_call | solution.py:70
  263.2 3.0 end_sums.5
  266.6 28.9 %conditional.26 = (bf16[48,6144]{1,0:T(8,128)(2,1)}, bf16[48,6144]{1,0:T(8,128)(2,1)}, bf16[48,6144]{1,0:T(8,128)(2,1)}, bf16[48,6144]{1,0:T(8,128)(2,1)}, bf16[...) conditional(s32[]{:T(128)} %bitcast.11, () %tuple.185, (bf16[48,6144]{1,0:T(8,128)(2,1)S(1)}, ...), branch_computations={%region_20.21_spmd, %region_21.22_spmd} | conditional | flops 11324620800 | bytes 37749116 | solution.py:875
  271.1 22.8 %expert_3.1 = (bf16[768,768]{1,0:T(8,128)(2,1)}, bf16[768,768]{1,0:T(8,128)(2,1)}) custom-call(s32[8]{0:T(128)S(1)} %get-tuple-element.559.rows_ref.order_ref, s32[8]{0:T(128)S(1)} %get-tuple-element.559.rows_ref.order_ref, s32[20]{0:T(128)S(1)} %get-tuple-element.560.counts_ref, bf16[768,768]{1,0:T(8,128)(2,1)} %get-tuple-element.561.rest_0_, ...), custom_call_target="tpu_custom_call" | custom-call | flops 11324620800 | bytes 23593104 | tf_op jit(solution)/shard_map/cond/branch_1_fun/expert_3/pallas_call | solution.py:70
  295.5 4.4 middle_sums.5
  300.0 28.9 %conditional.27 = (bf16[96,6144]{1,0:T(8,128)(2,1)}, bf16[96,6144]{1,0:T(8,128)(2,1)}, bf16[96,6144]{1,0:T(8,128)(2,1)}, bf16[96,6144]{1,0:T(8,128)(2,1)}, bf16[...) conditional(s32[]{:T(128)} %bitcast.11, () %tuple.165, ...), branch_computations={%region_22.23_spmd, %region_23.24_spmd} | conditional | flops 4831838208 | bytes 67698952 | solution.py:875
  302.0 4.6 middle_sums.4
  306.5 20.1 %combine.1 = (bf16[1024,768]{1,0:T(8,128)(2,1)}, f32[1024,768]{1,0:T(8,128)}, bf16[1024,768]{1,0:T(8,128)(2,1)}, bf16[384,896]{1,0:T(8,128)(2,1)S(1)}, bf16[384,896]{1,0:T(8,128)(2,1)}) custom-call(s32[8]{0:T(128)S(1)} %get-tuple-element.583.order_ref, s32[20]{0:T(128)S(1)} %get-tuple-element.584.counts_ref, s32[1024,128]{1,0:T(8,128)} %get-tuple-element.585.place_ref, ...), custom_call_target="tpu_custom_call" | custom-call | flops 4831838208 | bytes 35848304 | tf_op jit(solution)/shard_map/cond/branch_1_fun/combine/pallas_call | solution.py:70
  328.9 4.2 line_sums.4
  333.1 33.5 %conditional.28 = (bf16[96,6144]{1,0:T(8,128)(2,1)}, bf16[96,6144]{1,0:T(8,128)(2,1)}, bf16[24,6144]{1,0:T(8,128)(2,1)}, bf16[24,6144]{1,0:T(8,128)(2,1)}, bf16[...) conditional(s32[]{:T(128)} %bitcast.11, () %tuple.199, ...), branch_computations={%region_24.25_spmd, %region_25.26_spmd} | conditional | flops 6039797760 | bytes 35209480 | solution.py:875
  335.0 4.4 collective-permute-start.48
  339.4 2.9 collective-permute-start.49
  342.5 23.9 %attend_back.1 = (bf16[1024,768]{1,0:T(8,128)(2,1)}, bf16[1024,768]{1,0:T(8,128)(2,1)}, bf16[1024,768]{1,0:T(8,128)(2,1)}) custom-call(s32[1024,1]{1,0:T(8,128)S(1)} %copy.112.doc_ref, s32[1,1024]{1,0:T(1,128)S(1)} %get-tuple-element.610.doc_t_ref, bf16[1024,2304]{1,0:T(8,128)(2,1)} %get-tuple-element.611.q_ref.k_ref.v_ref, ...), custom_call_target="tpu_custom_call" | custom-call | flops 6039797760 | bytes 22224896 | tf_op jit(solution)/shard_map/cond/branch_1_fun/attend_back/pallas_call | solution.py:70
  366.6 4.5 line_sums.5
  371.1 11.4 %conditional.29 = (bf16[384,896]{1,0:T(8,128)(2,1)}, bf16[24,6144]{1,0:T(8,128)(2,1)}, bf16[384,2304]{1,0:T(8,128)(2,1)S(1)}, bf16[384,2304]{1,0:T(8,128)(2,1)}) conditional(s32[]{:T(128)} %bitcast.11, () %tuple.198, (bf16[384,896]{1,0:T(8,128)(2,1)}, bf16[24,6144]{1,0:T(8,128)(2,1)S(1)}, s32[8]{0:T(128)S(1)}, bf16[1024,768]{1,0:T(8,128)(2,1)S(1)}, ...), branch_computations={%region_26.27_spmd, %region_27.28_spmd} | conditional | flops 3623878656 | bytes 13787280 | solution.py:875
  371.2 8.8 %weigh.1 = (bf16[384,2304]{1,0:T(8,128)(2,1)S(1)}, bf16[384,2304]{1,0:T(8,128)(2,1)}) custom-call(s32[8]{0:T(128)S(1)} %get-tuple-element.620.order_ref, bf16[1024,768]{1,0:T(8,128)(2,1)S(1)} %get-tuple-element.621.inputs_ref, bf16[16,768]{1,0:T(8,128)(2,1)S(1)} %get-tuple-element.622.gain_ref, bf16[1024,768]{1,0:T(8,128)(2,1)} %get-tuple-element.623.dq_ref, ...), custom_call_target="tpu_custom_call" | custom-call | flops 3623878656 | bytes 9855008 | tf_op jit(solution)/shard_map/cond/branch_1_fun/weigh/pallas_call | solution.py:70
  380.0 2.5 collective-permute-done.51
  383.4 13.6 %conditional.30 = (bf16[384,2304]{1,0:T(8,128)(2,1)}, bf16[48,896]{1,0:T(8,128)(2,1)}, bf16[48,896]{1,0:T(8,128)(2,1)}, bf16[24,6144]{1,0:T(8,128)(2,1)}, f32[1024,768]{1,0:T(8,128)S(1)}) conditional(s32[]{:T(128)} %bitcast.11, () %tuple.197, (bf16[384,2304]{1,0:T(8,128)(2,1)}, bf16[48,896]{1,0:T(8,128)(2,1)S(1)}, bf16[48,896]{1,0:T(8,128)(2,1)S(1)}, ...), branch_computations={%region_28.29_spmd, %region_29.30_spmd} | conditional | flops 3623878656 | bytes 26468552 | solution.py:875
  385.0 1.7 collective-permute-start.54
  388.2 8.8 %finish.1 = f32[1024,768]{1,0:T(8,128)S(1)} custom-call(bf16[1024,768]{1,0:T(8,128)(2,1)} %get-tuple-element.632.inputs_ref, bf16[16,768]{1,0:T(8,128)(2,1)S(1)} %get-tuple-element.633.gain_ref, bf16[1024,768]{1,0:T(8,128)(2,1)} %get-tuple-element.634.dq_ref, bf16[1024,768]{1,0:T(8,128)(2,1)} %get-tuple-element.635.dk_ref, ...), custom_call_target="tpu_custom_call" | custom-call | flops 3623878656 | bytes 17522688 | tf_op jit(solution)/shard_map/cond/branch_1_fun/finish/pallas_call | solution.py:70
  397.0 2.2 end_sums.7
  399.2 1.9 middle_sums.6
  401.1 18.9 %conditional.31 = (bf16[48,2304]{1,0:T(8,128)(2,1)}, bf16[48,2304]{1,0:T(8,128)(2,1)}, bf16[96,896]{1,0:T(8,128)(2,1)}, bf16[96,896]{1,0:T(8,128)(2,1)}, bf16[24...) conditional(s32[]{:T(128)} %bitcast.11, () %tuple.204, (bf16[48,2304]{1,0:T(8,128)(2,1)}, ...), branch_computations={%region_30.31_spmd, %region_31.32_spmd} | conditional | flops 884736 | bytes 10518812 | solution.py:875
  403.4 1.7 collective-permute-start.62
  408.9 3.0 collective-permute-done.61
  412.3 7.7 %collective-permute-done.63 = bf16[24,6144]{1,0:T(8,128)(2,1)} collective-permute-done((bf16[24,6144]{1,0:T(8,128)(2,1)}, bf16[24,6144]{1,0:T(8,128)(2,1)}, u32[]{:S(2)}, u32[]{:S(2)}) %collective-permute-start.63) | collective-permute-done | bytes 294944 | tf_op jit(solution)/shard_map/cond/branch_1_fun/ppermute | solution.py:854
  420.0 2.3 middle_sums.7
  422.3 1.9 line_sums.6
  424.2 15.1 %conditional.32 = (bf16[96,2304]{1,0:T(8,128)(2,1)}, bf16[96,2304]{1,0:T(8,128)(2,1)}, bf16[24,896]{1,0:T(8,128)(2,1)}, bf16[24,896]{1,0:T(8,128)(2,1)}, bf16[24...) conditional(s32[]{:T(128)} %bitcast.11, () %tuple.203, ...), branch_computations={%region_32.33_spmd, %region_33.34_spmd} | conditional | flops 1179648 | bytes 19685744 | solution.py:875
  426.8 2.1 collective-permute-start.68
  434.5 1.9 copy.127
  441.8 10.5 %conditional.33 = (f32[24]{0:T(128)S(1)}, f32[24,2]{0,1:T(2,128)S(1)}, f32[24,2304]{1,0:T(8,128)S(1)}, f32[24,2304]{1,0:T(8,128)S(1)}, f32[24,2304]{1,0:T(8,128)S(1)}, /*index=5*/f32[24,768]{1,0:T(8,128)S(1)}) conditional(s32[]{:T(128)} %bitcast.11, () %tuple.207, (bf16[24,896]{1,0:T(8,128)(2,1)}, f32[24,896]{1,0:T(8,128)S(1)}, ...), branch_computations={%region_34.35_spmd, %region_35.36_spmd} | conditional | flops 294912 | bytes 3349224 | solution.py:875
  443.9 2.8 collective-permute-start.58
  450.2 2.0 collective-permute-done.57
  (326 shorter events, 109.7 us)
Async XLA Ops:
  7.2 53.8 %all-gather.10.cloned.1.call-start = ((), (), s32[]{:S(2)}) async-start(), calls=%async_computation.1 | async-start | bytes 1474560 | tf_op jit(solution)/shard_map/all_gather | solution.py:1088
  9.0 16.5 %collective-permute-start.69 = (bf16[24,3200]{1,0:T(8,128)(2,1)S(1)}, bf16[24,3200]{1,0:T(8,128)(2,1)S(1)}, u32[]{:S(2)}, u32[]{:S(2)}) collective-permute-start(bf16[24,3200]{1,0:T(8,128)(2,1)S(1)} %fusion.1.refs_0_), channel_id=1, source_target_pairs={{0,3},{1,0},{2,1},{3,2},{4,7},{5,4},{6,5},{7,6},{8,11},{9,8},{10,9... | collective-permute-start | bytes 460808 | tf_op jit(solution)/shard_map/ppermute | solution.py:854
  14.1 13.0 %collective-permute-start.70 = (bf16[24,3200]{1,0:T(8,128)(2,1)S(1)}, bf16[24,3200]{1,0:T(8,128)(2,1)S(1)}, u32[]{:S(2)}, u32[]{:S(2)}) collective-permute-start(bf16[24,3200]{1,0:T(8,128)(2,1)S(1)} %fusion.1.refs_0_), channel_id=1, source_target_pairs={{0,2},{1,3},{2,0},{3,1},{4,6},{5,7},{6,4},{7,5},{8,10},{9,11},{10,... | collective-permute-start | bytes 460808 | tf_op jit(solution)/shard_map/ppermute | solution.py:854
  14.1 13.0 %collective-permute-start.71 = (bf16[24,3200]{1,0:T(8,128)(2,1)S(1)}, bf16[24,3200]{1,0:T(8,128)(2,1)S(1)}, u32[]{:S(2)}, u32[]{:S(2)}) collective-permute-start(bf16[24,3200]{1,0:T(8,128)(2,1)S(1)} %fusion.1.refs_0_), channel_id=1, source_target_pairs={{0,1},{1,2},{2,3},{3,0},{4,5},{5,6},{6,7},{7,4},{8,9},{9,10},{10,1... | collective-permute-start | bytes 460808 | tf_op jit(solution)/shard_map/ppermute | solution.py:854
  28.1 92.5 %all-gather.8.cloned.1.call-start = ((), (), s32[]{:S(2)}) async-start(), calls=%async_computation | async-start | bytes 1474560 | tf_op jit(solution)/shard_map/all_gather | solution.py:1088
  29.4 15.6 %collective-permute-start = (bf16[96,3200]{1,0:T(8,128)(2,1)}, bf16[96,3200]{1,0:T(8,128)(2,1)}, u32[]{:S(2)}, u32[]{:S(2)}) collective-permute-start(bf16[96,3200]{1,0:T(8,128)(2,1)} %param.1), channel_id=1, source_target_pairs={{0,8},{1,9},{2,10},{3,11},{4,12},{5,13},{6,14},{7,15},{8,0},{9,1},... | collective-permute-start | bytes 1843208 | tf_op jit(solution)/shard_map/cond/branch_1_fun/ppermute | solution.py:854
  30.9 15.3 %collective-permute-start.1 = (bf16[96,3200]{1,0:T(8,128)(2,1)}, bf16[96,3200]{1,0:T(8,128)(2,1)}, u32[]{:S(2)}, u32[]{:S(2)}) collective-permute-start(bf16[96,3200]{1,0:T(8,128)(2,1)} %param.1), channel_id=1, source_target_pairs={{0,16},{1,17},{2,18},{3,19},{4,20},{5,21},{6,22},{7,23},{8,24},{9,... | collective-permute-start | bytes 1843208 | tf_op jit(solution)/shard_map/cond/branch_1_fun/ppermute | solution.py:854
  32.4 13.8 %collective-permute-start.2 = (bf16[96,3200]{1,0:T(8,128)(2,1)}, bf16[96,3200]{1,0:T(8,128)(2,1)}, u32[]{:S(2)}, u32[]{:S(2)}) collective-permute-start(bf16[96,3200]{1,0:T(8,128)(2,1)} %param.1), channel_id=1, source_target_pairs={{0,4},{1,5},{2,6},{3,7},{4,0},{5,1},{6,2},{7,3},{8,12},{9,13},{10,... | collective-permute-start | bytes 1843208 | tf_op jit(solution)/shard_map/cond/branch_1_fun/ppermute | solution.py:854
  46.2 131.6 %all-gather.12.cloned.1.call-start = ((), (), s32[]{:S(2)}) async-start(), calls=%async_computation.2 | async-start | bytes 1474560 | tf_op jit(solution)/shard_map/all_gather | solution.py:1088
  58.6 154.5 %all-gather.14.cloned.1.call-start = ((), (), s32[]{:S(2)}) async-start(), calls=%async_computation.3 | async-start | bytes 1474560 | tf_op jit(solution)/shard_map/all_gather | solution.py:1088
  61.2 37.5 %collective-permute-start.7 = (bf16[96,6144]{1,0:T(8,128)(2,1)}, bf16[96,6144]{1,0:T(8,128)(2,1)}, u32[]{:S(2)}, u32[]{:S(2)}) collective-permute-start(bf16[96,6144]{1,0:T(8,128)(2,1)} %get-tuple-element.418), channel_id=1, source_target_pairs={{0,8},{1,9},{2,10},{3,11},{4,12},{5,13},{6,14},{7,15},{8,0},{9,1},... | collective-permute-start | bytes 3538952 | tf_op jit(solution)/shard_map/cond/branch_1_fun/ppermute | solution.py:854
  61.8 36.9 %collective-permute-start.8 = (bf16[96,6144]{1,0:T(8,128)(2,1)}, bf16[96,6144]{1,0:T(8,128)(2,1)}, u32[]{:S(2)}, u32[]{:S(2)}) collective-permute-start(bf16[96,6144]{1,0:T(8,128)(2,1)} %get-tuple-element.418), channel_id=1, source_target_pairs={{0,16},{1,17},{2,18},{3,19},{4,20},{5,21},{6,22},{7,23},{8,24},{9,... | collective-permute-start | bytes 3538952 | tf_op jit(solution)/shard_map/cond/branch_1_fun/ppermute | solution.py:854
  62.4 36.4 %collective-permute-start.9 = (bf16[96,6144]{1,0:T(8,128)(2,1)}, bf16[96,6144]{1,0:T(8,128)(2,1)}, u32[]{:S(2)}, u32[]{:S(2)}) collective-permute-start(bf16[96,6144]{1,0:T(8,128)(2,1)} %get-tuple-element.418), channel_id=1, source_target_pairs={{0,4},{1,5},{2,6},{3,7},{4,0},{5,1},{6,2},{7,3},{8,12},{9,13},{10,... | collective-permute-start | bytes 3538952 | tf_op jit(solution)/shard_map/cond/branch_1_fun/ppermute | solution.py:854
  62.4 34.4 %collective-permute-start.10 = (bf16[24,6144]{1,0:T(8,128)(2,1)S(1)}, bf16[24,6144]{1,0:T(8,128)(2,1)}, u32[]{:S(2)}, u32[]{:S(2)}) collective-permute-start(bf16[24,6144]{1,0:T(8,128)(2,1)S(1)} %get-tuple-element.419), channel_id=1, source_target_pairs={{0,8},{1,9},{2,10},{3,11},{4,12},{5,13},{6,14},{7,15},{8,0},{9,1},... | collective-permute-start | bytes 884744 | tf_op jit(solution)/shard_map/cond/branch_1_fun/ppermute | solution.py:854
  63.8 33.9 %collective-permute-start.11 = (bf16[24,6144]{1,0:T(8,128)(2,1)S(1)}, bf16[24,6144]{1,0:T(8,128)(2,1)}, u32[]{:S(2)}, u32[]{:S(2)}) collective-permute-start(bf16[24,6144]{1,0:T(8,128)(2,1)S(1)} %get-tuple-element.419), channel_id=1, source_target_pairs={{0,16},{1,17},{2,18},{3,19},{4,20},{5,21},{6,22},{7,23},{8,24},{9,... | collective-permute-start | bytes 884744 | tf_op jit(solution)/shard_map/cond/branch_1_fun/ppermute | solution.py:854
  98.7 137.5 %all-gather.16.cloned.1.call-start = ((), (), s32[]{:S(2)}) async-start(), calls=%async_computation.4 | async-start | bytes 1474560 | tf_op jit(solution)/shard_map/all_gather | solution.py:1088
  99.3 136.9 %all-gather.18.cloned.1.call-start = ((), (), s32[]{:S(2)}) async-start(), calls=%async_computation.5 | async-start | bytes 1474560 | tf_op jit(solution)/shard_map/all_gather | solution.py:1088
  99.9 163.1 %all-gather.20.cloned.1.call-start = ((), (), s32[]{:S(2)}) async-start(), calls=%async_computation.6 | async-start | bytes 1474560 | tf_op jit(solution)/shard_map/all_gather | solution.py:1088
  104.0 16.0 %collective-permute-start.14 = (bf16[96,6144]{1,0:T(8,128)(2,1)}, bf16[96,6144]{1,0:T(8,128)(2,1)}, u32[]{:S(2)}, u32[]{:S(2)}) collective-permute-start(bf16[96,6144]{1,0:T(8,128)(2,1)} %get-tuple-element.440), channel_id=1, source_target_pairs={{0,4},{1,5},{2,6},{3,7},{4,0},{5,1},{6,2},{7,3},{8,12},{9,13},{10,... | collective-permute-start | bytes 3538952 | tf_op jit(solution)/shard_map/cond/branch_1_fun/ppermute | solution.py:854
  104.0 16.0 %collective-permute-start.15 = (bf16[96,6144]{1,0:T(8,128)(2,1)}, bf16[96,6144]{1,0:T(8,128)(2,1)}, u32[]{:S(2)}, u32[]{:S(2)}) collective-permute-start(bf16[96,6144]{1,0:T(8,128)(2,1)} %get-tuple-element.441), channel_id=1, source_target_pairs={{0,4},{1,5},{2,6},{3,7},{4,0},{5,1},{6,2},{7,3},{8,12},{9,13},{10,... | collective-permute-start | bytes 3538952 | tf_op jit(solution)/shard_map/cond/branch_1_fun/ppermute | solution.py:854
  104.5 15.4 %collective-permute-start.12 = (bf16[48,6144]{1,0:T(8,128)(2,1)S(1)}, bf16[48,6144]{1,0:T(8,128)(2,1)}, u32[]{:S(2)}, u32[]{:S(2)}) collective-permute-start(bf16[48,6144]{1,0:T(8,128)(2,1)S(1)} %get-tuple-element.438), channel_id=1, source_target_pairs={{0,16},{1,17},{2,18},{3,19},{4,20},{5,21},{6,22},{7,23},{8,24},{9,... | collective-permute-start | bytes 1769480 | tf_op jit(solution)/shard_map/cond/branch_1_fun/ppermute | solution.py:854
  104.9 15.1 %collective-permute-start.13 = (bf16[48,6144]{1,0:T(8,128)(2,1)S(1)}, bf16[48,6144]{1,0:T(8,128)(2,1)}, u32[]{:S(2)}, u32[]{:S(2)}) collective-permute-start(bf16[48,6144]{1,0:T(8,128)(2,1)S(1)} %get-tuple-element.439), channel_id=1, source_target_pairs={{0,8},{1,9},{2,10},{3,11},{4,12},{5,13},{6,14},{7,15},{8,0},{9,1},... | collective-permute-start | bytes 1769480 | tf_op jit(solution)/shard_map/cond/branch_1_fun/ppermute | solution.py:854
  123.6 32.9 %collective-permute-start.16 = (bf16[96,6144]{1,0:T(8,128)(2,1)}, bf16[96,6144]{1,0:T(8,128)(2,1)}, u32[]{:S(2)}, u32[]{:S(2)}) collective-permute-start(bf16[96,6144]{1,0:T(8,128)(2,1)} %get-tuple-element.456), channel_id=1, source_target_pairs={{0,8},{1,9},{2,10},{3,11},{4,12},{5,13},{6,14},{7,15},{8,0},{9,1},... | collective-permute-start | bytes 3538952 | tf_op jit(solution)/shard_map/cond/branch_1_fun/ppermute | solution.py:854
  124.2 32.3 %collective-permute-start.17 = (bf16[96,6144]{1,0:T(8,128)(2,1)}, bf16[96,6144]{1,0:T(8,128)(2,1)}, u32[]{:S(2)}, u32[]{:S(2)}) collective-permute-start(bf16[96,6144]{1,0:T(8,128)(2,1)} %get-tuple-element.456), channel_id=1, source_target_pairs={{0,16},{1,17},{2,18},{3,19},{4,20},{5,21},{6,22},{7,23},{8,24},{9,... | collective-permute-start | bytes 3538952 | tf_op jit(solution)/shard_map/cond/branch_1_fun/ppermute | solution.py:854
  125.7 30.8 %collective-permute-start.18 = (bf16[96,6144]{1,0:T(8,128)(2,1)}, bf16[96,6144]{1,0:T(8,128)(2,1)}, u32[]{:S(2)}, u32[]{:S(2)}) collective-permute-start(bf16[96,6144]{1,0:T(8,128)(2,1)} %get-tuple-element.456), channel_id=1, source_target_pairs={{0,4},{1,5},{2,6},{3,7},{4,0},{5,1},{6,2},{7,3},{8,12},{9,13},{10,... | collective-permute-start | bytes 3538952 | tf_op jit(solution)/shard_map/cond/branch_1_fun/ppermute | solution.py:854
  125.7 30.8 %collective-permute-start.19 = (bf16[12,6144]{1,0:T(8,128)(2,1)S(1)}, bf16[12,6144]{1,0:T(8,128)(2,1)}, u32[]{:S(2)}, u32[]{:S(2)}) collective-permute-start(bf16[12,6144]{1,0:T(8,128)(2,1)S(1)} %get-tuple-element.457), channel_id=1, source_target_pairs={{0,16},{1,17},{2,18},{3,19},{4,20},{5,21},{6,22},{7,23},{8,24},{9,... | collective-permute-start | bytes 442376 | tf_op jit(solution)/shard_map/cond/branch_1_fun/ppermute | solution.py:854
  126.2 30.2 %collective-permute-start.20 = (bf16[12,6144]{1,0:T(8,128)(2,1)S(1)}, bf16[12,6144]{1,0:T(8,128)(2,1)}, u32[]{:S(2)}, u32[]{:S(2)}) collective-permute-start(bf16[12,6144]{1,0:T(8,128)(2,1)S(1)} %get-tuple-element.458), channel_id=1, source_target_pairs={{0,8},{1,9},{2,10},{3,11},{4,12},{5,13},{6,14},{7,15},{8,0},{9,1},... | collective-permute-start | bytes 442376 | tf_op jit(solution)/shard_map/cond/branch_1_fun/ppermute | solution.py:854
  158.2 17.1 %collective-permute-start.23 = (bf16[96,6144]{1,0:T(8,128)(2,1)}, bf16[96,6144]{1,0:T(8,128)(2,1)}, u32[]{:S(2)}, u32[]{:S(2)}) collective-permute-start(bf16[96,6144]{1,0:T(8,128)(2,1)} %get-tuple-element.483), channel_id=1, source_target_pairs={{0,4},{1,5},{2,6},{3,7},{4,0},{5,1},{6,2},{7,3},{8,12},{9,13},{10,... | collective-permute-start | bytes 3538952 | tf_op jit(solution)/shard_map/cond/branch_1_fun/ppermute | solution.py:854
  158.2 17.1 %collective-permute-start.24 = (bf16[96,6144]{1,0:T(8,128)(2,1)}, bf16[96,6144]{1,0:T(8,128)(2,1)}, u32[]{:S(2)}, u32[]{:S(2)}) collective-permute-start(bf16[96,6144]{1,0:T(8,128)(2,1)} %get-tuple-element.484), channel_id=1, source_target_pairs={{0,4},{1,5},{2,6},{3,7},{4,0},{5,1},{6,2},{7,3},{8,12},{9,13},{10,... | collective-permute-start | bytes 3538952 | tf_op jit(solution)/shard_map/cond/branch_1_fun/ppermute | solution.py:854
  158.7 16.6 %collective-permute-start.21 = (bf16[48,6144]{1,0:T(8,128)(2,1)S(1)}, bf16[48,6144]{1,0:T(8,128)(2,1)}, u32[]{:S(2)}, u32[]{:S(2)}) collective-permute-start(bf16[48,6144]{1,0:T(8,128)(2,1)S(1)} %get-tuple-element.481), channel_id=1, source_target_pairs={{0,16},{1,17},{2,18},{3,19},{4,20},{5,21},{6,22},{7,23},{8,24},{9,... | collective-permute-start | bytes 1769480 | tf_op jit(solution)/shard_map/cond/branch_1_fun/ppermute | solution.py:854
  160.2 15.1 %collective-permute-start.22 = (bf16[48,6144]{1,0:T(8,128)(2,1)S(1)}, bf16[48,6144]{1,0:T(8,128)(2,1)}, u32[]{:S(2)}, u32[]{:S(2)}) collective-permute-start(bf16[48,6144]{1,0:T(8,128)(2,1)S(1)} %get-tuple-element.482), channel_id=1, source_target_pairs={{0,8},{1,9},{2,10},{3,11},{4,12},{5,13},{6,14},{7,15},{8,0},{9,1},... | collective-permute-start | bytes 1769480 | tf_op jit(solution)/shard_map/cond/branch_1_fun/ppermute | solution.py:854
  180.6 30.2 %collective-permute-start.28 = (bf16[384,3072]{1,0:T(8,128)(2,1)}, bf16[384,3072]{1,0:T(8,128)(2,1)}, u32[]{:S(2)}, u32[]{:S(2)}) collective-permute-start(bf16[384,3072]{1,0:T(8,128)(2,1)} %get-tuple-element.499), channel_id=1, source_target_pairs={{0,4},{1,5},{2,6},{3,7},{4,0},{5,1},{6,2},{7,3},{8,12},{9,13},{10,... | collective-permute-start | bytes 7077896 | tf_op jit(solution)/shard_map/cond/branch_1_fun/ppermute | solution.py:854
  180.8 30.0 %collective-permute-start.29 = (bf16[384,3072]{1,0:T(8,128)(2,1)}, bf16[384,3072]{1,0:T(8,128)(2,1)}, u32[]{:S(2)}, u32[]{:S(2)}) collective-permute-start(bf16[384,3072]{1,0:T(8,128)(2,1)} %get-tuple-element.500), channel_id=1, source_target_pairs={{0,4},{1,5},{2,6},{3,7},{4,0},{5,1},{6,2},{7,3},{8,12},{9,13},{10,... | collective-permute-start | bytes 7077896 | tf_op jit(solution)/shard_map/cond/branch_1_fun/ppermute | solution.py:854
  181.2 28.3 %collective-permute-start.25 = (bf16[96,6144]{1,0:T(8,128)(2,1)}, bf16[96,6144]{1,0:T(8,128)(2,1)}, u32[]{:S(2)}, u32[]{:S(2)}) collective-permute-start(bf16[96,6144]{1,0:T(8,128)(2,1)} %get-tuple-element.498), channel_id=1, source_target_pairs={{0,8},{1,9},{2,10},{3,11},{4,12},{5,13},{6,14},{7,15},{8,0},{9,1},... | collective-permute-start | bytes 3538952 | tf_op jit(solution)/shard_map/cond/branch_1_fun/ppermute | solution.py:854
  182.7 28.0 %collective-permute-start.26 = (bf16[96,6144]{1,0:T(8,128)(2,1)}, bf16[96,6144]{1,0:T(8,128)(2,1)}, u32[]{:S(2)}, u32[]{:S(2)}) collective-permute-start(bf16[96,6144]{1,0:T(8,128)(2,1)} %get-tuple-element.498), channel_id=1, source_target_pairs={{0,16},{1,17},{2,18},{3,19},{4,20},{5,21},{6,22},{7,23},{8,24},{9,... | collective-permute-start | bytes 3538952 | tf_op jit(solution)/shard_map/cond/branch_1_fun/ppermute | solution.py:854
  183.1 27.6 %collective-permute-start.27 = (bf16[96,6144]{1,0:T(8,128)(2,1)}, bf16[96,6144]{1,0:T(8,128)(2,1)}, u32[]{:S(2)}, u32[]{:S(2)}) collective-permute-start(bf16[96,6144]{1,0:T(8,128)(2,1)} %get-tuple-element.498), channel_id=1, source_target_pairs={{0,4},{1,5},{2,6},{3,7},{4,0},{5,1},{6,2},{7,3},{8,12},{9,13},{10,... | collective-permute-start | bytes 3538952 | tf_op jit(solution)/shard_map/cond/branch_1_fun/ppermute | solution.py:854
  213.1 22.6 %collective-permute-start.32 = (bf16[96,6144]{1,0:T(8,128)(2,1)}, bf16[96,6144]{1,0:T(8,128)(2,1)}, u32[]{:S(2)}, u32[]{:S(2)}) collective-permute-start(bf16[96,6144]{1,0:T(8,128)(2,1)} %get-tuple-element.525), channel_id=1, source_target_pairs={{0,4},{1,5},{2,6},{3,7},{4,0},{5,1},{6,2},{7,3},{8,12},{9,13},{10,... | collective-permute-start | bytes 3538952 | tf_op jit(solution)/shard_map/cond/branch_1_fun/ppermute | solution.py:854
  218.2 17.4 %collective-permute-start.33 = (bf16[96,6144]{1,0:T(8,128)(2,1)}, bf16[96,6144]{1,0:T(8,128)(2,1)}, u32[]{:S(2)}, u32[]{:S(2)}) collective-permute-start(bf16[96,6144]{1,0:T(8,128)(2,1)} %get-tuple-element.526), channel_id=1, source_target_pairs={{0,4},{1,5},{2,6},{3,7},{4,0},{5,1},{6,2},{7,3},{8,12},{9,13},{10,... | collective-permute-start | bytes 3538952 | tf_op jit(solution)/shard_map/cond/branch_1_fun/ppermute | solution.py:854
  218.2 17.4 %collective-permute-start.34 = (bf16[96,6144]{1,0:T(8,128)(2,1)}, bf16[96,6144]{1,0:T(8,128)(2,1)}, u32[]{:S(2)}, u32[]{:S(2)}) collective-permute-start(bf16[96,6144]{1,0:T(8,128)(2,1)} %get-tuple-element.527), channel_id=1, source_target_pairs={{0,4},{1,5},{2,6},{3,7},{4,0},{5,1},{6,2},{7,3},{8,12},{9,13},{10,... | collective-permute-start | bytes 3538952 | tf_op jit(solution)/shard_map/cond/branch_1_fun/ppermute | solution.py:854
  218.7 15.6 %collective-permute-start.30 = (bf16[48,6144]{1,0:T(8,128)(2,1)}, bf16[48,6144]{1,0:T(8,128)(2,1)}, u32[]{:S(2)}, u32[]{:S(2)}) collective-permute-start(bf16[48,6144]{1,0:T(8,128)(2,1)} %get-tuple-element.523), channel_id=1, source_target_pairs={{0,16},{1,17},{2,18},{3,19},{4,20},{5,21},{6,22},{7,23},{8,24},{9,... | collective-permute-start | bytes 1769480 | tf_op jit(solution)/shard_map/cond/branch_1_fun/ppermute | solution.py:854
  220.3 15.3 %collective-permute-start.31 = (bf16[48,6144]{1,0:T(8,128)(2,1)}, bf16[48,6144]{1,0:T(8,128)(2,1)}, u32[]{:S(2)}, u32[]{:S(2)}) collective-permute-start(bf16[48,6144]{1,0:T(8,128)(2,1)} %get-tuple-element.524), channel_id=1, source_target_pairs={{0,8},{1,9},{2,10},{3,11},{4,12},{5,13},{6,14},{7,15},{8,0},{9,1},... | collective-permute-start | bytes 1769480 | tf_op jit(solution)/shard_map/cond/branch_1_fun/ppermute | solution.py:854
  238.9 24.0 %collective-permute-start.37 = (bf16[384,3072]{1,0:T(8,128)(2,1)}, bf16[384,3072]{1,0:T(8,128)(2,1)}, u32[]{:S(2)}, u32[]{:S(2)}) collective-permute-start(bf16[384,3072]{1,0:T(8,128)(2,1)} %get-tuple-element.536), channel_id=1, source_target_pairs={{0,4},{1,5},{2,6},{3,7},{4,0},{5,1},{6,2},{7,3},{8,12},{9,13},{10,... | collective-permute-start | bytes 7077896 | tf_op jit(solution)/shard_map/cond/branch_1_fun/ppermute | solution.py:854
  239.0 23.9 %collective-permute-start.38 = (bf16[384,3072]{1,0:T(8,128)(2,1)}, bf16[384,3072]{1,0:T(8,128)(2,1)}, u32[]{:S(2)}, u32[]{:S(2)}) collective-permute-start(bf16[384,3072]{1,0:T(8,128)(2,1)} %get-tuple-element.537), channel_id=1, source_target_pairs={{0,4},{1,5},{2,6},{3,7},{4,0},{5,1},{6,2},{7,3},{8,12},{9,13},{10,... | collective-permute-start | bytes 7077896 | tf_op jit(solution)/shard_map/cond/branch_1_fun/ppermute | solution.py:854
  239.4 23.5 %collective-permute-start.35 = (bf16[96,6144]{1,0:T(8,128)(2,1)}, bf16[96,6144]{1,0:T(8,128)(2,1)}, u32[]{:S(2)}, u32[]{:S(2)}) collective-permute-start(bf16[96,6144]{1,0:T(8,128)(2,1)} %get-tuple-element.534), channel_id=1, source_target_pairs={{0,4},{1,5},{2,6},{3,7},{4,0},{5,1},{6,2},{7,3},{8,12},{9,13},{10,... | collective-permute-start | bytes 3538952 | tf_op jit(solution)/shard_map/cond/branch_1_fun/ppermute | solution.py:854
  239.5 23.4 %collective-permute-start.36 = (bf16[96,6144]{1,0:T(8,128)(2,1)}, bf16[96,6144]{1,0:T(8,128)(2,1)}, u32[]{:S(2)}, u32[]{:S(2)}) collective-permute-start(bf16[96,6144]{1,0:T(8,128)(2,1)} %get-tuple-element.535), channel_id=1, source_target_pairs={{0,4},{1,5},{2,6},{3,7},{4,0},{5,1},{6,2},{7,3},{8,12},{9,13},{10,... | collective-permute-start | bytes 3538952 | tf_op jit(solution)/shard_map/cond/branch_1_fun/ppermute | solution.py:854
  267.0 27.0 %collective-permute-start.39 = (bf16[48,6144]{1,0:T(8,128)(2,1)S(1)}, bf16[48,6144]{1,0:T(8,128)(2,1)}, u32[]{:S(2)}, u32[]{:S(2)}) collective-permute-start(bf16[48,6144]{1,0:T(8,128)(2,1)S(1)} %get-tuple-element.555), channel_id=1, source_target_pairs={{0,8},{1,9},{2,10},{3,11},{4,12},{5,13},{6,14},{7,15},{8,0},{9,1},... | collective-permute-start | bytes 1769480 | tf_op jit(solution)/shard_map/cond/branch_1_fun/ppermute | solution.py:854
  267.6 26.4 %collective-permute-start.40 = (bf16[48,6144]{1,0:T(8,128)(2,1)S(1)}, bf16[48,6144]{1,0:T(8,128)(2,1)}, u32[]{:S(2)}, u32[]{:S(2)}) collective-permute-start(bf16[48,6144]{1,0:T(8,128)(2,1)S(1)} %get-tuple-element.556), channel_id=1, source_target_pairs={{0,16},{1,17},{2,18},{3,19},{4,20},{5,21},{6,22},{7,23},{8,24},{9,... | collective-permute-start | bytes 1769480 | tf_op jit(solution)/shard_map/cond/branch_1_fun/ppermute | solution.py:854
  268.0 27.4 %collective-permute-start.41 = (bf16[48,6144]{1,0:T(8,128)(2,1)}, bf16[48,6144]{1,0:T(8,128)(2,1)}, u32[]{:S(2)}, u32[]{:S(2)}) collective-permute-start(bf16[48,6144]{1,0:T(8,128)(2,1)} %get-tuple-element.557), channel_id=1, source_target_pairs={{0,8},{1,9},{2,10},{3,11},{4,12},{5,13},{6,14},{7,15},{8,0},{9,1},... | collective-permute-start | bytes 1769480 | tf_op jit(solution)/shard_map/cond/branch_1_fun/ppermute | solution.py:854
  269.5 26.0 %collective-permute-start.42 = (bf16[48,6144]{1,0:T(8,128)(2,1)}, bf16[48,6144]{1,0:T(8,128)(2,1)}, u32[]{:S(2)}, u32[]{:S(2)}) collective-permute-start(bf16[48,6144]{1,0:T(8,128)(2,1)} %get-tuple-element.558), channel_id=1, source_target_pairs={{0,16},{1,17},{2,18},{3,19},{4,20},{5,21},{6,22},{7,23},{8,24},{9,... | collective-permute-start | bytes 1769480 | tf_op jit(solution)/shard_map/cond/branch_1_fun/ppermute | solution.py:854
  300.0 27.8 %collective-permute-start.43 = (bf16[96,6144]{1,0:T(8,128)(2,1)}, bf16[96,6144]{1,0:T(8,128)(2,1)}, u32[]{:S(2)}, u32[]{:S(2)}) collective-permute-start(bf16[96,6144]{1,0:T(8,128)(2,1)} %get-tuple-element.573), channel_id=1, source_target_pairs={{0,8},{1,9},{2,10},{3,11},{4,12},{5,13},{6,14},{7,15},{8,0},{9,1},... | collective-permute-start | bytes 3538952 | tf_op jit(solution)/shard_map/cond/branch_1_fun/ppermute | solution.py:854
  301.7 27.2 %collective-permute-start.44 = (bf16[96,6144]{1,0:T(8,128)(2,1)}, bf16[96,6144]{1,0:T(8,128)(2,1)}, u32[]{:S(2)}, u32[]{:S(2)}) collective-permute-start(bf16[96,6144]{1,0:T(8,128)(2,1)} %get-tuple-element.574), channel_id=1, source_target_pairs={{0,16},{1,17},{2,18},{3,19},{4,20},{5,21},{6,22},{7,23},{8,24},{9,... | collective-permute-start | bytes 3538952 | tf_op jit(solution)/shard_map/cond/branch_1_fun/ppermute | solution.py:854
  333.1 33.3 %collective-permute-start.45 = (bf16[96,6144]{1,0:T(8,128)(2,1)}, bf16[96,6144]{1,0:T(8,128)(2,1)}, u32[]{:S(2)}, u32[]{:S(2)}) collective-permute-start(bf16[96,6144]{1,0:T(8,128)(2,1)} %get-tuple-element.605), channel_id=1, source_target_pairs={{0,8},{1,9},{2,10},{3,11},{4,12},{5,13},{6,14},{7,15},{8,0},{9,1},... | collective-permute-start | bytes 3538952 | tf_op jit(solution)/shard_map/cond/branch_1_fun/ppermute | solution.py:854
  333.7 32.7 %collective-permute-start.46 = (bf16[96,6144]{1,0:T(8,128)(2,1)}, bf16[96,6144]{1,0:T(8,128)(2,1)}, u32[]{:S(2)}, u32[]{:S(2)}) collective-permute-start(bf16[96,6144]{1,0:T(8,128)(2,1)} %get-tuple-element.606), channel_id=1, source_target_pairs={{0,16},{1,17},{2,18},{3,19},{4,20},{5,21},{6,22},{7,23},{8,24},{9,... | collective-permute-start | bytes 3538952 | tf_op jit(solution)/shard_map/cond/branch_1_fun/ppermute | solution.py:854
  334.4 32.0 %collective-permute-start.47 = (bf16[24,6144]{1,0:T(8,128)(2,1)S(1)}, bf16[24,6144]{1,0:T(8,128)(2,1)}, u32[]{:S(2)}, u32[]{:S(2)}) collective-permute-start(bf16[24,6144]{1,0:T(8,128)(2,1)S(1)} %get-tuple-element.607), channel_id=1, source_target_pairs={{0,1},{1,2},{2,3},{3,0},{4,5},{5,6},{6,7},{7,4},{8,9},{9,10},{10,1... | collective-permute-start | bytes 884744 | tf_op jit(solution)/shard_map/cond/branch_1_fun/ppermute | solution.py:854
  335.0 31.4 %collective-permute-start.48 = (bf16[24,6144]{1,0:T(8,128)(2,1)}, bf16[24,6144]{1,0:T(8,128)(2,1)}, u32[]{:S(2)}, u32[]{:S(2)}) collective-permute-start(bf16[24,6144]{1,0:T(8,128)(2,1)} %get-tuple-element.608), channel_id=1, source_target_pairs={{0,2},{1,3},{2,0},{3,1},{4,6},{5,7},{6,4},{7,5},{8,10},{9,11},{10,... | collective-permute-start | bytes 884744 | tf_op jit(solution)/shard_map/cond/branch_1_fun/ppermute | solution.py:854
  339.4 27.0 %collective-permute-start.49 = (bf16[24,6144]{1,0:T(8,128)(2,1)}, bf16[24,6144]{1,0:T(8,128)(2,1)}, u32[]{:S(2)}, u32[]{:S(2)}) collective-permute-start(bf16[24,6144]{1,0:T(8,128)(2,1)} %get-tuple-element.609), channel_id=1, source_target_pairs={{0,3},{1,0},{2,1},{3,2},{4,7},{5,4},{6,5},{7,6},{8,11},{9,8},{10,9... | collective-permute-start | bytes 884744 | tf_op jit(solution)/shard_map/cond/branch_1_fun/ppermute | solution.py:854
  383.5 13.5 %collective-permute-start.52 = (bf16[384,2304]{1,0:T(8,128)(2,1)}, bf16[384,2304]{1,0:T(8,128)(2,1)}, u32[]{:S(2)}, u32[]{:S(2)}) collective-permute-start(bf16[384,2304]{1,0:T(8,128)(2,1)} %get-tuple-element.628), channel_id=1, source_target_pairs={{0,4},{1,5},{2,6},{3,7},{4,0},{5,1},{6,2},{7,3},{8,12},{9,13},{10,... | collective-permute-start | bytes 5308424 | tf_op jit(solution)/shard_map/cond/branch_1_fun/ppermute | solution.py:854
  383.6 13.4 %collective-permute-start.53 = (bf16[48,896]{1,0:T(8,128)(2,1)S(1)}, bf16[48,896]{1,0:T(8,128)(2,1)}, u32[]{:S(2)}, u32[]{:S(2)}) collective-permute-start(bf16[48,896]{1,0:T(8,128)(2,1)S(1)} %get-tuple-element.629), channel_id=1, source_target_pairs={{0,8},{1,9},{2,10},{3,11},{4,12},{5,13},{6,14},{7,15},{8,0},{9,1},... | collective-permute-start | bytes 258056 | tf_op jit(solution)/shard_map/cond/branch_1_fun/ppermute | solution.py:854
  405.1 14.8 %collective-permute-start.63 = (bf16[24,6144]{1,0:T(8,128)(2,1)}, bf16[24,6144]{1,0:T(8,128)(2,1)}, u32[]{:S(2)}, u32[]{:S(2)}) collective-permute-start(bf16[24,6144]{1,0:T(8,128)(2,1)} %get-tuple-element.643), channel_id=1, source_target_pairs={{0,2},{1,3},{2,0},{3,1},{4,6},{5,7},{6,4},{7,5},{8,10},{9,11},{10,... | collective-permute-start | bytes 884744 | tf_op jit(solution)/shard_map/cond/branch_1_fun/ppermute | solution.py:854
  424.2 15.0 %collective-permute-start.64 = (bf16[96,2304]{1,0:T(8,128)(2,1)}, bf16[96,2304]{1,0:T(8,128)(2,1)}, u32[]{:S(2)}, u32[]{:S(2)}) collective-permute-start(bf16[96,2304]{1,0:T(8,128)(2,1)} %get-tuple-element.648), channel_id=1, source_target_pairs={{0,8},{1,9},{2,10},{3,11},{4,12},{5,13},{6,14},{7,15},{8,0},{9,1},... | collective-permute-start | bytes 1327112 | tf_op jit(solution)/shard_map/cond/branch_1_fun/ppermute | solution.py:854
  424.8 14.4 %collective-permute-start.65 = (bf16[96,2304]{1,0:T(8,128)(2,1)}, bf16[96,2304]{1,0:T(8,128)(2,1)}, u32[]{:S(2)}, u32[]{:S(2)}) collective-permute-start(bf16[96,2304]{1,0:T(8,128)(2,1)} %get-tuple-element.649), channel_id=1, source_target_pairs={{0,16},{1,17},{2,18},{3,19},{4,20},{5,21},{6,22},{7,23},{8,24},{9,... | collective-permute-start | bytes 1327112 | tf_op jit(solution)/shard_map/cond/branch_1_fun/ppermute | solution.py:854
  425.1 14.1 %collective-permute-start.66 = (bf16[24,896]{1,0:T(8,128)(2,1)S(1)}, bf16[24,896]{1,0:T(8,128)(2,1)}, u32[]{:S(2)}, u32[]{:S(2)}) collective-permute-start(bf16[24,896]{1,0:T(8,128)(2,1)S(1)} %get-tuple-element.650), channel_id=1, source_target_pairs={{0,1},{1,2},{2,3},{3,0},{4,5},{5,6},{6,7},{7,4},{8,9},{9,10},{10,1... | collective-permute-start | bytes 129032 | tf_op jit(solution)/shard_map/cond/branch_1_fun/ppermute | solution.py:854
  425.1 14.1 %collective-permute-start.67 = (bf16[24,896]{1,0:T(8,128)(2,1)S(1)}, bf16[24,896]{1,0:T(8,128)(2,1)}, u32[]{:S(2)}, u32[]{:S(2)}) collective-permute-start(bf16[24,896]{1,0:T(8,128)(2,1)S(1)} %get-tuple-element.651), channel_id=1, source_target_pairs={{0,2},{1,3},{2,0},{3,1},{4,6},{5,7},{6,4},{7,5},{8,10},{9,11},{10,... | collective-permute-start | bytes 129032 | tf_op jit(solution)/shard_map/cond/branch_1_fun/ppermute | solution.py:854
  426.8 12.4 %collective-permute-start.68 = (bf16[24,896]{1,0:T(8,128)(2,1)}, bf16[24,896]{1,0:T(8,128)(2,1)}, u32[]{:S(2)}, u32[]{:S(2)}) collective-permute-start(bf16[24,896]{1,0:T(8,128)(2,1)} %get-tuple-element.652), channel_id=1, source_target_pairs={{0,3},{1,0},{2,1},{3,2},{4,7},{5,4},{6,5},{7,6},{8,11},{9,8},{10,9... | collective-permute-start | bytes 129032 | tf_op jit(solution)/shard_map/cond/branch_1_fun/ppermute | solution.py:854
  (66 other events, 382.7 us)
Sparse Core Ops, SparseCore 0:
  28.2 30.8 all-gather.9
  61.3 29.5 all-gather.7
  92.4 29.5 all-gather.11
  123.5 29.5 all-gather.13
  154.5 29.5 all-gather.15
  185.5 29.5 all-gather.17
  216.6 29.5 all-gather.19
